TPU v7x, 32 devices: a whole 2x2x4 slice. The times are simulated.
32 devices in a mesh: seq: 8 (over y, x, core), fsdp: 4 (over z).
Axes of the slice: x: 2, y: 2, z: 4, core: 2. Of those that a mesh axis runs over, the one named last changes fastest.
Arguments:
- block_input: bfloat16 [4, 1024, 2048], P('fsdp', 'seq'), may hold values from -6 to 6
- d_output: bfloat16 [4, 1024, 2048], P('fsdp', 'seq'), may hold values from -6 to 6
- segment_ids: int32 [4, 1024], P('fsdp', 'seq'), may hold values from 0 to 2, as said below
- positions: int32 [4, 1024], P('fsdp', 'seq'), may hold values from 0 to 2047, as said below
- attention_gain: bfloat16 [2048], P('fsdp'), may hold values from 0.5 to 1.5
- query_weight: bfloat16 [2048, 2048], P(None, 'fsdp'), may hold values from -0.125 to 0.125
- key_weight: bfloat16 [2048, 1024], P(None, 'fsdp'), may hold values from -0.125 to 0.125
- value_weight: bfloat16 [2048, 1024], P(None, 'fsdp'), may hold values from -0.125 to 0.125
- output_gate_weight: bfloat16 [2048, 2048], P(None, 'fsdp'), may hold values from -0.125 to 0.125
- output_weight: bfloat16 [2048, 2048], P(None, 'fsdp'), may hold values from -2 to 2
- query_gain: bfloat16 [128], P('fsdp'), may hold values from 0.5 to 1.5
- key_gain: bfloat16 [128], P('fsdp'), may hold values from 0.5 to 1.5
- feedforward_gain: bfloat16 [2048], P('fsdp'), may hold values from 0.5 to 1.5
- gate_weight: bfloat16 [2048, 6144], P(None, 'fsdp'), may hold values from -0.125 to 0.125
- up_weight: bfloat16 [2048, 6144], P(None, 'fsdp'), may hold values from -0.125 to 0.125
- down_weight: bfloat16 [6144, 2048], P(None, 'fsdp'), may hold values from -0.078125 to 0.078125
Outputs:
- block_output: bfloat16 [4, 1024, 2048], P('fsdp', 'seq')
- input_gradient: float32 [4, 1024, 2048], P('fsdp', 'seq')
- attention_gain_gradient: float32 [2048], P(('seq', 'fsdp'))
- query_weight_gradient: float32 [2048, 2048], P(None, ('seq', 'fsdp'))
- key_weight_gradient: float32 [2048, 1024], P(None, ('seq', 'fsdp'))
- value_weight_gradient: float32 [2048, 1024], P(None, ('seq', 'fsdp'))
- output_gate_weight_gradient: float32 [2048, 2048], P(None, ('seq', 'fsdp'))
- output_weight_gradient: float32 [2048, 2048], P(None, ('seq', 'fsdp'))
- query_gain_gradient: float32 [128], P(('seq', 'fsdp'))
- key_gain_gradient: float32 [128], P(('seq', 'fsdp'))
- feedforward_gain_gradient: float32 [2048], P(('seq', 'fsdp'))
- gate_weight_gradient: float32 [2048, 6144], P(None, ('seq', 'fsdp'))
- up_weight_gradient: float32 [2048, 6144], P(None, ('seq', 'fsdp'))
- down_weight_gradient: float32 [6144, 2048], P(None, ('seq', 'fsdp'))
Inputs may be any that keep to these rules, and one draw needn't show every extreme that they name: `segment_ids`: in each sequence, segment 0 holds the first a tokens, segment 1 the middle and segment 2 the last b tokens, with 1 <= a, b <= 64 drawn for each sequence. Within a segment the positions rise by one. Segment 0 starts at 0, segment 1 ends at 2047, and segment 2 starts at a value drawn for each sequence below 1024.
All inputs are finite; a program needn't handle non-finite values.
Results may differ from a plain program's by a relative error of at most 0.02.
Values may be sent and summed in bfloat16 or wider, within the bound.
No kernel may reach another device: no remote copies, remote signals or barrier semaphores. Data moves between devices by JAX's collectives and lax.ppermute only.
A program may use at most 512 MiB of HBM per device.

v0:
```python
import jax
import jax.numpy as jnp
from jax import lax
from jax.sharding import PartitionSpec as P

BLOCK = 512


EPSILON = 1e-06
ROPE_BASE = 5000000.0
MASKED = -1e30


def rms_norm(values, gain_vector):
    return (
        values
        * lax.rsqrt(jnp.mean(values * values, axis=-1, keepdims=True) + EPSILON)
        * gain_vector
    )


def rotation_tables(positions, head_width):
    half_width = head_width // 2
    inverse = ROPE_BASE ** (-2.0 * jnp.arange(half_width, dtype=jnp.float32) / head_width)
    angles = positions.astype(jnp.float32)[:, None] * inverse[None, :]
    return (jnp.cos(angles)[:, None, :], jnp.sin(angles)[:, None, :])


def prepare_heads(values, gain_vector, cosine, sine_part):
    normed = rms_norm(values, gain_vector)
    half_width = values.shape[-1] // 2
    first_half = normed[..., :half_width]
    second_half = normed[..., half_width:]
    return jnp.concatenate(
        [
            first_half * cosine - second_half * sine_part,
            second_half * cosine + first_half * sine_part,
        ],
        axis=-1,
    )


def weight_term(left_side, right_side, shard_count):
    tokens_here, width = right_side.shape
    shaped = right_side.reshape(tokens_here, shard_count, width // shard_count)
    return jnp.einsum("tr,tgc->gcr", left_side, shaped, preferred_element_type=jnp.float32)


def gain_term(vector, shard_count):
    return vector.reshape(shard_count, -1)


def weight_whole(pieces):
    piece_count, piece_width, rows_count = pieces.shape
    return pieces.transpose(2, 0, 1).reshape(rows_count, piece_count * piece_width)


def gain_whole(pieces):
    return pieces.reshape(-1)


def key_slices(key_number, key_heads, value_heads, segments):
    key_start = key_number * BLOCK
    return (
        key_start,
        lax.dynamic_slice_in_dim(key_heads, key_start, BLOCK, 0),
        lax.dynamic_slice_in_dim(value_heads, key_start, BLOCK, 0),
        lax.dynamic_slice_in_dim(segments, key_start, BLOCK, 0),
    )


def block_scores(
    query_block, key_block, query_start, key_start, query_segments, key_segments, score_scale
):
    scores = (
        jnp.einsum("qhd,khd->hqk", query_block, key_block, preferred_element_type=jnp.float32)
        * score_scale
    )
    query_index = query_start + jnp.arange(BLOCK, dtype=jnp.int32)
    key_index = key_start + jnp.arange(BLOCK, dtype=jnp.int32)
    allowed = (key_index[None, :] <= query_index[:, None]) & (
        key_segments[None, :] == query_segments[:, None]
    )
    return (scores, allowed[None])


def attention_forward(query_heads, key_heads, value_heads, segments):
    length, head_count, head_width = query_heads.shape
    block_count = length // BLOCK
    score_scale = head_width ** (-0.5)

    def one_block(block_index):
        row_start = block_index * BLOCK
        query_block = lax.dynamic_slice_in_dim(query_heads, row_start, BLOCK, 0)
        query_segments = lax.dynamic_slice_in_dim(segments, row_start, BLOCK, 0)

        def stats_step(key_number, loop_state):
            running_max, running_sum = loop_state
            key_start, key_block, value_block, key_segments = key_slices(
                key_number, key_heads, value_heads, segments
            )
            scores, allowed = block_scores(
                query_block,
                key_block,
                row_start,
                key_start,
                query_segments,
                key_segments,
                score_scale,
            )
            new_max = jnp.maximum(running_max, jnp.max(jnp.where(allowed, scores, MASKED), axis=-1))
            weights = jnp.where(allowed, jnp.exp(scores - new_max[..., None]), 0.0)
            return (
                new_max,
                running_sum * jnp.exp(running_max - new_max) + jnp.sum(weights, axis=-1),
            )

        start_state = (
            jnp.full((head_count, BLOCK), MASKED, jnp.float32),
            jnp.zeros((head_count, BLOCK), jnp.float32),
        )
        running_max, running_sum = lax.fori_loop(0, block_index + 1, stats_step, start_state)
        log_total = running_max + jnp.log(running_sum)

        def output_step(key_number, running_total):
            key_start, key_block, value_block, key_segments = key_slices(
                key_number, key_heads, value_heads, segments
            )
            scores, allowed = block_scores(
                query_block,
                key_block,
                row_start,
                key_start,
                query_segments,
                key_segments,
                score_scale,
            )
            probability = jnp.where(allowed, jnp.exp(scores - log_total[..., None]), 0.0).astype(
                jnp.bfloat16
            )
            return running_total + jnp.einsum(
                "hqk,khd->qhd", probability, value_block, preferred_element_type=jnp.float32
            )

        mixed_block = lax.fori_loop(
            0, block_index + 1, output_step, jnp.zeros((BLOCK, head_count, head_width), jnp.float32)
        )
        return (mixed_block, log_total)

    mixed_blocks, log_blocks = lax.map(one_block, jnp.arange(block_count, dtype=jnp.int32))
    return (
        mixed_blocks.reshape(length, head_count, head_width),
        log_blocks.transpose(1, 0, 2).reshape(head_count, length),
    )


def attention_backward(
    query_heads, key_heads, value_heads, segments, log_total, mixed_grad, row_delta
):
    length, head_count, head_width = query_heads.shape
    block_count = length // BLOCK
    score_scale = head_width ** (-0.5)

    def query_step(block_index, loop_state):
        query_all, key_all, value_all = loop_state
        row_start = block_index * BLOCK
        query_block = lax.dynamic_slice_in_dim(query_heads, row_start, BLOCK, 0)
        query_segments = lax.dynamic_slice_in_dim(segments, row_start, BLOCK, 0)
        grad_block = lax.dynamic_slice_in_dim(mixed_grad, row_start, BLOCK, 0)
        block_log = lax.dynamic_slice_in_dim(log_total, row_start, BLOCK, 1)
        block_delta = lax.dynamic_slice_in_dim(row_delta, row_start, BLOCK, 1)

        def key_step(key_number, inner_state):
            query_part, key_acc, value_acc = inner_state
            key_start, key_block, value_block, key_segments = key_slices(
                key_number, key_heads, value_heads, segments
            )
            scores, allowed = block_scores(
                query_block,
                key_block,
                row_start,
                key_start,
                query_segments,
                key_segments,
                score_scale,
            )
            probability = jnp.where(allowed, jnp.exp(scores - block_log[..., None]), 0.0)
            value_piece = jnp.einsum(
                "hqk,qhd->khd",
                probability.astype(jnp.bfloat16),
                grad_block,
                preferred_element_type=jnp.float32,
            )
            prob_grad = jnp.einsum(
                "qhd,khd->hqk", grad_block, value_block, preferred_element_type=jnp.float32
            )
            score_grad = (probability * (prob_grad - block_delta[..., None])).astype(jnp.bfloat16)
            query_part = (
                query_part
                + jnp.einsum(
                    "hqk,khd->qhd", score_grad, key_block, preferred_element_type=jnp.float32
                )
                * score_scale
            )
            key_piece = (
                jnp.einsum(
                    "hqk,qhd->khd", score_grad, query_block, preferred_element_type=jnp.float32
                )
                * score_scale
            )
            key_acc = lax.dynamic_update_slice_in_dim(
                key_acc,
                lax.dynamic_slice_in_dim(key_acc, key_start, BLOCK, 0) + key_piece,
                key_start,
                0,
            )
            value_acc = lax.dynamic_update_slice_in_dim(
                value_acc,
                lax.dynamic_slice_in_dim(value_acc, key_start, BLOCK, 0) + value_piece,
                key_start,
                0,
            )
            return (query_part, key_acc, value_acc)

        start_part = jnp.zeros((BLOCK, head_count, head_width), jnp.float32)
        query_part, key_all, value_all = lax.fori_loop(
            0, block_index + 1, key_step, (start_part, key_all, value_all)
        )
        query_all = lax.dynamic_update_slice_in_dim(query_all, query_part, row_start, 0)
        return (query_all, key_all, value_all)

    zero_heads = jnp.zeros((length, head_count, head_width), jnp.float32)
    return lax.fori_loop(0, block_count, query_step, (zero_heads, zero_heads, zero_heads))


def local(
    block_input,
    d_output,
    segment_ids,
    positions,
    attention_gain,
    query_weight,
    key_weight,
    value_weight,
    output_gate_weight,
    output_weight,
    query_gain,
    key_gain,
    feedforward_gain,
    gate_weight,
    up_weight,
    down_weight,
):
    shard_count = lax.axis_size("seq") * lax.axis_size("fsdp")
    inputs = block_input[0].astype(jnp.float32)
    token_count = inputs.shape[0]
    (
        gain_one,
        query_full,
        key_full,
        value_full,
        gate_logit_full,
        output_full,
        query_gain_full,
        key_gain_full,
    ) = (
        lax.all_gather(attention_gain, "fsdp", axis=0, tiled=True),
        lax.all_gather(query_weight, "fsdp", axis=1, tiled=True),
        lax.all_gather(key_weight, "fsdp", axis=1, tiled=True),
        lax.all_gather(value_weight, "fsdp", axis=1, tiled=True),
        lax.all_gather(output_gate_weight, "fsdp", axis=1, tiled=True),
        lax.all_gather(output_weight, "fsdp", axis=1, tiled=True),
        lax.all_gather(query_gain, "fsdp", axis=0, tiled=True),
        lax.all_gather(key_gain, "fsdp", axis=0, tiled=True),
    )
    head_width = query_gain_full.shape[0]
    head_count = query_full.shape[1] // head_width
    kv_count = key_full.shape[1] // head_width
    group_size = head_count // kv_count
    cosine, sine_part = rotation_tables(positions[0], head_width)

    def head_prepare(values, gain_vector):
        return prepare_heads(values, gain_vector, cosine, sine_part)

    normed_float, norm_pull = jax.vjp(rms_norm, inputs, gain_one.astype(jnp.float32))
    normed = normed_float.astype(jnp.bfloat16)
    query_heads = jnp.dot(normed, query_full, preferred_element_type=jnp.float32).reshape(
        token_count, head_count, head_width
    )
    key_heads = jnp.dot(normed, key_full, preferred_element_type=jnp.float32).reshape(
        token_count, kv_count, head_width
    )
    value_heads = jnp.dot(normed, value_full, preferred_element_type=jnp.float32).reshape(
        token_count, kv_count, head_width
    )
    gate_logits = jnp.dot(normed, gate_logit_full, preferred_element_type=jnp.float32).astype(
        jnp.bfloat16
    )
    query_rot, query_pull = jax.vjp(head_prepare, query_heads, query_gain_full.astype(jnp.float32))
    key_rot, key_pull = jax.vjp(head_prepare, key_heads, key_gain_full.astype(jnp.float32))
    key_copies = jnp.repeat(key_rot.astype(jnp.bfloat16), group_size, axis=1)
    value_copies = jnp.repeat(value_heads.astype(jnp.bfloat16), group_size, axis=1)
    head_queries, head_keys, head_values, head_gates = (
        lax.all_to_all(
            query_rot.astype(jnp.bfloat16), "seq", split_axis=1, concat_axis=0, tiled=True
        ),
        lax.all_to_all(key_copies, "seq", split_axis=1, concat_axis=0, tiled=True),
        lax.all_to_all(value_copies, "seq", split_axis=1, concat_axis=0, tiled=True),
        lax.all_to_all(
            gate_logits.reshape(token_count, head_count, head_width),
            "seq",
            split_axis=1,
            concat_axis=0,
            tiled=True,
        ),
    )
    all_segments = lax.all_gather(segment_ids[0], "seq", axis=0, tiled=True)
    mixed_heads, log_total = attention_forward(head_queries, head_keys, head_values, all_segments)
    gate_open = jax.nn.sigmoid(head_gates.astype(jnp.float32))
    gated_heads = (mixed_heads * gate_open).astype(jnp.bfloat16)
    gated_tokens = lax.all_to_all(
        gated_heads, "seq", split_axis=0, concat_axis=1, tiled=True
    ).reshape(token_count, head_count * head_width)
    middle = inputs + jnp.dot(gated_tokens, output_full, preferred_element_type=jnp.float32)
    gain_two, gate_full, up_full, down_full = (
        lax.all_gather(feedforward_gain, "fsdp", axis=0, tiled=True),
        lax.all_gather(gate_weight, "fsdp", axis=1, tiled=True),
        lax.all_gather(up_weight, "fsdp", axis=1, tiled=True),
        lax.all_gather(down_weight, "fsdp", axis=1, tiled=True),
    )
    normed_two_float, norm_two_pull = jax.vjp(rms_norm, middle, gain_two.astype(jnp.float32))
    normed_two = normed_two_float.astype(jnp.bfloat16)
    gate_values = jnp.dot(normed_two, gate_full, preferred_element_type=jnp.float32)
    up_values = jnp.dot(normed_two, up_full, preferred_element_type=jnp.float32)
    gate_sigma = jax.nn.sigmoid(gate_values)
    silu_values = gate_values * gate_sigma
    hidden = (silu_values * up_values).astype(jnp.bfloat16)
    result = middle + jnp.dot(hidden, down_full, preferred_element_type=jnp.float32)
    block_output = result.astype(jnp.bfloat16)[None]
    cotangent = d_output[0].astype(jnp.float32)
    gain_again, gate_back, up_back, down_back = (
        lax.all_gather(feedforward_gain, "fsdp", axis=0, tiled=True),
        lax.all_gather(gate_weight, "fsdp", axis=1, tiled=True),
        lax.all_gather(up_weight, "fsdp", axis=1, tiled=True),
        lax.all_gather(down_weight, "fsdp", axis=1, tiled=True),
    )
    branch_grad = cotangent.astype(jnp.bfloat16)
    hidden_grad = jnp.dot(branch_grad, down_back.T, preferred_element_type=jnp.float32)
    gate_grad = (
        hidden_grad * up_values * gate_sigma * (1.0 + gate_values * (1.0 - gate_sigma))
    ).astype(jnp.bfloat16)
    up_grad = (hidden_grad * silu_values).astype(jnp.bfloat16)
    normed_two_grad = jnp.dot(gate_grad, gate_back.T, preferred_element_type=jnp.float32) + jnp.dot(
        up_grad, up_back.T, preferred_element_type=jnp.float32
    )
    middle_part, gain_two_grad = norm_two_pull(normed_two_grad)
    middle_grad = cotangent + middle_part
    feed_gain_parts, gate_parts, up_parts, down_parts = (
        lax.psum_scatter(
            gain_term(gain_two_grad, shard_count), ("seq", "fsdp"), scatter_dimension=0, tiled=True
        ),
        lax.psum_scatter(
            weight_term(normed_two, gate_grad, shard_count),
            ("seq", "fsdp"),
            scatter_dimension=0,
            tiled=True,
        ),
        lax.psum_scatter(
            weight_term(normed_two, up_grad, shard_count),
            ("seq", "fsdp"),
            scatter_dimension=0,
            tiled=True,
        ),
        lax.psum_scatter(
            weight_term(hidden, branch_grad, shard_count),
            ("seq", "fsdp"),
            scatter_dimension=0,
            tiled=True,
        ),
    )
    (
        gain_again_one,
        query_back,
        key_back,
        value_back,
        gate_logit_back,
        output_back,
        query_gain_again,
        key_gain_again,
    ) = (
        lax.all_gather(attention_gain, "fsdp", axis=0, tiled=True),
        lax.all_gather(query_weight, "fsdp", axis=1, tiled=True),
        lax.all_gather(key_weight, "fsdp", axis=1, tiled=True),
        lax.all_gather(value_weight, "fsdp", axis=1, tiled=True),
        lax.all_gather(output_gate_weight, "fsdp", axis=1, tiled=True),
        lax.all_gather(output_weight, "fsdp", axis=1, tiled=True),
        lax.all_gather(query_gain, "fsdp", axis=0, tiled=True),
        lax.all_gather(key_gain, "fsdp", axis=0, tiled=True),
    )
    attention_grad = middle_grad.astype(jnp.bfloat16)
    gated_grad = jnp.dot(attention_grad, output_back.T, preferred_element_type=jnp.float32).astype(
        jnp.bfloat16
    )
    head_gated_grad = lax.all_to_all(
        gated_grad.reshape(token_count, head_count, head_width),
        "seq",
        split_axis=1,
        concat_axis=0,
        tiled=True,
    ).astype(jnp.float32)
    mixed_grad = (head_gated_grad * gate_open).astype(jnp.bfloat16)
    gate_logit_grad = (head_gated_grad * mixed_heads * gate_open * (1.0 - gate_open)).astype(
        jnp.bfloat16
    )
    row_delta = jnp.sum(mixed_grad.astype(jnp.float32) * mixed_heads, axis=-1).T
    query_rot_grad, key_copy_grad, value_copy_grad = attention_backward(
        head_queries, head_keys, head_values, all_segments, log_total, mixed_grad, row_delta
    )
    back_queries, back_keys, back_values, back_gates = (
        lax.all_to_all(
            query_rot_grad.astype(jnp.bfloat16), "seq", split_axis=0, concat_axis=1, tiled=True
        ),
        lax.all_to_all(
            key_copy_grad.astype(jnp.bfloat16), "seq", split_axis=0, concat_axis=1, tiled=True
        ),
        lax.all_to_all(
            value_copy_grad.astype(jnp.bfloat16), "seq", split_axis=0, concat_axis=1, tiled=True
        ),
        lax.all_to_all(gate_logit_grad, "seq", split_axis=0, concat_axis=1, tiled=True),
    )
    key_sum = (
        back_keys.astype(jnp.float32)
        .reshape(token_count, kv_count, group_size, head_width)
        .sum(axis=2)
    )
    value_sum = (
        back_values.astype(jnp.float32)
        .reshape(token_count, kv_count, group_size, head_width)
        .sum(axis=2)
    )
    value_grad = value_sum.astype(jnp.bfloat16).reshape(token_count, kv_count * head_width)
    query_pre, query_gain_grad = query_pull(back_queries.astype(jnp.float32))
    key_pre, key_gain_grad = key_pull(key_sum)
    query_grad = query_pre.astype(jnp.bfloat16).reshape(token_count, head_count * head_width)
    key_grad = key_pre.astype(jnp.bfloat16).reshape(token_count, kv_count * head_width)
    logit_grad = back_gates.reshape(token_count, head_count * head_width)
    normed_grad = (
        jnp.dot(query_grad, query_back.T, preferred_element_type=jnp.float32)
        + jnp.dot(key_grad, key_back.T, preferred_element_type=jnp.float32)
        + jnp.dot(value_grad, value_back.T, preferred_element_type=jnp.float32)
        + jnp.dot(logit_grad, gate_logit_back.T, preferred_element_type=jnp.float32)
    )
    input_part, gain_one_grad = norm_pull(normed_grad)
    input_gradient = (middle_grad + input_part)[None]
    (
        gain_one_parts,
        query_parts,
        key_parts,
        value_parts,
        logit_parts,
        output_parts,
        query_gain_parts,
        key_gain_parts,
    ) = (
        lax.psum_scatter(
            gain_term(gain_one_grad, shard_count), ("seq", "fsdp"), scatter_dimension=0, tiled=True
        ),
        lax.psum_scatter(
            weight_term(normed, query_grad, shard_count),
            ("seq", "fsdp"),
            scatter_dimension=0,
            tiled=True,
        ),
        lax.psum_scatter(
            weight_term(normed, key_grad, shard_count),
            ("seq", "fsdp"),
            scatter_dimension=0,
            tiled=True,
        ),
        lax.psum_scatter(
            weight_term(normed, value_grad, shard_count),
            ("seq", "fsdp"),
            scatter_dimension=0,
            tiled=True,
        ),
        lax.psum_scatter(
            weight_term(normed, logit_grad, shard_count),
            ("seq", "fsdp"),
            scatter_dimension=0,
            tiled=True,
        ),
        lax.psum_scatter(
            weight_term(gated_tokens, attention_grad, shard_count),
            ("seq", "fsdp"),
            scatter_dimension=0,
            tiled=True,
        ),
        lax.psum_scatter(
            gain_term(query_gain_grad, shard_count),
            ("seq", "fsdp"),
            scatter_dimension=0,
            tiled=True,
        ),
        lax.psum_scatter(
            gain_term(key_gain_grad, shard_count), ("seq", "fsdp"), scatter_dimension=0, tiled=True
        ),
    )
    return (
        block_output,
        input_gradient,
        gain_whole(gain_one_parts),
        weight_whole(query_parts),
        weight_whole(key_parts),
        weight_whole(value_parts),
        weight_whole(logit_parts),
        weight_whole(output_parts),
        gain_whole(query_gain_parts),
        gain_whole(key_gain_parts),
        gain_whole(feed_gain_parts),
        weight_whole(gate_parts),
        weight_whole(up_parts),
        weight_whole(down_parts),
    )


def solution(mesh):
    return jax.shard_map(
        local,
        mesh=mesh,
        in_specs=(
            P("fsdp", "seq", None),
            P("fsdp", "seq", None),
            P("fsdp", "seq"),
            P("fsdp", "seq"),
            P("fsdp"),
            P(None, "fsdp"),
            P(None, "fsdp"),
            P(None, "fsdp"),
            P(None, "fsdp"),
            P(None, "fsdp"),
            P("fsdp"),
            P("fsdp"),
            P("fsdp"),
            P(None, "fsdp"),
            P(None, "fsdp"),
            P(None, "fsdp"),
        ),
        out_specs=(
            P("fsdp", "seq", None),
            P("fsdp", "seq", None),
            P(("seq", "fsdp")),
            P(None, ("seq", "fsdp")),
            P(None, ("seq", "fsdp")),
            P(None, ("seq", "fsdp")),
            P(None, ("seq", "fsdp")),
            P(None, ("seq", "fsdp")),
            P(("seq", "fsdp")),
            P(("seq", "fsdp")),
            P(("seq", "fsdp")),
            P(None, ("seq", "fsdp")),
            P(None, ("seq", "fsdp")),
            P(None, ("seq", "fsdp")),
        ),
        check_vma=False,
    )
```

profile of v0, /device:TPU:4, one launch (start us, length us, event | category | flops | bytes accessed | tf_op | source)
XLA Modules:
  0.0 4793.0 jit_solution(2776703835815865858)
XLA Ops:
  12.7 12.2 all-gather.1
  26.7 22.0 all-reduce.11
  49.2 42.5 all-gather.14.cloned.1.call-done
  91.7 6.5 copy.116
  107.7 64.3 %all-gather.16.cloned.1.call-done = bf16[2048,1024]{1,0:T(8,128)(2,1)} async-done(((bf16[2048,256]{1,0:T(8,128)(2,1)}), bf16[2048,1024]{1,0:T(8,128)(2,1)}) %all-gather.16.cloned.1.call-update) | async-done | bytes 4194320 | tf_op jit(solution)/shard_map/all_gather | solution.py:270
  172.0 6.5 copy.119
  188.0 11.2 all-gather
  200.3 121.1 %all-gather.12.cloned.1.call-done = bf16[2048,2048]{1,0:T(8,128)(2,1)} async-done(((bf16[2048,512]{1,0:T(8,128)(2,1)}), bf16[2048,2048]{1,0:T(8,128)(2,1)}) %all-gather.12.cloned.1.call-update) | async-done | bytes 8388624 | tf_op jit(solution)/shard_map/all_gather | solution.py:268
  321.4 12.6 copy.114
  334.0 6.0 multiply_reduce_fusion.5
  346.5 124.2 %all-gather.18.cloned.1.call-done = bf16[2048,2048]{1,0:T(8,128)(2,1)} async-done(((bf16[2048,512]{1,0:T(8,128)(2,1)}), bf16[2048,2048]{1,0:T(8,128)(2,1)}) %all-gather.18.cloned.1.call-update) | async-done | bytes 8388624 | tf_op jit(solution)/shard_map/all_gather | solution.py:271
  476.4 14.2 all-to-all-start.3
  491.6 19.0 while.83
  519.9 12.1 all-gather.2
  533.2 87.0 %all-gather.20.cloned.1.call-done = bf16[2048,2048]{1,0:T(8,128)(2,1)} async-done(((bf16[2048,512]{1,0:T(8,128)(2,1)}), bf16[2048,2048]{1,0:T(8,128)(2,1)}) %all-gather.20.cloned.1.call-update) | async-done | bytes 8388624 | tf_op jit(solution)/shard_map/all_gather | solution.py:272
  625.1 419.8 %all-gather.22.cloned.1.call-done = bf16[2048,6144]{1,0:T(8,128)(2,1)} async-done(((bf16[2048,1536]{1,0:T(8,128)(2,1)}), bf16[2048,6144]{1,0:T(8,128)(2,1)}) %all-gather.22.cloned.1.call-update) | async-done | bytes 25165840 | tf_op jit(solution)/shard_map/all_gather | solution.py:327
  1044.9 14.5 fusion.100
  1059.4 410.5 %all-gather.24.cloned.1.call-done = bf16[2048,6144]{1,0:T(8,128)(2,1)} async-done(((bf16[2048,1536]{1,0:T(8,128)(2,1)}), bf16[2048,6144]{1,0:T(8,128)(2,1)}) %all-gather.24.cloned.1.call-update) | async-done | bytes 25165840 | tf_op jit(solution)/shard_map/all_gather | solution.py:328
  1469.9 14.5 fusion.101
  1484.4 410.5 %all-gather.26.cloned.1.call-done = bf16[6144,2048]{1,0:T(8,128)(2,1)} async-done(((bf16[6144,512]{1,0:T(8,128)(2,1)}), bf16[6144,2048]{1,0:T(8,128)(2,1)}) %all-gather.26.cloned.1.call-update) | async-done | bytes 25165840 | tf_op jit(solution)/shard_map/all_gather | solution.py:329
  1894.9 16.8 multiply_convert_fusion
  1911.7 14.3 fusion.102
  1926.0 14.6 multiply_reduce_fusion
  1941.0 6.5 fusion.48
  1954.5 6.5 all-to-all-done.5
  1967.4 21.1 while.85
  1977.9 9.5 while.88
  1989.5 12.3 all_to_all.129
  2012.1 13.9 all_to_all.132
  2034.0 8.1 fusion.105
  2043.1 13.9 all_to_all.130
  2059.2 8.3 fusion.93
  2068.5 14.6 all_to_all.131
  2083.5 8.3 fusion.87
  2093.9 19.6 fusion.70
  2115.5 19.6 fusion.68
  2136.7 19.7 fusion.72
  2157.7 11.1 fusion.40
  2168.7 6.5 fusion.103
  2176.8 6.5 fusion.104
  2186.5 42.1 all-reduce.10
  2232.4 147.0 %reduce-scatter.13.cloned.1.call-done = f32[1,32,2048]{2,1,0:T(8,128)} async-done(((f32[32,32,2048]{2,1,0:T(8,128)}), f32[1,32,2048]{2,1,0:T(8,128)}) %reduce-scatter.13.cloned.1.call-update) | async-done | bytes 262160 | tf_op jit(solution)/shard_map/reduce_scatter | solution.py:480
  2379.4 364.7 %reduce-scatter.17.cloned.1.call-done = f32[1,64,2048]{2,1,0:T(8,128)} async-done(((f32[32,64,2048]{2,1,0:T(8,128)}), f32[1,64,2048]{2,1,0:T(8,128)}) %reduce-scatter.17.cloned.1.call-update) | async-done | bytes 524304 | tf_op jit(solution)/shard_map/reduce_scatter | solution.py:492
  2744.1 364.9 %reduce-scatter.9.cloned.1.call-done = f32[1,64,2048]{2,1,0:T(8,128)} async-done(((f32[32,64,2048]{2,1,0:T(8,128)}), f32[1,64,2048]{2,1,0:T(8,128)}) %reduce-scatter.9.cloned.1.call-update) | async-done | bytes 524304 | tf_op jit(solution)/shard_map/reduce_scatter | solution.py:468
  3109.0 365.0 %reduce-scatter.15.cloned.1.call-done = f32[1,64,2048]{2,1,0:T(8,128)} async-done(((f32[32,64,2048]{2,1,0:T(8,128)}), f32[1,64,2048]{2,1,0:T(8,128)}) %reduce-scatter.15.cloned.1.call-update) | async-done | bytes 524304 | tf_op jit(solution)/shard_map/reduce_scatter | solution.py:486
  3474.0 437.2 %reduce-scatter.19.cloned.1.call-done = f32[1,192,2048]{2,1,0:T(8,128)} async-done(((f32[32,192,2048]{2,1,0:T(8,128)}), f32[1,192,2048]{2,1,0:T(8,128)}) %reduce-scatter.19.cloned.1.call-update) | async-done | bytes 1572880 | tf_op jit(solution)/shard_map/reduce_scatter | solution.py:362
  3911.2 437.5 %reduce-scatter.21.cloned.1.call-done = f32[1,192,2048]{2,1,0:T(8,128)} async-done(((f32[32,192,2048]{2,1,0:T(8,128)}), f32[1,192,2048]{2,1,0:T(8,128)}) %reduce-scatter.21.cloned.1.call-update) | async-done | bytes 1572880 | tf_op jit(solution)/shard_map/reduce_scatter | solution.py:368
  4348.7 437.5 %reduce-scatter.23.cloned.1.call-done = f32[1,64,6144]{2,1,0:T(8,128)} async-done(((f32[32,64,6144]{2,1,0:T(8,128)}), f32[1,64,6144]{2,1,0:T(8,128)}) %reduce-scatter.23.cloned.1.call-update) | async-done | bytes 1572880 | tf_op jit(solution)/shard_map/reduce_scatter | solution.py:374
  (390 shorter events, 160.3 us)
Async XLA Ops:
  7.2 84.5 %all-gather.14.cloned.1.call-start = ((), (), s32[]{:S(2)}) async-start(), calls=%async_computation.19 | async-start | bytes 5242880 | tf_op jit(solution)/shard_map/all_gather | solution.py:269
  7.9 164.1 %all-gather.16.cloned.1.call-start = ((), (), s32[]{:S(2)}) async-start(), calls=%async_computation.20 | async-start | bytes 5242880 | tf_op jit(solution)/shard_map/all_gather | solution.py:270
  8.7 312.8 %all-gather.12.cloned.1.call-start = ((), (), s32[]{:S(2)}) async-start(), calls=%async_computation.18 | async-start | bytes 10485760 | tf_op jit(solution)/shard_map/all_gather | solution.py:268
  9.4 461.3 %all-gather.18.cloned.1.call-start = ((), (), s32[]{:S(2)}) async-start(), calls=%async_computation.21 | async-start | bytes 10485760 | tf_op jit(solution)/shard_map/all_gather | solution.py:271
  10.0 610.2 %all-gather.20.cloned.1.call-start = ((), (), s32[]{:S(2)}) async-start(), calls=%async_computation.22 | async-start | bytes 10485760 | tf_op jit(solution)/shard_map/all_gather | solution.py:272
  10.6 1034.4 %all-gather.22.cloned.1.call-start = ((), (), s32[]{:S(2)}) async-start(), calls=%async_computation.23 | async-start | bytes 31457280 | tf_op jit(solution)/shard_map/all_gather | solution.py:327
  11.1 1458.8 %all-gather.24.cloned.1.call-start = ((), (), s32[]{:S(2)}) async-start(), calls=%async_computation.24 | async-start | bytes 31457280 | tf_op jit(solution)/shard_map/all_gather | solution.py:328
  11.9 36.8 copy-start.2
  11.9 37.0 copy-start.76
  12.0 1882.9 %all-gather.26.cloned.1.call-start = ((), (), s32[]{:S(2)}) async-start(), calls=%async_computation.25 | async-start | bytes 31457280 | tf_op jit(solution)/shard_map/all_gather | solution.py:329
  24.9 445.8 %copy-start.41 = (f32[4,1,512]{2,1,0:T(1,128)}, f32[4,1,512]{2,1,0:T(1,128)S(1)}, u32[]{:S(2)}) copy-start(f32[4,1,512]{2,1,0:T(1,128)S(1)} %convert_element_type.269) | copy-start | bytes 24580
  48.7 53.5 %copy-start.62 = (f32[128]{0:T(128)}, f32[128]{0:T(128)S(1)}, u32[]{:S(2)}) copy-start(f32[128]{0:T(128)S(1)} %convert_element_type.212) | copy-start | bytes 1540
  48.9 49.3 %copy-start.71 = (f32[128]{0:T(128)}, f32[128]{0:T(128)S(1)}, u32[]{:S(2)}) copy-start(f32[128]{0:T(128)S(1)} %fusion.51) | copy-start | bytes 1540
  48.9 421.8 %copy-start.55 = (f32[128]{0:T(128)}, f32[128]{0:T(128)S(1)}, u32[]{:S(2)}) copy-start(f32[128]{0:T(128)S(1)} %fusion.84) | copy-start | bytes 1540
  49.2 292.1 %copy-start.43 = (f32[128,64]{0,1:T(8,128)}, f32[128,64]{0,1:T(8,128)S(1)}, u32[]{:S(2)}) copy-start(f32[128,64]{0,1:T(8,128)S(1)} %get-tuple-element.666) | copy-start | bytes 98308
  49.2 292.1 %copy-start.45 = (f32[128,64]{0,1:T(8,128)}, f32[128,64]{0,1:T(8,128)S(1)}, u32[]{:S(2)}) copy-start(f32[128,64]{0,1:T(8,128)S(1)} %get-tuple-element.667) | copy-start | bytes 98308
  102.1 76.4 %copy-start.18 = (f32[128,8,128]{0,2,1:T(8,128)}, f32[128,8,128]{0,2,1:T(8,128)S(1)}, u32[]{:S(2)}) copy-start(f32[128,8,128]{0,2,1:T(8,128)S(1)} %get-tuple-element.671) | copy-start | bytes 1572868
  102.1 76.4 %copy-start.57 = (f32[128,8]{0,1:T(8,128)}, f32[128,8]{0,1:T(8,128)S(1)}, u32[]{:S(2)}) copy-start(f32[128,8]{0,1:T(8,128)S(1)} %get-tuple-element.670) | copy-start | bytes 12292
  102.2 76.4 %copy-start.53 = (f32[128,8]{0,1:T(8,128)}, f32[128,8]{0,1:T(8,128)S(1)}, u32[]{:S(2)}) copy-start(f32[128,8]{0,1:T(8,128)S(1)} %fusion.79) | copy-start | bytes 12292
  103.5 79.4 %all-to-all-start.1 = ((bf16[128,16,128]{2,0,1:T(8,128)(2,1)}), bf16[128,16,128]{2,0,1:T(8,128)(2,1)S(1)}, u32[]{:S(2)}, u32[]{:S(2)}) async-start(bf16[128,16,128]{2,0,1:T(8,128)(2,1)} %bitcast.26), calls=%async_computation.1 | async-start | bytes 1048576 | tf_op jit(solution)/shard_map/all_to_all | solution.py:307
  183.7 15.5 all-to-all-start.2
  188.0 152.1 %copy-start.64 = (f32[128]{0:T(128)}, f32[128]{0:T(128)S(1)}, u32[]{:S(2)}) copy-start(f32[128]{0:T(128)S(1)} %convert_element_type.209) | copy-start | bytes 1540
  199.3 134.7 %copy-start = (bf16[8,128,2,128]{3,1,0,2:T(8,128)(2,1)}, bf16[8,128,2,128]{3,1,0,2:T(8,128)(2,1)S(1)}, u32[]{:S(2)}) copy-start(bf16[8,128,2,128]{3,1,0,2:T(8,128)(2,1)S(1)} %copy.120) | copy-start | bytes 1572868
  340.0 135.4 %copy-start.51 = (f32[128,16]{0,1:T(8,128)}, f32[128,16]{0,1:T(8,128)S(1)}, u32[]{:S(2)}) copy-start(f32[128,16]{0,1:T(8,128)S(1)} %get-tuple-element.668) | copy-start | bytes 24580
  340.1 135.4 %copy-start.49 = (f32[128,16]{0,1:T(8,128)}, f32[128,16]{0,1:T(8,128)S(1)}, u32[]{:S(2)}) copy-start(f32[128,16]{0,1:T(8,128)S(1)} %fusion.78) | copy-start | bytes 24580
  342.3 134.1 %all-to-all-start = ((bf16[128,16,128]{0,2,1:T(8,128)(2,1)}), bf16[128,16,128]{0,2,1:T(8,128)(2,1)S(1)}, u32[]{:S(2)}, u32[]{:S(2)}) async-start(bf16[128,16,128]{0,2,1:T(8,128)(2,1)} %pad_maximum_fusion), calls=%async_computation | async-start | bytes 1048576 | tf_op jit(solution)/shard_map/all_to_all | solution.py:304
  476.4 35.8 all-to-all-start.3
  515.7 16.3 all-to-all-start.4
  532.0 1408.7 %copy-start.47 = (f32[4,1,512]{2,1,0:T(1,128)}, f32[4,1,512]{2,1,0:T(1,128)S(1)}, u32[]{:S(2)}) copy-start(f32[4,1,512]{2,1,0:T(1,128)S(1)} %convert_element_type.270) | copy-start | bytes 24580
  624.9 1315.7 %copy-start.4 = (f32[128,2048]{1,0:T(8,128)}, f32[128,2048]{1,0:T(8,128)S(1)}, u32[]{:S(2)}) copy-start(f32[128,2048]{1,0:T(8,128)S(1)} %get-tuple-element.673) | copy-start | bytes 3145732
  624.9 1315.7 %copy-start.60 = (f32[128]{0:T(128)}, f32[128]{0:T(128)S(1)}, u32[]{:S(2)}) copy-start(f32[128]{0:T(128)S(1)} %fusion.85) | copy-start | bytes 1540
  625.1 844.8 %copy-start.10 = (bf16[128,2048]{1,0:T(8,128)(2,1)}, bf16[128,2048]{1,0:T(8,128)(2,1)S(1)}, u32[]{:S(2)}) copy-start(bf16[128,2048]{1,0:T(8,128)(2,1)S(1)} %multiply_convert_fusion.4) | copy-start | bytes 1572868
  1059.4 835.5 %copy-start.21 = (bf16[1,128,2048]{2,1,0:T(8,128)(2,1)S(1)}, bf16[1,128,2048]{2,1,0:T(8,128)(2,1)}, u32[]{:S(2)}) copy-start(bf16[1,128,2048]{2,1,0:T(8,128)(2,1)} %param.27) | copy-start | bytes 1572868
  1948.5 12.5 all-to-all-start.5
  1952.7 279.7 %reduce-scatter.11.cloned.1.call-start = ((), (), s32[]{:S(2)}) async-start(), calls=%async_computation.27 | async-start | bytes 8650752 | tf_op jit(solution)/shard_map/reduce_scatter | solution.py:474
  2009.8 369.6 %reduce-scatter.13.cloned.1.call-start = ((), (), s32[]{:S(2)}) async-start(), calls=%async_computation.28 | async-start | bytes 8650752 | tf_op jit(solution)/shard_map/reduce_scatter | solution.py:480
  2032.3 711.8 %reduce-scatter.17.cloned.1.call-start = ((), (), s32[]{:S(2)}) async-start(), calls=%async_computation.30 | async-start | bytes 17301504 | tf_op jit(solution)/shard_map/reduce_scatter | solution.py:492
  2042.2 1066.9 %reduce-scatter.9.cloned.1.call-start = ((), (), s32[]{:S(2)}) async-start(), calls=%async_computation.26 | async-start | bytes 17301504 | tf_op jit(solution)/shard_map/reduce_scatter | solution.py:468
  2067.5 1406.6 %reduce-scatter.15.cloned.1.call-start = ((), (), s32[]{:S(2)}) async-start(), calls=%async_computation.29 | async-start | bytes 17301504 | tf_op jit(solution)/shard_map/reduce_scatter | solution.py:486
  2091.9 1819.3 %reduce-scatter.19.cloned.1.call-start = ((), (), s32[]{:S(2)}) async-start(), calls=%async_computation.31 | async-start | bytes 51904512 | tf_op jit(solution)/shard_map/reduce_scatter | solution.py:362
  2113.6 2235.2 %reduce-scatter.21.cloned.1.call-start = ((), (), s32[]{:S(2)}) async-start(), calls=%async_computation.32 | async-start | bytes 51904512 | tf_op jit(solution)/shard_map/reduce_scatter | solution.py:368
  2135.2 2651.0 %reduce-scatter.23.cloned.1.call-start = ((), (), s32[]{:S(2)}) async-start(), calls=%async_computation.33 | async-start | bytes 51904512 | tf_op jit(solution)/shard_map/reduce_scatter | solution.py:374
  2183.4 46.2 copy-start.72
  2183.4 46.2 copy-start.13
  2183.4 46.2 copy-start.24
  2183.4 46.2 copy-start.48
  2183.5 46.2 copy-start.61
  2183.5 46.2 copy-start.68
  (52 other events, 377.6 us)
Sparse Core Ops, SparseCore 0:
  9.6 82.0 all-gather.13
  93.2 78.7 all-gather.15
  173.6 147.8 all-gather.11
  322.9 147.8 all-gather.17
  472.1 147.9 all-gather.19
  621.6 423.3 all-gather.21
  1046.5 423.3 all-gather.23
  1471.5 423.3 all-gather.25
  2009.9 182.1 reduce-scatter.10
  2194.8 184.5 reduce-scatter.12
  2382.3 361.7 reduce-scatter.16
  2746.8 362.1 reduce-scatter.8
  3111.9 362.1 reduce-scatter.14
  3480.9 430.2 reduce-scatter.18
  3918.1 430.6 reduce-scatter.20
  4355.6 430.6 reduce-scatter.22
where the time goes:
time: 4800 us; the launch traced here: 4790 us
  waiting for transfers between devices  4250 us (89%)
  matrix products  246 us (5%)
  blocking collectives  154 us (3%)
  local copies, waits for them, and re-layouts  72.4 us (2%)
    reduce_scatter x1, waiting for transfers between devices, local(): lax.psum_scatter(weight_term(hidden, branch_grad, shard_count), ('seq', '...  438 us
    reduce_scatter x1, waiting for transfers between devices, local(): lax.psum_scatter(weight_term(normed_two, up_grad, shard_count), ('seq', '...  438 us
    reduce_scatter x1, waiting for transfers between devices, local(): lax.psum_scatter(weight_term(normed_two, gate_grad, shard_count), ('seq',...  437 us
    all_gather x1, waiting for transfers between devices, local(): lax.all_gather(gate_weight, 'fsdp', axis=1, tiled=True)  420 us
    all_gather x1, waiting for transfers between devices, local(): lax.all_gather(down_weight, 'fsdp', axis=1, tiled=True)  410 us
    all_gather x1, waiting for transfers between devices, local(): lax.all_gather(up_weight, 'fsdp', axis=1, tiled=True)  410 us
    reduce_scatter x1, waiting for transfers between devices, local(): lax.psum_scatter(weight_term(normed, logit_grad, shard_count), ('seq', 'f...  365 us
    reduce_scatter x1, waiting for transfers between devices, local(): lax.psum_scatter(weight_term(normed, query_grad, shard_count), ('seq', 'f...  365 us
  transfers between devices with their start and end apart: 22, of which 16 were waited for; matrix products, arithmetic and copies ran while one was open for 5% of the time, Pallas kernels for 0%

commit v1 on v0

v1 whole, which is shorter than its diff:
```python
import functools

import jax
import jax.numpy as jnp
from jax import lax
from jax.experimental import pallas as pl
from jax.experimental.pallas import tpu as pltpu
from jax.sharding import PartitionSpec as P

EPSILON = 1e-06
ROPE_BASE = 5000000.0
AXES = ("seq", "fsdp")
LOW = jnp.bfloat16
WIDE = jnp.float32


def dot(left, right, left_dim=1, right_dim=0):
    return lax.dot_general(
        left, right, (((left_dim,), (right_dim,)), ((), ())), preferred_element_type=WIDE
    )


def rms_norm(values, gain_vector):
    return (
        values
        * lax.rsqrt(jnp.mean(values * values, axis=-1, keepdims=True) + EPSILON)
        * gain_vector
    )


def rotation_tables(positions, head_width):
    half_width = head_width // 2
    inverse = ROPE_BASE ** (-2.0 * jnp.arange(half_width, dtype=WIDE) / head_width)
    angles = positions.astype(WIDE)[:, None] * inverse[None, :]
    return (jnp.cos(angles)[:, None, :], jnp.sin(angles)[:, None, :])


def prepare_heads(values, gain_vector, cosine, sine_part):
    normed = rms_norm(values, gain_vector)
    half_width = values.shape[-1] // 2
    first_half = normed[..., :half_width]
    second_half = normed[..., half_width:]
    return jnp.concatenate(
        [
            first_half * cosine - second_half * sine_part,
            second_half * cosine + first_half * sine_part,
        ],
        axis=-1,
    )


def block_weights(query, key, row_info, column_info, score_scale):
    scores = dot(query, key, 1, 1) * score_scale
    allowed = (column_info[0:1, :] <= row_info[:, 0:1]) & (
        column_info[1:2, :] == row_info[:, 1:2]
    )
    return jnp.where(allowed, jnp.exp(scores), 0.0)


def forward_kernel(scale, q_ref, k_ref, v_ref, gate_ref, row_ref, column_ref, gated_ref, mixed_ref):
    weights = block_weights(q_ref[...], k_ref[...], row_ref[...], column_ref[...], scale)
    total = jnp.sum(weights, axis=1, keepdims=True)
    mixed = dot(weights.astype(LOW), v_ref[...]) / total
    mixed_ref[...] = mixed
    gated_ref[...] = (mixed * jax.nn.sigmoid(gate_ref[...].astype(WIDE))).astype(LOW)


def backward_kernel(
    scale,
    group,
    q_ref,
    k_ref,
    v_ref,
    gate_ref,
    mixed_ref,
    grad_ref,
    row_ref,
    column_ref,
    dq_ref,
    dgate_ref,
    dk_ref,
    dv_ref,
):
    first = (pl.program_id(1) == 0) & (lax.rem(pl.program_id(0), group) == 0)

    @pl.when(first)
    def _():
        dk_ref[...] = jnp.zeros_like(dk_ref)
        dv_ref[...] = jnp.zeros_like(dv_ref)

    query, key, value = q_ref[...], k_ref[...], v_ref[...]
    mixed = mixed_ref[...]
    gated_grad = grad_ref[...].astype(WIDE)
    gate_open = jax.nn.sigmoid(gate_ref[...].astype(WIDE))
    mixed_grad = (gated_grad * gate_open).astype(LOW)
    dgate_ref[...] = (gated_grad * mixed * gate_open * (1.0 - gate_open)).astype(LOW)
    delta = jnp.sum(mixed_grad.astype(WIDE) * mixed, axis=1, keepdims=True)
    weights = block_weights(query, key, row_ref[...], column_ref[...], scale)
    probability = weights * (1.0 / jnp.sum(weights, axis=1, keepdims=True))
    prob_grad = dot(mixed_grad, value, 1, 1)
    score_grad = (probability * (prob_grad - delta)).astype(LOW)
    dq_ref[...] = dot(score_grad, key) * scale
    dk_ref[...] += dot(score_grad, query, 0, 0) * scale
    dv_ref[...] += dot(probability.astype(LOW), mixed_grad, 0, 0)


def attention_specs(length, head_width, group, block):
    per_query = pl.BlockSpec((block, head_width), lambda h, i: (i, h))
    per_key = pl.BlockSpec((length, head_width), lambda h, i: (0, h // group))
    rows = pl.BlockSpec((block, 2), lambda h, i: (i, 0))
    columns = pl.BlockSpec((2, length), lambda h, i: (0, 0))
    return per_query, per_key, rows, columns


def attention_forward(queries, keys, values, gates, row_info, column_info, head_width):
    length, width = queries.shape
    heads = width // head_width
    group = width // keys.shape[1]
    block = min(256, length)
    per_query, per_key, rows, columns = attention_specs(length, head_width, group, block)
    return pl.pallas_call(
        functools.partial(forward_kernel, head_width ** (-0.5)),
        grid=(heads, length // block),
        in_specs=[per_query, per_key, per_key, per_query, rows, columns],
        out_specs=[per_query, per_query],
        out_shape=[
            jax.ShapeDtypeStruct((length, width), LOW),
            jax.ShapeDtypeStruct((length, width), WIDE),
        ],
        compiler_params=pltpu.CompilerParams(vmem_limit_bytes=40 * 1024 * 1024),
        cost_estimate=pl.CostEstimate(
            flops=4 * length * length * width,
            bytes_accessed=12 * length * width,
            transcendentals=length * length * heads,
        ),
    )(queries, keys, values, gates, row_info, column_info)


def attention_backward(
    queries, keys, values, gates, mixed, gated_grad, row_info, column_info, head_width
):
    length, width = queries.shape
    heads = width // head_width
    group = width // keys.shape[1]
    block = min(256, length)
    per_query, per_key, rows, columns = attention_specs(length, head_width, group, block)
    return pl.pallas_call(
        functools.partial(backward_kernel, head_width ** (-0.5), group),
        grid=(heads, length // block),
        in_specs=[
            per_query,
            per_key,
            per_key,
            per_query,
            per_query,
            per_query,
            rows,
            columns,
        ],
        out_specs=[per_query, per_query, per_key, per_key],
        out_shape=[
            jax.ShapeDtypeStruct((length, width), WIDE),
            jax.ShapeDtypeStruct((length, width), LOW),
            jax.ShapeDtypeStruct(keys.shape, WIDE),
            jax.ShapeDtypeStruct(keys.shape, WIDE),
        ],
        compiler_params=pltpu.CompilerParams(vmem_limit_bytes=40 * 1024 * 1024),
        cost_estimate=pl.CostEstimate(
            flops=10 * length * length * width,
            bytes_accessed=24 * length * width,
            transcendentals=length * length * heads,
        ),
    )(queries, keys, values, gates, mixed, gated_grad, row_info, column_info)


def local(
    block_input,
    d_output,
    segment_ids,
    positions,
    attention_gain,
    query_weight,
    key_weight,
    value_weight,
    output_gate_weight,
    output_weight,
    query_gain,
    key_gain,
    feedforward_gain,
    gate_weight,
    up_weight,
    down_weight,
):
    seq_count, plane_count = lax.axis_size("seq"), lax.axis_size("fsdp")
    column_count = seq_count // 2
    assert column_count == plane_count
    shard_count = seq_count * plane_count
    seq_index, plane = lax.axis_index("seq"), lax.axis_index("fsdp")
    column, core = seq_index // 2, seq_index % 2

    def send(value, move):
        pairs = []
        for q in range(column_count):
            for c in range(2):
                for f in range(plane_count):
                    q2, c2, f2 = move(q, c, f)
                    pairs.append(
                        ((2 * q + c) * plane_count + f, (2 * q2 + c2) * plane_count + f2)
                    )
        return lax.ppermute(value, AXES, pairs)

    def to_core(value):
        return send(value, lambda q, c, f: (q, 1 - c, f))

    def to_column(value, distance):
        return send(value, lambda q, c, f: (q ^ distance, c, f))

    def up(value, distance=1):
        return send(value, lambda q, c, f: (q, c, (f + distance) % plane_count))

    def behind(steps):
        return lax.rem(plane + plane_count - steps, plane_count)

    def ring(value):
        blocks = [value]
        for _ in range(plane_count - 1):
            blocks.append(up(blocks[-1]))
        return blocks

    def ring_sum(pieces):
        running = pieces[1]
        for i in range(1, plane_count):
            running = up(running.astype(LOW)).astype(WIDE) + pieces[
                (i + 1) % plane_count
            ].astype(WIDE)
        return running

    def plane_gather(value):
        blocks = []
        for distance in range(column_count):
            block = value if distance == 0 else to_column(value, distance)
            blocks += [block, to_core(block)]
        return jnp.concatenate(blocks, axis=0)

    def plane_sum(partial):
        shaped = partial.astype(LOW).reshape(column_count, 2, -1, partial.shape[1])
        total = None
        for distance in reversed(range(column_count)):
            piece = shaped[distance, 0].astype(WIDE) + to_core(shaped[distance, 1]).astype(WIDE)
            if distance:
                piece = to_column(piece.astype(LOW), distance).astype(WIDE)
            total = piece if total is None else total + piece
        return total

    def take(array, start, size, axis=0):
        return lax.dynamic_slice_in_dim(array, start, size, axis)

    inputs_low = block_input[0]
    inputs = inputs_low.astype(WIDE)
    token_count, width = inputs.shape
    cotangent_low = d_output[0].astype(LOW)
    cotangent = d_output[0].astype(WIDE)
    head_width = query_gain.shape[0] * plane_count
    query_width = query_weight.shape[1] // 2
    kv_half = key_weight.shape[1] // 2
    key_width = max(head_width, kv_half)
    sharing = key_width // kv_half

    gathered_inputs = plane_gather(inputs_low)
    numbers = lax.all_gather(
        jnp.concatenate([segment_ids, positions], axis=0), "seq", axis=0, tiled=False
    )
    gains = jnp.concatenate([attention_gain, feedforward_gain, query_gain, key_gain])
    gain_parts = lax.all_gather(gains, "fsdp", axis=0, tiled=False).astype(WIDE)
    shard_width = attention_gain.shape[0]
    head_shard = query_gain.shape[0]
    gain_one = gain_parts[:, :shard_width].reshape(-1)
    gain_two = gain_parts[:, shard_width : 2 * shard_width].reshape(-1)
    query_gain_full = gain_parts[:, 2 * shard_width : 2 * shard_width + head_shard].reshape(-1)
    key_gain_full = gain_parts[:, 2 * shard_width + head_shard :].reshape(-1)

    row_chunk = width // column_count

    def head_weight(chunk):
        shards = jnp.stack(ring(chunk))
        result = jnp.zeros((width, chunk.shape[1]), LOW)
        for distance in range(column_count):
            target = column ^ distance
            piece = lax.dynamic_index_in_dim(
                shards, lax.rem(plane + plane_count - target, plane_count), 0, keepdims=False
            )
            if distance:
                piece = to_column(piece, distance)
            result = lax.dynamic_update_slice_in_dim(result, piece, target * row_chunk, 0)
        return result

    def my_chunk(weight, block_width):
        start = core * block_width if 2 * block_width <= weight.shape[1] else 0
        return lax.dynamic_slice(weight, (column * row_chunk, start), (row_chunk, block_width))

    key_value_weights = head_weight(
        jnp.concatenate([my_chunk(key_weight, key_width), my_chunk(value_weight, key_width)], axis=1)
    )
    key_weights = key_value_weights[:, :key_width]
    value_weights = key_value_weights[:, key_width:]
    query_weights = head_weight(my_chunk(query_weight, query_width))
    logit_weights = head_weight(my_chunk(output_gate_weight, query_width))

    output_columns = output_weight.shape[1]
    output_rows = jnp.zeros((query_width, width), LOW)
    for i, block in enumerate(ring(take(output_weight, seq_index * query_width, query_width))):
        output_rows = lax.dynamic_update_slice_in_dim(
            output_rows, block, behind(i) * output_columns, 1
        )

    hidden_width = gate_weight.shape[1] // 2
    gate_half = take(gate_weight, core * hidden_width, hidden_width, 1)
    up_half = take(up_weight, core * hidden_width, hidden_width, 1)
    down_chunk = hidden_width // column_count
    down_columns = down_weight.shape[1]
    down_piece = jnp.zeros((down_chunk, width), LOW)
    for distance in range(plane_count):
        target = lax.rem(plane + distance, plane_count)
        block = take(
            down_weight,
            (target * 2 + core) * hidden_width + column * down_chunk,
            down_chunk,
        )
        if distance:
            block = up(block, distance)
        down_piece = lax.dynamic_update_slice_in_dim(
            down_piece, block, behind(distance) * down_columns, 1
        )
    down_rows = jnp.zeros((hidden_width, width), LOW)
    for distance in range(column_count):
        block = to_column(down_piece, distance) if distance else down_piece
        down_rows = lax.dynamic_update_slice_in_dim(
            down_rows, block, (column ^ distance) * down_chunk, 0
        )
    cotangent_blocks = [
        jnp.concatenate([block, to_core(block)], axis=0) for block in ring(cotangent_low)
    ]

    order = [2 * (column ^ d) + (core ^ e) for d in range(column_count) for e in range(2)]
    ordered = jnp.stack(
        [lax.dynamic_index_in_dim(numbers, place, 0, keepdims=False) for place in order], axis=1
    )
    token_index = jnp.concatenate(
        [place * token_count + jnp.arange(token_count, dtype=jnp.int32) for place in order]
    )
    segments = ordered[0].reshape(-1)
    column_info = jnp.stack([token_index, segments])
    row_info = column_info.T
    cosine, sine_part = rotation_tables(ordered[1].reshape(-1), head_width)
    length = token_index.shape[0]

    def head_prepare(values, gain_vector):
        return prepare_heads(values, gain_vector, cosine, sine_part)

    gathered_wide = gathered_inputs.astype(WIDE)
    scale_one = lax.rsqrt(jnp.mean(gathered_wide * gathered_wide, axis=-1, keepdims=True) + EPSILON)
    normed = (gathered_wide * scale_one * gain_one).astype(LOW)
    query_heads = dot(normed, query_weights).reshape(length, -1, head_width)
    key_heads = dot(normed, key_weights).reshape(length, -1, head_width)
    values = dot(normed, value_weights).astype(LOW)
    gate_logits = dot(normed, logit_weights).astype(LOW)
    query_rot, query_pull = jax.vjp(head_prepare, query_heads, query_gain_full)
    key_rot, key_pull = jax.vjp(head_prepare, key_heads, key_gain_full)
    queries = query_rot.astype(LOW).reshape(length, -1)
    keys = key_rot.astype(LOW).reshape(length, -1)
    gated, mixed = attention_forward(
        queries, keys, values, gate_logits, row_info, column_info, head_width
    )
    middle = inputs + plane_sum(dot(gated, output_rows))

    scale_two = lax.rsqrt(jnp.mean(middle * middle, axis=-1, keepdims=True) + EPSILON)
    normed_two = (middle * scale_two * gain_two).astype(LOW)
    hidden_blocks, gate_grads, up_grads, normed_two_blocks, grad_pieces = [], [], [], [], []
    out_pieces = []
    for i, block in enumerate(ring(normed_two)):
        block = jnp.concatenate([block, to_core(block)], axis=0)
        gate_values = dot(block, gate_half)
        up_values = dot(block, up_half)
        gate_sigma = jax.nn.sigmoid(gate_values)
        silu_values = gate_values * gate_sigma
        hidden = (silu_values * up_values).astype(LOW)
        hidden_grad = dot(cotangent_blocks[i], down_rows, 1, 1)
        gate_grad = (
            hidden_grad * up_values * gate_sigma * (1.0 + gate_values * (1.0 - gate_sigma))
        ).astype(LOW)
        up_grad = (hidden_grad * silu_values).astype(LOW)
        partial = (dot(gate_grad, gate_half, 1, 1) + dot(up_grad, up_half, 1, 1)).astype(LOW)
        grad_pieces.append(
            partial[:token_count].astype(WIDE) + to_core(partial[token_count:]).astype(WIDE)
        )
        normed_two_blocks.append(block)
        hidden_blocks.append(hidden)
        gate_grads.append(gate_grad)
        up_grads.append(up_grad)
        out_partial = dot(hidden, down_rows).astype(LOW)
        out_pieces.append(
            out_partial[:token_count].astype(WIDE) + to_core(out_partial[token_count:]).astype(WIDE)
        )
    normed_two_grad = ring_sum(grad_pieces)
    block_output = (middle + ring_sum(out_pieces)).astype(LOW)[None]

    weighted = gain_two * normed_two_grad
    middle_grad = (
        cotangent
        + scale_two * weighted
        - middle * (scale_two**3) * jnp.mean(middle * weighted, axis=-1, keepdims=True)
    )
    feedforward_gain_terms = jnp.sum(normed_two_grad * (middle * scale_two), axis=0)
    attention_grad_local = middle_grad.astype(LOW)

    all_normed_two = jnp.concatenate(normed_two_blocks, axis=0)
    all_hidden = jnp.concatenate(hidden_blocks, axis=0)
    all_cotangent = jnp.concatenate(cotangent_blocks, axis=0)

    def columns_sum(pieces, piece_of):
        total = None
        for distance in reversed(range(column_count)):
            piece = lax.dynamic_index_in_dim(
                pieces, piece_of(column ^ distance), 0, keepdims=False
            )
            piece = to_column(piece, distance) if distance else piece
            total = piece.astype(WIDE) if total is None else total + piece.astype(WIDE)
        return total.astype(LOW)

    def column_block_gradient(grads):
        pieces = dot(jnp.concatenate(grads, axis=0), all_normed_two, 0, 0).astype(LOW)
        pieces = pieces.reshape(plane_count, -1, width)
        mine = columns_sum(pieces, lambda q: lax.rem(plane + q, plane_count))
        moved = send(mine, lambda q, c, f: (q, c, (f + q) % plane_count))
        moved = send(moved, lambda q, c, f: ((f - q) % plane_count, c, f))
        return moved.astype(WIDE).T

    down_terms = dot(all_cotangent, all_hidden, 0, 0).astype(LOW)
    down_mine = columns_sum(down_terms.reshape(column_count, -1, hidden_width), lambda q: q)
    down_mine = down_mine.reshape(2, plane_count, -1, hidden_width)
    own_half = lax.dynamic_index_in_dim(down_mine, core, 0, keepdims=False)
    other_half = to_core(lax.dynamic_index_in_dim(down_mine, 1 - core, 0, keepdims=False))
    down_pair = jnp.where(
        core == 0,
        jnp.concatenate([own_half, other_half], axis=2),
        jnp.concatenate([other_half, own_half], axis=2),
    )
    down_result = jnp.zeros((down_pair.shape[1], plane_count * 2 * hidden_width), LOW)
    for distance in range(plane_count):
        block = lax.dynamic_index_in_dim(
            down_pair, lax.rem(plane + distance, plane_count), 0, keepdims=False
        )
        if distance:
            block = up(block, distance)
        down_result = lax.dynamic_update_slice_in_dim(
            down_result, block, behind(distance) * 2 * hidden_width, 1
        )
    down_gradient = down_result.astype(WIDE).T
    gate_gradient = column_block_gradient(gate_grads)
    up_gradient = column_block_gradient(up_grads)

    attention_grad = plane_gather(attention_grad_local)
    gated_grad = dot(attention_grad, output_rows, 1, 1).astype(LOW)
    output_terms = dot(attention_grad, gated, 0, 0).astype(LOW)
    output_terms = output_terms.reshape(seq_count, plane_count, -1, query_width)
    output_mine = ring_sum(
        [
            lax.dynamic_index_in_dim(output_terms, behind(i), 1, keepdims=False)
            for i in range(plane_count)
        ]
    ).astype(LOW)
    output_spread = lax.all_to_all(output_mine, "seq", split_axis=0, concat_axis=0, tiled=True)
    output_gradient = (
        output_spread.astype(WIDE).transpose(0, 2, 1).reshape(-1, output_spread.shape[1])
    )
    query_rot_grad, logit_grad, key_rot_grad, value_sum = attention_backward(
        queries, keys, values, gate_logits, mixed, gated_grad, row_info, column_info, head_width
    )
    if sharing > 1:
        key_rot_grad = key_rot_grad + to_core(key_rot_grad)
        value_sum = value_sum + to_core(value_sum)
    query_pre, query_gain_grad = query_pull(query_rot_grad.reshape(length, -1, head_width))
    key_pre, key_gain_grad = key_pull(key_rot_grad.reshape(length, -1, head_width))
    query_grad = query_pre.astype(LOW).reshape(length, -1)
    key_grad = key_pre.astype(LOW).reshape(length, -1)
    value_grad = value_sum.astype(LOW)
    if sharing > 1:
        key_grad = take(key_grad, core * kv_half, kv_half, 1)
        value_grad = take(value_grad, core * kv_half, kv_half, 1)
        key_weights = take(key_weights, core * kv_half, kv_half, 1)
        value_weights = take(value_weights, core * kv_half, kv_half, 1)
    joined_grads = [query_grad, key_grad, value_grad, logit_grad]
    joined_weights = [query_weights, key_weights, value_weights, logit_weights]

    terms = [
        dot(part, normed, 0, 0).astype(LOW).reshape(plane_count, -1, width) for part in joined_grads
    ]
    sizes = [term.shape[1] for term in terms]
    attention_mine = ring_sum(
        [
            jnp.concatenate(
                [lax.dynamic_index_in_dim(term, behind(i), 0, keepdims=False) for term in terms],
                axis=0,
            )
            for i in range(plane_count)
        ]
    )
    attention_gradients, at = [], 0
    for size in sizes:
        attention_gradients.append(attention_mine[at : at + size].T)
        at += size

    normed_grad_partial = dot(
        jnp.concatenate(joined_grads, axis=1), jnp.concatenate(joined_weights, axis=1), 1, 1
    )
    attention_gain_terms = jnp.sum(normed_grad_partial * (gathered_wide * scale_one), axis=0)
    normed_grad = plane_sum(normed_grad_partial)
    weighted = gain_one * normed_grad
    own_scale = lax.rsqrt(jnp.mean(inputs * inputs, axis=-1, keepdims=True) + EPSILON)
    input_gradient = (
        middle_grad
        + own_scale * weighted
        - inputs * (own_scale**3) * jnp.mean(inputs * weighted, axis=-1, keepdims=True)
    )[None]

    place = seq_index * plane_count + plane

    def mine_of(vector):
        size = vector.shape[0] // shard_count
        return take(vector, place * size, size)

    feedforward_gain_total = lax.psum(feedforward_gain_terms, AXES)
    small = lax.psum(
        jnp.concatenate([attention_gain_terms, query_gain_grad, key_gain_grad / sharing]), AXES
    )
    query_gain_total = small[width : width + head_width]
    key_gain_total = small[width + head_width :]
    return (
        block_output,
        input_gradient,
        mine_of(small[:width]),
        *attention_gradients,
        output_gradient,
        mine_of(query_gain_total),
        mine_of(key_gain_total),
        mine_of(feedforward_gain_total),
        gate_gradient,
        up_gradient,
        down_gradient,
    )


def solution(mesh):
    whole = P(None, ("seq", "fsdp"))
    vector = P(("seq", "fsdp"))
    tokens = P("fsdp", "seq", None)
    weight = P(None, "fsdp")
    return jax.shard_map(
        local,
        mesh=mesh,
        in_specs=(
            tokens,
            tokens,
            P("fsdp", "seq"),
            P("fsdp", "seq"),
            P("fsdp"),
            weight,
            weight,
            weight,
            weight,
            weight,
            P("fsdp"),
            P("fsdp"),
            P("fsdp"),
            weight,
            weight,
            weight,
        ),
        out_specs=(
            tokens,
            tokens,
            vector,
            whole,
            whole,
            whole,
            whole,
            whole,
            vector,
            vector,
            vector,
            whole,
            whole,
            whole,
        ),
        check_vma=False,
    )
```

time: 4800 us -> 749 us (0.16)
  waiting for transfers between devices: 4250 us -> 356 us
  matrix products: 246 us -> 72.5 us
  blocking collectives: 154 us -> 70.4 us
  starting transfers between devices: 36.4 us -> 107 us
    reduce_scatter x8 -> x0, waiting for transfers between devices: 2550 us -> none  [the longest x1 438 us: local(): lax.psum_scatter(weight_term(hidden, branch_grad, shard_count), ('seq', '...]
    all_gather x8 -> x0, waiting for transfers between devices: 1680 us -> none  [the longest x1 420 us: local(): lax.all_gather(gate_weight, 'fsdp', axis=1, tiled=True)]
    ppermute x0 -> x106, waiting for transfers between devices: none -> 351 us  [send(): return lax.ppermute(value, AXES, pairs)]
    dot_general x44 -> x39, matrix products: 227 us -> 72.5 us  [dot(): lax.dot_general(left, right, (((left_dim,), (right_dim,)), ((), ())), pre...]
    ppermute x0 -> x106, starting transfers between devices: none -> 101 us  [send(): return lax.ppermute(value, AXES, pairs)]
    all_to_all x4 -> x0, blocking collectives: 54.7 us -> none  [the longest x1 14.6 us: local(): lax.all_to_all(gate_logit_grad, 'seq', split_axis=0, concat_axis=1, tiled...]
  transfers between devices with their start and end apart: 22 -> 107, of which waited for: 16 -> 39; matrix products, arithmetic and copies ran while one was open for 5% -> 24% of each run, Pallas kernels for 0% -> 2%
where the time goes in v1:
time: 749 us; the launch traced here: 741 us
  waiting for transfers between devices  356 us (48%)
  starting transfers between devices  107 us (14%)
  matrix products  72.5 us (10%)
  blocking collectives  70.4 us (9%)
  local copies, waits for them, and re-layouts  61 us (8%)
  other arithmetic  52.5 us (7%)
  Pallas kernels  16.2 us (2%)
    ppermute x106, waiting for transfers between devices, send(): return lax.ppermute(value, AXES, pairs)  351 us
    ppermute x106, starting transfers between devices, send(): return lax.ppermute(value, AXES, pairs)  101 us
    dot_general x39, matrix products, dot(): lax.dot_general(left, right, (((left_dim,), (right_dim,)), ((), ())), pre...  72.5 us
    psum x1, blocking collectives, local(): lax.psum(jnp.concatenate([attention_gain_terms, query_gain_grad, key_gain...  39.8 us
    unnamed x187, local copies, waits for them, and re-layouts  26.2 us
    unnamed x1, blocking collectives  22.8 us
  transfers between devices with their start and end apart: 107, of which 39 were waited for; matrix products, arithmetic and copies ran while one was open for 24% of the time, Pallas kernels for 2%

profile of v1, /device:TPU:4, one launch (start us, length us, event | category | flops | bytes accessed | tf_op | source)
XLA Modules:
  0.0 740.8 jit_solution(5266912712264975172)
XLA Ops:
  14.8 22.8 %all-reduce.4 = bf16[4352]{0:T(1024)(128)(2,1)S(1)} all-reduce(bf16[4352]{0:T(1024)(128)(2,1)S(1)} %dynamic-update-slice), channel_id=2, replica_groups=mesh['seq'=8,'fsdp'=4] {'fsdp'}, use_global_device_ids=true, to_apply=%add.4 | all-reduce | flops 4352 | bytes 17408
  40.1 7.9 %all-gather.2 = s32[8,2,128]{2,1,0:T(2,128)S(1)} all-gather(s32[1,2,128]{2,1,0:T(2,128)S(1)} %add_bitcast_fusion), channel_id=3, replica_groups=mesh['seq'=8,'fsdp'=4] {'seq'}, dimensions={0}, use_global_device_ids=true | all-gather | bytes 9216 | tf_op jit(solution)/shard_map/all_gather | solution.py:270
  54.4 4.1 collective-permute-start.8
  65.1 4.1 collective-permute-done.14
  71.2 9.3 %collective-permute-done.8 = bf16[512,256]{1,0:T(8,128)(2,1)S(1)} collective-permute-done((bf16[512,256]{1,0:T(8,128)(2,1)}, bf16[512,256]{1,0:T(8,128)(2,1)S(1)}, u32[]{:S(2)}, u32[]{:S(2)}) %collective-permute-start.8) | collective-permute-done | bytes 262176 | tf_op jit(solution)/shard_map/ppermute | solution.py:210
  82.0 4.1 collective-permute-done.20
  86.1 5.6 collective-permute-done.15
  92.9 4.4 collective-permute-done.9
  99.7 14.5 %collective-permute-done.21 = bf16[512,256]{1,0:T(8,128)(2,1)S(1)} collective-permute-done((bf16[512,256]{1,0:T(8,128)(2,1)S(1)}, bf16[512,256]{1,0:T(8,128)(2,1)S(1)}, u32[]{:S(2)}, u32[]{:S(2)}) %collective-permute-start.21) | collective-permute-done | bytes 262176 | tf_op jit(solution)/shard_map/ppermute | solution.py:210
  115.4 3.8 collective-permute-done.27
  126.7 12.7 %collective-permute-done.16 = bf16[512,256]{1,0:T(8,128)(2,1)S(1)} collective-permute-done((bf16[512,256]{1,0:T(8,128)(2,1)S(1)}, bf16[512,256]{1,0:T(8,128)(2,1)S(1)}, u32[]{:S(2)}, u32[]{:S(2)}) %collective-permute-start.16) | collective-permute-done | bytes 262176 | tf_op jit(solution)/shard_map/ppermute | solution.py:210
  143.1 10.1 %collective-permute-done.23 = bf16[512,256]{1,0:T(8,128)(2,1)S(1)} collective-permute-done((bf16[512,256]{1,0:T(8,128)(2,1)S(1)}, bf16[512,256]{1,0:T(8,128)(2,1)S(1)}, u32[]{:S(2)}, u32[]{:S(2)}) %collective-permute-start.23) | collective-permute-done | bytes 262176 | tf_op jit(solution)/shard_map/ppermute | solution.py:210
  157.6 6.5 collective-permute-done.24
  175.0 3.8 multiply_reduce_fusion.5
  181.3 5.5 shard_map.263
  210.6 15.4 %collective-permute-done.38 = bf16[192,512]{1,0:T(8,128)(2,1)S(1)} collective-permute-done((bf16[192,512]{1,0:T(8,128)(2,1)S(1)}, bf16[192,512]{1,0:T(8,128)(2,1)S(1)}, u32[]{:S(2)}, u32[]{:S(2)}) %collective-permute-start.38) | collective-permute-done | bytes 196640 | tf_op jit(solution)/shard_map/ppermute | solution.py:210
  230.2 4.5 collective-permute-done.33
  234.7 23.0 %collective-permute-done.31 = bf16[128,2048]{1,0:T(8,128)(2,1)S(1)} collective-permute-done((bf16[128,2048]{1,0:T(8,128)(2,1)S(1)}, bf16[128,2048]{1,0:T(8,128)(2,1)S(1)}, u32[]{:S(2)}, u32[]{:S(2)}) %collective-permute-start.31) | collective-permute-done | bytes 524320 | tf_op jit(solution)/shard_map/ppermute | solution.py:210
  260.3 6.9 collective-permute-done.40
  267.2 6.4 collective-permute-done.41
  281.2 9.5 %collective-permute-done.35 = bf16[128,2048]{1,0:T(8,128)(2,1)S(1)} collective-permute-done((bf16[128,2048]{1,0:T(8,128)(2,1)S(1)}, bf16[128,2048]{1,0:T(8,128)(2,1)S(1)}, u32[]{:S(2)}, u32[]{:S(2)}) %collective-permute-start.35) | collective-permute-done | bytes 524320 | tf_op jit(solution)/shard_map/ppermute | solution.py:210
  302.8 5.2 collective-permute-done.45
  317.0 8.4 %collective-permute-done.49 = bf16[128,2048]{1,0:T(8,128)(2,1)S(1)} collective-permute-done((bf16[128,2048]{1,0:T(8,128)(2,1)S(1)}, bf16[128,2048]{1,0:T(8,128)(2,1)S(1)}, u32[]{:S(2)}, u32[]{:S(2)}) %collective-permute-start.49) | collective-permute-done | bytes 524320 | tf_op jit(solution)/shard_map/ppermute | solution.py:210
  337.1 10.8 %collective-permute-done.58 = bf16[128,2048]{1,0:T(8,128)(2,1)S(1)} collective-permute-done((bf16[128,2048]{1,0:T(8,128)(2,1)S(1)}, bf16[128,2048]{1,0:T(8,128)(2,1)S(1)}, u32[]{:S(2)}, u32[]{:S(2)}) %collective-permute-start.58) | collective-permute-done | bytes 524320 | tf_op jit(solution)/shard_map/ppermute | solution.py:210
  349.4 5.9 convolution_convert_fusion.3
  355.4 5.9 convolution_convert_fusion.2
  373.1 9.9 %collective-permute-done.94 = bf16[192,2048]{1,0:T(8,128)(2,1)S(1)} collective-permute-done((bf16[192,2048]{1,0:T(8,128)(2,1)S(1)}, bf16[192,2048]{1,0:T(8,128)(2,1)S(1)}, u32[]{:S(2)}, u32[]{:S(2)}) %collective-permute-start.94) | collective-permute-done | bytes 786464 | tf_op jit(solution)/shard_map/ppermute | solution.py:210
  384.9 15.1 %collective-permute-done.96 = bf16[192,2048]{1,0:T(8,128)(2,1)S(1)} collective-permute-done((bf16[192,2048]{1,0:T(8,128)(2,1)S(1)}, bf16[192,2048]{1,0:T(8,128)(2,1)S(1)}, u32[]{:S(2)}, u32[]{:S(2)}) %collective-permute-start.96) | collective-permute-done | bytes 786464 | tf_op jit(solution)/shard_map/ppermute | solution.py:210
  401.1 15.7 %collective-permute-done.89 = bf16[192,2048]{1,0:T(8,128)(2,1)S(1)} collective-permute-done((bf16[192,2048]{1,0:T(8,128)(2,1)S(1)}, bf16[192,2048]{1,0:T(8,128)(2,1)S(1)}, u32[]{:S(2)}, u32[]{:S(2)}) %collective-permute-start.89) | collective-permute-done | bytes 786464 | tf_op jit(solution)/shard_map/ppermute | solution.py:210
  416.8 15.3 %collective-permute-done.91 = bf16[192,2048]{1,0:T(8,128)(2,1)S(1)} collective-permute-done((bf16[192,2048]{1,0:T(8,128)(2,1)S(1)}, bf16[192,2048]{1,0:T(8,128)(2,1)S(1)}, u32[]{:S(2)}, u32[]{:S(2)}) %collective-permute-start.91) | collective-permute-done | bytes 786464 | tf_op jit(solution)/shard_map/ppermute | solution.py:210
  432.1 6.0 collective-permute-start.97
  438.7 10.1 %collective-permute-done.66 = bf16[128,2048]{1,0:T(8,128)(2,1)S(1)} collective-permute-done((bf16[128,2048]{1,0:T(8,128)(2,1)S(1)}, bf16[128,2048]{1,0:T(8,128)(2,1)S(1)}, u32[]{:S(2)}, u32[]{:S(2)}) %collective-permute-start.66) | collective-permute-done | bytes 524320 | tf_op jit(solution)/shard_map/ppermute | solution.py:210
  458.0 3.8 convolution_convert_fusion.1
  468.4 13.3 %collective-permute-start.92 = (bf16[192,2048]{1,0:T(8,128)(2,1)S(1)}, bf16[192,2048]{1,0:T(8,128)(2,1)}, u32[]{:S(2)}, u32[]{:S(2)}) collective-permute-start(bf16[192,2048]{1,0:T(8,128)(2,1)S(1)} %fusion.45), channel_id=1, source_target_pairs={{0,0},{1,1},{2,2},{3,3},{4,4},{5,5},{6,6},{7,7},{8,9},{9,10},{10,1... | collective-permute-start | bytes 2359304 | tf_op jit(solution)/shard_map/ppermute | solution.py:210
  489.9 27.0 %collective-permute-done.92 = bf16[192,2048]{1,0:T(8,128)(2,1)} collective-permute-done((bf16[192,2048]{1,0:T(8,128)(2,1)S(1)}, bf16[192,2048]{1,0:T(8,128)(2,1)}, u32[]{:S(2)}, u32[]{:S(2)}) %collective-permute-start.92) | collective-permute-done | bytes 786464 | tf_op jit(solution)/shard_map/ppermute | solution.py:210
  518.1 7.4 %collective-permute-start.98 = (bf16[192,2048]{1,0:T(8,128)(2,1)}, bf16[192,2048]{1,0:T(8,128)(2,1)}, u32[]{:S(2)}, u32[]{:S(2)}) collective-permute-start(bf16[192,2048]{1,0:T(8,128)(2,1)} %collective-permute-done.97), channel_id=1, source_target_pairs={{0,0},{1,9},{2,18},{3,27},{4,4},{5,13},{6,22},{7,31},{8,24},{9,1},... | collective-permute-start | bytes 2359304 | tf_op jit(solution)/shard_map/ppermute | solution.py:210
  525.5 7.6 %collective-permute-start.93 = (bf16[192,2048]{1,0:T(8,128)(2,1)}, bf16[192,2048]{1,0:T(8,128)(2,1)}, u32[]{:S(2)}, u32[]{:S(2)}) collective-permute-start(bf16[192,2048]{1,0:T(8,128)(2,1)} %collective-permute-done.92), channel_id=1, source_target_pairs={{0,0},{1,9},{2,18},{3,27},{4,4},{5,13},{6,22},{7,31},{8,24},{9,1},... | collective-permute-start | bytes 2359304 | tf_op jit(solution)/shard_map/ppermute | solution.py:210
  540.8 10.8 %shard_map.264 = (f32[1024,256]{1,0:T(8,128)S(1)}, bf16[1024,256]{1,0:T(8,128)(2,1)S(1)}, f32[1024,128]{1,0:T(8,128)S(1)}, f32[1024,128]{1,0:T(8,128)S(1)}) custom-call(bf16[1024,256]{1,0:T(8,128)(2,1)S(1)} %copy.53.q_ref, bf16[1024,128]{1,0:T(8,128)(2,1)S(1)} %pad_maximum_fusion.9.k_ref, bf16[1024,128]{1,0:T(8,128)(2,1)S(1)} %copy-done.1, ...), custom_call_target="tpu_custom_call" | custom-call | flops 2684354560 | bytes 6291456 | tf_op jit(solution)/shard_map/pallas_call | solution.py:147
  564.1 8.6 %fusion.3 = (f32[2048]{0:T(1024)S(1)}, bf16[1024,2048]{1,0:T(8,128)(2,1)}) fusion(bf16[1024,2048]{1,0:T(8,128)(2,1)} %copy-done.13, f32[1024]{0:T(1024)S(1)} %copy-done.56, bf16[2048,256]{1,0:T(8,128)(2,1)} %copy-done.30, bf16[2048,256]{1,0:T(8,128)(2,1)S(1)} %copy-done.26, bf16[2048,256]{1,0:T(8,128)(2,1)} %constant_dynamic-update-slice_fusion.59, ...), kind=kOutput, calls=%fused_computation.5 | convolution fusion | flops 3247437824 | bytes 13119488 | tf_op jit(solution)/shard_map/dot_general | solution.py:18
  572.7 39.8 %all-reduce.5 = (f32[2304]{0:T(1024)S(1)}, f32[2048]{0:T(1024)S(1)}) all-reduce(f32[2304]{0:T(1024)S(1)} %pad_maximum_fusion.10, f32[2048]{0:T(1024)S(1)} %get-tuple-element.26), channel_id=1, replica_groups=mesh['seq'=8,'fsdp'=4] {'seq','fsdp'}, use_global_device_ids=true, to_apply=%region_12.13 | all-reduce | flops 4352 | bytes 34816 | tf_op jit(solution)/shard_map/psum | solution.py:533
  636.0 5.3 collective-permute-done.103
  642.4 10.2 %collective-permute-done.104 = bf16[64,1536]{1,0:T(8,128)(2,1)S(1)} collective-permute-done((bf16[64,1536]{1,0:T(8,128)(2,1)S(1)}, bf16[64,1536]{1,0:T(8,128)(2,1)S(1)}, u32[]{:S(2)}, u32[]{:S(2)}) %collective-permute-start.104) | collective-permute-done | bytes 196640 | tf_op jit(solution)/shard_map/ppermute | solution.py:210
  652.8 10.8 %collective-permute-done.87 = bf16[8,64,256]{2,1,0:T(8,128)(2,1)S(1)} collective-permute-done((bf16[8,64,256]{2,1,0:T(8,128)(2,1)S(1)}, bf16[8,64,256]{2,1,0:T(8,128)(2,1)S(1)}, u32[]{:S(2)}, u32[]{:S(2)}) %collective-permute-start.87) | collective-permute-done | bytes 262176 | tf_op jit(solution)/shard_map/ppermute | solution.py:210
  666.6 18.4 %collective-permute-done.88 = bf16[8,64,256]{2,1,0:T(8,128)(2,1)S(1)} collective-permute-done((bf16[8,64,256]{2,1,0:T(8,128)(2,1)S(1)}, bf16[8,64,256]{2,1,0:T(8,128)(2,1)S(1)}, u32[]{:S(2)}, u32[]{:S(2)}) %collective-permute-start.88) | collective-permute-done | bytes 262176 | tf_op jit(solution)/shard_map/ppermute | solution.py:210
  685.8 6.0 all-to-all-start
  695.6 5.5 all-to-all-done
  704.5 11.5 %collective-permute-done.84 = bf16[192,2048]{1,0:T(8,128)(2,1)} collective-permute-done((bf16[192,2048]{1,0:T(8,128)(2,1)}, bf16[192,2048]{1,0:T(8,128)(2,1)}, u32[]{:S(2)}, u32[]{:S(2)}) %collective-permute-start.84) | collective-permute-done | bytes 786464 | tf_op jit(solution)/shard_map/ppermute | solution.py:210
  720.5 17.7 %collective-permute-done.85 = bf16[192,2048]{1,0:T(8,128)(2,1)S(1)} collective-permute-done((bf16[192,2048]{1,0:T(8,128)(2,1)S(1)}, bf16[192,2048]{1,0:T(8,128)(2,1)S(1)}, u32[]{:S(2)}, u32[]{:S(2)}) %collective-permute-start.85) | collective-permute-done | bytes 786464 | tf_op jit(solution)/shard_map/ppermute | solution.py:210
  (558 shorter events, 239.5 us)
Async XLA Ops:
  0.7 68.5 %collective-permute-start.1 = (bf16[128,2048]{1,0:T(8,128)(2,1)}, bf16[128,2048]{1,0:T(8,128)(2,1)}, u32[]{:S(2)}, u32[]{:S(2)}) collective-permute-start(bf16[128,2048]{1,0:T(8,128)(2,1)} %bitcast.340), channel_id=1, source_target_pairs={{0,8},{1,9},{2,10},{3,11},{4,12},{5,13},{6,14},{7,15},{8,0},{9,1},... | collective-permute-start | bytes 1572872 | tf_op jit(solution)/shard_map/ppermute | solution.py:210
  2.3 52.1 %collective-permute-start = (bf16[128,2048]{1,0:T(8,128)(2,1)}, bf16[128,2048]{1,0:T(8,128)(2,1)}, u32[]{:S(2)}, u32[]{:S(2)}) collective-permute-start(bf16[128,2048]{1,0:T(8,128)(2,1)} %bitcast.341), channel_id=1, source_target_pairs={{0,4},{1,5},{2,6},{3,7},{4,0},{5,1},{6,2},{7,3},{8,12},{9,13},{10,... | collective-permute-start | bytes 1572872 | tf_op jit(solution)/shard_map/ppermute | solution.py:210
  4.9 47.6 %collective-permute-start.13 = (bf16[512,256]{1,0:T(8,128)(2,1)}, bf16[512,256]{1,0:T(8,128)(2,1)}, u32[]{:S(2)}, u32[]{:S(2)}) collective-permute-start(bf16[512,256]{1,0:T(8,128)(2,1)} %get-tuple-element.143), channel_id=1, source_target_pairs={{0,1},{1,2},{2,3},{3,0},{4,5},{5,6},{6,7},{7,4},{8,9},{9,10},{10,1... | collective-permute-start | bytes 786440 | tf_op jit(solution)/shard_map/ppermute | solution.py:210
  8.1 45.6 %collective-permute-start.7 = (bf16[512,256]{1,0:T(8,128)(2,1)}, bf16[512,256]{1,0:T(8,128)(2,1)}, u32[]{:S(2)}, u32[]{:S(2)}) collective-permute-start(bf16[512,256]{1,0:T(8,128)(2,1)} %dynamic_slice.228), channel_id=1, source_target_pairs={{0,1},{1,2},{2,3},{3,0},{4,5},{5,6},{6,7},{7,4},{8,9},{9,10},{10,1... | collective-permute-start | bytes 786440 | tf_op jit(solution)/shard_map/ppermute | solution.py:210
  11.5 41.0 %collective-permute-start.25 = (bf16[256,512]{1,0:T(8,128)(2,1)}, bf16[256,512]{1,0:T(8,128)(2,1)}, u32[]{:S(2)}, u32[]{:S(2)}) collective-permute-start(bf16[256,512]{1,0:T(8,128)(2,1)} %get-tuple-element.44), channel_id=1, source_target_pairs={{0,1},{1,2},{2,3},{3,0},{4,5},{5,6},{6,7},{7,4},{8,9},{9,10},{10,1... | collective-permute-start | bytes 786440 | tf_op jit(solution)/shard_map/ppermute | solution.py:210
  53.7 28.3 %collective-permute-start.26 = (bf16[256,512]{1,0:T(8,128)(2,1)}, bf16[256,512]{1,0:T(8,128)(2,1)S(1)}, u32[]{:S(2)}, u32[]{:S(2)}) collective-permute-start(bf16[256,512]{1,0:T(8,128)(2,1)} %collective-permute-done.25), channel_id=1, source_target_pairs={{0,1},{1,2},{2,3},{3,0},{4,5},{5,6},{6,7},{7,4},{8,9},{9,10},{10,1... | collective-permute-start | bytes 786440 | tf_op jit(solution)/shard_map/ppermute | solution.py:210
  63.6 34.9 %collective-permute-start.3 = (bf16[128,2048]{1,0:T(8,128)(2,1)S(1)}, bf16[128,2048]{1,0:T(8,128)(2,1)S(1)}, u32[]{:S(2)}, u32[]{:S(2)}) collective-permute-start(bf16[128,2048]{1,0:T(8,128)(2,1)S(1)} %bitcast.342), channel_id=1, source_target_pairs={{0,16},{1,17},{2,18},{3,19},{4,20},{5,21},{6,22},{7,23},{8,24},{9,... | collective-permute-start | bytes 1572872 | tf_op jit(solution)/shard_map/ppermute | solution.py:210
  86.1 110.9 %collective-permute-start.55 = (bf16[128,2048]{1,0:T(8,128)(2,1)}, bf16[128,2048]{1,0:T(8,128)(2,1)}, u32[]{:S(2)}, u32[]{:S(2)}) collective-permute-start(bf16[128,2048]{1,0:T(8,128)(2,1)} %bitcast.54), channel_id=1, source_target_pairs={{0,1},{1,2},{2,3},{3,0},{4,5},{5,6},{6,7},{7,4},{8,9},{9,10},{10,1... | collective-permute-start | bytes 1572872 | tf_op jit(solution)/shard_map/ppermute | solution.py:210
  119.2 54.2 %collective-permute-start.12 = (bf16[512,256]{1,0:T(8,128)(2,1)}, bf16[512,256]{1,0:T(8,128)(2,1)}, u32[]{:S(2)}, u32[]{:S(2)}) collective-permute-start(bf16[512,256]{1,0:T(8,128)(2,1)} %get-tuple-element.109), channel_id=1, source_target_pairs={{0,24},{1,25},{2,26},{3,27},{4,28},{5,29},{6,30},{7,31},{8,16},{9,... | collective-permute-start | bytes 786440 | tf_op jit(solution)/shard_map/ppermute | solution.py:210
  141.5 26.9 %collective-permute-start.11 = (bf16[512,256]{1,0:T(8,128)(2,1)}, bf16[512,256]{1,0:T(8,128)(2,1)}, u32[]{:S(2)}, u32[]{:S(2)}) collective-permute-start(bf16[512,256]{1,0:T(8,128)(2,1)} %get-tuple-element.110), channel_id=1, source_target_pairs={{0,16},{1,17},{2,18},{3,19},{4,20},{5,21},{6,22},{7,23},{8,24},{9,... | collective-permute-start | bytes 786440 | tf_op jit(solution)/shard_map/ppermute | solution.py:210
  199.0 27.0 %collective-permute-start.38 = (bf16[192,512]{1,0:T(8,128)(2,1)S(1)}, bf16[192,512]{1,0:T(8,128)(2,1)S(1)}, u32[]{:S(2)}, u32[]{:S(2)}) collective-permute-start(bf16[192,512]{1,0:T(8,128)(2,1)S(1)} %get-tuple-element.50), channel_id=1, source_target_pairs={{0,2},{1,3},{2,0},{3,1},{4,6},{5,7},{6,4},{7,5},{8,10},{9,11},{10,... | collective-permute-start | bytes 589832 | tf_op jit(solution)/shard_map/ppermute | solution.py:210
  199.0 29.2 %collective-permute-start.59 = (bf16[128,2048]{1,0:T(8,128)(2,1)}, bf16[128,2048]{1,0:T(8,128)(2,1)S(1)}, u32[]{:S(2)}, u32[]{:S(2)}) collective-permute-start(bf16[128,2048]{1,0:T(8,128)(2,1)} %collective-permute-done.55), channel_id=1, source_target_pairs={{0,1},{1,2},{2,3},{3,0},{4,5},{5,6},{6,7},{7,4},{8,9},{9,10},{10,1... | collective-permute-start | bytes 1572872 | tf_op jit(solution)/shard_map/ppermute | solution.py:210
  201.4 26.9 %collective-permute-start.34 = (bf16[128,2048]{1,0:T(8,128)(2,1)}, bf16[128,2048]{1,0:T(8,128)(2,1)S(1)}, u32[]{:S(2)}, u32[]{:S(2)}) collective-permute-start(bf16[128,2048]{1,0:T(8,128)(2,1)} %get-tuple-element.62), channel_id=1, source_target_pairs={{0,4},{1,5},{2,6},{3,7},{4,0},{5,1},{6,2},{7,3},{8,12},{9,13},{10,... | collective-permute-start | bytes 1572872 | tf_op jit(solution)/shard_map/ppermute | solution.py:210
  226.0 31.6 %collective-permute-start.31 = (bf16[128,2048]{1,0:T(8,128)(2,1)S(1)}, bf16[128,2048]{1,0:T(8,128)(2,1)S(1)}, u32[]{:S(2)}, u32[]{:S(2)}) collective-permute-start(bf16[128,2048]{1,0:T(8,128)(2,1)S(1)} %get-tuple-element.60), channel_id=1, source_target_pairs={{0,16},{1,17},{2,18},{3,19},{4,20},{5,21},{6,22},{7,23},{8,24},{9,... | collective-permute-start | bytes 1572872 | tf_op jit(solution)/shard_map/ppermute | solution.py:210
  228.3 48.5 %collective-permute-start.67 = (bf16[128,2048]{1,0:T(8,128)(2,1)}, bf16[128,2048]{1,0:T(8,128)(2,1)S(1)}, u32[]{:S(2)}, u32[]{:S(2)}) collective-permute-start(bf16[128,2048]{1,0:T(8,128)(2,1)} %bitcast.54), channel_id=1, source_target_pairs={{0,4},{1,5},{2,6},{3,7},{4,0},{5,1},{6,2},{7,3},{8,12},{9,13},{10,... | collective-permute-start | bytes 1572872 | tf_op jit(solution)/shard_map/ppermute | solution.py:210
  228.3 45.3 %collective-permute-start.42 = (bf16[192,2048]{1,0:T(8,128)(2,1)S(1)}, bf16[192,2048]{1,0:T(8,128)(2,1)S(1)}, u32[]{:S(2)}, u32[]{:S(2)}) collective-permute-start(bf16[192,2048]{1,0:T(8,128)(2,1)S(1)} %constant_dynamic-update-slice_fusion.46), channel_id=1, source_target_pairs={{0,24},{1,25},{2,26},{3,27},{4,28},{5,29},{6,30},{7,31},{8,16},{9,... | collective-permute-start | bytes 2359304 | tf_op jit(solution)/shard_map/ppermute | solution.py:210
  229.9 43.7 %collective-permute-start.41 = (bf16[192,2048]{1,0:T(8,128)(2,1)S(1)}, bf16[192,2048]{1,0:T(8,128)(2,1)S(1)}, u32[]{:S(2)}, u32[]{:S(2)}) collective-permute-start(bf16[192,2048]{1,0:T(8,128)(2,1)S(1)} %constant_dynamic-update-slice_fusion.46), channel_id=1, source_target_pairs={{0,16},{1,17},{2,18},{3,19},{4,20},{5,21},{6,22},{7,23},{8,24},{9,... | collective-permute-start | bytes 2359304 | tf_op jit(solution)/shard_map/ppermute | solution.py:210
  234.7 32.5 %collective-permute-start.40 = (bf16[192,2048]{1,0:T(8,128)(2,1)S(1)}, bf16[192,2048]{1,0:T(8,128)(2,1)S(1)}, u32[]{:S(2)}, u32[]{:S(2)}) collective-permute-start(bf16[192,2048]{1,0:T(8,128)(2,1)S(1)} %constant_dynamic-update-slice_fusion.46), channel_id=1, source_target_pairs={{0,8},{1,9},{2,10},{3,11},{4,12},{5,13},{6,14},{7,15},{8,0},{9,1},... | collective-permute-start | bytes 2359304 | tf_op jit(solution)/shard_map/ppermute | solution.py:210
  273.8 39.4 %collective-permute-start.60 = (bf16[128,2048]{1,0:T(8,128)(2,1)S(1)}, bf16[128,2048]{1,0:T(8,128)(2,1)S(1)}, u32[]{:S(2)}, u32[]{:S(2)}) collective-permute-start(bf16[128,2048]{1,0:T(8,128)(2,1)S(1)} %collective-permute-done.59), channel_id=1, source_target_pairs={{0,4},{1,5},{2,6},{3,7},{4,0},{5,1},{6,2},{7,3},{8,12},{9,13},{10,... | collective-permute-start | bytes 1572872 | tf_op jit(solution)/shard_map/ppermute | solution.py:210
  274.4 56.5 %collective-permute-start.64 = (bf16[128,2048]{1,0:T(8,128)(2,1)S(1)}, bf16[128,2048]{1,0:T(8,128)(2,1)S(1)}, u32[]{:S(2)}, u32[]{:S(2)}) collective-permute-start(bf16[128,2048]{1,0:T(8,128)(2,1)S(1)} %collective-permute-done.63), channel_id=1, source_target_pairs={{0,4},{1,5},{2,6},{3,7},{4,0},{5,1},{6,2},{7,3},{8,12},{9,13},{10,... | collective-permute-start | bytes 1572872 | tf_op jit(solution)/shard_map/ppermute | solution.py:210
  316.0 32.0 %collective-permute-start.58 = (bf16[128,2048]{1,0:T(8,128)(2,1)S(1)}, bf16[128,2048]{1,0:T(8,128)(2,1)S(1)}, u32[]{:S(2)}, u32[]{:S(2)}) collective-permute-start(bf16[128,2048]{1,0:T(8,128)(2,1)S(1)} %add_convert_fusion.4), channel_id=1, source_target_pairs={{0,1},{1,2},{2,3},{3,0},{4,5},{5,6},{6,7},{7,4},{8,9},{9,10},{10,1... | collective-permute-start | bytes 1572872 | tf_op jit(solution)/shard_map/ppermute | solution.py:210
  336.9 27.4 %collective-permute-start.48 = (bf16[128,2048]{1,0:T(8,128)(2,1)S(1)}, bf16[128,2048]{1,0:T(8,128)(2,1)S(1)}, u32[]{:S(2)}, u32[]{:S(2)}) collective-permute-start(bf16[128,2048]{1,0:T(8,128)(2,1)S(1)} %add_convert_fusion.7), channel_id=1, source_target_pairs={{0,1},{1,2},{2,3},{3,0},{4,5},{5,6},{6,7},{7,4},{8,9},{9,10},{10,1... | collective-permute-start | bytes 1572872 | tf_op jit(solution)/shard_map/ppermute | solution.py:210
  337.0 29.1 %collective-permute-start.51 = (bf16[128,2048]{1,0:T(8,128)(2,1)S(1)}, bf16[128,2048]{1,0:T(8,128)(2,1)S(1)}, u32[]{:S(2)}, u32[]{:S(2)}) collective-permute-start(bf16[128,2048]{1,0:T(8,128)(2,1)S(1)} %slice.230), channel_id=1, source_target_pairs={{0,4},{1,5},{2,6},{3,7},{4,0},{5,1},{6,2},{7,3},{8,12},{9,13},{10,... | collective-permute-start | bytes 1572872 | tf_op jit(solution)/shard_map/ppermute | solution.py:210
  364.3 35.7 %collective-permute-start.96 = (bf16[192,2048]{1,0:T(8,128)(2,1)S(1)}, bf16[192,2048]{1,0:T(8,128)(2,1)S(1)}, u32[]{:S(2)}, u32[]{:S(2)}) collective-permute-start(bf16[192,2048]{1,0:T(8,128)(2,1)S(1)} %get-tuple-element.69), channel_id=1, source_target_pairs={{0,8},{1,9},{2,10},{3,11},{4,12},{5,13},{6,14},{7,15},{8,0},{9,1},... | collective-permute-start | bytes 2359304 | tf_op jit(solution)/shard_map/ppermute | solution.py:210
  366.1 34.0 %collective-permute-start.95 = (bf16[192,2048]{1,0:T(8,128)(2,1)S(1)}, bf16[192,2048]{1,0:T(8,128)(2,1)S(1)}, u32[]{:S(2)}, u32[]{:S(2)}) collective-permute-start(bf16[192,2048]{1,0:T(8,128)(2,1)S(1)} %get-tuple-element.70), channel_id=1, source_target_pairs={{0,16},{1,17},{2,18},{3,19},{4,20},{5,21},{6,22},{7,23},{8,24},{9,... | collective-permute-start | bytes 2359304 | tf_op jit(solution)/shard_map/ppermute | solution.py:210
  370.0 46.8 %collective-permute-start.89 = (bf16[192,2048]{1,0:T(8,128)(2,1)S(1)}, bf16[192,2048]{1,0:T(8,128)(2,1)S(1)}, u32[]{:S(2)}, u32[]{:S(2)}) collective-permute-start(bf16[192,2048]{1,0:T(8,128)(2,1)S(1)} %get-tuple-element.71), channel_id=1, source_target_pairs={{0,24},{1,25},{2,26},{3,27},{4,28},{5,29},{6,30},{7,31},{8,16},{9,... | collective-permute-start | bytes 2359304 | tf_op jit(solution)/shard_map/ppermute | solution.py:210
  371.4 60.7 %collective-permute-start.91 = (bf16[192,2048]{1,0:T(8,128)(2,1)S(1)}, bf16[192,2048]{1,0:T(8,128)(2,1)S(1)}, u32[]{:S(2)}, u32[]{:S(2)}) collective-permute-start(bf16[192,2048]{1,0:T(8,128)(2,1)S(1)} %get-tuple-element.72), channel_id=1, source_target_pairs={{0,8},{1,9},{2,10},{3,11},{4,12},{5,13},{6,14},{7,15},{8,0},{9,1},... | collective-permute-start | bytes 2359304 | tf_op jit(solution)/shard_map/ppermute | solution.py:210
  383.0 49.1 %collective-permute-start.90 = (bf16[192,2048]{1,0:T(8,128)(2,1)S(1)}, bf16[192,2048]{1,0:T(8,128)(2,1)S(1)}, u32[]{:S(2)}, u32[]{:S(2)}) collective-permute-start(bf16[192,2048]{1,0:T(8,128)(2,1)S(1)} %get-tuple-element.73), channel_id=1, source_target_pairs={{0,16},{1,17},{2,18},{3,19},{4,20},{5,21},{6,22},{7,23},{8,24},{9,... | collective-permute-start | bytes 2359304 | tf_op jit(solution)/shard_map/ppermute | solution.py:210
  400.1 38.6 %collective-permute-start.54 = (bf16[128,2048]{1,0:T(8,128)(2,1)S(1)}, bf16[128,2048]{1,0:T(8,128)(2,1)S(1)}, u32[]{:S(2)}, u32[]{:S(2)}) collective-permute-start(bf16[128,2048]{1,0:T(8,128)(2,1)S(1)} %slice.232), channel_id=1, source_target_pairs={{0,4},{1,5},{2,6},{3,7},{4,0},{5,1},{6,2},{7,3},{8,12},{9,13},{10,... | collective-permute-start | bytes 1572872 | tf_op jit(solution)/shard_map/ppermute | solution.py:210
  400.1 38.7 %collective-permute-start.68 = (bf16[128,2048]{1,0:T(8,128)(2,1)S(1)}, bf16[128,2048]{1,0:T(8,128)(2,1)S(1)}, u32[]{:S(2)}, u32[]{:S(2)}) collective-permute-start(bf16[128,2048]{1,0:T(8,128)(2,1)S(1)} %slice.240), channel_id=1, source_target_pairs={{0,4},{1,5},{2,6},{3,7},{4,0},{5,1},{6,2},{7,3},{8,12},{9,13},{10,... | collective-permute-start | bytes 1572872 | tf_op jit(solution)/shard_map/ppermute | solution.py:210
  432.1 55.9 %collective-permute-start.97 = (bf16[192,2048]{1,0:T(8,128)(2,1)S(1)}, bf16[192,2048]{1,0:T(8,128)(2,1)}, u32[]{:S(2)}, u32[]{:S(2)}) collective-permute-start(bf16[192,2048]{1,0:T(8,128)(2,1)S(1)} %fusion.44), channel_id=1, source_target_pairs={{0,0},{1,1},{2,2},{3,3},{4,4},{5,5},{6,6},{7,7},{8,9},{9,10},{10,1... | collective-permute-start | bytes 2359304 | tf_op jit(solution)/shard_map/ppermute | solution.py:210
  454.4 27.3 %collective-permute-start.72 = (bf16[128,2048]{1,0:T(8,128)(2,1)S(1)}, bf16[128,2048]{1,0:T(8,128)(2,1)S(1)}, u32[]{:S(2)}, u32[]{:S(2)}) collective-permute-start(bf16[128,2048]{1,0:T(8,128)(2,1)S(1)} %get-tuple-element.39), channel_id=1, source_target_pairs={{0,16},{1,17},{2,18},{3,19},{4,20},{5,21},{6,22},{7,23},{8,24},{9,... | collective-permute-start | bytes 1572872 | tf_op jit(solution)/shard_map/ppermute | solution.py:210
  454.8 27.0 %collective-permute-start.70 = (bf16[128,2048]{1,0:T(8,128)(2,1)S(1)}, bf16[128,2048]{1,0:T(8,128)(2,1)S(1)}, u32[]{:S(2)}, u32[]{:S(2)}) collective-permute-start(bf16[128,2048]{1,0:T(8,128)(2,1)S(1)} %get-tuple-element.39), channel_id=1, source_target_pairs={{0,8},{1,9},{2,10},{3,11},{4,12},{5,13},{6,14},{7,15},{8,0},{9,1},... | collective-permute-start | bytes 1572872 | tf_op jit(solution)/shard_map/ppermute | solution.py:210
  468.4 48.5 %collective-permute-start.92 = (bf16[192,2048]{1,0:T(8,128)(2,1)S(1)}, bf16[192,2048]{1,0:T(8,128)(2,1)}, u32[]{:S(2)}, u32[]{:S(2)}) collective-permute-start(bf16[192,2048]{1,0:T(8,128)(2,1)S(1)} %fusion.45), channel_id=1, source_target_pairs={{0,0},{1,1},{2,2},{3,3},{4,4},{5,5},{6,6},{7,7},{8,9},{9,10},{10,1... | collective-permute-start | bytes 2359304 | tf_op jit(solution)/shard_map/ppermute | solution.py:210
  481.7 35.1 %collective-permute-start.99 = (bf16[512,768]{1,0:T(8,128)(2,1)}, bf16[512,768]{1,0:T(8,128)(2,1)}, u32[]{:S(2)}, u32[]{:S(2)}) collective-permute-start(bf16[512,768]{1,0:T(8,128)(2,1)} %get-tuple-element.65), channel_id=1, source_target_pairs={{0,24},{1,25},{2,26},{3,27},{4,28},{5,29},{6,30},{7,31},{8,16},{9,... | collective-permute-start | bytes 2359304 | tf_op jit(solution)/shard_map/ppermute | solution.py:210
  481.8 36.2 %collective-permute-start.101 = (bf16[512,768]{1,0:T(8,128)(2,1)}, bf16[512,768]{1,0:T(8,128)(2,1)}, u32[]{:S(2)}, u32[]{:S(2)}) collective-permute-start(bf16[512,768]{1,0:T(8,128)(2,1)} %get-tuple-element.66), channel_id=1, source_target_pairs={{0,8},{1,9},{2,10},{3,11},{4,12},{5,13},{6,14},{7,15},{8,0},{9,1},... | collective-permute-start | bytes 2359304 | tf_op jit(solution)/shard_map/ppermute | solution.py:210
  483.8 41.7 %collective-permute-start.100 = (bf16[512,768]{1,0:T(8,128)(2,1)}, bf16[512,768]{1,0:T(8,128)(2,1)}, u32[]{:S(2)}, u32[]{:S(2)}) collective-permute-start(bf16[512,768]{1,0:T(8,128)(2,1)} %get-tuple-element.67), channel_id=1, source_target_pairs={{0,16},{1,17},{2,18},{3,19},{4,20},{5,21},{6,22},{7,23},{8,24},{9,... | collective-permute-start | bytes 2359304 | tf_op jit(solution)/shard_map/ppermute | solution.py:210
  488.0 48.4 %collective-permute-start.71 = (bf16[128,2048]{1,0:T(8,128)(2,1)}, bf16[128,2048]{1,0:T(8,128)(2,1)S(1)}, u32[]{:S(2)}, u32[]{:S(2)}) collective-permute-start(bf16[128,2048]{1,0:T(8,128)(2,1)} %copy-done.41), channel_id=1, source_target_pairs={{0,4},{1,5},{2,6},{3,7},{4,0},{5,1},{6,2},{7,3},{8,12},{9,13},{10,... | collective-permute-start | bytes 1572872 | tf_op jit(solution)/shard_map/ppermute | solution.py:210
  518.1 110.9 %collective-permute-start.98 = (bf16[192,2048]{1,0:T(8,128)(2,1)}, bf16[192,2048]{1,0:T(8,128)(2,1)}, u32[]{:S(2)}, u32[]{:S(2)}) collective-permute-start(bf16[192,2048]{1,0:T(8,128)(2,1)} %collective-permute-done.97), channel_id=1, source_target_pairs={{0,0},{1,9},{2,18},{3,27},{4,4},{5,13},{6,22},{7,31},{8,24},{9,1},... | collective-permute-start | bytes 2359304 | tf_op jit(solution)/shard_map/ppermute | solution.py:210
  525.5 106.9 %collective-permute-start.93 = (bf16[192,2048]{1,0:T(8,128)(2,1)}, bf16[192,2048]{1,0:T(8,128)(2,1)}, u32[]{:S(2)}, u32[]{:S(2)}) collective-permute-start(bf16[192,2048]{1,0:T(8,128)(2,1)} %collective-permute-done.92), channel_id=1, source_target_pairs={{0,0},{1,9},{2,18},{3,27},{4,4},{5,13},{6,22},{7,31},{8,24},{9,1},... | collective-permute-start | bytes 2359304 | tf_op jit(solution)/shard_map/ppermute | solution.py:210
  536.4 90.4 %collective-permute-start.102 = (bf16[4,64,768]{2,1,0:T(8,128)(2,1)}, bf16[4,64,768]{2,1,0:T(8,128)(2,1)}, u32[]{:S(2)}, u32[]{:S(2)}) collective-permute-start(bf16[4,64,768]{2,1,0:T(8,128)(2,1)} %get-tuple-element.116), channel_id=1, source_target_pairs={{0,4},{1,5},{2,6},{3,7},{4,0},{5,1},{6,2},{7,3},{8,12},{9,13},{10,... | collective-permute-start | bytes 1179656 | tf_op jit(solution)/shard_map/ppermute | solution.py:210
  623.8 39.8 %collective-permute-start.76 = (bf16[128,2048]{1,0:T(8,128)(2,1)S(1)}, bf16[128,2048]{1,0:T(8,128)(2,1)S(1)}, u32[]{:S(2)}, u32[]{:S(2)}) collective-permute-start(bf16[128,2048]{1,0:T(8,128)(2,1)S(1)} %get-tuple-element.54), channel_id=1, source_target_pairs={{0,4},{1,5},{2,6},{3,7},{4,0},{5,1},{6,2},{7,3},{8,12},{9,13},{10,... | collective-permute-start | bytes 1572872 | tf_op jit(solution)/shard_map/ppermute | solution.py:210
  626.8 36.9 %collective-permute-start.80 = (bf16[128,2048]{1,0:T(8,128)(2,1)S(1)}, bf16[128,2048]{1,0:T(8,128)(2,1)S(1)}, u32[]{:S(2)}, u32[]{:S(2)}) collective-permute-start(bf16[128,2048]{1,0:T(8,128)(2,1)S(1)} %get-tuple-element.56), channel_id=1, source_target_pairs={{0,4},{1,5},{2,6},{3,7},{4,0},{5,1},{6,2},{7,3},{8,12},{9,13},{10,... | collective-permute-start | bytes 1572872 | tf_op jit(solution)/shard_map/ppermute | solution.py:210
  628.8 34.9 %collective-permute-start.78 = (bf16[128,2048]{1,0:T(8,128)(2,1)S(1)}, bf16[128,2048]{1,0:T(8,128)(2,1)S(1)}, u32[]{:S(2)}, u32[]{:S(2)}) collective-permute-start(bf16[128,2048]{1,0:T(8,128)(2,1)S(1)} %get-tuple-element.57), channel_id=1, source_target_pairs={{0,4},{1,5},{2,6},{3,7},{4,0},{5,1},{6,2},{7,3},{8,12},{9,13},{10,... | collective-permute-start | bytes 1572872 | tf_op jit(solution)/shard_map/ppermute | solution.py:210
  652.6 39.1 %collective-permute-start.83 = (bf16[192,2048]{1,0:T(8,128)(2,1)}, bf16[192,2048]{1,0:T(8,128)(2,1)}, u32[]{:S(2)}, u32[]{:S(2)}) collective-permute-start(bf16[192,2048]{1,0:T(8,128)(2,1)} %pad_maximum_fusion.4), channel_id=1, source_target_pairs={{0,1},{1,2},{2,3},{3,0},{4,5},{5,6},{6,7},{7,4},{8,9},{9,10},{10,1... | collective-permute-start | bytes 2359304 | tf_op jit(solution)/shard_map/ppermute | solution.py:210
  663.5 39.3 %collective-permute-start.82 = (bf16[128,2048]{1,0:T(8,128)(2,1)}, bf16[128,2048]{1,0:T(8,128)(2,1)S(1)}, u32[]{:S(2)}, u32[]{:S(2)}) collective-permute-start(bf16[128,2048]{1,0:T(8,128)(2,1)} %get-tuple-element.55), channel_id=1, source_target_pairs={{0,4},{1,5},{2,6},{3,7},{4,0},{5,1},{6,2},{7,3},{8,12},{9,13},{10,... | collective-permute-start | bytes 1572872 | tf_op jit(solution)/shard_map/ppermute | solution.py:210
  665.2 37.7 %collective-permute-start.77 = (bf16[128,2048]{1,0:T(8,128)(2,1)}, bf16[128,2048]{1,0:T(8,128)(2,1)S(1)}, u32[]{:S(2)}, u32[]{:S(2)}) collective-permute-start(bf16[128,2048]{1,0:T(8,128)(2,1)} %get-tuple-element.51), channel_id=1, source_target_pairs={{0,24},{1,25},{2,26},{3,27},{4,28},{5,29},{6,30},{7,31},{8,16},{9,... | collective-permute-start | bytes 1572872 | tf_op jit(solution)/shard_map/ppermute | solution.py:210
  666.6 36.2 %collective-permute-start.81 = (bf16[128,2048]{1,0:T(8,128)(2,1)}, bf16[128,2048]{1,0:T(8,128)(2,1)S(1)}, u32[]{:S(2)}, u32[]{:S(2)}) collective-permute-start(bf16[128,2048]{1,0:T(8,128)(2,1)} %get-tuple-element.52), channel_id=1, source_target_pairs={{0,8},{1,9},{2,10},{3,11},{4,12},{5,13},{6,14},{7,15},{8,0},{9,1},... | collective-permute-start | bytes 1572872 | tf_op jit(solution)/shard_map/ppermute | solution.py:210
  (137 other events, 2488.3 us)

commit v2 on v1

v2 whole, which is shorter than its diff:
```python
import functools

import jax
import jax.numpy as jnp
from jax import lax
from jax.experimental import pallas as pl
from jax.experimental.pallas import tpu as pltpu
from jax.sharding import PartitionSpec as P

EPSILON = 1e-06
ROPE_BASE = 5000000.0
AXES = ("seq", "fsdp")
LOW = jnp.bfloat16
WIDE = jnp.float32


def dot(left, right, left_dim=1, right_dim=0):
    return lax.dot_general(
        left, right, (((left_dim,), (right_dim,)), ((), ())), preferred_element_type=WIDE
    )


def rms_norm(values, gain_vector):
    return (
        values
        * lax.rsqrt(jnp.mean(values * values, axis=-1, keepdims=True) + EPSILON)
        * gain_vector
    )


def rotation_tables(positions, head_width):
    half_width = head_width // 2
    inverse = ROPE_BASE ** (-2.0 * jnp.arange(half_width, dtype=WIDE) / head_width)
    angles = positions.astype(WIDE)[:, None] * inverse[None, :]
    return (jnp.cos(angles), jnp.sin(angles))


def prepare_heads(values, gain_vector, cosine, sine_part):
    normed = rms_norm(values, gain_vector)
    half_width = values.shape[-1] // 2
    first_half = normed[..., :half_width]
    second_half = normed[..., half_width:]
    return jnp.concatenate(
        [
            first_half * cosine - second_half * sine_part,
            second_half * cosine + first_half * sine_part,
        ],
        axis=-1,
    )


def block_weights(query, key, row_info, column_info, score_scale):
    scores = dot(query, key, 1, 1) * score_scale
    allowed = (column_info[0:1, :] <= row_info[:, 0:1]) & (
        column_info[1:2, :] == row_info[:, 1:2]
    )
    return jnp.where(allowed, jnp.exp(scores), 0.0)


def forward_kernel(scale, q_ref, k_ref, v_ref, row_ref, column_ref, mixed_ref):
    weights = block_weights(q_ref[...], k_ref[...], row_ref[...], column_ref[...], scale)
    total = jnp.sum(weights, axis=1, keepdims=True)
    mixed_ref[...] = dot(weights.astype(LOW), v_ref[...]) / total


def backward_kernel(
    scale,
    group,
    q_ref,
    k_ref,
    v_ref,
    mixed_ref,
    grad_ref,
    row_ref,
    column_ref,
    dq_ref,
    dk_ref,
    dv_ref,
):
    first = (pl.program_id(1) == 0) & (lax.rem(pl.program_id(0), group) == 0)

    @pl.when(first)
    def _():
        dk_ref[...] = jnp.zeros_like(dk_ref)
        dv_ref[...] = jnp.zeros_like(dv_ref)

    query, key, value = q_ref[...], k_ref[...], v_ref[...]
    mixed_grad = grad_ref[...]
    delta = jnp.sum(mixed_grad.astype(WIDE) * mixed_ref[...], axis=1, keepdims=True)
    weights = block_weights(query, key, row_ref[...], column_ref[...], scale)
    probability = weights * (1.0 / jnp.sum(weights, axis=1, keepdims=True))
    prob_grad = dot(mixed_grad, value, 1, 1)
    score_grad = (probability * (prob_grad - delta)).astype(LOW)
    dq_ref[...] = dot(score_grad, key) * scale
    dk_ref[...] += dot(score_grad, query, 0, 0) * scale
    dv_ref[...] += dot(probability.astype(LOW), mixed_grad, 0, 0)


def attention_specs(length, head_width, group, block):
    per_query = pl.BlockSpec((block, head_width), lambda h, i: (i, h))
    per_key = pl.BlockSpec((length, head_width), lambda h, i: (0, h // group))
    rows = pl.BlockSpec((block, 2), lambda h, i: (i, 0))
    columns = pl.BlockSpec((2, length), lambda h, i: (0, 0))
    return per_query, per_key, rows, columns


def attention_forward(queries, keys, values, row_info, column_info, head_width):
    length, width = queries.shape
    heads = width // head_width
    group = width // keys.shape[1]
    block = min(256, length)
    per_query, per_key, rows, columns = attention_specs(length, head_width, group, block)
    return pl.pallas_call(
        functools.partial(forward_kernel, head_width ** (-0.5)),
        grid=(heads, length // block),
        in_specs=[per_query, per_key, per_key, rows, columns],
        out_specs=per_query,
        out_shape=jax.ShapeDtypeStruct((length, width), WIDE),
        compiler_params=pltpu.CompilerParams(vmem_limit_bytes=40 * 1024 * 1024),
        cost_estimate=pl.CostEstimate(
            flops=4 * length * length * width,
            bytes_accessed=12 * length * width,
            transcendentals=length * length * heads,
        ),
    )(queries, keys, values, row_info, column_info)


def attention_backward(
    queries, keys, values, mixed, mixed_grad, row_info, column_info, head_width
):
    length, width = queries.shape
    heads = width // head_width
    group = width // keys.shape[1]
    block = min(256, length)
    per_query, per_key, rows, columns = attention_specs(length, head_width, group, block)
    return pl.pallas_call(
        functools.partial(backward_kernel, head_width ** (-0.5), group),
        grid=(heads, length // block),
        in_specs=[
            per_query,
            per_key,
            per_key,
            per_query,
            per_query,
            rows,
            columns,
        ],
        out_specs=[per_query, per_key, per_key],
        out_shape=[
            jax.ShapeDtypeStruct((length, width), WIDE),
            jax.ShapeDtypeStruct(keys.shape, WIDE),
            jax.ShapeDtypeStruct(keys.shape, WIDE),
        ],
        compiler_params=pltpu.CompilerParams(vmem_limit_bytes=40 * 1024 * 1024),
        cost_estimate=pl.CostEstimate(
            flops=10 * length * length * width,
            bytes_accessed=24 * length * width,
            transcendentals=length * length * heads,
        ),
    )(queries, keys, values, mixed, mixed_grad, row_info, column_info)


def local(
    block_input,
    d_output,
    segment_ids,
    positions,
    attention_gain,
    query_weight,
    key_weight,
    value_weight,
    output_gate_weight,
    output_weight,
    query_gain,
    key_gain,
    feedforward_gain,
    gate_weight,
    up_weight,
    down_weight,
):
    seq_count, plane_count = lax.axis_size("seq"), lax.axis_size("fsdp")
    column_count = seq_count // 2
    assert column_count == plane_count
    shard_count = seq_count * plane_count
    seq_index, plane = lax.axis_index("seq"), lax.axis_index("fsdp")
    column, core = seq_index // 2, seq_index % 2

    def send(value, move):
        pairs = []
        for q in range(column_count):
            for c in range(2):
                for f in range(plane_count):
                    q2, c2, f2 = move(q, c, f)
                    pairs.append(
                        ((2 * q + c) * plane_count + f, (2 * q2 + c2) * plane_count + f2)
                    )
        return lax.ppermute(value, AXES, pairs)

    def to_core(value):
        return send(value, lambda q, c, f: (q, 1 - c, f))

    def to_column(value, distance):
        return send(value, lambda q, c, f: (q ^ distance, c, f))

    def up(value, distance=1):
        return send(value, lambda q, c, f: (q, c, (f + distance) % plane_count))

    def behind(steps):
        return lax.rem(plane + plane_count - steps, plane_count)

    fence = lax.optimization_barrier

    def named(label, function, *operands):
        with jax.named_scope(label):
            return function(*operands)

    def ring(value):
        blocks = [value]
        for _ in range(plane_count - 1):
            blocks.append(up(blocks[-1]))
        return blocks

    def spread(value):
        return [value] + [up(value, d) for d in range(1, plane_count)]

    def ring_step(running, piece, last=False):
        total = up(running).astype(WIDE) + piece.astype(WIDE)
        return total if last else total.astype(LOW)

    def ring_sum(pieces):
        running = pieces[1]
        for i in range(1, plane_count):
            running = ring_step(running, pieces[(i + 1) % plane_count], i == plane_count - 1)
        return running

    def plane_columns(value):
        return [value] + [to_column(value, d) for d in range(1, column_count)]

    def doubled_columns(value):
        distance = 1
        while distance < column_count:
            value = jnp.concatenate([value, to_column(value, distance)], axis=0)
            distance *= 2
        return value

    def to_plane(value, distance):
        return send(value, lambda q, c, f: (q, c, f ^ distance))

    def doubled_planes(value):
        distance = 1
        while distance < plane_count:
            value = jnp.concatenate([value, to_plane(value, distance)], axis=0)
            distance *= 2
        return value

    def with_core(half):
        return jnp.concatenate([half, to_core(half)], axis=0)

    def plane_gather(blocks):
        tokens, columns = blocks[0].shape
        half = jnp.zeros((column_count, tokens, columns), blocks[0].dtype)
        for d, block in enumerate(blocks):
            half = lax.dynamic_update_slice_in_dim(half, block[None], column ^ d, 0)
        other = to_core(half)
        return jnp.stack(
            [jnp.where(core == 0, half, other), jnp.where(core == 0, other, half)], axis=1
        ).reshape(-1, columns)

    def plane_chip_sum(partial):
        shaped = partial.reshape(column_count, 2, -1, partial.shape[1])
        other = to_core(lax.dynamic_index_in_dim(shaped, 1 - core, 1, keepdims=False))
        mine = lax.dynamic_index_in_dim(shaped, core, 1, keepdims=False)
        return (mine.astype(WIDE) + other.astype(WIDE)).astype(LOW)

    def plane_columns_sum(chip):
        total = lax.dynamic_index_in_dim(chip, column, 0, keepdims=False).astype(WIDE)
        for d in range(1, column_count):
            piece = lax.dynamic_index_in_dim(chip, column ^ d, 0, keepdims=False)
            total = total + to_column(piece, d).astype(WIDE)
        return total

    def plane_sum(partial):
        return plane_columns_sum(plane_chip_sum(partial))

    def small_sum(vector):
        shaped = vector.reshape(column_count, 2, plane_count, -1)
        total = lax.dynamic_index_in_dim(shaped, core, 1, keepdims=False)
        total = total + to_core(lax.dynamic_index_in_dim(shaped, 1 - core, 1, keepdims=False))
        for place, hop, count in (
            (column, to_column, column_count),
            (plane, to_plane, plane_count),
        ):
            parts = [
                lax.dynamic_index_in_dim(total, place ^ d, 0, keepdims=False) for d in range(count)
            ]
            total = sum(hop(part, d) if d else part for d, part in enumerate(parts))
        return total

    def take(array, start, size, axis=0):
        return lax.dynamic_slice_in_dim(array, start, size, axis)

    inputs_low = block_input[0]
    inputs = inputs_low.astype(WIDE)
    token_count, width = inputs.shape
    cotangent_low = d_output[0].astype(LOW)
    cotangent = d_output[0].astype(WIDE)
    head_width = query_gain.shape[0] * plane_count
    query_width = query_weight.shape[1] // 2
    kv_half = key_weight.shape[1] // 2
    key_width = max(head_width, kv_half)
    sharing = key_width // kv_half

    row_chunk = width // column_count
    hidden_width = gate_weight.shape[1] // 2
    down_chunk = hidden_width // column_count

    def shard_pieces(chunk):
        return [
            send(chunk, lambda q, c, f, d=d: (f, c, (f + q + d) % plane_count))
            for d in range(column_count)
        ]

    def shard_rows(pieces):
        result = jnp.zeros((width, pieces[0].shape[1]), pieces[0].dtype)
        for d, piece in enumerate(pieces):
            source = lax.rem(plane + 2 * plane_count - column - d, plane_count)
            result = lax.dynamic_update_slice_in_dim(result, piece, source * row_chunk, 0)
        return result

    def by_rows(pieces):
        rows = pieces[0].shape[0]
        result = jnp.zeros((rows * column_count, pieces[0].shape[1]), pieces[0].dtype)
        for distance, piece in enumerate(pieces):
            result = lax.dynamic_update_slice_in_dim(result, piece, (column ^ distance) * rows, 0)
        return result

    def by_columns(blocks):
        columns = blocks[0].shape[1]
        result = jnp.zeros((blocks[0].shape[0], columns * plane_count), blocks[0].dtype)
        for i, block in enumerate(blocks):
            result = lax.dynamic_update_slice_in_dim(result, block, behind(i) * columns, 1)
        return result

    def my_chunk(weight, block_width):
        start = core * block_width if 2 * block_width <= weight.shape[1] else 0
        return lax.dynamic_slice(weight, (column * row_chunk, start), (row_chunk, block_width))

    with jax.named_scope("input_gather"):
        gathered_inputs = lax.all_gather(inputs_low, "seq", axis=0, tiled=True)
    numbers = with_core(
        named(
            "number_gather", doubled_columns, jnp.concatenate([segment_ids, positions], axis=1)
        )
    )
    small_gains = jnp.concatenate([attention_gain, feedforward_gain, query_gain, key_gain])[None]
    gains_behind = named("gain_gather", doubled_planes, small_gains)
    numbers, gains_behind, weights = fence(
        (
            numbers,
            gains_behind,
            (query_weight, key_weight, value_weight, output_gate_weight, output_weight, down_weight),
        )
    )
    query_weight, key_weight, value_weight, output_gate_weight, output_weight, down_weight = weights

    head_pieces = named(
        "head_weights",
        shard_pieces,
        jnp.concatenate(
            [
                my_chunk(key_weight, key_width),
                my_chunk(value_weight, key_width),
                my_chunk(query_weight, query_width),
                my_chunk(output_gate_weight, query_width),
            ],
            axis=1,
        ),
    )
    down_chunks = [
        take(
            down_weight,
            (lax.rem(plane + d, plane_count) * 2 + core) * hidden_width + column * down_chunk,
            down_chunk,
        )
        for d in range(plane_count)
    ]
    down_chunks, last_pieces = fence((down_chunks, head_pieces[-2:]))
    head_pieces = head_pieces[:-2] + last_pieces
    down_blocks = [
        named("down_weight_planes", up, block, d) if d else block
        for d, block in enumerate(down_chunks)
    ]
    head_weights = shard_rows(head_pieces)
    with jax.named_scope("output_weight_gather"):
        output_rows = lax.all_gather(
            take(output_weight, seq_index * query_width, query_width), "fsdp", axis=1, tiled=True
        )
    gain_parts = jnp.concatenate(
        [
            take(gains_behind, plane ^ f, 1)
            for f in range(plane_count)
        ]
    ).astype(WIDE)
    shard_width = attention_gain.shape[0]
    head_shard = query_gain.shape[0]
    gain_one = gain_parts[:, :shard_width].reshape(-1)
    gain_two = gain_parts[:, shard_width : 2 * shard_width].reshape(-1)
    query_gain_full = gain_parts[:, 2 * shard_width : 2 * shard_width + head_shard].reshape(-1)
    key_gain_full = gain_parts[:, 2 * shard_width + head_shard :].reshape(-1)
    numbers = jnp.concatenate(
        [
            take(numbers, (core ^ c) * column_count + (column ^ q), 1)
            for q in range(column_count)
            for c in range(2)
        ]
    )
    token_index = jnp.arange(seq_count * token_count, dtype=jnp.int32)
    column_info = jnp.stack([token_index, numbers[:, :token_count].reshape(-1)])
    row_info = column_info.T
    cosine, sine_part = rotation_tables(numbers[:, token_count:].reshape(-1), head_width)
    length = token_index.shape[0]
    gathered_wide = gathered_inputs.astype(WIDE)
    scale_one = lax.rsqrt(jnp.mean(gathered_wide * gathered_wide, axis=-1, keepdims=True) + EPSILON)
    normed = (gathered_wide * scale_one * gain_one).astype(LOW)
    gate_half = take(gate_weight, core * hidden_width, hidden_width, 1)
    up_half = take(up_weight, core * hidden_width, hidden_width, 1)
    (
        head_weights,
        normed,
        cosine,
        sine_part,
        column_info,
        row_info,
        output_rows,
        down_blocks,
        gate_half,
        up_half,
        cotangent_low,
    ) = fence(
        (
            head_weights,
            normed,
            cosine,
            sine_part,
            column_info,
            row_info,
            output_rows,
            down_blocks,
            gate_half,
            up_half,
            cotangent_low,
        )
    )

    def cotangent_step(blocks):
        return blocks + [named("cotangent_ring", up, blocks[-1])]

    cotangent_ring = cotangent_step([cotangent_low])
    for _ in range(plane_count - 4):
        cotangent_ring = cotangent_step(cotangent_ring)

    def head_prepare(values, gain_vector):
        return prepare_heads(values, gain_vector, cosine, sine_part)

    def split_heads(array):
        return [array[:, i : i + head_width] for i in range(0, array.shape[1], head_width)]

    key_weights = head_weights[:, :key_width]
    value_weights = head_weights[:, key_width : 2 * key_width]
    query_weights = head_weights[:, 2 * key_width : 2 * key_width + query_width]
    logit_weights = head_weights[:, 2 * key_width + query_width :]
    query_prepared = [
        jax.vjp(head_prepare, head, query_gain_full)
        for head in split_heads(dot(normed, query_weights))
    ]
    key_prepared = [
        jax.vjp(head_prepare, head, key_gain_full) for head in split_heads(dot(normed, key_weights))
    ]
    values = dot(normed, value_weights).astype(LOW)
    queries = jnp.concatenate([head.astype(LOW) for head, _ in query_prepared], axis=1)
    keys = jnp.concatenate([head.astype(LOW) for head, _ in key_prepared], axis=1)
    queries, keys, values, cotangent_ring = fence((queries, keys, values, cotangent_ring))
    cotangent_ring = cotangent_step(cotangent_ring)
    gate_open = jax.nn.sigmoid(dot(normed, logit_weights).astype(LOW).astype(WIDE))
    mixed = attention_forward(queries, keys, values, row_info, column_info, head_width)
    gated = (mixed * gate_open).astype(LOW)
    attention_out = dot(gated, output_rows).astype(LOW)
    down_piece = by_columns(down_blocks)
    down_pieces = [
        named("down_weight_columns", to_column, down_piece, d) if d else down_piece
        for d in range(column_count)
    ]
    attention_out, down_pieces, cotangent_ring = fence((attention_out, down_pieces, cotangent_ring))

    middle = inputs + named("attention_out_sum", plane_sum, attention_out)
    scale_two = lax.rsqrt(jnp.mean(middle * middle, axis=-1, keepdims=True) + EPSILON)
    normed_two = (middle * scale_two * gain_two).astype(LOW)
    down_rows = by_rows(down_pieces)
    cotangent_ring = jnp.stack(cotangent_step(cotangent_ring))
    all_cotangent = jnp.concatenate(
        [cotangent_ring, named("cotangent_core", to_core, cotangent_ring)], axis=1
    )
    all_cotangent = all_cotangent.reshape(-1, width)
    normed_two, all_cotangent, down_rows = fence((normed_two, all_cotangent, down_rows))

    hidden_grads = dot(all_cotangent, down_rows, 1, 1).reshape(plane_count, -1, hidden_width)
    hidden_blocks, gate_grads, up_grads, normed_two_blocks = [], [], [], []
    grad_pieces, out_pieces = [], []
    arrived = normed_two
    for i in range(plane_count):
        block = arrived
        if i < plane_count - 1:
            arrived = named("normed_two_ring", up, block)
        block = jnp.concatenate([block, named("normed_two_core", to_core, block)], axis=0)
        gate_values = dot(block, gate_half)
        up_values = dot(block, up_half)
        gate_sigma = jax.nn.sigmoid(gate_values)
        silu_values = gate_values * gate_sigma
        hidden = (silu_values * up_values).astype(LOW)
        hidden_grad = hidden_grads[i]
        gate_grad = (
            hidden_grad * up_values * gate_sigma * (1.0 + gate_values * (1.0 - gate_sigma))
        ).astype(LOW)
        up_grad = (hidden_grad * silu_values).astype(LOW)
        partial = (dot(gate_grad, gate_half, 1, 1) + dot(up_grad, up_half, 1, 1)).astype(LOW)
        if i < plane_count - 1:
            arrived, partial = fence((arrived, partial))
        out_partial = dot(hidden, down_rows).astype(LOW)
        out_pieces.append((out_partial[:token_count], out_partial[token_count:]))
        grad_pieces.append(
            (
                partial[:token_count].astype(WIDE)
                + named("normed_two_grad_core", to_core, partial[token_count:]).astype(WIDE)
            ).astype(LOW if i else WIDE)
        )
        normed_two_blocks.append(block)
        hidden_blocks.append(hidden)
        gate_grads.append(gate_grad)
        up_grads.append(up_grad)
    last_piece, hidden_blocks, out_pieces = fence((grad_pieces[-1], hidden_blocks, out_pieces))
    grad_pieces[-1] = last_piece
    normed_two_grad = named("normed_two_grad_sum", ring_sum, grad_pieces)

    def columns_sum(pieces):
        total = lax.dynamic_index_in_dim(pieces, column, 0, keepdims=False).astype(WIDE)
        for d in range(1, column_count):
            piece = lax.dynamic_index_in_dim(pieces, column ^ d, 0, keepdims=False)
            total = total + to_column(piece, d).astype(WIDE)
        return total.astype(LOW)

    down_terms = dot(all_cotangent, jnp.concatenate(hidden_blocks), 0, 0).astype(LOW)
    down_mine = named(
        "down_gradient_columns", columns_sum, down_terms.reshape(column_count, -1, hidden_width)
    )
    out_other = named("out_core", to_core, jnp.stack([piece for _, piece in out_pieces]))

    weighted = gain_two * normed_two_grad
    middle_grad = (
        cotangent
        + scale_two * weighted
        - middle * (scale_two**3) * jnp.mean(middle * weighted, axis=-1, keepdims=True)
    )
    feedforward_gain_terms = jnp.sum(normed_two_grad * (middle * scale_two), axis=0)
    attention_grad_local = middle_grad.astype(LOW)
    attention_grad_local, down_mine, out_other = fence(
        (attention_grad_local, down_mine, out_other)
    )

    out_terms = [
        (piece.astype(WIDE) + out_other[i].astype(WIDE)).astype(LOW)
        for i, (piece, _) in enumerate(out_pieces)
    ]
    out_running = out_terms[1]
    for i in range(1, plane_count - 1):
        out_running = named("out_ring", ring_step, out_running, out_terms[i + 1])
    grad_columns = named("attention_grad_columns", plane_columns, attention_grad_local)
    first, gate_grads, up_grads = fence((grad_columns[1], gate_grads, up_grads))
    grad_columns[1] = first
    attention_grad = named("attention_grad_core", plane_gather, grad_columns)
    all_normed_two = jnp.concatenate(normed_two_blocks, axis=0)

    def column_block_terms(grads):
        terms = dot(jnp.concatenate(grads, axis=0), all_normed_two, 0, 0).astype(LOW)
        return terms.reshape(plane_count, -1, width)

    gate_terms = column_block_terms(gate_grads)
    up_terms = column_block_terms(up_grads)
    up_shift = plane_count // 2
    feed_terms = jnp.concatenate(
        [
            lax.dynamic_index_in_dim(
                terms, lax.rem(plane + q + shift, plane_count), 0, keepdims=False
            )
            for q in range(column_count)
            for terms, shift in ((gate_terms, 0), (up_terms, up_shift))
        ]
    )
    down_mine = down_mine.reshape(2, plane_count, -1, hidden_width)
    own_half = lax.dynamic_index_in_dim(down_mine, core, 0, keepdims=False)
    other_half = named(
        "down_gradient_core",
        to_core,
        lax.dynamic_index_in_dim(down_mine, 1 - core, 0, keepdims=False),
    )
    down_pair = jnp.where(
        core == 0,
        jnp.concatenate([own_half, other_half], axis=2),
        jnp.concatenate([other_half, own_half], axis=2),
    )
    attention_grad, feed_terms, out_running, down_pair = fence(
        (attention_grad, feed_terms, out_running, down_pair)
    )

    with jax.named_scope("feed_gradient_columns"):
        feed_mine = lax.psum_scatter(
            feed_terms,
            "seq",
            scatter_dimension=0,
            axis_index_groups=[[2 * q + c for q in range(column_count)] for c in range(2)],
            tiled=True,
        )
    out_total = named("out_ring", ring_step, out_running, out_terms[0], True)
    gated_grad = dot(attention_grad, output_rows, 1, 1).astype(LOW).astype(WIDE)
    logit_grad = (gated_grad * mixed * gate_open * (1.0 - gate_open)).astype(LOW)
    mixed_grad = (gated_grad * gate_open).astype(LOW)
    output_terms = dot(attention_grad, gated, 0, 0).astype(LOW)
    output_terms = output_terms.reshape(seq_count, plane_count, -1, query_width)
    output_terms = output_terms.transpose(1, 0, 2, 3).reshape(plane_count, -1, width)
    logit_terms = dot(logit_grad, normed, 0, 0).astype(LOW).reshape(plane_count, -1, width)
    logit_count = logit_terms.shape[1]
    early_terms = jnp.concatenate([logit_terms, output_terms], axis=1)

    def early_term(i):
        return lax.dynamic_index_in_dim(early_terms, behind(i % plane_count), 0, keepdims=False)

    early_running = early_term(1)
    for i in range(1, plane_count - 2):
        early_running = named("early_ring", ring_step, early_running, early_term(i + 1))
    query_rot_grad, key_rot_grad, value_sum = attention_backward(
        queries, keys, values, mixed, mixed_grad, row_info, column_info, head_width
    )
    query_rot_grad, key_rot_grad, value_sum, out_total, early_running = fence(
        (query_rot_grad, key_rot_grad, value_sum, out_total, early_running)
    )
    early_running = named("early_ring", ring_step, early_running, early_term(plane_count - 1))
    down_moved = []
    for d in range(plane_count):
        block = lax.dynamic_index_in_dim(
            down_pair, lax.rem(plane + d, plane_count), 0, keepdims=False
        )
        down_moved.append(named("down_gradient_planes", up, block, d) if d else block)
    if sharing > 1:
        key_rot_grad = key_rot_grad + to_core(key_rot_grad)
        value_sum = value_sum + to_core(value_sum)
    query_pulled = [
        pull(grad) for (_, pull), grad in zip(query_prepared, split_heads(query_rot_grad))
    ]
    key_pulled = [pull(grad) for (_, pull), grad in zip(key_prepared, split_heads(key_rot_grad))]
    query_grad = jnp.concatenate([grad.astype(LOW) for grad, _ in query_pulled], axis=1)
    key_grad = jnp.concatenate([grad.astype(LOW) for grad, _ in key_pulled], axis=1)
    query_gain_grad = sum(gain for _, gain in query_pulled)
    key_gain_grad = sum(gain for _, gain in key_pulled)
    value_grad = value_sum.astype(LOW)
    if sharing > 1:
        key_grad = take(key_grad, core * kv_half, kv_half, 1)
        value_grad = take(value_grad, core * kv_half, kv_half, 1)
        key_weights = take(key_weights, core * kv_half, kv_half, 1)
        value_weights = take(value_weights, core * kv_half, kv_half, 1)
    terms = [
        dot(part, normed, 0, 0).astype(LOW).reshape(plane_count, -1, width)
        for part in (query_grad, key_grad, value_grad)
    ]
    qkv_pieces = [
        jnp.concatenate(
            [lax.dynamic_index_in_dim(term, behind(i), 0, keepdims=False) for term in terms], axis=0
        )
        for i in range(plane_count)
    ]
    joined_grad = jnp.concatenate([query_grad, key_grad, value_grad, logit_grad], axis=1)
    qkv_pieces, joined_grad, early_running, feed_mine, down_moved = fence(
        (qkv_pieces, joined_grad, early_running, feed_mine, down_moved)
    )

    normed_grad_partial = dot(
        joined_grad,
        jnp.concatenate([query_weights, key_weights, value_weights, logit_weights], axis=1),
        1,
        1,
    )
    attention_gain_terms = jnp.sum(normed_grad_partial * (gathered_wide * scale_one), axis=0)
    with jax.named_scope("normed_grad_sum"):
        chip = plane_chip_sum(normed_grad_partial.astype(LOW))
        chip, qkv_pieces = fence((chip, qkv_pieces))
        normed_grad = plane_columns_sum(chip)
    qkv_total = named("qkv_gradient_sum", ring_sum, qkv_pieces)
    early_sum = named("early_ring", ring_step, early_running, early_term(0), True)

    vectors = [attention_gain_terms, query_gain_grad, key_gain_grad / sharing, feedforward_gain_terms]
    normed_grad, vectors = fence((normed_grad, vectors))
    vectors = [vector.reshape(seq_count, plane_count, -1) for vector in vectors]
    small = named("gain_sum", small_sum, jnp.concatenate(vectors, axis=2))
    small, qkv_total, feed_mine = fence((small, qkv_total, feed_mine))
    piece = feed_mine.shape[0] // 2
    gate_moved = named(
        "gate_gradient_move",
        send,
        feed_mine[:piece],
        lambda q, c, f: (f, c, (f + q) % plane_count),
    )
    up_moved = named(
        "up_gradient_move",
        send,
        feed_mine[piece:],
        lambda q, c, f: (f, c, (f + q + up_shift) % plane_count),
    )
    gain_totals, at = [], 0
    for vector in vectors:
        gain_totals.append(small[at : at + vector.shape[2]])
        at += vector.shape[2]

    attention_gradients, at = [], 0
    for term in terms:
        attention_gradients.append(qkv_total[at : at + term.shape[1]].T)
        at += term.shape[1]
    attention_gradients.append(early_sum[:logit_count].T)
    output_mine = early_sum[logit_count:].astype(LOW).reshape(seq_count, -1, query_width)
    output_spread = lax.all_to_all(output_mine, "seq", split_axis=0, concat_axis=0, tiled=True)
    output_gradient = (
        output_spread.astype(WIDE).transpose(0, 2, 1).reshape(-1, output_spread.shape[1])
    )
    weighted = gain_one * normed_grad
    own_scale = lax.rsqrt(jnp.mean(inputs * inputs, axis=-1, keepdims=True) + EPSILON)
    input_gradient = (
        middle_grad
        + own_scale * weighted
        - inputs * (own_scale**3) * jnp.mean(inputs * weighted, axis=-1, keepdims=True)
    )[None]
    block_output = (middle + out_total.astype(WIDE)).astype(LOW)[None]
    down_gradient = by_columns(down_moved).astype(WIDE).T
    gate_gradient = gate_moved.astype(WIDE).T
    up_gradient = up_moved.astype(WIDE).T
    return (
        block_output,
        input_gradient,
        gain_totals[0],
        *attention_gradients,
        output_gradient,
        *gain_totals[1:],
        gate_gradient,
        up_gradient,
        down_gradient,
    )


def solution(mesh):
    whole = P(None, ("seq", "fsdp"))
    vector = P(("seq", "fsdp"))
    tokens = P("fsdp", "seq", None)
    weight = P(None, "fsdp")
    return jax.shard_map(
        local,
        mesh=mesh,
        in_specs=(
            tokens,
            tokens,
            P("fsdp", "seq"),
            P("fsdp", "seq"),
            P("fsdp"),
            weight,
            weight,
            weight,
            weight,
            weight,
            P("fsdp"),
            P("fsdp"),
            P("fsdp"),
            weight,
            weight,
            weight,
        ),
        out_specs=(
            tokens,
            tokens,
            vector,
            whole,
            whole,
            whole,
            whole,
            whole,
            vector,
            vector,
            vector,
            whole,
            whole,
            whole,
        ),
        check_vma=False,
    )
```

time: 749 us -> 631 us (0.84)
  waiting for transfers between devices: 356 us -> 260 us
  blocking collectives: 70.4 us -> 0 us
  starting transfers between devices: 107 us -> 129 us
  local copies, waits for them, and re-layouts: 61 us -> 75.4 us
  between operations: 4.46 us -> 15.9 us
    ppermute x106 -> x71, waiting for transfers between devices: 351 us -> 253 us  [send(): return lax.ppermute(value, AXES, pairs)]
    psum x1 -> x0, blocking collectives: 39.8 us -> none  [local(): lax.psum(jnp.concatenate([attention_gain_terms, query_gain_grad, key_gain...]
    ppermute x106 -> x71, starting transfers between devices: 101 us -> 124 us  [send(): return lax.ppermute(value, AXES, pairs)]
    unnamed x1 -> x0, blocking collectives: 22.8 us -> none
    dynamic_update_slice x27 -> x20, local copies, waits for them, and re-layouts: 6.72 us -> 20.7 us  [the longest x4 8.43 us: shard_rows(): lax.dynamic_update_slice_in_dim(result, piece, source * row_chunk, 0)]
    unnamed x187 -> x124, local copies, waits for them, and re-layouts: 26.2 us -> 12.5 us
    all_gather x1 -> x0, blocking collectives: 7.91 us -> none  [local(): lax.all_gather(jnp.concatenate([segment_ids, positions], axis=0), 'seq',...]
    dot_general x39 -> x36, matrix products: 72.5 us -> 71.5 us  [dot(): lax.dot_general(left, right, (((left_dim,), (right_dim,)), ((), ())), pre...]
  transfers between devices with their start and end apart: 107 -> 75, of which waited for: 39 -> 35; matrix products, arithmetic and copies ran while one was open for 24% -> 29% of each run, Pallas kernels for 2% -> 2%
where the time goes in v2:
time: 631 us; the launch traced here: 622 us
  waiting for transfers between devices  260 us (41%)
  starting transfers between devices  129 us (20%)
  local copies, waits for them, and re-layouts  75.4 us (12%)
  matrix products  71.5 us (11%)
  other arithmetic  55.2 us (9%)
  between operations  15.9 us (3%)
  Pallas kernels  15.1 us (2%)
    ppermute x71, waiting for transfers between devices, send(): return lax.ppermute(value, AXES, pairs)  253 us
    ppermute x71, starting transfers between devices, send(): return lax.ppermute(value, AXES, pairs)  124 us
    dot_general x36, matrix products, dot(): lax.dot_general(left, right, (((left_dim,), (right_dim,)), ((), ())), pre...  71.5 us
  transfers between devices with their start and end apart: 75, of which 35 were waited for; matrix products, arithmetic and copies ran while one was open for 29% of the time, Pallas kernels for 2%

profile of v2, /device:TPU:4, one launch (start us, length us, event | category | flops | bytes accessed | tf_op | source)
XLA Modules:
  0.0 621.7 jit_solution(6940472307140581653)
XLA Ops:
  15.2 6.0 constant_dynamic-slice_fusion.10
  31.3 3.3 collective-permute-start.7
  34.6 4.3 collective-permute-start.8
  41.2 5.5 collective-permute-start.6
  51.2 37.4 %collective-permute-done.7 = bf16[512,768]{1,0:T(8,128)(2,1)} collective-permute-done((bf16[512,768]{1,0:T(8,128)(2,1)}, bf16[512,768]{1,0:T(8,128)(2,1)}, u32[]{:S(2)}, u32[]{:S(2)}) %collective-permute-start.7) | collective-permute-done | bytes 786464 | tf_op jit(solution)/shard_map/head_weights/ppermute | solution.py:197
  88.6 40.7 %collective-permute-start.11 = (bf16[192,512]{1,0:T(8,128)(2,1)S(1)}, bf16[192,512]{1,0:T(8,128)(2,1)S(1)}, u32[]{:S(2)}, u32[]{:S(2)}) collective-permute-start(bf16[192,512]{1,0:T(8,128)(2,1)S(1)} %get-tuple-element.138), channel_id=1, source_target_pairs={{0,3},{1,0},{2,1},{3,2},{4,7},{5,4},{6,5},{7,6},{8,11},{9,8},{10,9... | collective-permute-start | bytes 589832 | tf_op jit(solution)/shard_map/down_weight_planes/ppermute | solution.py:197
  139.7 3.2 fusion.4
  143.2 3.0 fusion.2
  149.9 10.9 %collective-permute-start.13 = (bf16[192,2048]{1,0:T(8,128)(2,1)}, bf16[192,2048]{1,0:T(8,128)(2,1)}, u32[]{:S(2)}, u32[]{:S(2)}) collective-permute-start(bf16[192,2048]{1,0:T(8,128)(2,1)} %constant_dynamic-update-slice_fusion.30), channel_id=1, source_target_pairs={{0,8},{1,9},{2,10},{3,11},{4,12},{5,13},{6,14},{7,15},{8,0},{9,1},... | collective-permute-start | bytes 2359304 | tf_op jit(solution)/shard_map/down_weight_columns/ppermute | solution.py:197
  163.4 3.7 fusion.109
  167.2 3.7 multiply_reduce_fusion.9
  179.3 3.7 convolution_convert_fusion.15.v_ref
  183.0 3.5 collective-permute-done.12
  187.8 5.1 shard_map.263.mixed_ref
  192.9 3.5 multiply_convert_fusion.1
  204.6 13.1 %collective-permute-done.21 = bf16[128,2048]{1,0:T(8,128)(2,1)} collective-permute-done((bf16[128,2048]{1,0:T(8,128)(2,1)}, bf16[128,2048]{1,0:T(8,128)(2,1)}, u32[]{:S(2)}, u32[]{:S(2)}) %collective-permute-start.21) | collective-permute-done | bytes 524320 | tf_op jit(solution)/shard_map/cotangent_ring/ppermute | solution.py:197
  229.8 7.2 %collective-permute-done.18 = bf16[128,2048]{1,0:T(8,128)(2,1)S(1)} collective-permute-done((bf16[128,2048]{1,0:T(8,128)(2,1)S(1)}, bf16[128,2048]{1,0:T(8,128)(2,1)S(1)}, u32[]{:S(2)}, u32[]{:S(2)}) %collective-permute-start.18) | collective-permute-done | bytes 524320 | tf_op jit(solution)/shard_map/attention_out_sum/ppermute | solution.py:197
  237.0 12.6 %collective-permute-done.19 = bf16[128,2048]{1,0:T(8,128)(2,1)S(1)} collective-permute-done((bf16[128,2048]{1,0:T(8,128)(2,1)S(1)}, bf16[128,2048]{1,0:T(8,128)(2,1)S(1)}, u32[]{:S(2)}, u32[]{:S(2)}) %collective-permute-start.19) | collective-permute-done | bytes 524320 | tf_op jit(solution)/shard_map/attention_out_sum/ppermute | solution.py:197
  252.8 3.5 fusion.124
  262.5 6.4 %collective-permute-done.23 = bf16[128,2048]{1,0:T(8,128)(2,1)S(1)} collective-permute-done((bf16[128,2048]{1,0:T(8,128)(2,1)S(1)}, bf16[128,2048]{1,0:T(8,128)(2,1)S(1)}, u32[]{:S(2)}, u32[]{:S(2)}) %collective-permute-start.23) | collective-permute-done | bytes 524320 | tf_op jit(solution)/shard_map/normed_two_ring/ppermute | solution.py:197
  276.0 9.0 %collective-permute-done.25 = bf16[128,2048]{1,0:T(8,128)(2,1)S(1)} collective-permute-done((bf16[128,2048]{1,0:T(8,128)(2,1)S(1)}, bf16[128,2048]{1,0:T(8,128)(2,1)S(1)}, u32[]{:S(2)}, u32[]{:S(2)}) %collective-permute-start.25) | collective-permute-done | bytes 524320 | tf_op jit(solution)/shard_map/normed_two_ring/ppermute | solution.py:197
  291.5 9.8 %collective-permute-done.29 = bf16[128,2048]{1,0:T(8,128)(2,1)S(1)} collective-permute-done((bf16[128,2048]{1,0:T(8,128)(2,1)S(1)}, bf16[128,2048]{1,0:T(8,128)(2,1)S(1)}, u32[]{:S(2)}, u32[]{:S(2)}) %collective-permute-start.29) | collective-permute-done | bytes 524320 | tf_op jit(solution)/shard_map/normed_two_ring/ppermute | solution.py:197
  307.9 10.9 %collective-permute-done.28 = bf16[128,2048]{1,0:T(8,128)(2,1)S(1)} collective-permute-done((bf16[128,2048]{1,0:T(8,128)(2,1)S(1)}, bf16[128,2048]{1,0:T(8,128)(2,1)S(1)}, u32[]{:S(2)}, u32[]{:S(2)}) %collective-permute-start.28) | collective-permute-done | bytes 524320 | tf_op jit(solution)/shard_map/normed_two_grad_sum/ppermute | solution.py:197
  321.4 14.0 %collective-permute-done.32 = bf16[128,2048]{1,0:T(8,128)(2,1)S(1)} collective-permute-done((bf16[128,2048]{1,0:T(8,128)(2,1)S(1)}, bf16[128,2048]{1,0:T(8,128)(2,1)S(1)}, u32[]{:S(2)}, u32[]{:S(2)}) %collective-permute-start.32) | collective-permute-done | bytes 524320 | tf_op jit(solution)/shard_map/normed_two_grad_sum/ppermute | solution.py:197
  335.6 3.8 convolution_convert_fusion.3
  343.2 6.9 %collective-permute-done.35 = bf16[128,2048]{1,0:T(8,128)(2,1)S(1)} collective-permute-done((bf16[128,2048]{1,0:T(8,128)(2,1)S(1)}, bf16[128,2048]{1,0:T(8,128)(2,1)S(1)}, u32[]{:S(2)}, u32[]{:S(2)}) %collective-permute-start.35) | collective-permute-done | bytes 524320 | tf_op jit(solution)/shard_map/normed_two_grad_sum/ppermute | solution.py:197
  352.6 7.6 %collective-permute-done.37 = bf16[512,768]{1,0:T(8,128)(2,1)S(1)} collective-permute-done((bf16[512,768]{1,0:T(8,128)(2,1)S(1)}, bf16[512,768]{1,0:T(8,128)(2,1)S(1)}, u32[]{:S(2)}, u32[]{:S(2)}) %collective-permute-start.37) | collective-permute-done | bytes 786464 | tf_op jit(solution)/shard_map/down_gradient_columns/ppermute | solution.py:197
  360.1 14.0 %collective-permute-done.38 = bf16[512,768]{1,0:T(8,128)(2,1)S(1)} collective-permute-done((bf16[512,768]{1,0:T(8,128)(2,1)S(1)}, bf16[512,768]{1,0:T(8,128)(2,1)S(1)}, u32[]{:S(2)}, u32[]{:S(2)}) %collective-permute-start.38) | collective-permute-done | bytes 786464 | tf_op jit(solution)/shard_map/down_gradient_columns/ppermute | solution.py:197
  383.8 12.6 %collective-permute-done.45 = bf16[128,2048]{1,0:T(8,128)(2,1)S(1)} collective-permute-done((bf16[128,2048]{1,0:T(8,128)(2,1)S(1)}, bf16[128,2048]{1,0:T(8,128)(2,1)S(1)}, u32[]{:S(2)}, u32[]{:S(2)}) %collective-permute-start.45) | collective-permute-done | bytes 524320 | tf_op jit(solution)/shard_map/out_ring/ppermute | solution.py:197
  401.3 3.8 convolution_convert_fusion.2
  406.0 3.8 convolution_convert_fusion.1
  423.8 3.6 convolution_convert_fusion.5
  430.8 5.2 fusion.49
  437.5 4.1 fusion.115
  442.9 10.0 %shard_map.264 = (f32[1024,256]{1,0:T(8,128)S(1)}, f32[1024,128]{1,0:T(8,128)S(1)}, f32[1024,128]{1,0:T(8,128)S(1)}) custom-call(bf16[1024,256]{1,0:T(8,128)(2,1)S(1)} %pad_maximum_fusion.5.q_ref, bf16[1024,128]{1,0:T(8,128)(2,1)S(1)} %pad_maximum_fusion.10.k_ref, bf16[1024,128]{1,0:T(8,128)(2,1)S(1)} %convolution_convert_fusion.15.v_ref, ...), custom_call_target="tpu_custom_call" | custom-call | flops 2684354560 | bytes 6291456 | tf_op jit(solution)/shard_map/pallas_call | solution.py:136
  453.1 2.9 collective-permute-start.51
  458.9 6.5 %collective-permute-done.48 = bf16[128,2048]{1,0:T(8,128)(2,1)S(1)} collective-permute-done((bf16[128,2048]{1,0:T(8,128)(2,1)S(1)}, bf16[128,2048]{1,0:T(8,128)(2,1)S(1)}, u32[]{:S(2)}, u32[]{:S(2)}) %collective-permute-start.48) | collective-permute-done | bytes 524320 | tf_op jit(solution)/shard_map/out_ring/ppermute | solution.py:197
  478.0 10.7 %collective-permute-done.50 = bf16[128,2048]{1,0:T(8,128)(2,1)S(1)} collective-permute-done((bf16[128,2048]{1,0:T(8,128)(2,1)S(1)}, bf16[128,2048]{1,0:T(8,128)(2,1)S(1)}, u32[]{:S(2)}, u32[]{:S(2)}) %collective-permute-start.50) | collective-permute-done | bytes 524320 | tf_op jit(solution)/shard_map/early_ring/ppermute | solution.py:197
  489.7 5.4 reduce-scatter.2.cloned.1.call-done
  496.5 6.8 %fusion.3 = (f32[2048]{0:T(1024)S(1)}, bf16[1024,2048]{1,0:T(8,128)(2,1)S(1)}) fusion(bf16[1,1024,2048]{2,1,0:T(8,128)(2,1)} %all-gather.6.cloned.1.call-done, f32[1024]{0:T(1024)S(1)} %copy-done.47, bf16[1024,768]{1,0:T(8,128)(2,1)} %copy-done.40, bf16[2048,256]{1,0:T(8,128)(2,1)} %get-tuple-element.278, bf16[2048,256]{1,0:T(8,128)(2,1)} %get-tuple-element.277, ...), kind=kOutput, calls=%fused_computation.5 | convolution fusion | flops 3241146368 | bytes 13119488 | tf_op jit(solution)/shard_map/dot_general | solution.py:18
  506.1 4.7 collective-permute-done.68
  513.6 4.1 all-to-all-start
  529.0 5.9 collective-permute-done.55
  534.9 10.9 %collective-permute-done.56 = bf16[128,2048]{1,0:T(8,128)(2,1)} collective-permute-done((bf16[128,2048]{1,0:T(8,128)(2,1)}, bf16[128,2048]{1,0:T(8,128)(2,1)}, u32[]{:S(2)}, u32[]{:S(2)}) %collective-permute-start.56) | collective-permute-done | bytes 524320 | tf_op jit(solution)/shard_map/normed_grad_sum/ppermute | solution.py:197
  557.1 3.2 collective-permute-start.63
  565.7 9.3 %collective-permute-done.67 = bf16[128,2048]{1,0:T(8,128)(2,1)S(1)} collective-permute-done((bf16[128,2048]{1,0:T(8,128)(2,1)S(1)}, bf16[128,2048]{1,0:T(8,128)(2,1)S(1)}, u32[]{:S(2)}, u32[]{:S(2)}) %collective-permute-start.67) | collective-permute-done | bytes 524320 | tf_op jit(solution)/shard_map/qkv_gradient_sum/ppermute | solution.py:197
  577.8 5.2 collective-permute-start.69
  585.9 25.6 %collective-permute-done.70 = bf16[192,2048]{1,0:T(8,128)(2,1)S(1)} collective-permute-done((bf16[192,2048]{1,0:T(8,128)(2,1)S(1)}, bf16[192,2048]{1,0:T(8,128)(2,1)S(1)}, u32[]{:S(2)}, u32[]{:S(2)}) %collective-permute-start.70) | collective-permute-done | bytes 786464 | tf_op jit(solution)/shard_map/up_gradient_move/ppermute | solution.py:197
  (434 shorter events, 204.9 us)
Async XLA Ops:
  7.2 132.5 %all-gather.6.cloned.1.call-start = ((), (), s32[]{:S(2)}) async-start(), calls=%async_computation.4 | async-start | bytes 4718592 | tf_op jit(solution)/shard_map/input_gather/all_gather | solution.py:349
  7.9 138.2 %all-gather.4.cloned.1.call-start = ((), (), s32[]{:S(2)}) async-start(), calls=%async_computation.2 | async-start | bytes 1310720 | tf_op jit(solution)/shard_map/output_weight_gather/all_gather | solution.py:395
  31.3 57.3 %collective-permute-start.7 = (bf16[512,768]{1,0:T(8,128)(2,1)}, bf16[512,768]{1,0:T(8,128)(2,1)}, u32[]{:S(2)}, u32[]{:S(2)}) collective-permute-start(bf16[512,768]{1,0:T(8,128)(2,1)} %pad_maximum_fusion.4), channel_id=1, source_target_pairs={{0,2},{1,11},{2,16},{3,25},{4,6},{5,15},{6,20},{7,29},{8,3},{9,8},... | collective-permute-start | bytes 2359304 | tf_op jit(solution)/shard_map/head_weights/ppermute | solution.py:197
  34.6 54.0 %collective-permute-start.8 = (bf16[512,768]{1,0:T(8,128)(2,1)}, bf16[512,768]{1,0:T(8,128)(2,1)}, u32[]{:S(2)}, u32[]{:S(2)}) collective-permute-start(bf16[512,768]{1,0:T(8,128)(2,1)} %pad_maximum_fusion.4), channel_id=1, source_target_pairs={{0,3},{1,8},{2,17},{3,26},{4,7},{5,12},{6,21},{7,30},{8,0},{9,9},{... | collective-permute-start | bytes 2359304 | tf_op jit(solution)/shard_map/head_weights/ppermute | solution.py:197
  39.0 90.4 %collective-permute-start.5 = (bf16[512,768]{1,0:T(8,128)(2,1)}, bf16[512,768]{1,0:T(8,128)(2,1)}, u32[]{:S(2)}, u32[]{:S(2)}) collective-permute-start(bf16[512,768]{1,0:T(8,128)(2,1)} %pad_maximum_fusion.4), channel_id=1, source_target_pairs={{0,0},{1,9},{2,18},{3,27},{4,4},{5,13},{6,22},{7,31},{8,1},{9,10},... | collective-permute-start | bytes 2359304 | tf_op jit(solution)/shard_map/head_weights/ppermute | solution.py:197
  41.2 92.2 %collective-permute-start.6 = (bf16[512,768]{1,0:T(8,128)(2,1)}, bf16[512,768]{1,0:T(8,128)(2,1)}, u32[]{:S(2)}, u32[]{:S(2)}) collective-permute-start(bf16[512,768]{1,0:T(8,128)(2,1)} %pad_maximum_fusion.4), channel_id=1, source_target_pairs={{0,1},{1,10},{2,19},{3,24},{4,5},{5,14},{6,23},{7,28},{8,2},{9,11}... | collective-permute-start | bytes 2359304 | tf_op jit(solution)/shard_map/head_weights/ppermute | solution.py:197
  47.8 447.2 %reduce-scatter.2.cloned.1.call-start = ((), (), s32[]{:S(2)}) async-start(), calls=%async_computation.3 | async-start | bytes 7864320 | tf_op jit(solution)/shard_map/feed_gradient_columns/reduce_scatter | solution.py:615
  88.6 57.5 %collective-permute-start.10 = (bf16[192,512]{1,0:T(8,128)(2,1)S(1)}, bf16[192,512]{1,0:T(8,128)(2,1)S(1)}, u32[]{:S(2)}, u32[]{:S(2)}) collective-permute-start(bf16[192,512]{1,0:T(8,128)(2,1)S(1)} %get-tuple-element.137), channel_id=1, source_target_pairs={{0,2},{1,3},{2,0},{3,1},{4,6},{5,7},{6,4},{7,5},{8,10},{9,11},{10,... | collective-permute-start | bytes 589832 | tf_op jit(solution)/shard_map/down_weight_planes/ppermute | solution.py:197
  88.6 57.5 %collective-permute-start.11 = (bf16[192,512]{1,0:T(8,128)(2,1)S(1)}, bf16[192,512]{1,0:T(8,128)(2,1)S(1)}, u32[]{:S(2)}, u32[]{:S(2)}) collective-permute-start(bf16[192,512]{1,0:T(8,128)(2,1)S(1)} %get-tuple-element.138), channel_id=1, source_target_pairs={{0,3},{1,0},{2,1},{3,2},{4,7},{5,4},{6,5},{7,6},{8,11},{9,8},{10,9... | collective-permute-start | bytes 589832 | tf_op jit(solution)/shard_map/down_weight_planes/ppermute | solution.py:197
  129.4 16.8 %collective-permute-start.9 = (bf16[192,512]{1,0:T(8,128)(2,1)S(1)}, bf16[192,512]{1,0:T(8,128)(2,1)S(1)}, u32[]{:S(2)}, u32[]{:S(2)}) collective-permute-start(bf16[192,512]{1,0:T(8,128)(2,1)S(1)} %get-tuple-element.136), channel_id=1, source_target_pairs={{0,1},{1,2},{2,3},{3,0},{4,5},{5,6},{6,7},{7,4},{8,9},{9,10},{10,1... | collective-permute-start | bytes 589832 | tf_op jit(solution)/shard_map/down_weight_planes/ppermute | solution.py:197
  149.9 47.8 %collective-permute-start.13 = (bf16[192,2048]{1,0:T(8,128)(2,1)}, bf16[192,2048]{1,0:T(8,128)(2,1)}, u32[]{:S(2)}, u32[]{:S(2)}) collective-permute-start(bf16[192,2048]{1,0:T(8,128)(2,1)} %constant_dynamic-update-slice_fusion.30), channel_id=1, source_target_pairs={{0,8},{1,9},{2,10},{3,11},{4,12},{5,13},{6,14},{7,15},{8,0},{9,1},... | collective-permute-start | bytes 2359304 | tf_op jit(solution)/shard_map/down_weight_columns/ppermute | solution.py:197
  160.8 36.9 %collective-permute-start.14 = (bf16[192,2048]{1,0:T(8,128)(2,1)}, bf16[192,2048]{1,0:T(8,128)(2,1)}, u32[]{:S(2)}, u32[]{:S(2)}) collective-permute-start(bf16[192,2048]{1,0:T(8,128)(2,1)} %constant_dynamic-update-slice_fusion.30), channel_id=1, source_target_pairs={{0,16},{1,17},{2,18},{3,19},{4,20},{5,21},{6,22},{7,23},{8,24},{9,... | collective-permute-start | bytes 2359304 | tf_op jit(solution)/shard_map/down_weight_columns/ppermute | solution.py:197
  163.4 34.3 %collective-permute-start.15 = (bf16[192,2048]{1,0:T(8,128)(2,1)}, bf16[192,2048]{1,0:T(8,128)(2,1)}, u32[]{:S(2)}, u32[]{:S(2)}) collective-permute-start(bf16[192,2048]{1,0:T(8,128)(2,1)} %constant_dynamic-update-slice_fusion.30), channel_id=1, source_target_pairs={{0,24},{1,25},{2,26},{3,27},{4,28},{5,29},{6,30},{7,31},{8,16},{9,... | collective-permute-start | bytes 2359304 | tf_op jit(solution)/shard_map/down_weight_columns/ppermute | solution.py:197
  201.3 18.3 %collective-permute-start.17 = (bf16[4,128,2048]{2,1,0:T(8,128)(2,1)}, bf16[4,128,2048]{2,1,0:T(8,128)(2,1)}, u32[]{:S(2)}, u32[]{:S(2)}) collective-permute-start(bf16[4,128,2048]{2,1,0:T(8,128)(2,1)} %dynamic-slice_bitcast_fusion.1), channel_id=1, source_target_pairs={{0,4},{1,5},{2,6},{3,7},{4,0},{5,1},{6,2},{7,3},{8,12},{9,13},{10,... | collective-permute-start | bytes 6291464 | tf_op jit(solution)/shard_map/attention_out_sum/ppermute | solution.py:197
  201.3 16.4 %collective-permute-start.21 = (bf16[128,2048]{1,0:T(8,128)(2,1)}, bf16[128,2048]{1,0:T(8,128)(2,1)}, u32[]{:S(2)}, u32[]{:S(2)}) collective-permute-start(bf16[128,2048]{1,0:T(8,128)(2,1)} %collective-permute-done.16), channel_id=1, source_target_pairs={{0,1},{1,2},{2,3},{3,0},{4,5},{5,6},{6,7},{7,4},{8,9},{9,10},{10,1... | collective-permute-start | bytes 1572872 | tf_op jit(solution)/shard_map/cotangent_ring/ppermute | solution.py:197
  219.6 30.8 %collective-permute-start.22 = (bf16[4,128,2048]{2,1,0:T(8,128)(2,1)S(1)}, bf16[4,128,2048]{2,1,0:T(8,128)(2,1)S(1)}, u32[]{:S(2)}, u32[]{:S(2)}) collective-permute-start(bf16[4,128,2048]{2,1,0:T(8,128)(2,1)S(1)} %pad_maximum_fusion.2), channel_id=1, source_target_pairs={{0,4},{1,5},{2,6},{3,7},{4,0},{5,1},{6,2},{7,3},{8,12},{9,13},{10,... | collective-permute-start | bytes 6291464 | tf_op jit(solution)/shard_map/cotangent_core/ppermute | solution.py:197
  223.8 25.8 %collective-permute-start.19 = (bf16[128,2048]{1,0:T(8,128)(2,1)S(1)}, bf16[128,2048]{1,0:T(8,128)(2,1)S(1)}, u32[]{:S(2)}, u32[]{:S(2)}) collective-permute-start(bf16[128,2048]{1,0:T(8,128)(2,1)S(1)} %get-tuple-element.291), channel_id=1, source_target_pairs={{0,16},{1,17},{2,18},{3,19},{4,20},{5,21},{6,22},{7,23},{8,24},{9,... | collective-permute-start | bytes 1572872 | tf_op jit(solution)/shard_map/attention_out_sum/ppermute | solution.py:197
  226.1 23.5 %collective-permute-start.20 = (bf16[128,2048]{1,0:T(8,128)(2,1)S(1)}, bf16[128,2048]{1,0:T(8,128)(2,1)S(1)}, u32[]{:S(2)}, u32[]{:S(2)}) collective-permute-start(bf16[128,2048]{1,0:T(8,128)(2,1)S(1)} %get-tuple-element.290), channel_id=1, source_target_pairs={{0,24},{1,25},{2,26},{3,27},{4,28},{5,29},{6,30},{7,31},{8,16},{9,... | collective-permute-start | bytes 1572872 | tf_op jit(solution)/shard_map/attention_out_sum/ppermute | solution.py:197
  252.3 16.5 %collective-permute-start.23 = (bf16[128,2048]{1,0:T(8,128)(2,1)S(1)}, bf16[128,2048]{1,0:T(8,128)(2,1)S(1)}, u32[]{:S(2)}, u32[]{:S(2)}) collective-permute-start(bf16[128,2048]{1,0:T(8,128)(2,1)S(1)} %multiply_convert_fusion), channel_id=1, source_target_pairs={{0,1},{1,2},{2,3},{3,0},{4,5},{5,6},{6,7},{7,4},{8,9},{9,10},{10,1... | collective-permute-start | bytes 1572872 | tf_op jit(solution)/shard_map/normed_two_ring/ppermute | solution.py:197
  268.9 16.1 %collective-permute-start.25 = (bf16[128,2048]{1,0:T(8,128)(2,1)S(1)}, bf16[128,2048]{1,0:T(8,128)(2,1)S(1)}, u32[]{:S(2)}, u32[]{:S(2)}) collective-permute-start(bf16[128,2048]{1,0:T(8,128)(2,1)S(1)} %collective-permute-done.23), channel_id=1, source_target_pairs={{0,1},{1,2},{2,3},{3,0},{4,5},{5,6},{6,7},{7,4},{8,9},{9,10},{10,1... | collective-permute-start | bytes 1572872 | tf_op jit(solution)/shard_map/normed_two_ring/ppermute | solution.py:197
  270.1 71.7 %collective-permute-start.36 = (bf16[128,2048]{1,0:T(8,128)(2,1)S(1)}, bf16[128,2048]{1,0:T(8,128)(2,1)S(1)}, u32[]{:S(2)}, u32[]{:S(2)}) collective-permute-start(bf16[128,2048]{1,0:T(8,128)(2,1)S(1)} %slice.210), channel_id=1, source_target_pairs={{0,4},{1,5},{2,6},{3,7},{4,0},{5,1},{6,2},{7,3},{8,12},{9,13},{10,... | collective-permute-start | bytes 1572872 | tf_op jit(solution)/shard_map/normed_two_grad_core/ppermute | solution.py:197
  285.0 16.3 %collective-permute-start.29 = (bf16[128,2048]{1,0:T(8,128)(2,1)S(1)}, bf16[128,2048]{1,0:T(8,128)(2,1)S(1)}, u32[]{:S(2)}, u32[]{:S(2)}) collective-permute-start(bf16[128,2048]{1,0:T(8,128)(2,1)S(1)} %collective-permute-done.25), channel_id=1, source_target_pairs={{0,1},{1,2},{2,3},{3,0},{4,5},{5,6},{6,7},{7,4},{8,9},{9,10},{10,1... | collective-permute-start | bytes 1572872 | tf_op jit(solution)/shard_map/normed_two_ring/ppermute | solution.py:197
  286.3 16.0 %collective-permute-start.27 = (bf16[128,2048]{1,0:T(8,128)(2,1)S(1)}, bf16[128,2048]{1,0:T(8,128)(2,1)S(1)}, u32[]{:S(2)}, u32[]{:S(2)}) collective-permute-start(bf16[128,2048]{1,0:T(8,128)(2,1)S(1)} %slice.194), channel_id=1, source_target_pairs={{0,4},{1,5},{2,6},{3,7},{4,0},{5,1},{6,2},{7,3},{8,12},{9,13},{10,... | collective-permute-start | bytes 1572872 | tf_op jit(solution)/shard_map/normed_two_grad_core/ppermute | solution.py:197
  302.6 16.2 %collective-permute-start.28 = (bf16[128,2048]{1,0:T(8,128)(2,1)S(1)}, bf16[128,2048]{1,0:T(8,128)(2,1)S(1)}, u32[]{:S(2)}, u32[]{:S(2)}) collective-permute-start(bf16[128,2048]{1,0:T(8,128)(2,1)S(1)} %add_convert_fusion.9), channel_id=1, source_target_pairs={{0,1},{1,2},{2,3},{3,0},{4,5},{5,6},{6,7},{7,4},{8,9},{9,10},{10,1... | collective-permute-start | bytes 1572872 | tf_op jit(solution)/shard_map/normed_two_grad_sum/ppermute | solution.py:197
  302.7 16.1 %collective-permute-start.31 = (bf16[128,2048]{1,0:T(8,128)(2,1)S(1)}, bf16[128,2048]{1,0:T(8,128)(2,1)S(1)}, u32[]{:S(2)}, u32[]{:S(2)}) collective-permute-start(bf16[128,2048]{1,0:T(8,128)(2,1)S(1)} %slice.197), channel_id=1, source_target_pairs={{0,4},{1,5},{2,6},{3,7},{4,0},{5,1},{6,2},{7,3},{8,12},{9,13},{10,... | collective-permute-start | bytes 1572872 | tf_op jit(solution)/shard_map/normed_two_grad_core/ppermute | solution.py:197
  321.3 55.1 %collective-permute-start.40 = (bf16[4,128,2048]{2,1,0:T(8,128)(2,1)S(1)}, bf16[4,128,2048]{2,1,0:T(8,128)(2,1)S(1)}, u32[]{:S(2)}, u32[]{:S(2)}) collective-permute-start(bf16[4,128,2048]{2,1,0:T(8,128)(2,1)S(1)} %pad_maximum_fusion.3), channel_id=1, source_target_pairs={{0,4},{1,5},{2,6},{3,7},{4,0},{5,1},{6,2},{7,3},{8,12},{9,13},{10,... | collective-permute-start | bytes 6291464 | tf_op jit(solution)/shard_map/out_core/ppermute | solution.py:197
  339.6 20.5 %collective-permute-start.37 = (bf16[512,768]{1,0:T(8,128)(2,1)S(1)}, bf16[512,768]{1,0:T(8,128)(2,1)S(1)}, u32[]{:S(2)}, u32[]{:S(2)}) collective-permute-start(bf16[512,768]{1,0:T(8,128)(2,1)S(1)} %get-tuple-element.279), channel_id=1, source_target_pairs={{0,8},{1,9},{2,10},{3,11},{4,12},{5,13},{6,14},{7,15},{8,0},{9,1},... | collective-permute-start | bytes 2359304 | tf_op jit(solution)/shard_map/down_gradient_columns/ppermute | solution.py:197
  341.1 33.1 %collective-permute-start.38 = (bf16[512,768]{1,0:T(8,128)(2,1)S(1)}, bf16[512,768]{1,0:T(8,128)(2,1)S(1)}, u32[]{:S(2)}, u32[]{:S(2)}) collective-permute-start(bf16[512,768]{1,0:T(8,128)(2,1)S(1)} %get-tuple-element.281), channel_id=1, source_target_pairs={{0,16},{1,17},{2,18},{3,19},{4,20},{5,21},{6,22},{7,23},{8,24},{9,... | collective-permute-start | bytes 2359304 | tf_op jit(solution)/shard_map/down_gradient_columns/ppermute | solution.py:197
  341.8 34.2 %collective-permute-start.39 = (bf16[512,768]{1,0:T(8,128)(2,1)S(1)}, bf16[512,768]{1,0:T(8,128)(2,1)S(1)}, u32[]{:S(2)}, u32[]{:S(2)}) collective-permute-start(bf16[512,768]{1,0:T(8,128)(2,1)S(1)} %get-tuple-element.280), channel_id=1, source_target_pairs={{0,24},{1,25},{2,26},{3,27},{4,28},{5,29},{6,30},{7,31},{8,16},{9,... | collective-permute-start | bytes 2359304 | tf_op jit(solution)/shard_map/down_gradient_columns/ppermute | solution.py:197
  376.4 21.4 %collective-permute-start.41 = (bf16[128,2048]{1,0:T(8,128)(2,1)S(1)}, bf16[128,2048]{1,0:T(8,128)(2,1)S(1)}, u32[]{:S(2)}, u32[]{:S(2)}) collective-permute-start(bf16[128,2048]{1,0:T(8,128)(2,1)S(1)} %get-tuple-element.184), channel_id=1, source_target_pairs={{0,8},{1,9},{2,10},{3,11},{4,12},{5,13},{6,14},{7,15},{8,0},{9,1},... | collective-permute-start | bytes 1572872 | tf_op jit(solution)/shard_map/attention_grad_columns/ppermute | solution.py:197
  377.0 22.5 %collective-permute-start.42 = (bf16[128,2048]{1,0:T(8,128)(2,1)S(1)}, bf16[128,2048]{1,0:T(8,128)(2,1)S(1)}, u32[]{:S(2)}, u32[]{:S(2)}) collective-permute-start(bf16[128,2048]{1,0:T(8,128)(2,1)S(1)} %get-tuple-element.184), channel_id=1, source_target_pairs={{0,16},{1,17},{2,18},{3,19},{4,20},{5,21},{6,22},{7,23},{8,24},{9,... | collective-permute-start | bytes 1572872 | tf_op jit(solution)/shard_map/attention_grad_columns/ppermute | solution.py:197
  378.8 21.7 %collective-permute-start.43 = (bf16[128,2048]{1,0:T(8,128)(2,1)S(1)}, bf16[128,2048]{1,0:T(8,128)(2,1)S(1)}, u32[]{:S(2)}, u32[]{:S(2)}) collective-permute-start(bf16[128,2048]{1,0:T(8,128)(2,1)S(1)} %get-tuple-element.184), channel_id=1, source_target_pairs={{0,24},{1,25},{2,26},{3,27},{4,28},{5,29},{6,30},{7,31},{8,16},{9,... | collective-permute-start | bytes 1572872 | tf_op jit(solution)/shard_map/attention_grad_columns/ppermute | solution.py:197
  380.2 16.2 %collective-permute-start.45 = (bf16[128,2048]{1,0:T(8,128)(2,1)S(1)}, bf16[128,2048]{1,0:T(8,128)(2,1)S(1)}, u32[]{:S(2)}, u32[]{:S(2)}) collective-permute-start(bf16[128,2048]{1,0:T(8,128)(2,1)S(1)} %fusion.62), channel_id=1, source_target_pairs={{0,1},{1,2},{2,3},{3,0},{4,5},{5,6},{6,7},{7,4},{8,9},{9,10},{10,1... | collective-permute-start | bytes 1572872 | tf_op jit(solution)/shard_map/out_ring/ppermute | solution.py:197
  397.4 19.0 %collective-permute-start.46 = (bf16[128,2048]{1,0:T(8,128)(2,1)}, bf16[128,2048]{1,0:T(8,128)(2,1)}, u32[]{:S(2)}, u32[]{:S(2)}) collective-permute-start(bf16[128,2048]{1,0:T(8,128)(2,1)} %add_convert_fusion.4), channel_id=1, source_target_pairs={{0,1},{1,2},{2,3},{3,0},{4,5},{5,6},{6,7},{7,4},{8,9},{9,10},{10,1... | collective-permute-start | bytes 1572872 | tf_op jit(solution)/shard_map/out_ring/ppermute | solution.py:197
  401.3 17.6 %collective-permute-start.44 = (bf16[4,128,2048]{2,1,0:T(8,128)(2,1)}, bf16[4,128,2048]{2,1,0:T(8,128)(2,1)}, u32[]{:S(2)}, u32[]{:S(2)}) collective-permute-start(bf16[4,128,2048]{2,1,0:T(8,128)(2,1)} %bitcast_dynamic-update-slice_fusion.8), channel_id=1, source_target_pairs={{0,4},{1,5},{2,6},{3,7},{4,0},{5,1},{6,2},{7,3},{8,12},{9,13},{10,... | collective-permute-start | bytes 6291464 | tf_op jit(solution)/shard_map/attention_grad_core/ppermute | solution.py:197
  437.4 21.4 %collective-permute-start.49 = (bf16[128,2048]{1,0:T(8,128)(2,1)S(1)}, bf16[128,2048]{1,0:T(8,128)(2,1)S(1)}, u32[]{:S(2)}, u32[]{:S(2)}) collective-permute-start(bf16[128,2048]{1,0:T(8,128)(2,1)S(1)} %fusion.76), channel_id=1, source_target_pairs={{0,1},{1,2},{2,3},{3,0},{4,5},{5,6},{6,7},{7,4},{8,9},{9,10},{10,1... | collective-permute-start | bytes 1572872 | tf_op jit(solution)/shard_map/early_ring/ppermute | solution.py:197
  441.6 23.9 %collective-permute-start.48 = (bf16[128,2048]{1,0:T(8,128)(2,1)S(1)}, bf16[128,2048]{1,0:T(8,128)(2,1)S(1)}, u32[]{:S(2)}, u32[]{:S(2)}) collective-permute-start(bf16[128,2048]{1,0:T(8,128)(2,1)S(1)} %copy-done.37), channel_id=1, source_target_pairs={{0,1},{1,2},{2,3},{3,0},{4,5},{5,6},{6,7},{7,4},{8,9},{9,10},{10,1... | collective-permute-start | bytes 1572872 | tf_op jit(solution)/shard_map/out_ring/ppermute | solution.py:197
  453.1 36.6 %collective-permute-start.51 = (bf16[64,1536]{1,0:T(8,128)(2,1)S(1)}, bf16[64,1536]{1,0:T(8,128)(2,1)S(1)}, u32[]{:S(2)}, u32[]{:S(2)}) collective-permute-start(bf16[64,1536]{1,0:T(8,128)(2,1)S(1)} %get-tuple-element.334), channel_id=1, source_target_pairs={{0,1},{1,2},{2,3},{3,0},{4,5},{5,6},{6,7},{7,4},{8,9},{9,10},{10,1... | collective-permute-start | bytes 589832 | tf_op jit(solution)/shard_map/down_gradient_planes/ppermute | solution.py:197
  456.0 33.7 %collective-permute-start.52 = (bf16[64,1536]{1,0:T(8,128)(2,1)S(1)}, bf16[64,1536]{1,0:T(8,128)(2,1)S(1)}, u32[]{:S(2)}, u32[]{:S(2)}) collective-permute-start(bf16[64,1536]{1,0:T(8,128)(2,1)S(1)} %get-tuple-element.333), channel_id=1, source_target_pairs={{0,2},{1,3},{2,0},{3,1},{4,6},{5,7},{6,4},{7,5},{8,10},{9,11},{10,... | collective-permute-start | bytes 589832 | tf_op jit(solution)/shard_map/down_gradient_planes/ppermute | solution.py:197
  456.2 33.5 %collective-permute-start.53 = (bf16[64,1536]{1,0:T(8,128)(2,1)S(1)}, bf16[64,1536]{1,0:T(8,128)(2,1)}, u32[]{:S(2)}, u32[]{:S(2)}) collective-permute-start(bf16[64,1536]{1,0:T(8,128)(2,1)S(1)} %get-tuple-element.332), channel_id=1, source_target_pairs={{0,3},{1,0},{2,1},{3,2},{4,7},{5,4},{6,5},{7,6},{8,11},{9,8},{10,9... | collective-permute-start | bytes 589832 | tf_op jit(solution)/shard_map/down_gradient_planes/ppermute | solution.py:197
  466.8 22.0 %collective-permute-start.50 = (bf16[128,2048]{1,0:T(8,128)(2,1)S(1)}, bf16[128,2048]{1,0:T(8,128)(2,1)S(1)}, u32[]{:S(2)}, u32[]{:S(2)}) collective-permute-start(bf16[128,2048]{1,0:T(8,128)(2,1)S(1)} %fusion.58), channel_id=1, source_target_pairs={{0,1},{1,2},{2,3},{3,0},{4,5},{5,6},{6,7},{7,4},{8,9},{9,10},{10,1... | collective-permute-start | bytes 1572872 | tf_op jit(solution)/shard_map/early_ring/ppermute | solution.py:197
  495.1 15.7 %collective-permute-start.68 = (bf16[128,2048]{1,0:T(8,128)(2,1)}, bf16[128,2048]{1,0:T(8,128)(2,1)S(1)}, u32[]{:S(2)}, u32[]{:S(2)}) collective-permute-start(bf16[128,2048]{1,0:T(8,128)(2,1)} %fusion.57), channel_id=1, source_target_pairs={{0,1},{1,2},{2,3},{3,0},{4,5},{5,6},{6,7},{7,4},{8,9},{9,10},{10,1... | collective-permute-start | bytes 1572872 | tf_op jit(solution)/shard_map/early_ring/ppermute | solution.py:197
  518.8 16.1 %collective-permute-start.55 = (bf16[128,2048]{1,0:T(8,128)(2,1)}, bf16[128,2048]{1,0:T(8,128)(2,1)}, u32[]{:S(2)}, u32[]{:S(2)}) collective-permute-start(bf16[128,2048]{1,0:T(8,128)(2,1)} %get-tuple-element.282), channel_id=1, source_target_pairs={{0,8},{1,9},{2,10},{3,11},{4,12},{5,13},{6,14},{7,15},{8,0},{9,1},... | collective-permute-start | bytes 1572872 | tf_op jit(solution)/shard_map/normed_grad_sum/ppermute | solution.py:197
  520.3 25.5 %collective-permute-start.56 = (bf16[128,2048]{1,0:T(8,128)(2,1)}, bf16[128,2048]{1,0:T(8,128)(2,1)}, u32[]{:S(2)}, u32[]{:S(2)}) collective-permute-start(bf16[128,2048]{1,0:T(8,128)(2,1)} %get-tuple-element.284), channel_id=1, source_target_pairs={{0,16},{1,17},{2,18},{3,19},{4,20},{5,21},{6,22},{7,23},{8,24},{9,... | collective-permute-start | bytes 1572872 | tf_op jit(solution)/shard_map/normed_grad_sum/ppermute | solution.py:197
  520.8 25.0 %collective-permute-start.57 = (bf16[128,2048]{1,0:T(8,128)(2,1)}, bf16[128,2048]{1,0:T(8,128)(2,1)}, u32[]{:S(2)}, u32[]{:S(2)}) collective-permute-start(bf16[128,2048]{1,0:T(8,128)(2,1)} %get-tuple-element.283), channel_id=1, source_target_pairs={{0,24},{1,25},{2,26},{3,27},{4,28},{5,29},{6,30},{7,31},{8,16},{9,... | collective-permute-start | bytes 1572872 | tf_op jit(solution)/shard_map/normed_grad_sum/ppermute | solution.py:197
  528.8 31.6 %collective-permute-start.66 = (bf16[128,2048]{1,0:T(8,128)(2,1)}, bf16[128,2048]{1,0:T(8,128)(2,1)}, u32[]{:S(2)}, u32[]{:S(2)}) collective-permute-start(bf16[128,2048]{1,0:T(8,128)(2,1)} %add_convert_fusion.1), channel_id=1, source_target_pairs={{0,1},{1,2},{2,3},{3,0},{4,5},{5,6},{6,7},{7,4},{8,9},{9,10},{10,1... | collective-permute-start | bytes 1572872 | tf_op jit(solution)/shard_map/qkv_gradient_sum/ppermute | solution.py:197
  575.4 36.1 %collective-permute-start.70 = (bf16[192,2048]{1,0:T(8,128)(2,1)S(1)}, bf16[192,2048]{1,0:T(8,128)(2,1)S(1)}, u32[]{:S(2)}, u32[]{:S(2)}) collective-permute-start(bf16[192,2048]{1,0:T(8,128)(2,1)S(1)} %get-tuple-element.292), channel_id=1, source_target_pairs={{0,2},{1,11},{2,16},{3,25},{4,6},{5,15},{6,20},{7,29},{8,3},{9,8},... | collective-permute-start | bytes 2359304 | tf_op jit(solution)/shard_map/up_gradient_move/ppermute | solution.py:197
  577.8 35.8 %collective-permute-start.69 = (bf16[192,2048]{1,0:T(8,128)(2,1)S(1)}, bf16[192,2048]{1,0:T(8,128)(2,1)S(1)}, u32[]{:S(2)}, u32[]{:S(2)}) collective-permute-start(bf16[192,2048]{1,0:T(8,128)(2,1)S(1)} %get-tuple-element.293), channel_id=1, source_target_pairs={{0,0},{1,9},{2,18},{3,27},{4,4},{5,13},{6,22},{7,31},{8,1},{9,10},... | collective-permute-start | bytes 2359304 | tf_op jit(solution)/shard_map/gate_gradient_move/ppermute | solution.py:197
  (80 other events, 1514.7 us)
Sparse Core Ops, SparseCore 0:
  9.9 60.9 all-gather.5
  73.1 53.6 all-gather.3
  423.9 71.1 reduce-scatter.1

commit v3 on v2

--- a/solution.py
+++ b/solution.py
@@ -57,10 +57,19 @@
     return jnp.where(allowed, jnp.exp(scores), 0.0)
 
 
+def query_blocks(length):
+    block = min(256, length)
+    for start in range(0, length, block):
+        yield slice(start, start + block), slice(0, start + block)
+
+
 def forward_kernel(scale, q_ref, k_ref, v_ref, row_ref, column_ref, mixed_ref):
-    weights = block_weights(q_ref[...], k_ref[...], row_ref[...], column_ref[...], scale)
-    total = jnp.sum(weights, axis=1, keepdims=True)
-    mixed_ref[...] = dot(weights.astype(LOW), v_ref[...]) / total
+    for rows, keys in query_blocks(q_ref.shape[0]):
+        weights = block_weights(
+            q_ref[rows, :], k_ref[keys, :], row_ref[rows, :], column_ref[:, keys], scale
+        )
+        total = jnp.sum(weights, axis=1, keepdims=True)
+        mixed_ref[rows, :] = dot(weights.astype(LOW), v_ref[keys, :]) / total
 
 
 def backward_kernel(
@@ -77,30 +86,28 @@
     dk_ref,
     dv_ref,
 ):
-    first = (pl.program_id(1) == 0) & (lax.rem(pl.program_id(0), group) == 0)
-
-    @pl.when(first)
+    @pl.when(lax.rem(pl.program_id(0), group) == 0)
     def _():
         dk_ref[...] = jnp.zeros_like(dk_ref)
         dv_ref[...] = jnp.zeros_like(dv_ref)
 
-    query, key, value = q_ref[...], k_ref[...], v_ref[...]
-    mixed_grad = grad_ref[...]
-    delta = jnp.sum(mixed_grad.astype(WIDE) * mixed_ref[...], axis=1, keepdims=True)
-    weights = block_weights(query, key, row_ref[...], column_ref[...], scale)
-    probability = weights * (1.0 / jnp.sum(weights, axis=1, keepdims=True))
-    prob_grad = dot(mixed_grad, value, 1, 1)
-    score_grad = (probability * (prob_grad - delta)).astype(LOW)
-    dq_ref[...] = dot(score_grad, key) * scale
-    dk_ref[...] += dot(score_grad, query, 0, 0) * scale
-    dv_ref[...] += dot(probability.astype(LOW), mixed_grad, 0, 0)
-
-
-def attention_specs(length, head_width, group, block):
-    per_query = pl.BlockSpec((block, head_width), lambda h, i: (i, h))
-    per_key = pl.BlockSpec((length, head_width), lambda h, i: (0, h // group))
-    rows = pl.BlockSpec((block, 2), lambda h, i: (i, 0))
-    columns = pl.BlockSpec((2, length), lambda h, i: (0, 0))
+    for rows, keys in query_blocks(q_ref.shape[0]):
+        query, key, mixed_grad = q_ref[rows, :], k_ref[keys, :], grad_ref[rows, :]
+        delta = jnp.sum(mixed_grad.astype(WIDE) * mixed_ref[rows, :], axis=1, keepdims=True)
+        weights = block_weights(query, key, row_ref[rows, :], column_ref[:, keys], scale)
+        probability = weights * (1.0 / jnp.sum(weights, axis=1, keepdims=True))
+        prob_grad = dot(mixed_grad, v_ref[keys, :], 1, 1)
+        score_grad = (probability * (prob_grad - delta)).astype(LOW)
+        dq_ref[rows, :] = dot(score_grad, key) * scale
+        dk_ref[keys, :] += dot(score_grad, query, 0, 0) * scale
+        dv_ref[keys, :] += dot(probability.astype(LOW), mixed_grad, 0, 0)
+
+
+def attention_specs(length, head_width, group):
+    per_query = pl.BlockSpec((length, head_width), lambda h: (0, h))
+    per_key = pl.BlockSpec((length, head_width), lambda h: (0, h // group))
+    rows = pl.BlockSpec((length, 2), lambda h: (0, 0))
+    columns = pl.BlockSpec((2, length), lambda h: (0, 0))
     return per_query, per_key, rows, columns
 
 
@@ -108,17 +115,16 @@
     length, width = queries.shape
     heads = width // head_width
     group = width // keys.shape[1]
-    block = min(256, length)
-    per_query, per_key, rows, columns = attention_specs(length, head_width, group, block)
+    per_query, per_key, rows, columns = attention_specs(length, head_width, group)
     return pl.pallas_call(
         functools.partial(forward_kernel, head_width ** (-0.5)),
-        grid=(heads, length // block),
+        grid=(heads,),
         in_specs=[per_query, per_key, per_key, rows, columns],
         out_specs=per_query,
         out_shape=jax.ShapeDtypeStruct((length, width), WIDE),
-        compiler_params=pltpu.CompilerParams(vmem_limit_bytes=40 * 1024 * 1024),
+        compiler_params=pltpu.CompilerParams(vmem_limit_bytes=48 * 1024 * 1024),
         cost_estimate=pl.CostEstimate(
-            flops=4 * length * length * width,
+            flops=3 * length * length * width,
             bytes_accessed=12 * length * width,
             transcendentals=length * length * heads,
         ),
@@ -131,29 +137,20 @@
     length, width = queries.shape
     heads = width // head_width
     group = width // keys.shape[1]
-    block = min(256, length)
-    per_query, per_key, rows, columns = attention_specs(length, head_width, group, block)
+    per_query, per_key, rows, columns = attention_specs(length, head_width, group)
     return pl.pallas_call(
         functools.partial(backward_kernel, head_width ** (-0.5), group),
-        grid=(heads, length // block),
-        in_specs=[
-            per_query,
-            per_key,
-            per_key,
-            per_query,
-            per_query,
-            rows,
-            columns,
-        ],
+        grid=(heads,),
+        in_specs=[per_query, per_key, per_key, per_query, per_query, rows, columns],
         out_specs=[per_query, per_key, per_key],
         out_shape=[
             jax.ShapeDtypeStruct((length, width), WIDE),
             jax.ShapeDtypeStruct(keys.shape, WIDE),
             jax.ShapeDtypeStruct(keys.shape, WIDE),
         ],
-        compiler_params=pltpu.CompilerParams(vmem_limit_bytes=40 * 1024 * 1024),
+        compiler_params=pltpu.CompilerParams(vmem_limit_bytes=48 * 1024 * 1024),
         cost_estimate=pl.CostEstimate(
-            flops=10 * length * length * width,
+            flops=7 * length * length * width,
             bytes_accessed=24 * length * width,
             transcendentals=length * length * heads,
         ),
@@ -282,19 +279,22 @@
     def plane_sum(partial):
         return plane_columns_sum(plane_chip_sum(partial))
 
-    def small_sum(vector):
+    def small_columns(vector):
         shaped = vector.reshape(column_count, 2, plane_count, -1)
-        total = lax.dynamic_index_in_dim(shaped, core, 1, keepdims=False)
-        total = total + to_core(lax.dynamic_index_in_dim(shaped, 1 - core, 1, keepdims=False))
-        for place, hop, count in (
-            (column, to_column, column_count),
-            (plane, to_plane, plane_count),
-        ):
-            parts = [
-                lax.dynamic_index_in_dim(total, place ^ d, 0, keepdims=False) for d in range(count)
-            ]
-            total = sum(hop(part, d) if d else part for d, part in enumerate(parts))
-        return total
+        chip = lax.dynamic_index_in_dim(shaped, core, 1, keepdims=False)
+        chip = chip + to_core(lax.dynamic_index_in_dim(shaped, 1 - core, 1, keepdims=False))
+        parts = [
+            lax.dynamic_index_in_dim(chip, column ^ d, 0, keepdims=False)
+            for d in range(column_count)
+        ]
+        return sum(to_column(part, d) if d else part for d, part in enumerate(parts))
+
+    def small_planes(vector):
+        parts = [
+            lax.dynamic_index_in_dim(vector, plane ^ d, 0, keepdims=False)
+            for d in range(plane_count)
+        ]
+        return sum(to_plane(part, d) if d else part for d, part in enumerate(parts))
 
     def take(array, start, size, axis=0):
         return lax.dynamic_slice_in_dim(array, start, size, axis)
@@ -354,28 +354,23 @@
     )
     small_gains = jnp.concatenate([attention_gain, feedforward_gain, query_gain, key_gain])[None]
     gains_behind = named("gain_gather", doubled_planes, small_gains)
-    numbers, gains_behind, weights = fence(
-        (
-            numbers,
-            gains_behind,
-            (query_weight, key_weight, value_weight, output_gate_weight, output_weight, down_weight),
-        )
-    )
-    query_weight, key_weight, value_weight, output_gate_weight, output_weight, down_weight = weights
-
-    head_pieces = named(
-        "head_weights",
-        shard_pieces,
-        jnp.concatenate(
-            [
-                my_chunk(key_weight, key_width),
-                my_chunk(value_weight, key_width),
-                my_chunk(query_weight, query_width),
-                my_chunk(output_gate_weight, query_width),
-            ],
-            axis=1,
-        ),
-    )
+    head_chunk = jnp.concatenate(
+        [
+            my_chunk(key_weight, key_width),
+            my_chunk(value_weight, key_width),
+            my_chunk(query_weight, query_width),
+            my_chunk(output_gate_weight, query_width),
+        ],
+        axis=1,
+    )
+    numbers, gains_behind, head_chunk = fence((numbers, gains_behind, head_chunk))
+
+    head_pieces = named("head_weights", shard_pieces, head_chunk)
+    output_weight, down_weight, gate_weight, up_weight, first_piece = fence(
+        (output_weight, down_weight, gate_weight, up_weight, head_pieces[0])
+    )
+    head_pieces[0] = first_piece
+    output_chunk = take(output_weight, seq_index * query_width, query_width)
     down_chunks = [
         take(
             down_weight,
@@ -384,17 +379,8 @@
         )
         for d in range(plane_count)
     ]
-    down_chunks, last_pieces = fence((down_chunks, head_pieces[-2:]))
-    head_pieces = head_pieces[:-2] + last_pieces
-    down_blocks = [
-        named("down_weight_planes", up, block, d) if d else block
-        for d, block in enumerate(down_chunks)
-    ]
-    head_weights = shard_rows(head_pieces)
     with jax.named_scope("output_weight_gather"):
-        output_rows = lax.all_gather(
-            take(output_weight, seq_index * query_width, query_width), "fsdp", axis=1, tiled=True
-        )
+        output_rows = lax.all_gather(output_chunk, "fsdp", axis=1, tiled=True)
     gain_parts = jnp.concatenate(
         [
             take(gains_behind, plane ^ f, 1)
@@ -422,6 +408,15 @@
     gathered_wide = gathered_inputs.astype(WIDE)
     scale_one = lax.rsqrt(jnp.mean(gathered_wide * gathered_wide, axis=-1, keepdims=True) + EPSILON)
     normed = (gathered_wide * scale_one * gain_one).astype(LOW)
+    down_chunks, last_pieces, normed, cosine, sine_part = fence(
+        (down_chunks, head_pieces[-2:], normed, cosine, sine_part)
+    )
+    head_pieces = head_pieces[:-2] + last_pieces
+    down_blocks = [
+        named("down_weight_planes", up, block, d) if d else block
+        for d, block in enumerate(down_chunks)
+    ]
+    head_weights = shard_rows(head_pieces)
     gate_half = take(gate_weight, core * hidden_width, hidden_width, 1)
     up_half = take(up_weight, core * hidden_width, hidden_width, 1)
     (
@@ -458,6 +453,10 @@
     cotangent_ring = cotangent_step([cotangent_low])
     for _ in range(plane_count - 4):
         cotangent_ring = cotangent_step(cotangent_ring)
+    query_heads = dot(normed, head_weights[:, 2 * key_width : 2 * key_width + query_width])
+    key_heads = dot(normed, head_weights[:, :key_width])
+    query_heads, key_heads, cotangent_ring = fence((query_heads, key_heads, cotangent_ring))
+    cotangent_ring = cotangent_step(cotangent_ring)
 
     def head_prepare(values, gain_vector):
         return prepare_heads(values, gain_vector, cosine, sine_part)
@@ -471,10 +470,10 @@
     logit_weights = head_weights[:, 2 * key_width + query_width :]
     query_prepared = [
         jax.vjp(head_prepare, head, query_gain_full)
-        for head in split_heads(dot(normed, query_weights))
+        for head in split_heads(query_heads)
     ]
     key_prepared = [
-        jax.vjp(head_prepare, head, key_gain_full) for head in split_heads(dot(normed, key_weights))
+        jax.vjp(head_prepare, head, key_gain_full) for head in split_heads(key_heads)
     ]
     values = dot(normed, value_weights).astype(LOW)
     queries = jnp.concatenate([head.astype(LOW) for head, _ in query_prepared], axis=1)
@@ -496,7 +495,7 @@
     scale_two = lax.rsqrt(jnp.mean(middle * middle, axis=-1, keepdims=True) + EPSILON)
     normed_two = (middle * scale_two * gain_two).astype(LOW)
     down_rows = by_rows(down_pieces)
-    cotangent_ring = jnp.stack(cotangent_step(cotangent_ring))
+    cotangent_ring = jnp.stack(cotangent_ring)
     all_cotangent = jnp.concatenate(
         [cotangent_ring, named("cotangent_core", to_core, cotangent_ring)], axis=1
     )
@@ -539,19 +538,24 @@
         up_grads.append(up_grad)
     last_piece, hidden_blocks, out_pieces = fence((grad_pieces[-1], hidden_blocks, out_pieces))
     grad_pieces[-1] = last_piece
-    normed_two_grad = named("normed_two_grad_sum", ring_sum, grad_pieces)
-
-    def columns_sum(pieces):
-        total = lax.dynamic_index_in_dim(pieces, column, 0, keepdims=False).astype(WIDE)
-        for d in range(1, column_count):
-            piece = lax.dynamic_index_in_dim(pieces, column ^ d, 0, keepdims=False)
-            total = total + to_column(piece, d).astype(WIDE)
-        return total.astype(LOW)
-
     down_terms = dot(all_cotangent, jnp.concatenate(hidden_blocks), 0, 0).astype(LOW)
-    down_mine = named(
-        "down_gradient_columns", columns_sum, down_terms.reshape(column_count, -1, hidden_width)
-    )
+    running = named("normed_two_grad_sum", ring_step, grad_pieces[1], grad_pieces[2])
+    running, down_terms = fence((running, down_terms))
+    for i in range(2, plane_count):
+        last = i == plane_count - 1
+        running = named(
+            "normed_two_grad_sum", ring_step, running, grad_pieces[(i + 1) % plane_count], last
+        )
+    normed_two_grad = running
+
+    down_terms = down_terms.reshape(column_count, -1, hidden_width)
+    down_sent = [
+        lax.dynamic_index_in_dim(down_terms, column ^ d, 0, keepdims=False)
+        for d in range(column_count)
+    ]
+    down_sent[1:3] = [
+        named("down_gradient_columns", to_column, down_sent[d], d) for d in (1, 2)
+    ]
     out_other = named("out_core", to_core, jnp.stack([piece for _, piece in out_pieces]))
 
     weighted = gain_two * normed_two_grad
@@ -562,20 +566,19 @@
     )
     feedforward_gain_terms = jnp.sum(normed_two_grad * (middle * scale_two), axis=0)
     attention_grad_local = middle_grad.astype(LOW)
-    attention_grad_local, down_mine, out_other = fence(
-        (attention_grad_local, down_mine, out_other)
+    attention_grad_local, down_sent, out_other = fence(
+        (attention_grad_local, down_sent, out_other)
     )
 
     out_terms = [
         (piece.astype(WIDE) + out_other[i].astype(WIDE)).astype(LOW)
         for i, (piece, _) in enumerate(out_pieces)
     ]
+    out_terms, gate_grads, up_grads = fence((out_terms, gate_grads, up_grads))
     out_running = out_terms[1]
-    for i in range(1, plane_count - 1):
+    for i in range(1, plane_count - 2):
         out_running = named("out_ring", ring_step, out_running, out_terms[i + 1])
     grad_columns = named("attention_grad_columns", plane_columns, attention_grad_local)
-    first, gate_grads, up_grads = fence((grad_columns[1], gate_grads, up_grads))
-    grad_columns[1] = first
     attention_grad = named("attention_grad_core", plane_gather, grad_columns)
     all_normed_two = jnp.concatenate(normed_two_blocks, axis=0)
 
@@ -595,6 +598,9 @@
             for terms, shift in ((gate_terms, 0), (up_terms, up_shift))
         ]
     )
+    for d in range(3, column_count):
+        down_sent[d] = named("down_gradient_columns", to_column, down_sent[d], d)
+    down_mine = sum(block.astype(WIDE) for block in down_sent).astype(LOW)
     down_mine = down_mine.reshape(2, plane_count, -1, hidden_width)
     own_half = lax.dynamic_index_in_dim(down_mine, core, 0, keepdims=False)
     other_half = named(
@@ -619,7 +625,7 @@
             axis_index_groups=[[2 * q + c for q in range(column_count)] for c in range(2)],
             tiled=True,
         )
-    out_total = named("out_ring", ring_step, out_running, out_terms[0], True)
+    out_running = named("out_ring", ring_step, out_running, out_terms[plane_count - 1])
     gated_grad = dot(attention_grad, output_rows, 1, 1).astype(LOW).astype(WIDE)
     logit_grad = (gated_grad * mixed * gate_open * (1.0 - gate_open)).astype(LOW)
     mixed_grad = (gated_grad * gate_open).astype(LOW)
@@ -639,9 +645,10 @@
     query_rot_grad, key_rot_grad, value_sum = attention_backward(
         queries, keys, values, mixed, mixed_grad, row_info, column_info, head_width
     )
-    query_rot_grad, key_rot_grad, value_sum, out_total, early_running = fence(
-        (query_rot_grad, key_rot_grad, value_sum, out_total, early_running)
-    )
+    query_rot_grad, key_rot_grad, value_sum, out_running, early_running = fence(
+        (query_rot_grad, key_rot_grad, value_sum, out_running, early_running)
+    )
+    out_total = named("out_ring", ring_step, out_running, out_terms[0], True)
     early_running = named("early_ring", ring_step, early_running, early_term(plane_count - 1))
     down_moved = []
     for d in range(plane_count):
@@ -677,8 +684,8 @@
         for i in range(plane_count)
     ]
     joined_grad = jnp.concatenate([query_grad, key_grad, value_grad, logit_grad], axis=1)
-    qkv_pieces, joined_grad, early_running, feed_mine, down_moved = fence(
-        (qkv_pieces, joined_grad, early_running, feed_mine, down_moved)
+    qkv_pieces, joined_grad, early_running, feed_mine, down_moved, out_total = fence(
+        (qkv_pieces, joined_grad, early_running, feed_mine, down_moved, out_total)
     )
 
     normed_grad_partial = dot(
@@ -698,8 +705,9 @@
     vectors = [attention_gain_terms, query_gain_grad, key_gain_grad / sharing, feedforward_gain_terms]
     normed_grad, vectors = fence((normed_grad, vectors))
     vectors = [vector.reshape(seq_count, plane_count, -1) for vector in vectors]
-    small = named("gain_sum", small_sum, jnp.concatenate(vectors, axis=2))
-    small, qkv_total, feed_mine = fence((small, qkv_total, feed_mine))
+    small = named("gain_columns", small_columns, jnp.concatenate(vectors, axis=2))
+    small, feed_mine = fence((small, feed_mine))
+    small = named("gain_planes", small_planes, small)
     piece = feed_mine.shape[0] // 2
     gate_moved = named(
         "gate_gradient_move",

time: 631 us -> 611 us (0.968)
  starting transfers between devices: 129 us -> 82.2 us
  waiting for transfers between devices: 260 us -> 278 us
  other arithmetic: 55.2 us -> 63.5 us
  local copies, waits for them, and re-layouts: 75.4 us -> 81.9 us
  Pallas kernels: 15.1 us -> 8.77 us
    ppermute x71, starting transfers between devices: 124 us -> 77.4 us  [send(): return lax.ppermute(value, AXES, pairs)]
    ppermute x71, waiting for transfers between devices: 253 us -> 276 us  [send(): return lax.ppermute(value, AXES, pairs)]
    unnamed x124 -> x216, local copies, waits for them, and re-layouts: 12.5 us -> 14.2 us
  transfers between devices with their start and end apart: 75 -> 75, of which waited for: 35 -> 31; matrix products, arithmetic and copies ran while one was open for 29% -> 32% of each run, Pallas kernels for 2% -> 1%
where the time goes in v3:
time: 611 us; the launch traced here: 600 us
  waiting for transfers between devices  278 us (45%)
  starting transfers between devices  82.2 us (13%)
  local copies, waits for them, and re-layouts  81.9 us (13%)
  matrix products  70 us (11%)
  other arithmetic  63.5 us (10%)
  between operations  16.2 us (3%)
  Pallas kernels  8.77 us (1%)
    ppermute x71, waiting for transfers between devices, send(): return lax.ppermute(value, AXES, pairs)  276 us
    ppermute x71, starting transfers between devices, send(): return lax.ppermute(value, AXES, pairs)  77.4 us
    dot_general x36, matrix products, dot(): lax.dot_general(left, right, (((left_dim,), (right_dim,)), ((), ())), pre...  70 us
    unnamed x216, local copies, waits for them, and re-layouts  14.2 us
  transfers between devices with their start and end apart: 75, of which 31 were waited for; matrix products, arithmetic and copies ran while one was open for 32% of the time, Pallas kernels for 1%

profile of v3, /device:TPU:4, one launch (start us, length us, event | category | flops | bytes accessed | tf_op | source)
XLA Modules:
  0.0 600.4 jit_solution(1078113915027371786)
XLA Ops:
  10.8 2.8 concatenate.124
  25.3 5.5 collective-permute-start.5
  30.7 5.4 collective-permute-start.7
  40.2 3.0 multiply_sine_fusion
  43.5 37.9 %collective-permute-done.5 = bf16[512,768]{1,0:T(8,128)(2,1)} collective-permute-done((bf16[512,768]{1,0:T(8,128)(2,1)}, bf16[512,768]{1,0:T(8,128)(2,1)}, u32[]{:S(2)}, u32[]{:S(2)}) %collective-permute-start.5) | collective-permute-done | bytes 786464 | tf_op jit(solution)/shard_map/head_weights/ppermute | solution.py:194
  84.1 2.9 constant_dynamic-update-slice_fusion.37
  88.3 5.1 constant_dynamic-slice_fusion.10
  93.3 21.9 %collective-permute-done.6 = bf16[512,768]{1,0:T(8,128)(2,1)} collective-permute-done((bf16[512,768]{1,0:T(8,128)(2,1)}, bf16[512,768]{1,0:T(8,128)(2,1)}, u32[]{:S(2)}, u32[]{:S(2)}) %collective-permute-start.6) | collective-permute-done | bytes 786464 | tf_op jit(solution)/shard_map/head_weights/ppermute | solution.py:194
  117.4 3.2 fusion.4
  120.9 3.0 fusion.2
  130.1 6.7 %collective-permute-done.10 = bf16[192,512]{1,0:T(8,128)(2,1)S(1)} collective-permute-done((bf16[192,512]{1,0:T(8,128)(2,1)S(1)}, bf16[192,512]{1,0:T(8,128)(2,1)S(1)}, u32[]{:S(2)}, u32[]{:S(2)}) %collective-permute-start.10) | collective-permute-done | bytes 196640 | tf_op jit(solution)/shard_map/down_weight_planes/ppermute | solution.py:194
  142.1 4.3 collective-permute-start.15
  148.1 3.5 convolution_convert_fusion.15.v_ref
  154.2 3.7 fusion.106
  157.9 2.8 collective-permute-done.12
  163.8 11.6 %collective-permute-done.13 = bf16[128,2048]{1,0:T(8,128)(2,1)S(1)} collective-permute-done((bf16[128,2048]{1,0:T(8,128)(2,1)}, bf16[128,2048]{1,0:T(8,128)(2,1)S(1)}, u32[]{:S(2)}, u32[]{:S(2)}) %collective-permute-start.13) | collective-permute-done | bytes 524320 | tf_op jit(solution)/shard_map/cotangent_ring/ppermute | solution.py:194
  178.3 3.6 multiply_convert_fusion.1
  183.2 4.7 collective-permute-done.17
  206.6 7.9 %collective-permute-done.19 = bf16[128,2048]{1,0:T(8,128)(2,1)S(1)} collective-permute-done((bf16[128,2048]{1,0:T(8,128)(2,1)S(1)}, bf16[128,2048]{1,0:T(8,128)(2,1)S(1)}, u32[]{:S(2)}, u32[]{:S(2)}) %collective-permute-start.19) | collective-permute-done | bytes 524320 | tf_op jit(solution)/shard_map/attention_out_sum/ppermute | solution.py:194
  214.6 11.5 %collective-permute-done.20 = bf16[128,2048]{1,0:T(8,128)(2,1)S(1)} collective-permute-done((bf16[128,2048]{1,0:T(8,128)(2,1)S(1)}, bf16[128,2048]{1,0:T(8,128)(2,1)S(1)}, u32[]{:S(2)}, u32[]{:S(2)}) %collective-permute-start.20) | collective-permute-done | bytes 524320 | tf_op jit(solution)/shard_map/attention_out_sum/ppermute | solution.py:194
  228.3 3.5 fusion.121
  238.1 6.3 %collective-permute-done.23 = bf16[128,2048]{1,0:T(8,128)(2,1)S(1)} collective-permute-done((bf16[128,2048]{1,0:T(8,128)(2,1)S(1)}, bf16[128,2048]{1,0:T(8,128)(2,1)S(1)}, u32[]{:S(2)}, u32[]{:S(2)}) %collective-permute-start.23) | collective-permute-done | bytes 524320 | tf_op jit(solution)/shard_map/normed_two_ring/ppermute | solution.py:194
  250.9 9.7 %collective-permute-done.25 = bf16[128,2048]{1,0:T(8,128)(2,1)S(1)} collective-permute-done((bf16[128,2048]{1,0:T(8,128)(2,1)S(1)}, bf16[128,2048]{1,0:T(8,128)(2,1)S(1)}, u32[]{:S(2)}, u32[]{:S(2)}) %collective-permute-start.25) | collective-permute-done | bytes 524320 | tf_op jit(solution)/shard_map/normed_two_ring/ppermute | solution.py:194
  267.8 9.0 %collective-permute-done.29 = bf16[128,2048]{1,0:T(8,128)(2,1)S(1)} collective-permute-done((bf16[128,2048]{1,0:T(8,128)(2,1)S(1)}, bf16[128,2048]{1,0:T(8,128)(2,1)S(1)}, u32[]{:S(2)}, u32[]{:S(2)}) %collective-permute-start.29) | collective-permute-done | bytes 524320 | tf_op jit(solution)/shard_map/normed_two_ring/ppermute | solution.py:194
  286.1 8.1 %collective-permute-done.28 = bf16[128,2048]{1,0:T(8,128)(2,1)S(1)} collective-permute-done((bf16[128,2048]{1,0:T(8,128)(2,1)S(1)}, bf16[128,2048]{1,0:T(8,128)(2,1)S(1)}, u32[]{:S(2)}, u32[]{:S(2)}) %collective-permute-start.28) | collective-permute-done | bytes 524320 | tf_op jit(solution)/shard_map/normed_two_grad_sum/ppermute | solution.py:194
  294.6 5.0 convolution_convert_fusion.3
  302.5 12.4 %collective-permute-done.34 = bf16[128,2048]{1,0:T(8,128)(2,1)S(1)} collective-permute-done((bf16[128,2048]{1,0:T(8,128)(2,1)S(1)}, bf16[128,2048]{1,0:T(8,128)(2,1)S(1)}, u32[]{:S(2)}, u32[]{:S(2)}) %collective-permute-start.34) | collective-permute-done | bytes 524320 | tf_op jit(solution)/shard_map/normed_two_grad_sum/ppermute | solution.py:194
  315.9 3.4 dynamic-slice_bitcast_fusion.2
  321.4 9.2 %collective-permute-done.35 = bf16[128,2048]{1,0:T(8,128)(2,1)S(1)} collective-permute-done((bf16[128,2048]{1,0:T(8,128)(2,1)}, bf16[128,2048]{1,0:T(8,128)(2,1)S(1)}, u32[]{:S(2)}, u32[]{:S(2)}) %collective-permute-start.35) | collective-permute-done | bytes 524320 | tf_op jit(solution)/shard_map/normed_two_grad_sum/ppermute | solution.py:194
  343.5 3.3 fusion.56
  349.9 3.8 convolution_convert_fusion.2
  354.6 3.8 convolution_convert_fusion.1
  362.1 16.5 %collective-permute-done.41 = bf16[128,2048]{1,0:T(8,128)(2,1)S(1)} collective-permute-done((bf16[128,2048]{1,0:T(8,128)(2,1)S(1)}, bf16[128,2048]{1,0:T(8,128)(2,1)S(1)}, u32[]{:S(2)}, u32[]{:S(2)}) %collective-permute-start.41) | collective-permute-done | bytes 524320 | tf_op jit(solution)/shard_map/attention_grad_columns/ppermute | solution.py:194
  396.0 3.5 convolution_convert_fusion.5
  402.9 4.3 fusion.46
  408.8 4.4 fusion.112
  413.9 6.1 %shard_map.264 = (f32[1024,256]{1,0:T(8,128)S(1)}, f32[1024,128]{1,0:T(8,128)S(1)}, f32[1024,128]{1,0:T(8,128)S(1)}) custom-call(bf16[1024,256]{1,0:T(8,128)(2,1)S(1)} %pad_maximum_fusion.5.q_ref, bf16[1024,128]{1,0:T(8,128)(2,1)S(1)} %pad_maximum_fusion.10.k_ref, bf16[1024,128]{1,0:T(8,128)(2,1)S(1)} %convolution_convert_fusion.15.v_ref, ...), custom_call_target="tpu_custom_call" | custom-call | flops 1879048192 | bytes 6291456 | tf_op jit(solution)/shard_map/pallas_call | solution.py:141
  420.1 3.0 collective-permute-start.50
  426.6 10.1 %collective-permute-done.47 = bf16[128,2048]{1,0:T(8,128)(2,1)S(1)} collective-permute-done((bf16[128,2048]{1,0:T(8,128)(2,1)S(1)}, bf16[128,2048]{1,0:T(8,128)(2,1)S(1)}, u32[]{:S(2)}, u32[]{:S(2)}) %collective-permute-start.47) | collective-permute-done | bytes 524320 | tf_op jit(solution)/shard_map/out_ring/ppermute | solution.py:194
  449.3 11.3 %collective-permute-done.53 = bf16[128,2048]{1,0:T(8,128)(2,1)S(1)} collective-permute-done((bf16[128,2048]{1,0:T(8,128)(2,1)S(1)}, bf16[128,2048]{1,0:T(8,128)(2,1)S(1)}, u32[]{:S(2)}, u32[]{:S(2)}) %collective-permute-start.53) | collective-permute-done | bytes 524320 | tf_op jit(solution)/shard_map/out_ring/ppermute | solution.py:194
  460.7 10.2 %collective-permute-done.49 = bf16[128,2048]{1,0:T(8,128)(2,1)S(1)} collective-permute-done((bf16[128,2048]{1,0:T(8,128)(2,1)S(1)}, bf16[128,2048]{1,0:T(8,128)(2,1)S(1)}, u32[]{:S(2)}, u32[]{:S(2)}) %collective-permute-start.49) | collective-permute-done | bytes 524320 | tf_op jit(solution)/shard_map/early_ring/ppermute | solution.py:194
  472.5 3.3 collective-permute-start.68
  475.8 6.8 %fusion.3 = (f32[2048]{0:T(1024)S(1)}, bf16[1024,2048]{1,0:T(8,128)(2,1)S(1)}) fusion(bf16[1,1024,2048]{2,1,0:T(8,128)(2,1)} %all-gather.6.cloned.1.call-done, f32[1024]{0:T(1024)S(1)} %copy-done.89, bf16[1024,768]{1,0:T(8,128)(2,1)} %copy-done.80, bf16[2048,256]{1,0:T(8,128)(2,1)} %get-tuple-element.312, bf16[2048,256]{1,0:T(8,128)(2,1)} %get-tuple-element.311, ...), kind=kOutput, calls=%fused_computation.5 | convolution fusion | flops 3241146368 | bytes 13119488 | tf_op jit(solution)/shard_map/dot_general | solution.py:18
  492.5 4.7 all-to-all-start
  506.8 7.7 %collective-permute-done.55 = bf16[128,2048]{1,0:T(8,128)(2,1)} collective-permute-done((bf16[128,2048]{1,0:T(8,128)(2,1)}, bf16[128,2048]{1,0:T(8,128)(2,1)}, u32[]{:S(2)}, u32[]{:S(2)}) %collective-permute-start.55) | collective-permute-done | bytes 524320 | tf_op jit(solution)/shard_map/normed_grad_sum/ppermute | solution.py:194
  514.6 10.9 %collective-permute-done.56 = bf16[128,2048]{1,0:T(8,128)(2,1)} collective-permute-done((bf16[128,2048]{1,0:T(8,128)(2,1)}, bf16[128,2048]{1,0:T(8,128)(2,1)}, u32[]{:S(2)}, u32[]{:S(2)}) %collective-permute-start.56) | collective-permute-done | bytes 524320 | tf_op jit(solution)/shard_map/normed_grad_sum/ppermute | solution.py:194
  542.6 5.3 collective-permute-start.69
  549.3 39.8 %collective-permute-done.70 = bf16[192,2048]{1,0:T(8,128)(2,1)S(1)} collective-permute-done((bf16[192,2048]{1,0:T(8,128)(2,1)S(1)}, bf16[192,2048]{1,0:T(8,128)(2,1)S(1)}, u32[]{:S(2)}, u32[]{:S(2)}) %collective-permute-start.70) | collective-permute-done | bytes 786464 | tf_op jit(solution)/shard_map/up_gradient_move/ppermute | solution.py:194
  (526 shorter events, 207.7 us)
Async XLA Ops:
  7.2 110.2 %all-gather.6.cloned.1.call-start = ((), (), s32[]{:S(2)}) async-start(), calls=%async_computation.4 | async-start | bytes 4718592 | tf_op jit(solution)/shard_map/input_gather/all_gather | solution.py:349
  7.9 122.2 %all-gather.4.cloned.1.call-start = ((), (), s32[]{:S(2)}) async-start(), calls=%async_computation.2 | async-start | bytes 1310720 | tf_op jit(solution)/shard_map/output_weight_gather/all_gather | solution.py:383
  25.3 56.0 %collective-permute-start.5 = (bf16[512,768]{1,0:T(8,128)(2,1)}, bf16[512,768]{1,0:T(8,128)(2,1)}, u32[]{:S(2)}, u32[]{:S(2)}) collective-permute-start(bf16[512,768]{1,0:T(8,128)(2,1)} %pad_maximum_fusion.4), channel_id=1, source_target_pairs={{0,0},{1,9},{2,18},{3,27},{4,4},{5,13},{6,22},{7,31},{8,1},{9,10},... | collective-permute-start | bytes 2359304 | tf_op jit(solution)/shard_map/head_weights/ppermute | solution.py:194
  30.7 93.1 %collective-permute-start.7 = (bf16[512,768]{1,0:T(8,128)(2,1)}, bf16[512,768]{1,0:T(8,128)(2,1)}, u32[]{:S(2)}, u32[]{:S(2)}) collective-permute-start(bf16[512,768]{1,0:T(8,128)(2,1)} %pad_maximum_fusion.4), channel_id=1, source_target_pairs={{0,2},{1,11},{2,16},{3,25},{4,6},{5,15},{6,20},{7,29},{8,3},{9,8},... | collective-permute-start | bytes 2359304 | tf_op jit(solution)/shard_map/head_weights/ppermute | solution.py:194
  36.2 87.7 %collective-permute-start.8 = (bf16[512,768]{1,0:T(8,128)(2,1)}, bf16[512,768]{1,0:T(8,128)(2,1)}, u32[]{:S(2)}, u32[]{:S(2)}) collective-permute-start(bf16[512,768]{1,0:T(8,128)(2,1)} %pad_maximum_fusion.4), channel_id=1, source_target_pairs={{0,3},{1,8},{2,17},{3,26},{4,7},{5,12},{6,21},{7,30},{8,0},{9,9},{... | collective-permute-start | bytes 2359304 | tf_op jit(solution)/shard_map/head_weights/ppermute | solution.py:194
  38.1 77.2 %collective-permute-start.6 = (bf16[512,768]{1,0:T(8,128)(2,1)}, bf16[512,768]{1,0:T(8,128)(2,1)}, u32[]{:S(2)}, u32[]{:S(2)}) collective-permute-start(bf16[512,768]{1,0:T(8,128)(2,1)} %pad_maximum_fusion.4), channel_id=1, source_target_pairs={{0,1},{1,10},{2,19},{3,24},{4,5},{5,14},{6,23},{7,28},{8,2},{9,11}... | collective-permute-start | bytes 2359304 | tf_op jit(solution)/shard_map/head_weights/ppermute | solution.py:194
  82.1 390.4 %reduce-scatter.2.cloned.1.call-start = ((), (), s32[]{:S(2)}) async-start(), calls=%async_computation.3 | async-start | bytes 7864320 | tf_op jit(solution)/shard_map/feed_gradient_columns/reduce_scatter | solution.py:621
  123.9 14.4 %collective-permute-start.11 = (bf16[192,512]{1,0:T(8,128)(2,1)S(1)}, bf16[192,512]{1,0:T(8,128)(2,1)S(1)}, u32[]{:S(2)}, u32[]{:S(2)}) collective-permute-start(bf16[192,512]{1,0:T(8,128)(2,1)S(1)} %get-tuple-element.156), channel_id=1, source_target_pairs={{0,3},{1,0},{2,1},{3,2},{4,7},{5,4},{6,5},{7,6},{8,11},{9,8},{10,9... | collective-permute-start | bytes 589832 | tf_op jit(solution)/shard_map/down_weight_planes/ppermute | solution.py:194
  142.1 41.1 %collective-permute-start.14 = (bf16[192,2048]{1,0:T(8,128)(2,1)}, bf16[192,2048]{1,0:T(8,128)(2,1)}, u32[]{:S(2)}, u32[]{:S(2)}) collective-permute-start(bf16[192,2048]{1,0:T(8,128)(2,1)} %constant_dynamic-update-slice_fusion.30), channel_id=1, source_target_pairs={{0,8},{1,9},{2,10},{3,11},{4,12},{5,13},{6,14},{7,15},{8,0},{9,1},... | collective-permute-start | bytes 2359304 | tf_op jit(solution)/shard_map/down_weight_columns/ppermute | solution.py:194
  142.1 41.1 %collective-permute-start.15 = (bf16[192,2048]{1,0:T(8,128)(2,1)}, bf16[192,2048]{1,0:T(8,128)(2,1)}, u32[]{:S(2)}, u32[]{:S(2)}) collective-permute-start(bf16[192,2048]{1,0:T(8,128)(2,1)} %constant_dynamic-update-slice_fusion.30), channel_id=1, source_target_pairs={{0,16},{1,17},{2,18},{3,19},{4,20},{5,21},{6,22},{7,23},{8,24},{9,... | collective-permute-start | bytes 2359304 | tf_op jit(solution)/shard_map/down_weight_columns/ppermute | solution.py:194
  146.4 36.8 %collective-permute-start.16 = (bf16[192,2048]{1,0:T(8,128)(2,1)}, bf16[192,2048]{1,0:T(8,128)(2,1)}, u32[]{:S(2)}, u32[]{:S(2)}) collective-permute-start(bf16[192,2048]{1,0:T(8,128)(2,1)} %constant_dynamic-update-slice_fusion.30), channel_id=1, source_target_pairs={{0,24},{1,25},{2,26},{3,27},{4,28},{5,29},{6,30},{7,31},{8,16},{9,... | collective-permute-start | bytes 2359304 | tf_op jit(solution)/shard_map/down_weight_columns/ppermute | solution.py:194
  146.4 14.4 %collective-permute-start.12 = (bf16[128,2048]{1,0:T(8,128)(2,1)}, bf16[128,2048]{1,0:T(8,128)(2,1)}, u32[]{:S(2)}, u32[]{:S(2)}) collective-permute-start(bf16[128,2048]{1,0:T(8,128)(2,1)} %bitcast.6), channel_id=1, source_target_pairs={{0,1},{1,2},{2,3},{3,0},{4,5},{5,6},{6,7},{7,4},{8,9},{9,10},{10,1... | collective-permute-start | bytes 1572872 | tf_op jit(solution)/shard_map/cotangent_ring/ppermute | solution.py:194
  199.7 14.8 %collective-permute-start.19 = (bf16[128,2048]{1,0:T(8,128)(2,1)S(1)}, bf16[128,2048]{1,0:T(8,128)(2,1)S(1)}, u32[]{:S(2)}, u32[]{:S(2)}) collective-permute-start(bf16[128,2048]{1,0:T(8,128)(2,1)S(1)} %get-tuple-element.328), channel_id=1, source_target_pairs={{0,8},{1,9},{2,10},{3,11},{4,12},{5,13},{6,14},{7,15},{8,0},{9,1},... | collective-permute-start | bytes 1572872 | tf_op jit(solution)/shard_map/attention_out_sum/ppermute | solution.py:194
  201.2 24.9 %collective-permute-start.20 = (bf16[128,2048]{1,0:T(8,128)(2,1)S(1)}, bf16[128,2048]{1,0:T(8,128)(2,1)S(1)}, u32[]{:S(2)}, u32[]{:S(2)}) collective-permute-start(bf16[128,2048]{1,0:T(8,128)(2,1)S(1)} %get-tuple-element.330), channel_id=1, source_target_pairs={{0,16},{1,17},{2,18},{3,19},{4,20},{5,21},{6,22},{7,23},{8,24},{9,... | collective-permute-start | bytes 1572872 | tf_op jit(solution)/shard_map/attention_out_sum/ppermute | solution.py:194
  202.4 23.7 %collective-permute-start.21 = (bf16[128,2048]{1,0:T(8,128)(2,1)S(1)}, bf16[128,2048]{1,0:T(8,128)(2,1)S(1)}, u32[]{:S(2)}, u32[]{:S(2)}) collective-permute-start(bf16[128,2048]{1,0:T(8,128)(2,1)S(1)} %get-tuple-element.329), channel_id=1, source_target_pairs={{0,24},{1,25},{2,26},{3,27},{4,28},{5,29},{6,30},{7,31},{8,16},{9,... | collective-permute-start | bytes 1572872 | tf_op jit(solution)/shard_map/attention_out_sum/ppermute | solution.py:194
  227.9 16.5 %collective-permute-start.23 = (bf16[128,2048]{1,0:T(8,128)(2,1)S(1)}, bf16[128,2048]{1,0:T(8,128)(2,1)S(1)}, u32[]{:S(2)}, u32[]{:S(2)}) collective-permute-start(bf16[128,2048]{1,0:T(8,128)(2,1)S(1)} %multiply_convert_fusion), channel_id=1, source_target_pairs={{0,1},{1,2},{2,3},{3,0},{4,5},{5,6},{6,7},{7,4},{8,9},{9,10},{10,1... | collective-permute-start | bytes 1572872 | tf_op jit(solution)/shard_map/normed_two_ring/ppermute | solution.py:194
  244.4 16.1 %collective-permute-start.25 = (bf16[128,2048]{1,0:T(8,128)(2,1)S(1)}, bf16[128,2048]{1,0:T(8,128)(2,1)S(1)}, u32[]{:S(2)}, u32[]{:S(2)}) collective-permute-start(bf16[128,2048]{1,0:T(8,128)(2,1)S(1)} %collective-permute-done.23), channel_id=1, source_target_pairs={{0,1},{1,2},{2,3},{3,0},{4,5},{5,6},{6,7},{7,4},{8,9},{9,10},{10,1... | collective-permute-start | bytes 1572872 | tf_op jit(solution)/shard_map/normed_two_ring/ppermute | solution.py:194
  260.5 16.3 %collective-permute-start.29 = (bf16[128,2048]{1,0:T(8,128)(2,1)S(1)}, bf16[128,2048]{1,0:T(8,128)(2,1)S(1)}, u32[]{:S(2)}, u32[]{:S(2)}) collective-permute-start(bf16[128,2048]{1,0:T(8,128)(2,1)S(1)} %collective-permute-done.25), channel_id=1, source_target_pairs={{0,1},{1,2},{2,3},{3,0},{4,5},{5,6},{6,7},{7,4},{8,9},{9,10},{10,1... | collective-permute-start | bytes 1572872 | tf_op jit(solution)/shard_map/normed_two_ring/ppermute | solution.py:194
  261.9 15.9 %collective-permute-start.27 = (bf16[128,2048]{1,0:T(8,128)(2,1)S(1)}, bf16[128,2048]{1,0:T(8,128)(2,1)S(1)}, u32[]{:S(2)}, u32[]{:S(2)}) collective-permute-start(bf16[128,2048]{1,0:T(8,128)(2,1)S(1)} %slice.196), channel_id=1, source_target_pairs={{0,4},{1,5},{2,6},{3,7},{4,0},{5,1},{6,2},{7,3},{8,12},{9,13},{10,... | collective-permute-start | bytes 1572872 | tf_op jit(solution)/shard_map/normed_two_grad_core/ppermute | solution.py:194
  278.0 16.2 %collective-permute-start.28 = (bf16[128,2048]{1,0:T(8,128)(2,1)S(1)}, bf16[128,2048]{1,0:T(8,128)(2,1)S(1)}, u32[]{:S(2)}, u32[]{:S(2)}) collective-permute-start(bf16[128,2048]{1,0:T(8,128)(2,1)S(1)} %add_convert_fusion.10), channel_id=1, source_target_pairs={{0,1},{1,2},{2,3},{3,0},{4,5},{5,6},{6,7},{7,4},{8,9},{9,10},{10,1... | collective-permute-start | bytes 1572872 | tf_op jit(solution)/shard_map/normed_two_grad_sum/ppermute | solution.py:194
  278.2 16.1 %collective-permute-start.31 = (bf16[128,2048]{1,0:T(8,128)(2,1)S(1)}, bf16[128,2048]{1,0:T(8,128)(2,1)S(1)}, u32[]{:S(2)}, u32[]{:S(2)}) collective-permute-start(bf16[128,2048]{1,0:T(8,128)(2,1)S(1)} %slice.199), channel_id=1, source_target_pairs={{0,4},{1,5},{2,6},{3,7},{4,0},{5,1},{6,2},{7,3},{8,12},{9,13},{10,... | collective-permute-start | bytes 1572872 | tf_op jit(solution)/shard_map/normed_two_grad_core/ppermute | solution.py:194
  299.6 15.4 %collective-permute-start.34 = (bf16[128,2048]{1,0:T(8,128)(2,1)S(1)}, bf16[128,2048]{1,0:T(8,128)(2,1)S(1)}, u32[]{:S(2)}, u32[]{:S(2)}) collective-permute-start(bf16[128,2048]{1,0:T(8,128)(2,1)S(1)} %add_convert_fusion.8), channel_id=1, source_target_pairs={{0,1},{1,2},{2,3},{3,0},{4,5},{5,6},{6,7},{7,4},{8,9},{9,10},{10,1... | collective-permute-start | bytes 1572872 | tf_op jit(solution)/shard_map/normed_two_grad_sum/ppermute | solution.py:194
  301.2 37.1 %collective-permute-start.39 = (bf16[4,128,2048]{2,1,0:T(8,128)(2,1)}, bf16[4,128,2048]{2,1,0:T(8,128)(2,1)}, u32[]{:S(2)}, u32[]{:S(2)}) collective-permute-start(bf16[4,128,2048]{2,1,0:T(8,128)(2,1)} %pad_maximum_fusion.3), channel_id=1, source_target_pairs={{0,4},{1,5},{2,6},{3,7},{4,0},{5,1},{6,2},{7,3},{8,12},{9,13},{10,... | collective-permute-start | bytes 6291464 | tf_op jit(solution)/shard_map/out_core/ppermute | solution.py:194
  302.0 19.4 %collective-permute-start.36 = (bf16[128,2048]{1,0:T(8,128)(2,1)}, bf16[128,2048]{1,0:T(8,128)(2,1)}, u32[]{:S(2)}, u32[]{:S(2)}) collective-permute-start(bf16[128,2048]{1,0:T(8,128)(2,1)} %slice.212), channel_id=1, source_target_pairs={{0,4},{1,5},{2,6},{3,7},{4,0},{5,1},{6,2},{7,3},{8,12},{9,13},{10,... | collective-permute-start | bytes 1572872 | tf_op jit(solution)/shard_map/normed_two_grad_core/ppermute | solution.py:194
  315.9 14.7 %collective-permute-start.35 = (bf16[128,2048]{1,0:T(8,128)(2,1)}, bf16[128,2048]{1,0:T(8,128)(2,1)S(1)}, u32[]{:S(2)}, u32[]{:S(2)}) collective-permute-start(bf16[128,2048]{1,0:T(8,128)(2,1)} %add_convert_fusion.6), channel_id=1, source_target_pairs={{0,1},{1,2},{2,3},{3,0},{4,5},{5,6},{6,7},{7,4},{8,9},{9,10},{10,1... | collective-permute-start | bytes 1572872 | tf_op jit(solution)/shard_map/normed_two_grad_sum/ppermute | solution.py:194
  319.3 18.3 %collective-permute-start.37 = (bf16[512,768]{1,0:T(8,128)(2,1)S(1)}, bf16[512,768]{1,0:T(8,128)(2,1)S(1)}, u32[]{:S(2)}, u32[]{:S(2)}) collective-permute-start(bf16[512,768]{1,0:T(8,128)(2,1)S(1)} %get-tuple-element.315), channel_id=1, source_target_pairs={{0,8},{1,9},{2,10},{3,11},{4,12},{5,13},{6,14},{7,15},{8,0},{9,1},... | collective-permute-start | bytes 2359304 | tf_op jit(solution)/shard_map/down_gradient_columns/ppermute | solution.py:194
  320.2 18.1 %collective-permute-start.38 = (bf16[512,768]{1,0:T(8,128)(2,1)S(1)}, bf16[512,768]{1,0:T(8,128)(2,1)S(1)}, u32[]{:S(2)}, u32[]{:S(2)}) collective-permute-start(bf16[512,768]{1,0:T(8,128)(2,1)S(1)} %get-tuple-element.314), channel_id=1, source_target_pairs={{0,16},{1,17},{2,18},{3,19},{4,20},{5,21},{6,22},{7,23},{8,24},{9,... | collective-permute-start | bytes 2359304 | tf_op jit(solution)/shard_map/down_gradient_columns/ppermute | solution.py:194
  338.3 23.0 %collective-permute-start.40 = (bf16[128,2048]{1,0:T(8,128)(2,1)S(1)}, bf16[128,2048]{1,0:T(8,128)(2,1)S(1)}, u32[]{:S(2)}, u32[]{:S(2)}) collective-permute-start(bf16[128,2048]{1,0:T(8,128)(2,1)S(1)} %get-tuple-element.212), channel_id=1, source_target_pairs={{0,8},{1,9},{2,10},{3,11},{4,12},{5,13},{6,14},{7,15},{8,0},{9,1},... | collective-permute-start | bytes 1572872 | tf_op jit(solution)/shard_map/attention_grad_columns/ppermute | solution.py:194
  339.4 39.3 %collective-permute-start.41 = (bf16[128,2048]{1,0:T(8,128)(2,1)S(1)}, bf16[128,2048]{1,0:T(8,128)(2,1)S(1)}, u32[]{:S(2)}, u32[]{:S(2)}) collective-permute-start(bf16[128,2048]{1,0:T(8,128)(2,1)S(1)} %get-tuple-element.212), channel_id=1, source_target_pairs={{0,16},{1,17},{2,18},{3,19},{4,20},{5,21},{6,22},{7,23},{8,24},{9,... | collective-permute-start | bytes 1572872 | tf_op jit(solution)/shard_map/attention_grad_columns/ppermute | solution.py:194
  340.6 38.9 %collective-permute-start.42 = (bf16[128,2048]{1,0:T(8,128)(2,1)S(1)}, bf16[128,2048]{1,0:T(8,128)(2,1)S(1)}, u32[]{:S(2)}, u32[]{:S(2)}) collective-permute-start(bf16[128,2048]{1,0:T(8,128)(2,1)S(1)} %get-tuple-element.212), channel_id=1, source_target_pairs={{0,24},{1,25},{2,26},{3,27},{4,28},{5,29},{6,30},{7,31},{8,16},{9,... | collective-permute-start | bytes 1572872 | tf_op jit(solution)/shard_map/attention_grad_columns/ppermute | solution.py:194
  341.7 42.4 %collective-permute-start.45 = (bf16[512,768]{1,0:T(8,128)(2,1)}, bf16[512,768]{1,0:T(8,128)(2,1)}, u32[]{:S(2)}, u32[]{:S(2)}) collective-permute-start(bf16[512,768]{1,0:T(8,128)(2,1)} %get-tuple-element.231), channel_id=1, source_target_pairs={{0,24},{1,25},{2,26},{3,27},{4,28},{5,29},{6,30},{7,31},{8,16},{9,... | collective-permute-start | bytes 2359304 | tf_op jit(solution)/shard_map/down_gradient_columns/ppermute | solution.py:194
  346.9 40.2 %collective-permute-start.44 = (bf16[128,2048]{1,0:T(8,128)(2,1)}, bf16[128,2048]{1,0:T(8,128)(2,1)}, u32[]{:S(2)}, u32[]{:S(2)}) collective-permute-start(bf16[128,2048]{1,0:T(8,128)(2,1)} %get-tuple-element.226), channel_id=1, source_target_pairs={{0,1},{1,2},{2,3},{3,0},{4,5},{5,6},{6,7},{7,4},{8,9},{9,10},{10,1... | collective-permute-start | bytes 1572872 | tf_op jit(solution)/shard_map/out_ring/ppermute | solution.py:194
  408.6 17.9 %collective-permute-start.48 = (bf16[128,2048]{1,0:T(8,128)(2,1)S(1)}, bf16[128,2048]{1,0:T(8,128)(2,1)S(1)}, u32[]{:S(2)}, u32[]{:S(2)}) collective-permute-start(bf16[128,2048]{1,0:T(8,128)(2,1)S(1)} %fusion.73), channel_id=1, source_target_pairs={{0,1},{1,2},{2,3},{3,0},{4,5},{5,6},{6,7},{7,4},{8,9},{9,10},{10,1... | collective-permute-start | bytes 1572872 | tf_op jit(solution)/shard_map/early_ring/ppermute | solution.py:194
  413.2 23.5 %collective-permute-start.47 = (bf16[128,2048]{1,0:T(8,128)(2,1)S(1)}, bf16[128,2048]{1,0:T(8,128)(2,1)S(1)}, u32[]{:S(2)}, u32[]{:S(2)}) collective-permute-start(bf16[128,2048]{1,0:T(8,128)(2,1)S(1)} %copy-done.53), channel_id=1, source_target_pairs={{0,1},{1,2},{2,3},{3,0},{4,5},{5,6},{6,7},{7,4},{8,9},{9,10},{10,1... | collective-permute-start | bytes 1572872 | tf_op jit(solution)/shard_map/out_ring/ppermute | solution.py:194
  420.1 51.7 %collective-permute-start.50 = (bf16[64,1536]{1,0:T(8,128)(2,1)S(1)}, bf16[64,1536]{1,0:T(8,128)(2,1)S(1)}, u32[]{:S(2)}, u32[]{:S(2)}) collective-permute-start(bf16[64,1536]{1,0:T(8,128)(2,1)S(1)} %get-tuple-element.373), channel_id=1, source_target_pairs={{0,1},{1,2},{2,3},{3,0},{4,5},{5,6},{6,7},{7,4},{8,9},{9,10},{10,1... | collective-permute-start | bytes 589832 | tf_op jit(solution)/shard_map/down_gradient_planes/ppermute | solution.py:194
  423.1 48.7 %collective-permute-start.51 = (bf16[64,1536]{1,0:T(8,128)(2,1)S(1)}, bf16[64,1536]{1,0:T(8,128)(2,1)S(1)}, u32[]{:S(2)}, u32[]{:S(2)}) collective-permute-start(bf16[64,1536]{1,0:T(8,128)(2,1)S(1)} %get-tuple-element.372), channel_id=1, source_target_pairs={{0,2},{1,3},{2,0},{3,1},{4,6},{5,7},{6,4},{7,5},{8,10},{9,11},{10,... | collective-permute-start | bytes 589832 | tf_op jit(solution)/shard_map/down_gradient_planes/ppermute | solution.py:194
  424.0 48.5 %collective-permute-start.52 = (bf16[64,1536]{1,0:T(8,128)(2,1)S(1)}, bf16[64,1536]{1,0:T(8,128)(2,1)}, u32[]{:S(2)}, u32[]{:S(2)}) collective-permute-start(bf16[64,1536]{1,0:T(8,128)(2,1)S(1)} %get-tuple-element.371), channel_id=1, source_target_pairs={{0,3},{1,0},{2,1},{3,2},{4,7},{5,4},{6,5},{7,6},{8,11},{9,8},{10,9... | collective-permute-start | bytes 589832 | tf_op jit(solution)/shard_map/down_gradient_planes/ppermute | solution.py:194
  436.9 23.7 %collective-permute-start.53 = (bf16[128,2048]{1,0:T(8,128)(2,1)S(1)}, bf16[128,2048]{1,0:T(8,128)(2,1)S(1)}, u32[]{:S(2)}, u32[]{:S(2)}) collective-permute-start(bf16[128,2048]{1,0:T(8,128)(2,1)S(1)} %add_convert_fusion.4), channel_id=1, source_target_pairs={{0,1},{1,2},{2,3},{3,0},{4,5},{5,6},{6,7},{7,4},{8,9},{9,10},{10,1... | collective-permute-start | bytes 1572872 | tf_op jit(solution)/shard_map/out_ring/ppermute | solution.py:194
  436.9 33.9 %collective-permute-start.49 = (bf16[128,2048]{1,0:T(8,128)(2,1)S(1)}, bf16[128,2048]{1,0:T(8,128)(2,1)S(1)}, u32[]{:S(2)}, u32[]{:S(2)}) collective-permute-start(bf16[128,2048]{1,0:T(8,128)(2,1)S(1)} %fusion.55), channel_id=1, source_target_pairs={{0,1},{1,2},{2,3},{3,0},{4,5},{5,6},{6,7},{7,4},{8,9},{9,10},{10,1... | collective-permute-start | bytes 1572872 | tf_op jit(solution)/shard_map/early_ring/ppermute | solution.py:194
  472.5 15.2 %collective-permute-start.68 = (bf16[128,2048]{1,0:T(8,128)(2,1)}, bf16[128,2048]{1,0:T(8,128)(2,1)S(1)}, u32[]{:S(2)}, u32[]{:S(2)}) collective-permute-start(bf16[128,2048]{1,0:T(8,128)(2,1)} %fusion.54), channel_id=1, source_target_pairs={{0,1},{1,2},{2,3},{3,0},{4,5},{5,6},{6,7},{7,4},{8,9},{9,10},{10,1... | collective-permute-start | bytes 1572872 | tf_op jit(solution)/shard_map/early_ring/ppermute | solution.py:194
  488.6 15.6 %collective-permute-start.65 = (bf16[128,2048]{1,0:T(8,128)(2,1)}, bf16[128,2048]{1,0:T(8,128)(2,1)}, u32[]{:S(2)}, u32[]{:S(2)}) collective-permute-start(bf16[128,2048]{1,0:T(8,128)(2,1)} %pad_maximum_fusion.7), channel_id=1, source_target_pairs={{0,1},{1,2},{2,3},{3,0},{4,5},{5,6},{6,7},{7,4},{8,9},{9,10},{10,1... | collective-permute-start | bytes 1572872 | tf_op jit(solution)/shard_map/qkv_gradient_sum/ppermute | solution.py:194
  498.5 16.1 %collective-permute-start.55 = (bf16[128,2048]{1,0:T(8,128)(2,1)}, bf16[128,2048]{1,0:T(8,128)(2,1)}, u32[]{:S(2)}, u32[]{:S(2)}) collective-permute-start(bf16[128,2048]{1,0:T(8,128)(2,1)} %get-tuple-element.317), channel_id=1, source_target_pairs={{0,8},{1,9},{2,10},{3,11},{4,12},{5,13},{6,14},{7,15},{8,0},{9,1},... | collective-permute-start | bytes 1572872 | tf_op jit(solution)/shard_map/normed_grad_sum/ppermute | solution.py:194
  499.9 25.5 %collective-permute-start.56 = (bf16[128,2048]{1,0:T(8,128)(2,1)}, bf16[128,2048]{1,0:T(8,128)(2,1)}, u32[]{:S(2)}, u32[]{:S(2)}) collective-permute-start(bf16[128,2048]{1,0:T(8,128)(2,1)} %get-tuple-element.319), channel_id=1, source_target_pairs={{0,16},{1,17},{2,18},{3,19},{4,20},{5,21},{6,22},{7,23},{8,24},{9,... | collective-permute-start | bytes 1572872 | tf_op jit(solution)/shard_map/normed_grad_sum/ppermute | solution.py:194
  500.5 25.0 %collective-permute-start.57 = (bf16[128,2048]{1,0:T(8,128)(2,1)}, bf16[128,2048]{1,0:T(8,128)(2,1)}, u32[]{:S(2)}, u32[]{:S(2)}) collective-permute-start(bf16[128,2048]{1,0:T(8,128)(2,1)} %get-tuple-element.318), channel_id=1, source_target_pairs={{0,24},{1,25},{2,26},{3,27},{4,28},{5,29},{6,30},{7,31},{8,16},{9,... | collective-permute-start | bytes 1572872 | tf_op jit(solution)/shard_map/normed_grad_sum/ppermute | solution.py:194
  506.2 42.9 %collective-permute-start.66 = (bf16[128,2048]{1,0:T(8,128)(2,1)}, bf16[128,2048]{1,0:T(8,128)(2,1)S(1)}, u32[]{:S(2)}, u32[]{:S(2)}) collective-permute-start(bf16[128,2048]{1,0:T(8,128)(2,1)} %add_convert_fusion.2), channel_id=1, source_target_pairs={{0,1},{1,2},{2,3},{3,0},{4,5},{5,6},{6,7},{7,4},{8,9},{9,10},{10,1... | collective-permute-start | bytes 1572872 | tf_op jit(solution)/shard_map/qkv_gradient_sum/ppermute | solution.py:194
  540.3 48.8 %collective-permute-start.70 = (bf16[192,2048]{1,0:T(8,128)(2,1)S(1)}, bf16[192,2048]{1,0:T(8,128)(2,1)S(1)}, u32[]{:S(2)}, u32[]{:S(2)}) collective-permute-start(bf16[192,2048]{1,0:T(8,128)(2,1)S(1)} %get-tuple-element.331), channel_id=1, source_target_pairs={{0,2},{1,11},{2,16},{3,25},{4,6},{5,15},{6,20},{7,29},{8,3},{9,8},... | collective-permute-start | bytes 2359304 | tf_op jit(solution)/shard_map/up_gradient_move/ppermute | solution.py:194
  542.6 47.9 %collective-permute-start.69 = (bf16[192,2048]{1,0:T(8,128)(2,1)S(1)}, bf16[192,2048]{1,0:T(8,128)(2,1)S(1)}, u32[]{:S(2)}, u32[]{:S(2)}) collective-permute-start(bf16[192,2048]{1,0:T(8,128)(2,1)S(1)} %get-tuple-element.332), channel_id=1, source_target_pairs={{0,0},{1,9},{2,18},{3,27},{4,4},{5,13},{6,22},{7,31},{8,1},{9,10},... | collective-permute-start | bytes 2359304 | tf_op jit(solution)/shard_map/gate_gradient_move/ppermute | solution.py:194
  549.3 42.5 %collective-permute-start.67 = (bf16[128,2048]{1,0:T(8,128)(2,1)S(1)}, bf16[128,2048]{1,0:T(8,128)(2,1)S(1)}, u32[]{:S(2)}, u32[]{:S(2)}) collective-permute-start(bf16[128,2048]{1,0:T(8,128)(2,1)S(1)} %add_convert_fusion.1), channel_id=1, source_target_pairs={{0,1},{1,2},{2,3},{3,0},{4,5},{5,6},{6,7},{7,4},{8,9},{9,10},{10,1... | collective-permute-start | bytes 1572872 | tf_op jit(solution)/shard_map/qkv_gradient_sum/ppermute | solution.py:194
  (126 other events, 1610.4 us)
Sparse Core Ops, SparseCore 0:
  9.9 59.3 all-gather.5
  82.2 34.4 all-gather.3
  395.1 69.9 reduce-scatter.1

commit v4 on v3

--- a/solution.py
+++ b/solution.py
@@ -478,10 +478,9 @@
     values = dot(normed, value_weights).astype(LOW)
     queries = jnp.concatenate([head.astype(LOW) for head, _ in query_prepared], axis=1)
     keys = jnp.concatenate([head.astype(LOW) for head, _ in key_prepared], axis=1)
-    queries, keys, values, cotangent_ring = fence((queries, keys, values, cotangent_ring))
-    cotangent_ring = cotangent_step(cotangent_ring)
     gate_open = jax.nn.sigmoid(dot(normed, logit_weights).astype(LOW).astype(WIDE))
     mixed = attention_forward(queries, keys, values, row_info, column_info, head_width)
+    mixed, cotangent_ring = fence((mixed, cotangent_ring))
     gated = (mixed * gate_open).astype(LOW)
     attention_out = dot(gated, output_rows).astype(LOW)
     down_piece = by_columns(down_blocks)
@@ -495,14 +494,20 @@
     scale_two = lax.rsqrt(jnp.mean(middle * middle, axis=-1, keepdims=True) + EPSILON)
     normed_two = (middle * scale_two * gain_two).astype(LOW)
     down_rows = by_rows(down_pieces)
-    cotangent_ring = jnp.stack(cotangent_ring)
-    all_cotangent = jnp.concatenate(
-        [cotangent_ring, named("cotangent_core", to_core, cotangent_ring)], axis=1
-    )
-    all_cotangent = all_cotangent.reshape(-1, width)
-    normed_two, all_cotangent, down_rows = fence((normed_two, all_cotangent, down_rows))
-
-    hidden_grads = dot(all_cotangent, down_rows, 1, 1).reshape(plane_count, -1, hidden_width)
+    cotangent_first = jnp.stack(cotangent_ring)
+    cotangent_other = named("cotangent_core", to_core, cotangent_first)
+    normed_two, cotangent_first, cotangent_other, down_rows = fence(
+        (normed_two, cotangent_first, cotangent_other, down_rows)
+    )
+
+    cotangent_blocks = [
+        jnp.concatenate([cotangent_first[i], cotangent_other[i]])
+        for i in range(plane_count - 1)
+    ]
+    cotangent_last = cotangent_step(cotangent_ring)[-1]
+    cotangent_blocks.append(
+        jnp.concatenate([cotangent_last, named("cotangent_core", to_core, cotangent_last)])
+    )
     hidden_blocks, gate_grads, up_grads, normed_two_blocks = [], [], [], []
     grad_pieces, out_pieces = [], []
     arrived = normed_two
@@ -516,7 +521,7 @@
         gate_sigma = jax.nn.sigmoid(gate_values)
         silu_values = gate_values * gate_sigma
         hidden = (silu_values * up_values).astype(LOW)
-        hidden_grad = hidden_grads[i]
+        hidden_grad = dot(cotangent_blocks[i], down_rows, 1, 1)
         gate_grad = (
             hidden_grad * up_values * gate_sigma * (1.0 + gate_values * (1.0 - gate_sigma))
         ).astype(LOW)
@@ -538,14 +543,24 @@
         up_grads.append(up_grad)
     last_piece, hidden_blocks, out_pieces = fence((grad_pieces[-1], hidden_blocks, out_pieces))
     grad_pieces[-1] = last_piece
-    down_terms = dot(all_cotangent, jnp.concatenate(hidden_blocks), 0, 0).astype(LOW)
+    down_terms = dot(jnp.concatenate(cotangent_blocks), jnp.concatenate(hidden_blocks), 0, 0).astype(LOW)
     running = named("normed_two_grad_sum", ring_step, grad_pieces[1], grad_pieces[2])
-    running, down_terms = fence((running, down_terms))
+    all_normed_two = jnp.concatenate(normed_two_blocks, axis=0)
+
+    def column_block_terms(grads):
+        terms = dot(jnp.concatenate(grads, axis=0), all_normed_two, 0, 0).astype(LOW)
+        return terms.reshape(plane_count, -1, width)
+
+    running, down_terms, gate_grads = fence((running, down_terms, gate_grads))
     for i in range(2, plane_count):
         last = i == plane_count - 1
         running = named(
             "normed_two_grad_sum", ring_step, running, grad_pieces[(i + 1) % plane_count], last
         )
+        if i == 2:
+            gate_terms = column_block_terms(gate_grads)
+            running, gate_terms, up_grads = fence((running, gate_terms, up_grads))
+            up_terms = column_block_terms(up_grads)
     normed_two_grad = running
 
     down_terms = down_terms.reshape(column_count, -1, hidden_width)
@@ -553,8 +568,9 @@
         lax.dynamic_index_in_dim(down_terms, column ^ d, 0, keepdims=False)
         for d in range(column_count)
     ]
-    down_sent[1:3] = [
-        named("down_gradient_columns", to_column, down_sent[d], d) for d in (1, 2)
+    down_sent[1:] = [
+        named("down_gradient_columns", to_column, down_sent[d], d)
+        for d in range(1, column_count)
     ]
     out_other = named("out_core", to_core, jnp.stack([piece for _, piece in out_pieces]))
 
@@ -566,28 +582,6 @@
     )
     feedforward_gain_terms = jnp.sum(normed_two_grad * (middle * scale_two), axis=0)
     attention_grad_local = middle_grad.astype(LOW)
-    attention_grad_local, down_sent, out_other = fence(
-        (attention_grad_local, down_sent, out_other)
-    )
-
-    out_terms = [
-        (piece.astype(WIDE) + out_other[i].astype(WIDE)).astype(LOW)
-        for i, (piece, _) in enumerate(out_pieces)
-    ]
-    out_terms, gate_grads, up_grads = fence((out_terms, gate_grads, up_grads))
-    out_running = out_terms[1]
-    for i in range(1, plane_count - 2):
-        out_running = named("out_ring", ring_step, out_running, out_terms[i + 1])
-    grad_columns = named("attention_grad_columns", plane_columns, attention_grad_local)
-    attention_grad = named("attention_grad_core", plane_gather, grad_columns)
-    all_normed_two = jnp.concatenate(normed_two_blocks, axis=0)
-
-    def column_block_terms(grads):
-        terms = dot(jnp.concatenate(grads, axis=0), all_normed_two, 0, 0).astype(LOW)
-        return terms.reshape(plane_count, -1, width)
-
-    gate_terms = column_block_terms(gate_grads)
-    up_terms = column_block_terms(up_grads)
     up_shift = plane_count // 2
     feed_terms = jnp.concatenate(
         [
@@ -598,8 +592,21 @@
             for terms, shift in ((gate_terms, 0), (up_terms, up_shift))
         ]
     )
-    for d in range(3, column_count):
-        down_sent[d] = named("down_gradient_columns", to_column, down_sent[d], d)
+    attention_grad_local, down_sent, out_other, feed_terms = fence(
+        (attention_grad_local, down_sent, out_other, feed_terms)
+    )
+
+    out_terms = [
+        (piece.astype(WIDE) + out_other[i].astype(WIDE)).astype(LOW)
+        for i, (piece, _) in enumerate(out_pieces)
+    ]
+    out_running = out_terms[1]
+    for i in range(1, plane_count - 2):
+        out_running = named("out_ring", ring_step, out_running, out_terms[i + 1])
+    grad_columns = named("attention_grad_columns", plane_columns, attention_grad_local)
+    grad_columns, out_running = fence((grad_columns, out_running))
+    out_running = named("out_ring", ring_step, out_running, out_terms[plane_count - 1])
+    attention_grad = named("attention_grad_core", plane_gather, grad_columns)
     down_mine = sum(block.astype(WIDE) for block in down_sent).astype(LOW)
     down_mine = down_mine.reshape(2, plane_count, -1, hidden_width)
     own_half = lax.dynamic_index_in_dim(down_mine, core, 0, keepdims=False)
@@ -613,8 +620,8 @@
         jnp.concatenate([own_half, other_half], axis=2),
         jnp.concatenate([other_half, own_half], axis=2),
     )
-    attention_grad, feed_terms, out_running, down_pair = fence(
-        (attention_grad, feed_terms, out_running, down_pair)
+    attention_grad, out_running, down_pair, feed_terms = fence(
+        (attention_grad, out_running, down_pair, feed_terms)
     )
 
     with jax.named_scope("feed_gradient_columns"):
@@ -625,7 +632,7 @@
             axis_index_groups=[[2 * q + c for q in range(column_count)] for c in range(2)],
             tiled=True,
         )
-    out_running = named("out_ring", ring_step, out_running, out_terms[plane_count - 1])
+    out_total = named("out_ring", ring_step, out_running, out_terms[0], True)
     gated_grad = dot(attention_grad, output_rows, 1, 1).astype(LOW).astype(WIDE)
     logit_grad = (gated_grad * mixed * gate_open * (1.0 - gate_open)).astype(LOW)
     mixed_grad = (gated_grad * gate_open).astype(LOW)
@@ -645,10 +652,9 @@
     query_rot_grad, key_rot_grad, value_sum = attention_backward(
         queries, keys, values, mixed, mixed_grad, row_info, column_info, head_width
     )
-    query_rot_grad, key_rot_grad, value_sum, out_running, early_running = fence(
-        (query_rot_grad, key_rot_grad, value_sum, out_running, early_running)
-    )
-    out_total = named("out_ring", ring_step, out_running, out_terms[0], True)
+    query_rot_grad, key_rot_grad, value_sum, early_running, out_total = fence(
+        (query_rot_grad, key_rot_grad, value_sum, early_running, out_total)
+    )
     early_running = named("early_ring", ring_step, early_running, early_term(plane_count - 1))
     down_moved = []
     for d in range(plane_count):
@@ -684,8 +690,8 @@
         for i in range(plane_count)
     ]
     joined_grad = jnp.concatenate([query_grad, key_grad, value_grad, logit_grad], axis=1)
-    qkv_pieces, joined_grad, early_running, feed_mine, down_moved, out_total = fence(
-        (qkv_pieces, joined_grad, early_running, feed_mine, down_moved, out_total)
+    qkv_pieces, joined_grad, early_running, feed_mine, down_moved = fence(
+        (qkv_pieces, joined_grad, early_running, feed_mine, down_moved)
     )
 
     normed_grad_partial = dot(

time: 611 us -> 597 us (0.977)
  waiting for transfers between devices: 278 us -> 270 us
    ppermute x71 -> x72, waiting for transfers between devices: 276 us -> 264 us  [send(): return lax.ppermute(value, AXES, pairs)]
    ppermute x71 -> x72, starting transfers between devices: 77.4 us -> 76 us  [send(): return lax.ppermute(value, AXES, pairs)]
    dot_general x36 -> x39, matrix products: 70 us -> 69.3 us  [dot(): lax.dot_general(left, right, (((left_dim,), (right_dim,)), ((), ())), pre...]
    unnamed x216 -> x157, local copies, waits for them, and re-layouts: 14.2 us -> 14.7 us
  transfers between devices with their start and end apart: 75 -> 76, of which waited for: 31 -> 37; matrix products, arithmetic and copies ran while one was open for 32% -> 32% of each run, Pallas kernels for 1% -> 1%
where the time goes in v4:
time: 597 us; the launch traced here: 588 us
  waiting for transfers between devices  270 us (45%)
  local copies, waits for them, and re-layouts  81.2 us (14%)
  starting transfers between devices  80.2 us (13%)
  matrix products  69.3 us (12%)
  other arithmetic  62.2 us (10%)
  between operations  16 us (3%)
  Pallas kernels  8.77 us (1%)
    ppermute x72, waiting for transfers between devices, send(): return lax.ppermute(value, AXES, pairs)  264 us
    ppermute x72, starting transfers between devices, send(): return lax.ppermute(value, AXES, pairs)  76 us
    dot_general x39, matrix products, dot(): lax.dot_general(left, right, (((left_dim,), (right_dim,)), ((), ())), pre...  69.3 us
    unnamed x157, local copies, waits for them, and re-layouts  14.7 us
  transfers between devices with their start and end apart: 76, of which 37 were waited for; matrix products, arithmetic and copies ran while one was open for 32% of the time, Pallas kernels for 1%

profile of v4, /device:TPU:4, one launch (start us, length us, event | category | flops | bytes accessed | tf_op | source)
XLA Modules:
  0.0 587.5 jit_solution(16803705485861202309)
XLA Ops:
  10.8 2.8 concatenate.137
  25.3 5.5 collective-permute-start.5
  30.7 5.4 collective-permute-start.7
  40.2 3.0 multiply_sine_fusion
  43.4 37.9 %collective-permute-done.5 = bf16[512,768]{1,0:T(8,128)(2,1)} collective-permute-done((bf16[512,768]{1,0:T(8,128)(2,1)}, bf16[512,768]{1,0:T(8,128)(2,1)}, u32[]{:S(2)}, u32[]{:S(2)}) %collective-permute-start.5) | collective-permute-done | bytes 786464 | tf_op jit(solution)/shard_map/head_weights/ppermute | solution.py:194
  84.0 2.9 constant_dynamic-update-slice_fusion.45
  88.2 5.1 constant_dynamic-slice_fusion.10
  93.3 22.0 %collective-permute-done.6 = bf16[512,768]{1,0:T(8,128)(2,1)} collective-permute-done((bf16[512,768]{1,0:T(8,128)(2,1)}, bf16[512,768]{1,0:T(8,128)(2,1)}, u32[]{:S(2)}, u32[]{:S(2)}) %collective-permute-start.6) | collective-permute-done | bytes 786464 | tf_op jit(solution)/shard_map/head_weights/ppermute | solution.py:194
  117.3 3.2 fusion.4
  120.8 3.0 fusion.2
  130.1 6.7 %collective-permute-done.10 = bf16[192,512]{1,0:T(8,128)(2,1)S(1)} collective-permute-done((bf16[192,512]{1,0:T(8,128)(2,1)S(1)}, bf16[192,512]{1,0:T(8,128)(2,1)S(1)}, u32[]{:S(2)}, u32[]{:S(2)}) %collective-permute-start.10) | collective-permute-done | bytes 196640 | tf_op jit(solution)/shard_map/down_weight_planes/ppermute | solution.py:194
  142.0 4.4 collective-permute-start.15
  148.1 3.5 convolution_convert_fusion.15.v_ref
  154.2 3.7 fusion.126
  158.0 2.8 collective-permute-done.12
  166.1 9.0 %collective-permute-done.13 = bf16[128,2048]{1,0:T(8,128)(2,1)} collective-permute-done((bf16[128,2048]{1,0:T(8,128)(2,1)}, bf16[128,2048]{1,0:T(8,128)(2,1)}, u32[]{:S(2)}, u32[]{:S(2)}) %collective-permute-start.13) | collective-permute-done | bytes 524320 | tf_op jit(solution)/shard_map/cotangent_ring/ppermute | solution.py:194
  175.1 3.5 multiply_convert_fusion.1
  199.9 5.5 collective-permute-done.18
  205.3 11.6 %collective-permute-done.19 = bf16[128,2048]{1,0:T(8,128)(2,1)S(1)} collective-permute-done((bf16[128,2048]{1,0:T(8,128)(2,1)S(1)}, bf16[128,2048]{1,0:T(8,128)(2,1)S(1)}, u32[]{:S(2)}, u32[]{:S(2)}) %collective-permute-start.19) | collective-permute-done | bytes 524320 | tf_op jit(solution)/shard_map/attention_out_sum/ppermute | solution.py:194
  230.1 5.0 collective-permute-done.22
  242.8 8.3 %collective-permute-done.24 = bf16[128,2048]{1,0:T(8,128)(2,1)S(1)} collective-permute-done((bf16[128,2048]{1,0:T(8,128)(2,1)S(1)}, bf16[128,2048]{1,0:T(8,128)(2,1)S(1)}, u32[]{:S(2)}, u32[]{:S(2)}) %collective-permute-start.24) | collective-permute-done | bytes 524320 | tf_op jit(solution)/shard_map/normed_two_ring/ppermute | solution.py:194
  258.3 9.2 %collective-permute-done.28 = bf16[128,2048]{1,0:T(8,128)(2,1)S(1)} collective-permute-done((bf16[128,2048]{1,0:T(8,128)(2,1)S(1)}, bf16[128,2048]{1,0:T(8,128)(2,1)S(1)}, u32[]{:S(2)}, u32[]{:S(2)}) %collective-permute-start.28) | collective-permute-done | bytes 524320 | tf_op jit(solution)/shard_map/normed_two_ring/ppermute | solution.py:194
  277.8 7.1 %collective-permute-done.27 = bf16[128,2048]{1,0:T(8,128)(2,1)S(1)} collective-permute-done((bf16[128,2048]{1,0:T(8,128)(2,1)S(1)}, bf16[128,2048]{1,0:T(8,128)(2,1)S(1)}, u32[]{:S(2)}, u32[]{:S(2)}) %collective-permute-start.27) | collective-permute-done | bytes 524320 | tf_op jit(solution)/shard_map/normed_two_grad_sum/ppermute | solution.py:194
  285.3 3.8 convolution_convert_fusion.3
  294.5 3.7 convolution_convert_fusion.2
  298.2 6.3 %collective-permute-done.35 = bf16[128,2048]{1,0:T(8,128)(2,1)S(1)} collective-permute-done((bf16[128,2048]{1,0:T(8,128)(2,1)S(1)}, bf16[128,2048]{1,0:T(8,128)(2,1)S(1)}, u32[]{:S(2)}, u32[]{:S(2)}) %collective-permute-start.35) | collective-permute-done | bytes 524320 | tf_op jit(solution)/shard_map/normed_two_grad_sum/ppermute | solution.py:194
  306.8 3.7 convolution_convert_fusion.1
  320.6 2.7 multiply_reduce_fusion
  323.3 3.0 fusion.131
  326.3 10.2 %collective-permute-done.40 = bf16[512,768]{1,0:T(8,128)(2,1)S(1)} collective-permute-done((bf16[512,768]{1,0:T(8,128)(2,1)}, bf16[512,768]{1,0:T(8,128)(2,1)S(1)}, u32[]{:S(2)}, u32[]{:S(2)}) %collective-permute-start.40) | collective-permute-done | bytes 786464 | tf_op jit(solution)/shard_map/down_gradient_columns/ppermute | solution.py:194
  341.4 10.0 %collective-permute-done.45 = bf16[128,2048]{1,0:T(8,128)(2,1)S(1)} collective-permute-done((bf16[128,2048]{1,0:T(8,128)(2,1)S(1)}, bf16[128,2048]{1,0:T(8,128)(2,1)S(1)}, u32[]{:S(2)}, u32[]{:S(2)}) %collective-permute-start.45) | collective-permute-done | bytes 524320 | tf_op jit(solution)/shard_map/out_ring/ppermute | solution.py:194
  353.4 6.7 %collective-permute-done.43 = bf16[128,2048]{1,0:T(8,128)(2,1)S(1)} collective-permute-done((bf16[128,2048]{1,0:T(8,128)(2,1)S(1)}, bf16[128,2048]{1,0:T(8,128)(2,1)S(1)}, u32[]{:S(2)}, u32[]{:S(2)}) %collective-permute-start.43) | collective-permute-done | bytes 524320 | tf_op jit(solution)/shard_map/attention_grad_columns/ppermute | solution.py:194
  374.0 11.9 %collective-permute-done.47 = bf16[128,2048]{1,0:T(8,128)(2,1)} collective-permute-done((bf16[128,2048]{1,0:T(8,128)(2,1)}, bf16[128,2048]{1,0:T(8,128)(2,1)}, u32[]{:S(2)}, u32[]{:S(2)}) %collective-permute-start.47) | collective-permute-done | bytes 524320 | tf_op jit(solution)/shard_map/out_ring/ppermute | solution.py:194
  394.0 3.5 convolution_convert_fusion.5
  401.1 4.3 fusion.46
  406.9 3.9 fusion.132
  412.9 6.1 %shard_map.264 = (f32[1024,256]{1,0:T(8,128)S(1)}, f32[1024,128]{1,0:T(8,128)S(1)}, f32[1024,128]{1,0:T(8,128)S(1)}) custom-call(bf16[1024,256]{1,0:T(8,128)(2,1)S(1)} %pad_maximum_fusion.4.q_ref, bf16[1024,128]{1,0:T(8,128)(2,1)S(1)} %pad_maximum_fusion.9.k_ref, bf16[1024,128]{1,0:T(8,128)(2,1)S(1)} %convolution_convert_fusion.15.v_ref, ...), custom_call_target="tpu_custom_call" | custom-call | flops 1879048192 | bytes 6291456 | tf_op jit(solution)/shard_map/pallas_call | solution.py:141
  424.4 10.6 %collective-permute-done.50 = bf16[128,2048]{1,0:T(8,128)(2,1)S(1)} collective-permute-done((bf16[128,2048]{1,0:T(8,128)(2,1)S(1)}, bf16[128,2048]{1,0:T(8,128)(2,1)S(1)}, u32[]{:S(2)}, u32[]{:S(2)}) %collective-permute-start.50) | collective-permute-done | bytes 524320 | tf_op jit(solution)/shard_map/out_ring/ppermute | solution.py:194
  448.2 8.5 %collective-permute-done.51 = bf16[128,2048]{1,0:T(8,128)(2,1)S(1)} collective-permute-done((bf16[128,2048]{1,0:T(8,128)(2,1)S(1)}, bf16[128,2048]{1,0:T(8,128)(2,1)S(1)}, u32[]{:S(2)}, u32[]{:S(2)}) %collective-permute-start.51) | collective-permute-done | bytes 524320 | tf_op jit(solution)/shard_map/early_ring/ppermute | solution.py:194
  457.6 4.2 reduce-scatter.2.cloned.1.call-done
  463.5 6.8 %fusion.3 = (f32[2048]{0:T(1024)S(1)}, bf16[1024,2048]{1,0:T(8,128)(2,1)S(1)}) fusion(bf16[1,1024,2048]{2,1,0:T(8,128)(2,1)} %all-gather.6.cloned.1.call-done, f32[1024]{0:T(1024)S(1)} %copy-done.59, bf16[1024,768]{1,0:T(8,128)(2,1)} %copy-done.50, bf16[2048,256]{1,0:T(8,128)(2,1)} %get-tuple-element.306, bf16[2048,256]{1,0:T(8,128)(2,1)} %get-tuple-element.305, ...), kind=kOutput, calls=%fused_computation.5 | convolution fusion | flops 3241146368 | bytes 13119488 | tf_op jit(solution)/shard_map/dot_general | solution.py:18
  473.4 4.0 collective-permute-done.69
  480.3 4.0 all-to-all-start
  495.5 6.1 %collective-permute-done.56 = bf16[128,2048]{1,0:T(8,128)(2,1)} collective-permute-done((bf16[128,2048]{1,0:T(8,128)(2,1)}, bf16[128,2048]{1,0:T(8,128)(2,1)}, u32[]{:S(2)}, u32[]{:S(2)}) %collective-permute-start.56) | collective-permute-done | bytes 524320 | tf_op jit(solution)/shard_map/normed_grad_sum/ppermute | solution.py:194
  501.6 10.9 %collective-permute-done.57 = bf16[128,2048]{1,0:T(8,128)(2,1)} collective-permute-done((bf16[128,2048]{1,0:T(8,128)(2,1)}, bf16[128,2048]{1,0:T(8,128)(2,1)}, u32[]{:S(2)}, u32[]{:S(2)}) %collective-permute-start.57) | collective-permute-done | bytes 524320 | tf_op jit(solution)/shard_map/normed_grad_sum/ppermute | solution.py:194
  523.8 3.2 collective-permute-start.64
  529.6 5.3 collective-permute-start.70
  538.9 37.3 %collective-permute-done.71 = bf16[192,2048]{1,0:T(8,128)(2,1)S(1)} collective-permute-done((bf16[192,2048]{1,0:T(8,128)(2,1)S(1)}, bf16[192,2048]{1,0:T(8,128)(2,1)S(1)}, u32[]{:S(2)}, u32[]{:S(2)}) %collective-permute-start.71) | collective-permute-done | bytes 786464 | tf_op jit(solution)/shard_map/up_gradient_move/ppermute | solution.py:194
  (474 shorter events, 219.8 us)
Async XLA Ops:
  7.2 110.1 %all-gather.6.cloned.1.call-start = ((), (), s32[]{:S(2)}) async-start(), calls=%async_computation.4 | async-start | bytes 4718592 | tf_op jit(solution)/shard_map/input_gather/all_gather | solution.py:349
  7.9 122.2 %all-gather.4.cloned.1.call-start = ((), (), s32[]{:S(2)}) async-start(), calls=%async_computation.2 | async-start | bytes 1310720 | tf_op jit(solution)/shard_map/output_weight_gather/all_gather | solution.py:383
  25.3 56.0 %collective-permute-start.5 = (bf16[512,768]{1,0:T(8,128)(2,1)}, bf16[512,768]{1,0:T(8,128)(2,1)}, u32[]{:S(2)}, u32[]{:S(2)}) collective-permute-start(bf16[512,768]{1,0:T(8,128)(2,1)} %pad_maximum_fusion.3), channel_id=1, source_target_pairs={{0,0},{1,9},{2,18},{3,27},{4,4},{5,13},{6,22},{7,31},{8,1},{9,10},... | collective-permute-start | bytes 2359304 | tf_op jit(solution)/shard_map/head_weights/ppermute | solution.py:194
  30.7 93.0 %collective-permute-start.7 = (bf16[512,768]{1,0:T(8,128)(2,1)}, bf16[512,768]{1,0:T(8,128)(2,1)}, u32[]{:S(2)}, u32[]{:S(2)}) collective-permute-start(bf16[512,768]{1,0:T(8,128)(2,1)} %pad_maximum_fusion.3), channel_id=1, source_target_pairs={{0,2},{1,11},{2,16},{3,25},{4,6},{5,15},{6,20},{7,29},{8,3},{9,8},... | collective-permute-start | bytes 2359304 | tf_op jit(solution)/shard_map/head_weights/ppermute | solution.py:194
  36.2 87.6 %collective-permute-start.8 = (bf16[512,768]{1,0:T(8,128)(2,1)}, bf16[512,768]{1,0:T(8,128)(2,1)}, u32[]{:S(2)}, u32[]{:S(2)}) collective-permute-start(bf16[512,768]{1,0:T(8,128)(2,1)} %pad_maximum_fusion.3), channel_id=1, source_target_pairs={{0,3},{1,8},{2,17},{3,26},{4,7},{5,12},{6,21},{7,30},{8,0},{9,9},{... | collective-permute-start | bytes 2359304 | tf_op jit(solution)/shard_map/head_weights/ppermute | solution.py:194
  38.1 77.2 %collective-permute-start.6 = (bf16[512,768]{1,0:T(8,128)(2,1)}, bf16[512,768]{1,0:T(8,128)(2,1)}, u32[]{:S(2)}, u32[]{:S(2)}) collective-permute-start(bf16[512,768]{1,0:T(8,128)(2,1)} %pad_maximum_fusion.3), channel_id=1, source_target_pairs={{0,1},{1,10},{2,19},{3,24},{4,5},{5,14},{6,23},{7,28},{8,2},{9,11}... | collective-permute-start | bytes 2359304 | tf_op jit(solution)/shard_map/head_weights/ppermute | solution.py:194
  82.1 379.7 %reduce-scatter.2.cloned.1.call-start = ((), (), s32[]{:S(2)}) async-start(), calls=%async_computation.3 | async-start | bytes 7864320 | tf_op jit(solution)/shard_map/feed_gradient_columns/reduce_scatter | solution.py:628
  142.0 37.9 %collective-permute-start.14 = (bf16[192,2048]{1,0:T(8,128)(2,1)}, bf16[192,2048]{1,0:T(8,128)(2,1)}, u32[]{:S(2)}, u32[]{:S(2)}) collective-permute-start(bf16[192,2048]{1,0:T(8,128)(2,1)} %constant_dynamic-update-slice_fusion.38), channel_id=1, source_target_pairs={{0,8},{1,9},{2,10},{3,11},{4,12},{5,13},{6,14},{7,15},{8,0},{9,1},... | collective-permute-start | bytes 2359304 | tf_op jit(solution)/shard_map/down_weight_columns/ppermute | solution.py:194
  142.0 38.0 %collective-permute-start.15 = (bf16[192,2048]{1,0:T(8,128)(2,1)}, bf16[192,2048]{1,0:T(8,128)(2,1)}, u32[]{:S(2)}, u32[]{:S(2)}) collective-permute-start(bf16[192,2048]{1,0:T(8,128)(2,1)} %constant_dynamic-update-slice_fusion.38), channel_id=1, source_target_pairs={{0,16},{1,17},{2,18},{3,19},{4,20},{5,21},{6,22},{7,23},{8,24},{9,... | collective-permute-start | bytes 2359304 | tf_op jit(solution)/shard_map/down_weight_columns/ppermute | solution.py:194
  146.4 33.6 %collective-permute-start.16 = (bf16[192,2048]{1,0:T(8,128)(2,1)}, bf16[192,2048]{1,0:T(8,128)(2,1)}, u32[]{:S(2)}, u32[]{:S(2)}) collective-permute-start(bf16[192,2048]{1,0:T(8,128)(2,1)} %constant_dynamic-update-slice_fusion.38), channel_id=1, source_target_pairs={{0,24},{1,25},{2,26},{3,27},{4,28},{5,29},{6,30},{7,31},{8,16},{9,... | collective-permute-start | bytes 2359304 | tf_op jit(solution)/shard_map/down_weight_columns/ppermute | solution.py:194
  183.5 16.4 %collective-permute-start.31 = (bf16[128,2048]{1,0:T(8,128)(2,1)}, bf16[128,2048]{1,0:T(8,128)(2,1)S(1)}, u32[]{:S(2)}, u32[]{:S(2)}) collective-permute-start(bf16[128,2048]{1,0:T(8,128)(2,1)} %collective-permute-done.13), channel_id=1, source_target_pairs={{0,1},{1,2},{2,3},{3,0},{4,5},{5,6},{6,7},{7,4},{8,9},{9,10},{10,1... | collective-permute-start | bytes 1572872 | tf_op jit(solution)/shard_map/cotangent_ring/ppermute | solution.py:194
  185.1 32.6 %collective-permute-start.21 = (bf16[3,128,2048]{2,1,0:T(8,128)(2,1)S(1)}, bf16[3,128,2048]{2,1,0:T(8,128)(2,1)S(1)}, u32[]{:S(2)}, u32[]{:S(2)}) collective-permute-start(bf16[3,128,2048]{2,1,0:T(8,128)(2,1)S(1)} %pad_maximum_fusion.2), channel_id=1, source_target_pairs={{0,4},{1,5},{2,6},{3,7},{4,0},{5,1},{6,2},{7,3},{8,12},{9,13},{10,... | collective-permute-start | bytes 4718600 | tf_op jit(solution)/shard_map/cotangent_core/ppermute | solution.py:194
  192.1 24.9 %collective-permute-start.19 = (bf16[128,2048]{1,0:T(8,128)(2,1)S(1)}, bf16[128,2048]{1,0:T(8,128)(2,1)S(1)}, u32[]{:S(2)}, u32[]{:S(2)}) collective-permute-start(bf16[128,2048]{1,0:T(8,128)(2,1)S(1)} %get-tuple-element.320), channel_id=1, source_target_pairs={{0,16},{1,17},{2,18},{3,19},{4,20},{5,21},{6,22},{7,23},{8,24},{9,... | collective-permute-start | bytes 1572872 | tf_op jit(solution)/shard_map/attention_out_sum/ppermute | solution.py:194
  193.5 23.5 %collective-permute-start.20 = (bf16[128,2048]{1,0:T(8,128)(2,1)S(1)}, bf16[128,2048]{1,0:T(8,128)(2,1)S(1)}, u32[]{:S(2)}, u32[]{:S(2)}) collective-permute-start(bf16[128,2048]{1,0:T(8,128)(2,1)S(1)} %get-tuple-element.319), channel_id=1, source_target_pairs={{0,24},{1,25},{2,26},{3,27},{4,28},{5,29},{6,30},{7,31},{8,16},{9,... | collective-permute-start | bytes 1572872 | tf_op jit(solution)/shard_map/attention_out_sum/ppermute | solution.py:194
  199.9 23.6 %collective-permute-start.32 = (bf16[128,2048]{1,0:T(8,128)(2,1)S(1)}, bf16[128,2048]{1,0:T(8,128)(2,1)S(1)}, u32[]{:S(2)}, u32[]{:S(2)}) collective-permute-start(bf16[128,2048]{1,0:T(8,128)(2,1)S(1)} %collective-permute-done.31), channel_id=1, source_target_pairs={{0,4},{1,5},{2,6},{3,7},{4,0},{5,1},{6,2},{7,3},{8,12},{9,13},{10,... | collective-permute-start | bytes 1572872 | tf_op jit(solution)/shard_map/cotangent_core/ppermute | solution.py:194
  218.5 16.5 %collective-permute-start.22 = (bf16[128,2048]{1,0:T(8,128)(2,1)S(1)}, bf16[128,2048]{1,0:T(8,128)(2,1)S(1)}, u32[]{:S(2)}, u32[]{:S(2)}) collective-permute-start(bf16[128,2048]{1,0:T(8,128)(2,1)S(1)} %multiply_convert_fusion), channel_id=1, source_target_pairs={{0,1},{1,2},{2,3},{3,0},{4,5},{5,6},{6,7},{7,4},{8,9},{9,10},{10,1... | collective-permute-start | bytes 1572872 | tf_op jit(solution)/shard_map/normed_two_ring/ppermute | solution.py:194
  235.0 16.1 %collective-permute-start.24 = (bf16[128,2048]{1,0:T(8,128)(2,1)S(1)}, bf16[128,2048]{1,0:T(8,128)(2,1)S(1)}, u32[]{:S(2)}, u32[]{:S(2)}) collective-permute-start(bf16[128,2048]{1,0:T(8,128)(2,1)S(1)} %collective-permute-done.22), channel_id=1, source_target_pairs={{0,1},{1,2},{2,3},{3,0},{4,5},{5,6},{6,7},{7,4},{8,9},{9,10},{10,1... | collective-permute-start | bytes 1572872 | tf_op jit(solution)/shard_map/normed_two_ring/ppermute | solution.py:194
  237.0 80.1 %collective-permute-start.37 = (bf16[128,2048]{1,0:T(8,128)(2,1)}, bf16[128,2048]{1,0:T(8,128)(2,1)}, u32[]{:S(2)}, u32[]{:S(2)}) collective-permute-start(bf16[128,2048]{1,0:T(8,128)(2,1)} %slice.216), channel_id=1, source_target_pairs={{0,4},{1,5},{2,6},{3,7},{4,0},{5,1},{6,2},{7,3},{8,12},{9,13},{10,... | collective-permute-start | bytes 1572872 | tf_op jit(solution)/shard_map/normed_two_grad_core/ppermute | solution.py:194
  251.2 16.3 %collective-permute-start.28 = (bf16[128,2048]{1,0:T(8,128)(2,1)S(1)}, bf16[128,2048]{1,0:T(8,128)(2,1)S(1)}, u32[]{:S(2)}, u32[]{:S(2)}) collective-permute-start(bf16[128,2048]{1,0:T(8,128)(2,1)S(1)} %collective-permute-done.24), channel_id=1, source_target_pairs={{0,1},{1,2},{2,3},{3,0},{4,5},{5,6},{6,7},{7,4},{8,9},{9,10},{10,1... | collective-permute-start | bytes 1572872 | tf_op jit(solution)/shard_map/normed_two_ring/ppermute | solution.py:194
  252.5 16.0 %collective-permute-start.26 = (bf16[128,2048]{1,0:T(8,128)(2,1)S(1)}, bf16[128,2048]{1,0:T(8,128)(2,1)S(1)}, u32[]{:S(2)}, u32[]{:S(2)}) collective-permute-start(bf16[128,2048]{1,0:T(8,128)(2,1)S(1)} %slice.200), channel_id=1, source_target_pairs={{0,4},{1,5},{2,6},{3,7},{4,0},{5,1},{6,2},{7,3},{8,12},{9,13},{10,... | collective-permute-start | bytes 1572872 | tf_op jit(solution)/shard_map/normed_two_grad_core/ppermute | solution.py:194
  268.7 16.2 %collective-permute-start.27 = (bf16[128,2048]{1,0:T(8,128)(2,1)S(1)}, bf16[128,2048]{1,0:T(8,128)(2,1)S(1)}, u32[]{:S(2)}, u32[]{:S(2)}) collective-permute-start(bf16[128,2048]{1,0:T(8,128)(2,1)S(1)} %add_convert_fusion.10), channel_id=1, source_target_pairs={{0,1},{1,2},{2,3},{3,0},{4,5},{5,6},{6,7},{7,4},{8,9},{9,10},{10,1... | collective-permute-start | bytes 1572872 | tf_op jit(solution)/shard_map/normed_two_grad_sum/ppermute | solution.py:194
  268.8 16.1 %collective-permute-start.30 = (bf16[128,2048]{1,0:T(8,128)(2,1)S(1)}, bf16[128,2048]{1,0:T(8,128)(2,1)S(1)}, u32[]{:S(2)}, u32[]{:S(2)}) collective-permute-start(bf16[128,2048]{1,0:T(8,128)(2,1)S(1)} %slice.204), channel_id=1, source_target_pairs={{0,4},{1,5},{2,6},{3,7},{4,0},{5,1},{6,2},{7,3},{8,12},{9,13},{10,... | collective-permute-start | bytes 1572872 | tf_op jit(solution)/shard_map/normed_two_grad_core/ppermute | solution.py:194
  289.1 15.4 %collective-permute-start.35 = (bf16[128,2048]{1,0:T(8,128)(2,1)S(1)}, bf16[128,2048]{1,0:T(8,128)(2,1)S(1)}, u32[]{:S(2)}, u32[]{:S(2)}) collective-permute-start(bf16[128,2048]{1,0:T(8,128)(2,1)S(1)} %add_convert_fusion.8), channel_id=1, source_target_pairs={{0,1},{1,2},{2,3},{3,0},{4,5},{5,6},{6,7},{7,4},{8,9},{9,10},{10,1... | collective-permute-start | bytes 1572872 | tf_op jit(solution)/shard_map/normed_two_grad_sum/ppermute | solution.py:194
  290.7 45.8 %collective-permute-start.41 = (bf16[4,128,2048]{2,1,0:T(8,128)(2,1)}, bf16[4,128,2048]{2,1,0:T(8,128)(2,1)}, u32[]{:S(2)}, u32[]{:S(2)}) collective-permute-start(bf16[4,128,2048]{2,1,0:T(8,128)(2,1)} %pad_maximum_fusion.1), channel_id=1, source_target_pairs={{0,4},{1,5},{2,6},{3,7},{4,0},{5,1},{6,2},{7,3},{8,12},{9,13},{10,... | collective-permute-start | bytes 6291464 | tf_op jit(solution)/shard_map/out_core/ppermute | solution.py:194
  292.4 33.9 %collective-permute-start.38 = (bf16[512,768]{1,0:T(8,128)(2,1)}, bf16[512,768]{1,0:T(8,128)(2,1)}, u32[]{:S(2)}, u32[]{:S(2)}) collective-permute-start(bf16[512,768]{1,0:T(8,128)(2,1)} %get-tuple-element.309), channel_id=1, source_target_pairs={{0,8},{1,9},{2,10},{3,11},{4,12},{5,13},{6,14},{7,15},{8,0},{9,1},... | collective-permute-start | bytes 2359304 | tf_op jit(solution)/shard_map/down_gradient_columns/ppermute | solution.py:194
  293.6 32.7 %collective-permute-start.39 = (bf16[512,768]{1,0:T(8,128)(2,1)}, bf16[512,768]{1,0:T(8,128)(2,1)}, u32[]{:S(2)}, u32[]{:S(2)}) collective-permute-start(bf16[512,768]{1,0:T(8,128)(2,1)} %get-tuple-element.308), channel_id=1, source_target_pairs={{0,16},{1,17},{2,18},{3,19},{4,20},{5,21},{6,22},{7,23},{8,24},{9,... | collective-permute-start | bytes 2359304 | tf_op jit(solution)/shard_map/down_gradient_columns/ppermute | solution.py:194
  305.4 15.2 %collective-permute-start.36 = (bf16[128,2048]{1,0:T(8,128)(2,1)}, bf16[128,2048]{1,0:T(8,128)(2,1)}, u32[]{:S(2)}, u32[]{:S(2)}) collective-permute-start(bf16[128,2048]{1,0:T(8,128)(2,1)} %add_convert_fusion.6), channel_id=1, source_target_pairs={{0,1},{1,2},{2,3},{3,0},{4,5},{5,6},{6,7},{7,4},{8,9},{9,10},{10,1... | collective-permute-start | bytes 1572872 | tf_op jit(solution)/shard_map/normed_two_grad_sum/ppermute | solution.py:194
  317.2 19.4 %collective-permute-start.40 = (bf16[512,768]{1,0:T(8,128)(2,1)}, bf16[512,768]{1,0:T(8,128)(2,1)S(1)}, u32[]{:S(2)}, u32[]{:S(2)}) collective-permute-start(bf16[512,768]{1,0:T(8,128)(2,1)} %get-tuple-element.307), channel_id=1, source_target_pairs={{0,24},{1,25},{2,26},{3,27},{4,28},{5,29},{6,30},{7,31},{8,16},{9,... | collective-permute-start | bytes 2359304 | tf_op jit(solution)/shard_map/down_gradient_columns/ppermute | solution.py:194
  337.8 15.6 %collective-permute-start.42 = (bf16[128,2048]{1,0:T(8,128)(2,1)S(1)}, bf16[128,2048]{1,0:T(8,128)(2,1)S(1)}, u32[]{:S(2)}, u32[]{:S(2)}) collective-permute-start(bf16[128,2048]{1,0:T(8,128)(2,1)S(1)} %get-tuple-element.225), channel_id=1, source_target_pairs={{0,8},{1,9},{2,10},{3,11},{4,12},{5,13},{6,14},{7,15},{8,0},{9,1},... | collective-permute-start | bytes 1572872 | tf_op jit(solution)/shard_map/attention_grad_columns/ppermute | solution.py:194
  339.1 21.1 %collective-permute-start.43 = (bf16[128,2048]{1,0:T(8,128)(2,1)S(1)}, bf16[128,2048]{1,0:T(8,128)(2,1)S(1)}, u32[]{:S(2)}, u32[]{:S(2)}) collective-permute-start(bf16[128,2048]{1,0:T(8,128)(2,1)S(1)} %get-tuple-element.225), channel_id=1, source_target_pairs={{0,16},{1,17},{2,18},{3,19},{4,20},{5,21},{6,22},{7,23},{8,24},{9,... | collective-permute-start | bytes 1572872 | tf_op jit(solution)/shard_map/attention_grad_columns/ppermute | solution.py:194
  339.9 21.9 %collective-permute-start.44 = (bf16[128,2048]{1,0:T(8,128)(2,1)S(1)}, bf16[128,2048]{1,0:T(8,128)(2,1)S(1)}, u32[]{:S(2)}, u32[]{:S(2)}) collective-permute-start(bf16[128,2048]{1,0:T(8,128)(2,1)S(1)} %get-tuple-element.225), channel_id=1, source_target_pairs={{0,24},{1,25},{2,26},{3,27},{4,28},{5,29},{6,30},{7,31},{8,16},{9,... | collective-permute-start | bytes 1572872 | tf_op jit(solution)/shard_map/attention_grad_columns/ppermute | solution.py:194
  366.7 21.4 %collective-permute-start.46 = (bf16[4,128,2048]{2,1,0:T(8,128)(2,1)}, bf16[4,128,2048]{2,1,0:T(8,128)(2,1)}, u32[]{:S(2)}, u32[]{:S(2)}) collective-permute-start(bf16[4,128,2048]{2,1,0:T(8,128)(2,1)} %bitcast_dynamic-update-slice_fusion.8), channel_id=1, source_target_pairs={{0,4},{1,5},{2,6},{3,7},{4,0},{5,1},{6,2},{7,3},{8,12},{9,13},{10,... | collective-permute-start | bytes 6291464 | tf_op jit(solution)/shard_map/attention_grad_core/ppermute | solution.py:194
  369.8 16.0 %collective-permute-start.47 = (bf16[128,2048]{1,0:T(8,128)(2,1)}, bf16[128,2048]{1,0:T(8,128)(2,1)}, u32[]{:S(2)}, u32[]{:S(2)}) collective-permute-start(bf16[128,2048]{1,0:T(8,128)(2,1)} %add_convert_fusion.5), channel_id=1, source_target_pairs={{0,1},{1,2},{2,3},{3,0},{4,5},{5,6},{6,7},{7,4},{8,9},{9,10},{10,1... | collective-permute-start | bytes 1572872 | tf_op jit(solution)/shard_map/out_ring/ppermute | solution.py:194
  406.8 17.4 %collective-permute-start.49 = (bf16[128,2048]{1,0:T(8,128)(2,1)S(1)}, bf16[128,2048]{1,0:T(8,128)(2,1)S(1)}, u32[]{:S(2)}, u32[]{:S(2)}) collective-permute-start(bf16[128,2048]{1,0:T(8,128)(2,1)S(1)} %fusion.89), channel_id=1, source_target_pairs={{0,1},{1,2},{2,3},{3,0},{4,5},{5,6},{6,7},{7,4},{8,9},{9,10},{10,1... | collective-permute-start | bytes 1572872 | tf_op jit(solution)/shard_map/early_ring/ppermute | solution.py:194
  410.8 24.2 %collective-permute-start.50 = (bf16[128,2048]{1,0:T(8,128)(2,1)S(1)}, bf16[128,2048]{1,0:T(8,128)(2,1)S(1)}, u32[]{:S(2)}, u32[]{:S(2)}) collective-permute-start(bf16[128,2048]{1,0:T(8,128)(2,1)S(1)} %copy-done.43), channel_id=1, source_target_pairs={{0,1},{1,2},{2,3},{3,0},{4,5},{5,6},{6,7},{7,4},{8,9},{9,10},{10,1... | collective-permute-start | bytes 1572872 | tf_op jit(solution)/shard_map/out_ring/ppermute | solution.py:194
  419.0 37.9 %collective-permute-start.52 = (bf16[64,1536]{1,0:T(8,128)(2,1)S(1)}, bf16[64,1536]{1,0:T(8,128)(2,1)S(1)}, u32[]{:S(2)}, u32[]{:S(2)}) collective-permute-start(bf16[64,1536]{1,0:T(8,128)(2,1)S(1)} %get-tuple-element.377), channel_id=1, source_target_pairs={{0,1},{1,2},{2,3},{3,0},{4,5},{5,6},{6,7},{7,4},{8,9},{9,10},{10,1... | collective-permute-start | bytes 589832 | tf_op jit(solution)/shard_map/down_gradient_planes/ppermute | solution.py:194
  419.8 37.1 %collective-permute-start.53 = (bf16[64,1536]{1,0:T(8,128)(2,1)S(1)}, bf16[64,1536]{1,0:T(8,128)(2,1)S(1)}, u32[]{:S(2)}, u32[]{:S(2)}) collective-permute-start(bf16[64,1536]{1,0:T(8,128)(2,1)S(1)} %get-tuple-element.376), channel_id=1, source_target_pairs={{0,2},{1,3},{2,0},{3,1},{4,6},{5,7},{6,4},{7,5},{8,10},{9,11},{10,... | collective-permute-start | bytes 589832 | tf_op jit(solution)/shard_map/down_gradient_planes/ppermute | solution.py:194
  421.6 36.0 %collective-permute-start.54 = (bf16[64,1536]{1,0:T(8,128)(2,1)S(1)}, bf16[64,1536]{1,0:T(8,128)(2,1)}, u32[]{:S(2)}, u32[]{:S(2)}) collective-permute-start(bf16[64,1536]{1,0:T(8,128)(2,1)S(1)} %get-tuple-element.375), channel_id=1, source_target_pairs={{0,3},{1,0},{2,1},{3,2},{4,7},{5,4},{6,5},{7,6},{8,11},{9,8},{10,9... | collective-permute-start | bytes 589832 | tf_op jit(solution)/shard_map/down_gradient_planes/ppermute | solution.py:194
  436.3 20.4 %collective-permute-start.51 = (bf16[128,2048]{1,0:T(8,128)(2,1)S(1)}, bf16[128,2048]{1,0:T(8,128)(2,1)S(1)}, u32[]{:S(2)}, u32[]{:S(2)}) collective-permute-start(bf16[128,2048]{1,0:T(8,128)(2,1)S(1)} %fusion.72), channel_id=1, source_target_pairs={{0,1},{1,2},{2,3},{3,0},{4,5},{5,6},{6,7},{7,4},{8,9},{9,10},{10,1... | collective-permute-start | bytes 1572872 | tf_op jit(solution)/shard_map/early_ring/ppermute | solution.py:194
  461.8 15.7 %collective-permute-start.69 = (bf16[128,2048]{1,0:T(8,128)(2,1)S(1)}, bf16[128,2048]{1,0:T(8,128)(2,1)S(1)}, u32[]{:S(2)}, u32[]{:S(2)}) collective-permute-start(bf16[128,2048]{1,0:T(8,128)(2,1)S(1)} %fusion.70), channel_id=1, source_target_pairs={{0,1},{1,2},{2,3},{3,0},{4,5},{5,6},{6,7},{7,4},{8,9},{9,10},{10,1... | collective-permute-start | bytes 1572872 | tf_op jit(solution)/shard_map/early_ring/ppermute | solution.py:194
  478.4 15.0 %collective-permute-start.66 = (bf16[128,2048]{1,0:T(8,128)(2,1)}, bf16[128,2048]{1,0:T(8,128)(2,1)}, u32[]{:S(2)}, u32[]{:S(2)}) collective-permute-start(bf16[128,2048]{1,0:T(8,128)(2,1)} %pad_maximum_fusion.6), channel_id=1, source_target_pairs={{0,1},{1,2},{2,3},{3,0},{4,5},{5,6},{6,7},{7,4},{8,9},{9,10},{10,1... | collective-permute-start | bytes 1572872 | tf_op jit(solution)/shard_map/qkv_gradient_sum/ppermute | solution.py:194
  485.5 16.1 %collective-permute-start.56 = (bf16[128,2048]{1,0:T(8,128)(2,1)}, bf16[128,2048]{1,0:T(8,128)(2,1)}, u32[]{:S(2)}, u32[]{:S(2)}) collective-permute-start(bf16[128,2048]{1,0:T(8,128)(2,1)} %get-tuple-element.311), channel_id=1, source_target_pairs={{0,8},{1,9},{2,10},{3,11},{4,12},{5,13},{6,14},{7,15},{8,0},{9,1},... | collective-permute-start | bytes 1572872 | tf_op jit(solution)/shard_map/normed_grad_sum/ppermute | solution.py:194
  487.0 25.5 %collective-permute-start.57 = (bf16[128,2048]{1,0:T(8,128)(2,1)}, bf16[128,2048]{1,0:T(8,128)(2,1)}, u32[]{:S(2)}, u32[]{:S(2)}) collective-permute-start(bf16[128,2048]{1,0:T(8,128)(2,1)} %get-tuple-element.313), channel_id=1, source_target_pairs={{0,16},{1,17},{2,18},{3,19},{4,20},{5,21},{6,22},{7,23},{8,24},{9,... | collective-permute-start | bytes 1572872 | tf_op jit(solution)/shard_map/normed_grad_sum/ppermute | solution.py:194
  487.5 25.0 %collective-permute-start.58 = (bf16[128,2048]{1,0:T(8,128)(2,1)}, bf16[128,2048]{1,0:T(8,128)(2,1)}, u32[]{:S(2)}, u32[]{:S(2)}) collective-permute-start(bf16[128,2048]{1,0:T(8,128)(2,1)} %get-tuple-element.312), channel_id=1, source_target_pairs={{0,24},{1,25},{2,26},{3,27},{4,28},{5,29},{6,30},{7,31},{8,16},{9,... | collective-permute-start | bytes 1572872 | tf_op jit(solution)/shard_map/normed_grad_sum/ppermute | solution.py:194
  495.5 40.6 %collective-permute-start.67 = (bf16[128,2048]{1,0:T(8,128)(2,1)}, bf16[128,2048]{1,0:T(8,128)(2,1)}, u32[]{:S(2)}, u32[]{:S(2)}) collective-permute-start(bf16[128,2048]{1,0:T(8,128)(2,1)} %add_convert_fusion.2), channel_id=1, source_target_pairs={{0,1},{1,2},{2,3},{3,0},{4,5},{5,6},{6,7},{7,4},{8,9},{9,10},{10,1... | collective-permute-start | bytes 1572872 | tf_op jit(solution)/shard_map/qkv_gradient_sum/ppermute | solution.py:194
  527.3 49.0 %collective-permute-start.71 = (bf16[192,2048]{1,0:T(8,128)(2,1)S(1)}, bf16[192,2048]{1,0:T(8,128)(2,1)S(1)}, u32[]{:S(2)}, u32[]{:S(2)}) collective-permute-start(bf16[192,2048]{1,0:T(8,128)(2,1)S(1)} %get-tuple-element.321), channel_id=1, source_target_pairs={{0,2},{1,11},{2,16},{3,25},{4,6},{5,15},{6,20},{7,29},{8,3},{9,8},... | collective-permute-start | bytes 2359304 | tf_op jit(solution)/shard_map/up_gradient_move/ppermute | solution.py:194
  529.6 48.0 %collective-permute-start.70 = (bf16[192,2048]{1,0:T(8,128)(2,1)S(1)}, bf16[192,2048]{1,0:T(8,128)(2,1)S(1)}, u32[]{:S(2)}, u32[]{:S(2)}) collective-permute-start(bf16[192,2048]{1,0:T(8,128)(2,1)S(1)} %get-tuple-element.322), channel_id=1, source_target_pairs={{0,0},{1,9},{2,18},{3,27},{4,4},{5,13},{6,22},{7,31},{8,1},{9,10},... | collective-permute-start | bytes 2359304 | tf_op jit(solution)/shard_map/gate_gradient_move/ppermute | solution.py:194
  537.4 41.6 %collective-permute-start.68 = (bf16[128,2048]{1,0:T(8,128)(2,1)S(1)}, bf16[128,2048]{1,0:T(8,128)(2,1)S(1)}, u32[]{:S(2)}, u32[]{:S(2)}) collective-permute-start(bf16[128,2048]{1,0:T(8,128)(2,1)S(1)} %add_convert_fusion.1), channel_id=1, source_target_pairs={{0,1},{1,2},{2,3},{3,0},{4,5},{5,6},{6,7},{7,4},{8,9},{9,10},{10,1... | collective-permute-start | bytes 1572872 | tf_op jit(solution)/shard_map/qkv_gradient_sum/ppermute | solution.py:194
  (94 other events, 1336.4 us)
Sparse Core Ops, SparseCore 0:
  9.9 59.3 all-gather.5
  82.2 34.4 all-gather.3
  393.1 68.6 reduce-scatter.1

commit v5 on v4

--- a/solution.py
+++ b/solution.py
@@ -574,6 +574,11 @@
     ]
     out_other = named("out_core", to_core, jnp.stack([piece for _, piece in out_pieces]))
 
+    out_terms = [
+        (piece.astype(WIDE) + out_other[i].astype(WIDE)).astype(LOW)
+        for i, (piece, _) in enumerate(out_pieces)
+    ]
+    normed_two_grad, out_terms = fence((normed_two_grad, out_terms))
     weighted = gain_two * normed_two_grad
     middle_grad = (
         cotangent
@@ -592,38 +597,16 @@
             for terms, shift in ((gate_terms, 0), (up_terms, up_shift))
         ]
     )
-    attention_grad_local, down_sent, out_other, feed_terms = fence(
-        (attention_grad_local, down_sent, out_other, feed_terms)
-    )
-
-    out_terms = [
-        (piece.astype(WIDE) + out_other[i].astype(WIDE)).astype(LOW)
-        for i, (piece, _) in enumerate(out_pieces)
-    ]
     out_running = out_terms[1]
     for i in range(1, plane_count - 2):
         out_running = named("out_ring", ring_step, out_running, out_terms[i + 1])
+    attention_grad_local, down_sent, out_running, feed_terms = fence(
+        (attention_grad_local, down_sent, out_running, feed_terms)
+    )
+
     grad_columns = named("attention_grad_columns", plane_columns, attention_grad_local)
-    grad_columns, out_running = fence((grad_columns, out_running))
     out_running = named("out_ring", ring_step, out_running, out_terms[plane_count - 1])
-    attention_grad = named("attention_grad_core", plane_gather, grad_columns)
-    down_mine = sum(block.astype(WIDE) for block in down_sent).astype(LOW)
-    down_mine = down_mine.reshape(2, plane_count, -1, hidden_width)
-    own_half = lax.dynamic_index_in_dim(down_mine, core, 0, keepdims=False)
-    other_half = named(
-        "down_gradient_core",
-        to_core,
-        lax.dynamic_index_in_dim(down_mine, 1 - core, 0, keepdims=False),
-    )
-    down_pair = jnp.where(
-        core == 0,
-        jnp.concatenate([own_half, other_half], axis=2),
-        jnp.concatenate([other_half, own_half], axis=2),
-    )
-    attention_grad, out_running, down_pair, feed_terms = fence(
-        (attention_grad, out_running, down_pair, feed_terms)
-    )
-
+    grad_columns, out_running, feed_terms = fence((grad_columns, out_running, feed_terms))
     with jax.named_scope("feed_gradient_columns"):
         feed_mine = lax.psum_scatter(
             feed_terms,
@@ -633,6 +616,28 @@
             tiled=True,
         )
     out_total = named("out_ring", ring_step, out_running, out_terms[0], True)
+    attention_grad = named("attention_grad_core", plane_gather, grad_columns)
+    down_mine = sum(block.astype(WIDE) for block in down_sent).astype(LOW)
+    down_mine = down_mine.reshape(2, plane_count, -1, hidden_width)
+    own_half = lax.dynamic_index_in_dim(down_mine, core, 0, keepdims=False)
+    other_half = named(
+        "down_gradient_core",
+        to_core,
+        lax.dynamic_index_in_dim(down_mine, 1 - core, 0, keepdims=False),
+    )
+    down_pair = jnp.where(
+        core == 0,
+        jnp.concatenate([own_half, other_half], axis=2),
+        jnp.concatenate([other_half, own_half], axis=2),
+    )
+    down_moved = []
+    for d in range(plane_count):
+        block = lax.dynamic_index_in_dim(
+            down_pair, lax.rem(plane + d, plane_count), 0, keepdims=False
+        )
+        down_moved.append(named("down_gradient_planes", up, block, d) if d else block)
+    attention_grad, out_total, down_moved = fence((attention_grad, out_total, down_moved))
+
     gated_grad = dot(attention_grad, output_rows, 1, 1).astype(LOW).astype(WIDE)
     logit_grad = (gated_grad * mixed * gate_open * (1.0 - gate_open)).astype(LOW)
     mixed_grad = (gated_grad * gate_open).astype(LOW)
@@ -652,16 +657,10 @@
     query_rot_grad, key_rot_grad, value_sum = attention_backward(
         queries, keys, values, mixed, mixed_grad, row_info, column_info, head_width
     )
-    query_rot_grad, key_rot_grad, value_sum, early_running, out_total = fence(
-        (query_rot_grad, key_rot_grad, value_sum, early_running, out_total)
+    query_rot_grad, key_rot_grad, value_sum, early_running = fence(
+        (query_rot_grad, key_rot_grad, value_sum, early_running)
     )
     early_running = named("early_ring", ring_step, early_running, early_term(plane_count - 1))
-    down_moved = []
-    for d in range(plane_count):
-        block = lax.dynamic_index_in_dim(
-            down_pair, lax.rem(plane + d, plane_count), 0, keepdims=False
-        )
-        down_moved.append(named("down_gradient_planes", up, block, d) if d else block)
     if sharing > 1:
         key_rot_grad = key_rot_grad + to_core(key_rot_grad)
         value_sum = value_sum + to_core(value_sum)
@@ -690,8 +689,8 @@
         for i in range(plane_count)
     ]
     joined_grad = jnp.concatenate([query_grad, key_grad, value_grad, logit_grad], axis=1)
-    qkv_pieces, joined_grad, early_running, feed_mine, down_moved = fence(
-        (qkv_pieces, joined_grad, early_running, feed_mine, down_moved)
+    qkv_pieces, joined_grad, early_running, feed_mine = fence(
+        (qkv_pieces, joined_grad, early_running, feed_mine)
     )
 
     normed_grad_partial = dot(

time: 597 us -> 577 us (0.966)
  waiting for transfers between devices: 270 us -> 253 us
  starting transfers between devices: 80.2 us -> 88.3 us
  other arithmetic: 62.2 us -> 56.2 us
    ppermute x72, waiting for transfers between devices: 264 us -> 251 us  [send(): return lax.ppermute(value, AXES, pairs)]
    ppermute x72, starting transfers between devices: 76 us -> 82.6 us  [send(): return lax.ppermute(value, AXES, pairs)]
    unnamed x157 -> x167, local copies, waits for them, and re-layouts: 14.7 us -> 13.9 us
  transfers between devices with their start and end apart: 76 -> 76, of which waited for: 37 -> 36; matrix products, arithmetic and copies ran while one was open for 32% -> 33% of each run, Pallas kernels for 1% -> 2%
where the time goes in v5:
time: 577 us; the launch traced here: 569 us
  waiting for transfers between devices  253 us (44%)
  starting transfers between devices  88.3 us (15%)
  local copies, waits for them, and re-layouts  79.3 us (14%)
  matrix products  67.3 us (12%)
  other arithmetic  56.2 us (10%)
  between operations  16.2 us (3%)
  Pallas kernels  8.77 us (2%)
    ppermute x72, waiting for transfers between devices, send(): return lax.ppermute(value, AXES, pairs)  251 us
    ppermute x72, starting transfers between devices, send(): return lax.ppermute(value, AXES, pairs)  82.6 us
    dot_general x39, matrix products, dot(): lax.dot_general(left, right, (((left_dim,), (right_dim,)), ((), ())), pre...  67.3 us
    unnamed x167, local copies, waits for them, and re-layouts  13.9 us
  transfers between devices with their start and end apart: 76, of which 36 were waited for; matrix products, arithmetic and copies ran while one was open for 33% of the time, Pallas kernels for 2%

profile of v5, /device:TPU:4, one launch (start us, length us, event | category | flops | bytes accessed | tf_op | source)
XLA Modules:
  0.0 568.5 jit_solution(436477357424949598)
XLA Ops:
  10.8 2.8 concatenate.137
  25.3 5.5 collective-permute-start.5
  30.7 5.4 collective-permute-start.7
  40.2 3.0 multiply_sine_fusion
  43.4 37.9 %collective-permute-done.5 = bf16[512,768]{1,0:T(8,128)(2,1)} collective-permute-done((bf16[512,768]{1,0:T(8,128)(2,1)}, bf16[512,768]{1,0:T(8,128)(2,1)}, u32[]{:S(2)}, u32[]{:S(2)}) %collective-permute-start.5) | collective-permute-done | bytes 786464 | tf_op jit(solution)/shard_map/head_weights/ppermute | solution.py:194
  84.0 2.9 constant_dynamic-update-slice_fusion.45
  88.2 5.1 constant_dynamic-slice_fusion.10
  93.3 22.0 %collective-permute-done.6 = bf16[512,768]{1,0:T(8,128)(2,1)} collective-permute-done((bf16[512,768]{1,0:T(8,128)(2,1)}, bf16[512,768]{1,0:T(8,128)(2,1)}, u32[]{:S(2)}, u32[]{:S(2)}) %collective-permute-start.6) | collective-permute-done | bytes 786464 | tf_op jit(solution)/shard_map/head_weights/ppermute | solution.py:194
  117.4 3.2 fusion.4
  120.8 3.0 fusion.2
  130.1 6.7 %collective-permute-done.10 = bf16[192,512]{1,0:T(8,128)(2,1)S(1)} collective-permute-done((bf16[192,512]{1,0:T(8,128)(2,1)S(1)}, bf16[192,512]{1,0:T(8,128)(2,1)S(1)}, u32[]{:S(2)}, u32[]{:S(2)}) %collective-permute-start.10) | collective-permute-done | bytes 196640 | tf_op jit(solution)/shard_map/down_weight_planes/ppermute | solution.py:194
  142.0 4.4 collective-permute-start.15
  148.1 3.5 convolution_convert_fusion.15.v_ref
  154.2 3.7 fusion.126
  157.9 2.9 collective-permute-done.12
  166.2 9.0 %collective-permute-done.13 = bf16[128,2048]{1,0:T(8,128)(2,1)} collective-permute-done((bf16[128,2048]{1,0:T(8,128)(2,1)}, bf16[128,2048]{1,0:T(8,128)(2,1)}, u32[]{:S(2)}, u32[]{:S(2)}) %collective-permute-start.13) | collective-permute-done | bytes 524320 | tf_op jit(solution)/shard_map/cotangent_ring/ppermute | solution.py:194
  175.2 3.5 multiply_convert_fusion.1
  200.0 5.5 collective-permute-done.18
  205.4 11.6 %collective-permute-done.19 = bf16[128,2048]{1,0:T(8,128)(2,1)S(1)} collective-permute-done((bf16[128,2048]{1,0:T(8,128)(2,1)S(1)}, bf16[128,2048]{1,0:T(8,128)(2,1)S(1)}, u32[]{:S(2)}, u32[]{:S(2)}) %collective-permute-start.19) | collective-permute-done | bytes 524320 | tf_op jit(solution)/shard_map/attention_out_sum/ppermute | solution.py:194
  230.0 5.1 collective-permute-done.22
  242.9 8.4 %collective-permute-done.24 = bf16[128,2048]{1,0:T(8,128)(2,1)S(1)} collective-permute-done((bf16[128,2048]{1,0:T(8,128)(2,1)S(1)}, bf16[128,2048]{1,0:T(8,128)(2,1)S(1)}, u32[]{:S(2)}, u32[]{:S(2)}) %collective-permute-start.24) | collective-permute-done | bytes 524320 | tf_op jit(solution)/shard_map/normed_two_ring/ppermute | solution.py:194
  258.3 9.2 %collective-permute-done.28 = bf16[128,2048]{1,0:T(8,128)(2,1)S(1)} collective-permute-done((bf16[128,2048]{1,0:T(8,128)(2,1)S(1)}, bf16[128,2048]{1,0:T(8,128)(2,1)S(1)}, u32[]{:S(2)}, u32[]{:S(2)}) %collective-permute-start.28) | collective-permute-done | bytes 524320 | tf_op jit(solution)/shard_map/normed_two_ring/ppermute | solution.py:194
  277.9 7.1 %collective-permute-done.27 = bf16[128,2048]{1,0:T(8,128)(2,1)S(1)} collective-permute-done((bf16[128,2048]{1,0:T(8,128)(2,1)S(1)}, bf16[128,2048]{1,0:T(8,128)(2,1)S(1)}, u32[]{:S(2)}, u32[]{:S(2)}) %collective-permute-start.27) | collective-permute-done | bytes 524320 | tf_op jit(solution)/shard_map/normed_two_grad_sum/ppermute | solution.py:194
  285.4 3.8 convolution_convert_fusion.3
  294.6 3.7 convolution_convert_fusion.2
  298.3 6.3 %collective-permute-done.35 = bf16[128,2048]{1,0:T(8,128)(2,1)S(1)} collective-permute-done((bf16[128,2048]{1,0:T(8,128)(2,1)S(1)}, bf16[128,2048]{1,0:T(8,128)(2,1)S(1)}, u32[]{:S(2)}, u32[]{:S(2)}) %collective-permute-start.35) | collective-permute-done | bytes 524320 | tf_op jit(solution)/shard_map/normed_two_grad_sum/ppermute | solution.py:194
  306.8 3.7 convolution_convert_fusion.1
  322.0 3.8 fusion.72
  329.1 10.2 %collective-permute-done.42 = bf16[128,2048]{1,0:T(8,128)(2,1)S(1)} collective-permute-done((bf16[128,2048]{1,0:T(8,128)(2,1)S(1)}, bf16[128,2048]{1,0:T(8,128)(2,1)S(1)}, u32[]{:S(2)}, u32[]{:S(2)}) %collective-permute-start.42) | collective-permute-done | bytes 524320 | tf_op jit(solution)/shard_map/out_ring/ppermute | solution.py:194
  343.1 9.0 %collective-permute-done.46 = bf16[128,2048]{1,0:T(8,128)(2,1)S(1)} collective-permute-done((bf16[128,2048]{1,0:T(8,128)(2,1)S(1)}, bf16[128,2048]{1,0:T(8,128)(2,1)S(1)}, u32[]{:S(2)}, u32[]{:S(2)}) %collective-permute-start.46) | collective-permute-done | bytes 524320 | tf_op jit(solution)/shard_map/out_ring/ppermute | solution.py:194
  354.5 6.5 %collective-permute-done.44 = bf16[128,2048]{1,0:T(8,128)(2,1)S(1)} collective-permute-done((bf16[128,2048]{1,0:T(8,128)(2,1)S(1)}, bf16[128,2048]{1,0:T(8,128)(2,1)S(1)}, u32[]{:S(2)}, u32[]{:S(2)}) %collective-permute-start.44) | collective-permute-done | bytes 524320 | tf_op jit(solution)/shard_map/attention_grad_columns/ppermute | solution.py:194
  371.8 3.6 fusion.132
  380.0 2.7 collective-permute-start.52
  382.7 6.0 %collective-permute-done.48 = bf16[128,2048]{1,0:T(8,128)(2,1)S(1)} collective-permute-done((bf16[128,2048]{1,0:T(8,128)(2,1)}, bf16[128,2048]{1,0:T(8,128)(2,1)S(1)}, u32[]{:S(2)}, u32[]{:S(2)}) %collective-permute-start.48) | collective-permute-done | bytes 524320 | tf_op jit(solution)/shard_map/out_ring/ppermute | solution.py:194
  389.8 2.9 select_bitcast_fusion.1
  393.2 7.3 %collective-permute-done.51 = bf16[64,1536]{1,0:T(8,128)(2,1)S(1)} collective-permute-done((bf16[64,1536]{1,0:T(8,128)(2,1)S(1)}, bf16[64,1536]{1,0:T(8,128)(2,1)S(1)}, u32[]{:S(2)}, u32[]{:S(2)}) %collective-permute-start.51) | collective-permute-done | bytes 196640 | tf_op jit(solution)/shard_map/down_gradient_planes/ppermute | solution.py:194
  405.3 4.3 fusion.46
  411.1 4.9 collective-permute-start.53
  416.1 6.1 %shard_map.264 = (f32[1024,256]{1,0:T(8,128)S(1)}, f32[1024,128]{1,0:T(8,128)S(1)}, f32[1024,128]{1,0:T(8,128)S(1)}) custom-call(bf16[1024,256]{1,0:T(8,128)(2,1)S(1)} %pad_maximum_fusion.4.q_ref, bf16[1024,128]{1,0:T(8,128)(2,1)S(1)} %pad_maximum_fusion.9.k_ref, bf16[1024,128]{1,0:T(8,128)(2,1)S(1)} %convolution_convert_fusion.15.v_ref, ...), custom_call_target="tpu_custom_call" | custom-call | flops 1879048192 | bytes 6291456 | tf_op jit(solution)/shard_map/pallas_call | solution.py:141
  422.3 5.1 collective-permute-done.53
  443.7 6.8 %fusion.3 = (f32[2048]{0:T(1024)S(1)}, bf16[1024,2048]{1,0:T(8,128)(2,1)S(1)}) fusion(bf16[1,1024,2048]{2,1,0:T(8,128)(2,1)} %all-gather.6.cloned.1.call-done, f32[1024]{0:T(1024)S(1)} %copy-done.66, bf16[1024,768]{1,0:T(8,128)(2,1)} %copy-done.57, bf16[2048,256]{1,0:T(8,128)(2,1)} %get-tuple-element.312, bf16[2048,256]{1,0:T(8,128)(2,1)} %get-tuple-element.311, ...), kind=kOutput, calls=%fused_computation.5 | convolution fusion | flops 3241146368 | bytes 13119488 | tf_op jit(solution)/shard_map/dot_general | solution.py:18
  453.8 3.0 collective-permute-done.69
  459.7 5.6 all-to-all-start
  474.4 8.2 %collective-permute-done.56 = bf16[128,2048]{1,0:T(8,128)(2,1)} collective-permute-done((bf16[128,2048]{1,0:T(8,128)(2,1)}, bf16[128,2048]{1,0:T(8,128)(2,1)}, u32[]{:S(2)}, u32[]{:S(2)}) %collective-permute-start.56) | collective-permute-done | bytes 524320 | tf_op jit(solution)/shard_map/normed_grad_sum/ppermute | solution.py:194
  482.6 10.9 %collective-permute-done.57 = bf16[128,2048]{1,0:T(8,128)(2,1)} collective-permute-done((bf16[128,2048]{1,0:T(8,128)(2,1)}, bf16[128,2048]{1,0:T(8,128)(2,1)}, u32[]{:S(2)}, u32[]{:S(2)}) %collective-permute-start.57) | collective-permute-done | bytes 524320 | tf_op jit(solution)/shard_map/normed_grad_sum/ppermute | solution.py:194
  503.7 4.2 collective-permute-start.64
  510.6 5.3 collective-permute-start.70
  519.9 37.3 %collective-permute-done.71 = bf16[192,2048]{1,0:T(8,128)(2,1)S(1)} collective-permute-done((bf16[192,2048]{1,0:T(8,128)(2,1)S(1)}, bf16[192,2048]{1,0:T(8,128)(2,1)S(1)}, u32[]{:S(2)}, u32[]{:S(2)}) %collective-permute-start.71) | collective-permute-done | bytes 786464 | tf_op jit(solution)/shard_map/up_gradient_move/ppermute | solution.py:194
  (485 shorter events, 209.7 us)
Async XLA Ops:
  7.2 110.2 %all-gather.6.cloned.1.call-start = ((), (), s32[]{:S(2)}) async-start(), calls=%async_computation.4 | async-start | bytes 4718592 | tf_op jit(solution)/shard_map/input_gather/all_gather | solution.py:349
  7.9 122.1 %all-gather.4.cloned.1.call-start = ((), (), s32[]{:S(2)}) async-start(), calls=%async_computation.2 | async-start | bytes 1310720 | tf_op jit(solution)/shard_map/output_weight_gather/all_gather | solution.py:383
  25.3 56.0 %collective-permute-start.5 = (bf16[512,768]{1,0:T(8,128)(2,1)}, bf16[512,768]{1,0:T(8,128)(2,1)}, u32[]{:S(2)}, u32[]{:S(2)}) collective-permute-start(bf16[512,768]{1,0:T(8,128)(2,1)} %pad_maximum_fusion.3), channel_id=1, source_target_pairs={{0,0},{1,9},{2,18},{3,27},{4,4},{5,13},{6,22},{7,31},{8,1},{9,10},... | collective-permute-start | bytes 2359304 | tf_op jit(solution)/shard_map/head_weights/ppermute | solution.py:194
  30.7 93.1 %collective-permute-start.7 = (bf16[512,768]{1,0:T(8,128)(2,1)}, bf16[512,768]{1,0:T(8,128)(2,1)}, u32[]{:S(2)}, u32[]{:S(2)}) collective-permute-start(bf16[512,768]{1,0:T(8,128)(2,1)} %pad_maximum_fusion.3), channel_id=1, source_target_pairs={{0,2},{1,11},{2,16},{3,25},{4,6},{5,15},{6,20},{7,29},{8,3},{9,8},... | collective-permute-start | bytes 2359304 | tf_op jit(solution)/shard_map/head_weights/ppermute | solution.py:194
  36.2 87.6 %collective-permute-start.8 = (bf16[512,768]{1,0:T(8,128)(2,1)}, bf16[512,768]{1,0:T(8,128)(2,1)}, u32[]{:S(2)}, u32[]{:S(2)}) collective-permute-start(bf16[512,768]{1,0:T(8,128)(2,1)} %pad_maximum_fusion.3), channel_id=1, source_target_pairs={{0,3},{1,8},{2,17},{3,26},{4,7},{5,12},{6,21},{7,30},{8,0},{9,9},{... | collective-permute-start | bytes 2359304 | tf_op jit(solution)/shard_map/head_weights/ppermute | solution.py:194
  38.1 77.2 %collective-permute-start.6 = (bf16[512,768]{1,0:T(8,128)(2,1)}, bf16[512,768]{1,0:T(8,128)(2,1)}, u32[]{:S(2)}, u32[]{:S(2)}) collective-permute-start(bf16[512,768]{1,0:T(8,128)(2,1)} %pad_maximum_fusion.3), channel_id=1, source_target_pairs={{0,1},{1,10},{2,19},{3,24},{4,5},{5,14},{6,23},{7,28},{8,2},{9,11}... | collective-permute-start | bytes 2359304 | tf_op jit(solution)/shard_map/head_weights/ppermute | solution.py:194
  82.1 360.6 %reduce-scatter.2.cloned.1.call-start = ((), (), s32[]{:S(2)}) async-start(), calls=%async_computation.3 | async-start | bytes 7864320 | tf_op jit(solution)/shard_map/feed_gradient_columns/reduce_scatter | solution.py:611
  123.9 14.4 %collective-permute-start.11 = (bf16[192,512]{1,0:T(8,128)(2,1)S(1)}, bf16[192,512]{1,0:T(8,128)(2,1)S(1)}, u32[]{:S(2)}, u32[]{:S(2)}) collective-permute-start(bf16[192,512]{1,0:T(8,128)(2,1)S(1)} %get-tuple-element.160), channel_id=1, source_target_pairs={{0,3},{1,0},{2,1},{3,2},{4,7},{5,4},{6,5},{7,6},{8,11},{9,8},{10,9... | collective-permute-start | bytes 589832 | tf_op jit(solution)/shard_map/down_weight_planes/ppermute | solution.py:194
  142.0 38.0 %collective-permute-start.14 = (bf16[192,2048]{1,0:T(8,128)(2,1)}, bf16[192,2048]{1,0:T(8,128)(2,1)}, u32[]{:S(2)}, u32[]{:S(2)}) collective-permute-start(bf16[192,2048]{1,0:T(8,128)(2,1)} %constant_dynamic-update-slice_fusion.38), channel_id=1, source_target_pairs={{0,8},{1,9},{2,10},{3,11},{4,12},{5,13},{6,14},{7,15},{8,0},{9,1},... | collective-permute-start | bytes 2359304 | tf_op jit(solution)/shard_map/down_weight_columns/ppermute | solution.py:194
  142.0 38.0 %collective-permute-start.15 = (bf16[192,2048]{1,0:T(8,128)(2,1)}, bf16[192,2048]{1,0:T(8,128)(2,1)}, u32[]{:S(2)}, u32[]{:S(2)}) collective-permute-start(bf16[192,2048]{1,0:T(8,128)(2,1)} %constant_dynamic-update-slice_fusion.38), channel_id=1, source_target_pairs={{0,16},{1,17},{2,18},{3,19},{4,20},{5,21},{6,22},{7,23},{8,24},{9,... | collective-permute-start | bytes 2359304 | tf_op jit(solution)/shard_map/down_weight_columns/ppermute | solution.py:194
  146.4 33.7 %collective-permute-start.16 = (bf16[192,2048]{1,0:T(8,128)(2,1)}, bf16[192,2048]{1,0:T(8,128)(2,1)}, u32[]{:S(2)}, u32[]{:S(2)}) collective-permute-start(bf16[192,2048]{1,0:T(8,128)(2,1)} %constant_dynamic-update-slice_fusion.38), channel_id=1, source_target_pairs={{0,24},{1,25},{2,26},{3,27},{4,28},{5,29},{6,30},{7,31},{8,16},{9,... | collective-permute-start | bytes 2359304 | tf_op jit(solution)/shard_map/down_weight_columns/ppermute | solution.py:194
  146.4 14.4 %collective-permute-start.12 = (bf16[128,2048]{1,0:T(8,128)(2,1)}, bf16[128,2048]{1,0:T(8,128)(2,1)}, u32[]{:S(2)}, u32[]{:S(2)}) collective-permute-start(bf16[128,2048]{1,0:T(8,128)(2,1)} %bitcast.6), channel_id=1, source_target_pairs={{0,1},{1,2},{2,3},{3,0},{4,5},{5,6},{6,7},{7,4},{8,9},{9,10},{10,1... | collective-permute-start | bytes 1572872 | tf_op jit(solution)/shard_map/cotangent_ring/ppermute | solution.py:194
  183.6 16.4 %collective-permute-start.31 = (bf16[128,2048]{1,0:T(8,128)(2,1)}, bf16[128,2048]{1,0:T(8,128)(2,1)S(1)}, u32[]{:S(2)}, u32[]{:S(2)}) collective-permute-start(bf16[128,2048]{1,0:T(8,128)(2,1)} %collective-permute-done.13), channel_id=1, source_target_pairs={{0,1},{1,2},{2,3},{3,0},{4,5},{5,6},{6,7},{7,4},{8,9},{9,10},{10,1... | collective-permute-start | bytes 1572872 | tf_op jit(solution)/shard_map/cotangent_ring/ppermute | solution.py:194
  185.2 32.6 %collective-permute-start.21 = (bf16[3,128,2048]{2,1,0:T(8,128)(2,1)S(1)}, bf16[3,128,2048]{2,1,0:T(8,128)(2,1)S(1)}, u32[]{:S(2)}, u32[]{:S(2)}) collective-permute-start(bf16[3,128,2048]{2,1,0:T(8,128)(2,1)S(1)} %pad_maximum_fusion.2), channel_id=1, source_target_pairs={{0,4},{1,5},{2,6},{3,7},{4,0},{5,1},{6,2},{7,3},{8,12},{9,13},{10,... | collective-permute-start | bytes 4718600 | tf_op jit(solution)/shard_map/cotangent_core/ppermute | solution.py:194
  190.6 14.8 %collective-permute-start.18 = (bf16[128,2048]{1,0:T(8,128)(2,1)S(1)}, bf16[128,2048]{1,0:T(8,128)(2,1)S(1)}, u32[]{:S(2)}, u32[]{:S(2)}) collective-permute-start(bf16[128,2048]{1,0:T(8,128)(2,1)S(1)} %get-tuple-element.328), channel_id=1, source_target_pairs={{0,8},{1,9},{2,10},{3,11},{4,12},{5,13},{6,14},{7,15},{8,0},{9,1},... | collective-permute-start | bytes 1572872 | tf_op jit(solution)/shard_map/attention_out_sum/ppermute | solution.py:194
  192.1 24.9 %collective-permute-start.19 = (bf16[128,2048]{1,0:T(8,128)(2,1)S(1)}, bf16[128,2048]{1,0:T(8,128)(2,1)S(1)}, u32[]{:S(2)}, u32[]{:S(2)}) collective-permute-start(bf16[128,2048]{1,0:T(8,128)(2,1)S(1)} %get-tuple-element.330), channel_id=1, source_target_pairs={{0,16},{1,17},{2,18},{3,19},{4,20},{5,21},{6,22},{7,23},{8,24},{9,... | collective-permute-start | bytes 1572872 | tf_op jit(solution)/shard_map/attention_out_sum/ppermute | solution.py:194
  193.6 23.5 %collective-permute-start.20 = (bf16[128,2048]{1,0:T(8,128)(2,1)S(1)}, bf16[128,2048]{1,0:T(8,128)(2,1)S(1)}, u32[]{:S(2)}, u32[]{:S(2)}) collective-permute-start(bf16[128,2048]{1,0:T(8,128)(2,1)S(1)} %get-tuple-element.329), channel_id=1, source_target_pairs={{0,24},{1,25},{2,26},{3,27},{4,28},{5,29},{6,30},{7,31},{8,16},{9,... | collective-permute-start | bytes 1572872 | tf_op jit(solution)/shard_map/attention_out_sum/ppermute | solution.py:194
  200.0 23.4 %collective-permute-start.32 = (bf16[128,2048]{1,0:T(8,128)(2,1)S(1)}, bf16[128,2048]{1,0:T(8,128)(2,1)S(1)}, u32[]{:S(2)}, u32[]{:S(2)}) collective-permute-start(bf16[128,2048]{1,0:T(8,128)(2,1)S(1)} %collective-permute-done.31), channel_id=1, source_target_pairs={{0,4},{1,5},{2,6},{3,7},{4,0},{5,1},{6,2},{7,3},{8,12},{9,13},{10,... | collective-permute-start | bytes 1572872 | tf_op jit(solution)/shard_map/cotangent_core/ppermute | solution.py:194
  218.6 16.5 %collective-permute-start.22 = (bf16[128,2048]{1,0:T(8,128)(2,1)S(1)}, bf16[128,2048]{1,0:T(8,128)(2,1)S(1)}, u32[]{:S(2)}, u32[]{:S(2)}) collective-permute-start(bf16[128,2048]{1,0:T(8,128)(2,1)S(1)} %multiply_convert_fusion), channel_id=1, source_target_pairs={{0,1},{1,2},{2,3},{3,0},{4,5},{5,6},{6,7},{7,4},{8,9},{9,10},{10,1... | collective-permute-start | bytes 1572872 | tf_op jit(solution)/shard_map/normed_two_ring/ppermute | solution.py:194
  235.1 16.1 %collective-permute-start.24 = (bf16[128,2048]{1,0:T(8,128)(2,1)S(1)}, bf16[128,2048]{1,0:T(8,128)(2,1)S(1)}, u32[]{:S(2)}, u32[]{:S(2)}) collective-permute-start(bf16[128,2048]{1,0:T(8,128)(2,1)S(1)} %collective-permute-done.22), channel_id=1, source_target_pairs={{0,1},{1,2},{2,3},{3,0},{4,5},{5,6},{6,7},{7,4},{8,9},{9,10},{10,1... | collective-permute-start | bytes 1572872 | tf_op jit(solution)/shard_map/normed_two_ring/ppermute | solution.py:194
  237.0 80.2 %collective-permute-start.37 = (bf16[128,2048]{1,0:T(8,128)(2,1)}, bf16[128,2048]{1,0:T(8,128)(2,1)}, u32[]{:S(2)}, u32[]{:S(2)}) collective-permute-start(bf16[128,2048]{1,0:T(8,128)(2,1)} %slice.216), channel_id=1, source_target_pairs={{0,4},{1,5},{2,6},{3,7},{4,0},{5,1},{6,2},{7,3},{8,12},{9,13},{10,... | collective-permute-start | bytes 1572872 | tf_op jit(solution)/shard_map/normed_two_grad_core/ppermute | solution.py:194
  251.2 16.3 %collective-permute-start.28 = (bf16[128,2048]{1,0:T(8,128)(2,1)S(1)}, bf16[128,2048]{1,0:T(8,128)(2,1)S(1)}, u32[]{:S(2)}, u32[]{:S(2)}) collective-permute-start(bf16[128,2048]{1,0:T(8,128)(2,1)S(1)} %collective-permute-done.24), channel_id=1, source_target_pairs={{0,1},{1,2},{2,3},{3,0},{4,5},{5,6},{6,7},{7,4},{8,9},{9,10},{10,1... | collective-permute-start | bytes 1572872 | tf_op jit(solution)/shard_map/normed_two_ring/ppermute | solution.py:194
  252.5 16.0 %collective-permute-start.26 = (bf16[128,2048]{1,0:T(8,128)(2,1)S(1)}, bf16[128,2048]{1,0:T(8,128)(2,1)S(1)}, u32[]{:S(2)}, u32[]{:S(2)}) collective-permute-start(bf16[128,2048]{1,0:T(8,128)(2,1)S(1)} %slice.200), channel_id=1, source_target_pairs={{0,4},{1,5},{2,6},{3,7},{4,0},{5,1},{6,2},{7,3},{8,12},{9,13},{10,... | collective-permute-start | bytes 1572872 | tf_op jit(solution)/shard_map/normed_two_grad_core/ppermute | solution.py:194
  268.8 16.2 %collective-permute-start.27 = (bf16[128,2048]{1,0:T(8,128)(2,1)S(1)}, bf16[128,2048]{1,0:T(8,128)(2,1)S(1)}, u32[]{:S(2)}, u32[]{:S(2)}) collective-permute-start(bf16[128,2048]{1,0:T(8,128)(2,1)S(1)} %add_convert_fusion.10), channel_id=1, source_target_pairs={{0,1},{1,2},{2,3},{3,0},{4,5},{5,6},{6,7},{7,4},{8,9},{9,10},{10,1... | collective-permute-start | bytes 1572872 | tf_op jit(solution)/shard_map/normed_two_grad_sum/ppermute | solution.py:194
  268.9 16.1 %collective-permute-start.30 = (bf16[128,2048]{1,0:T(8,128)(2,1)S(1)}, bf16[128,2048]{1,0:T(8,128)(2,1)S(1)}, u32[]{:S(2)}, u32[]{:S(2)}) collective-permute-start(bf16[128,2048]{1,0:T(8,128)(2,1)S(1)} %slice.204), channel_id=1, source_target_pairs={{0,4},{1,5},{2,6},{3,7},{4,0},{5,1},{6,2},{7,3},{8,12},{9,13},{10,... | collective-permute-start | bytes 1572872 | tf_op jit(solution)/shard_map/normed_two_grad_core/ppermute | solution.py:194
  289.1 15.4 %collective-permute-start.35 = (bf16[128,2048]{1,0:T(8,128)(2,1)S(1)}, bf16[128,2048]{1,0:T(8,128)(2,1)S(1)}, u32[]{:S(2)}, u32[]{:S(2)}) collective-permute-start(bf16[128,2048]{1,0:T(8,128)(2,1)S(1)} %add_convert_fusion.8), channel_id=1, source_target_pairs={{0,1},{1,2},{2,3},{3,0},{4,5},{5,6},{6,7},{7,4},{8,9},{9,10},{10,1... | collective-permute-start | bytes 1572872 | tf_op jit(solution)/shard_map/normed_two_grad_sum/ppermute | solution.py:194
  290.8 31.2 %collective-permute-start.38 = (bf16[4,128,2048]{2,1,0:T(8,128)(2,1)}, bf16[4,128,2048]{2,1,0:T(8,128)(2,1)}, u32[]{:S(2)}, u32[]{:S(2)}) collective-permute-start(bf16[4,128,2048]{2,1,0:T(8,128)(2,1)} %pad_maximum_fusion.1), channel_id=1, source_target_pairs={{0,4},{1,5},{2,6},{3,7},{4,0},{5,1},{6,2},{7,3},{8,12},{9,13},{10,... | collective-permute-start | bytes 6291464 | tf_op jit(solution)/shard_map/out_core/ppermute | solution.py:194
  292.5 47.0 %collective-permute-start.39 = (bf16[512,768]{1,0:T(8,128)(2,1)}, bf16[512,768]{1,0:T(8,128)(2,1)}, u32[]{:S(2)}, u32[]{:S(2)}) collective-permute-start(bf16[512,768]{1,0:T(8,128)(2,1)} %get-tuple-element.315), channel_id=1, source_target_pairs={{0,8},{1,9},{2,10},{3,11},{4,12},{5,13},{6,14},{7,15},{8,0},{9,1},... | collective-permute-start | bytes 2359304 | tf_op jit(solution)/shard_map/down_gradient_columns/ppermute | solution.py:194
  293.7 45.8 %collective-permute-start.40 = (bf16[512,768]{1,0:T(8,128)(2,1)}, bf16[512,768]{1,0:T(8,128)(2,1)}, u32[]{:S(2)}, u32[]{:S(2)}) collective-permute-start(bf16[512,768]{1,0:T(8,128)(2,1)} %get-tuple-element.314), channel_id=1, source_target_pairs={{0,16},{1,17},{2,18},{3,19},{4,20},{5,21},{6,22},{7,23},{8,24},{9,... | collective-permute-start | bytes 2359304 | tf_op jit(solution)/shard_map/down_gradient_columns/ppermute | solution.py:194
  305.5 15.1 %collective-permute-start.36 = (bf16[128,2048]{1,0:T(8,128)(2,1)}, bf16[128,2048]{1,0:T(8,128)(2,1)S(1)}, u32[]{:S(2)}, u32[]{:S(2)}) collective-permute-start(bf16[128,2048]{1,0:T(8,128)(2,1)} %add_convert_fusion.6), channel_id=1, source_target_pairs={{0,1},{1,2},{2,3},{3,0},{4,5},{5,6},{6,7},{7,4},{8,9},{9,10},{10,1... | collective-permute-start | bytes 1572872 | tf_op jit(solution)/shard_map/normed_two_grad_sum/ppermute | solution.py:194
  317.2 22.3 %collective-permute-start.41 = (bf16[512,768]{1,0:T(8,128)(2,1)}, bf16[512,768]{1,0:T(8,128)(2,1)S(1)}, u32[]{:S(2)}, u32[]{:S(2)}) collective-permute-start(bf16[512,768]{1,0:T(8,128)(2,1)} %get-tuple-element.313), channel_id=1, source_target_pairs={{0,24},{1,25},{2,26},{3,27},{4,28},{5,29},{6,30},{7,31},{8,16},{9,... | collective-permute-start | bytes 2359304 | tf_op jit(solution)/shard_map/down_gradient_columns/ppermute | solution.py:194
  339.6 14.9 %collective-permute-start.43 = (bf16[128,2048]{1,0:T(8,128)(2,1)S(1)}, bf16[128,2048]{1,0:T(8,128)(2,1)S(1)}, u32[]{:S(2)}, u32[]{:S(2)}) collective-permute-start(bf16[128,2048]{1,0:T(8,128)(2,1)S(1)} %get-tuple-element.235), channel_id=1, source_target_pairs={{0,8},{1,9},{2,10},{3,11},{4,12},{5,13},{6,14},{7,15},{8,0},{9,1},... | collective-permute-start | bytes 1572872 | tf_op jit(solution)/shard_map/attention_grad_columns/ppermute | solution.py:194
  340.8 20.2 %collective-permute-start.44 = (bf16[128,2048]{1,0:T(8,128)(2,1)S(1)}, bf16[128,2048]{1,0:T(8,128)(2,1)S(1)}, u32[]{:S(2)}, u32[]{:S(2)}) collective-permute-start(bf16[128,2048]{1,0:T(8,128)(2,1)S(1)} %get-tuple-element.235), channel_id=1, source_target_pairs={{0,16},{1,17},{2,18},{3,19},{4,20},{5,21},{6,22},{7,23},{8,24},{9,... | collective-permute-start | bytes 1572872 | tf_op jit(solution)/shard_map/attention_grad_columns/ppermute | solution.py:194
  341.7 21.0 %collective-permute-start.45 = (bf16[128,2048]{1,0:T(8,128)(2,1)S(1)}, bf16[128,2048]{1,0:T(8,128)(2,1)}, u32[]{:S(2)}, u32[]{:S(2)}) collective-permute-start(bf16[128,2048]{1,0:T(8,128)(2,1)S(1)} %get-tuple-element.235), channel_id=1, source_target_pairs={{0,24},{1,25},{2,26},{3,27},{4,28},{5,29},{6,30},{7,31},{8,16},{9,... | collective-permute-start | bytes 1572872 | tf_op jit(solution)/shard_map/attention_grad_columns/ppermute | solution.py:194
  368.8 21.1 %collective-permute-start.47 = (bf16[4,128,2048]{2,1,0:T(8,128)(2,1)}, bf16[4,128,2048]{2,1,0:T(8,128)(2,1)}, u32[]{:S(2)}, u32[]{:S(2)}) collective-permute-start(bf16[4,128,2048]{2,1,0:T(8,128)(2,1)} %bitcast_dynamic-update-slice_fusion.8), channel_id=1, source_target_pairs={{0,4},{1,5},{2,6},{3,7},{4,0},{5,1},{6,2},{7,3},{8,12},{9,13},{10,... | collective-permute-start | bytes 6291464 | tf_op jit(solution)/shard_map/attention_grad_core/ppermute | solution.py:194
  371.7 17.0 %collective-permute-start.48 = (bf16[128,2048]{1,0:T(8,128)(2,1)}, bf16[128,2048]{1,0:T(8,128)(2,1)S(1)}, u32[]{:S(2)}, u32[]{:S(2)}) collective-permute-start(bf16[128,2048]{1,0:T(8,128)(2,1)} %add_convert_fusion.4), channel_id=1, source_target_pairs={{0,1},{1,2},{2,3},{3,0},{4,5},{5,6},{6,7},{7,4},{8,9},{9,10},{10,1... | collective-permute-start | bytes 1572872 | tf_op jit(solution)/shard_map/out_ring/ppermute | solution.py:194
  375.7 17.5 %collective-permute-start.50 = (bf16[64,1536]{1,0:T(8,128)(2,1)S(1)}, bf16[64,1536]{1,0:T(8,128)(2,1)S(1)}, u32[]{:S(2)}, u32[]{:S(2)}) collective-permute-start(bf16[64,1536]{1,0:T(8,128)(2,1)S(1)} %get-tuple-element.387), channel_id=1, source_target_pairs={{0,1},{1,2},{2,3},{3,0},{4,5},{5,6},{6,7},{7,4},{8,9},{9,10},{10,1... | collective-permute-start | bytes 589832 | tf_op jit(solution)/shard_map/down_gradient_planes/ppermute | solution.py:194
  377.5 23.0 %collective-permute-start.51 = (bf16[64,1536]{1,0:T(8,128)(2,1)S(1)}, bf16[64,1536]{1,0:T(8,128)(2,1)S(1)}, u32[]{:S(2)}, u32[]{:S(2)}) collective-permute-start(bf16[64,1536]{1,0:T(8,128)(2,1)S(1)} %get-tuple-element.386), channel_id=1, source_target_pairs={{0,2},{1,3},{2,0},{3,1},{4,6},{5,7},{6,4},{7,5},{8,10},{9,11},{10,... | collective-permute-start | bytes 589832 | tf_op jit(solution)/shard_map/down_gradient_planes/ppermute | solution.py:194
  380.0 20.5 %collective-permute-start.52 = (bf16[64,1536]{1,0:T(8,128)(2,1)S(1)}, bf16[64,1536]{1,0:T(8,128)(2,1)S(1)}, u32[]{:S(2)}, u32[]{:S(2)}) collective-permute-start(bf16[64,1536]{1,0:T(8,128)(2,1)S(1)} %get-tuple-element.385), channel_id=1, source_target_pairs={{0,3},{1,0},{2,1},{3,2},{4,7},{5,4},{6,5},{7,6},{8,11},{9,8},{10,9... | collective-permute-start | bytes 589832 | tf_op jit(solution)/shard_map/down_gradient_planes/ppermute | solution.py:194
  411.1 16.3 %collective-permute-start.53 = (bf16[128,2048]{1,0:T(8,128)(2,1)S(1)}, bf16[128,2048]{1,0:T(8,128)(2,1)S(1)}, u32[]{:S(2)}, u32[]{:S(2)}) collective-permute-start(bf16[128,2048]{1,0:T(8,128)(2,1)S(1)} %fusion.89), channel_id=1, source_target_pairs={{0,1},{1,2},{2,3},{3,0},{4,5},{5,6},{6,7},{7,4},{8,9},{9,10},{10,1... | collective-permute-start | bytes 1572872 | tf_op jit(solution)/shard_map/early_ring/ppermute | solution.py:194
  427.6 14.9 %collective-permute-start.54 = (bf16[128,2048]{1,0:T(8,128)(2,1)S(1)}, bf16[128,2048]{1,0:T(8,128)(2,1)S(1)}, u32[]{:S(2)}, u32[]{:S(2)}) collective-permute-start(bf16[128,2048]{1,0:T(8,128)(2,1)S(1)} %fusion.71), channel_id=1, source_target_pairs={{0,1},{1,2},{2,3},{3,0},{4,5},{5,6},{6,7},{7,4},{8,9},{9,10},{10,1... | collective-permute-start | bytes 1572872 | tf_op jit(solution)/shard_map/early_ring/ppermute | solution.py:194
  466.5 16.1 %collective-permute-start.56 = (bf16[128,2048]{1,0:T(8,128)(2,1)}, bf16[128,2048]{1,0:T(8,128)(2,1)}, u32[]{:S(2)}, u32[]{:S(2)}) collective-permute-start(bf16[128,2048]{1,0:T(8,128)(2,1)} %get-tuple-element.317), channel_id=1, source_target_pairs={{0,8},{1,9},{2,10},{3,11},{4,12},{5,13},{6,14},{7,15},{8,0},{9,1},... | collective-permute-start | bytes 1572872 | tf_op jit(solution)/shard_map/normed_grad_sum/ppermute | solution.py:194
  468.0 25.5 %collective-permute-start.57 = (bf16[128,2048]{1,0:T(8,128)(2,1)}, bf16[128,2048]{1,0:T(8,128)(2,1)}, u32[]{:S(2)}, u32[]{:S(2)}) collective-permute-start(bf16[128,2048]{1,0:T(8,128)(2,1)} %get-tuple-element.319), channel_id=1, source_target_pairs={{0,16},{1,17},{2,18},{3,19},{4,20},{5,21},{6,22},{7,23},{8,24},{9,... | collective-permute-start | bytes 1572872 | tf_op jit(solution)/shard_map/normed_grad_sum/ppermute | solution.py:194
  468.5 25.0 %collective-permute-start.58 = (bf16[128,2048]{1,0:T(8,128)(2,1)}, bf16[128,2048]{1,0:T(8,128)(2,1)}, u32[]{:S(2)}, u32[]{:S(2)}) collective-permute-start(bf16[128,2048]{1,0:T(8,128)(2,1)} %get-tuple-element.318), channel_id=1, source_target_pairs={{0,24},{1,25},{2,26},{3,27},{4,28},{5,29},{6,30},{7,31},{8,16},{9,... | collective-permute-start | bytes 1572872 | tf_op jit(solution)/shard_map/normed_grad_sum/ppermute | solution.py:194
  474.4 42.8 %collective-permute-start.67 = (bf16[128,2048]{1,0:T(8,128)(2,1)}, bf16[128,2048]{1,0:T(8,128)(2,1)}, u32[]{:S(2)}, u32[]{:S(2)}) collective-permute-start(bf16[128,2048]{1,0:T(8,128)(2,1)} %add_convert_fusion.2), channel_id=1, source_target_pairs={{0,1},{1,2},{2,3},{3,0},{4,5},{5,6},{6,7},{7,4},{8,9},{9,10},{10,1... | collective-permute-start | bytes 1572872 | tf_op jit(solution)/shard_map/qkv_gradient_sum/ppermute | solution.py:194
  508.3 49.0 %collective-permute-start.71 = (bf16[192,2048]{1,0:T(8,128)(2,1)S(1)}, bf16[192,2048]{1,0:T(8,128)(2,1)S(1)}, u32[]{:S(2)}, u32[]{:S(2)}) collective-permute-start(bf16[192,2048]{1,0:T(8,128)(2,1)S(1)} %get-tuple-element.331), channel_id=1, source_target_pairs={{0,2},{1,11},{2,16},{3,25},{4,6},{5,15},{6,20},{7,29},{8,3},{9,8},... | collective-permute-start | bytes 2359304 | tf_op jit(solution)/shard_map/up_gradient_move/ppermute | solution.py:194
  510.6 48.0 %collective-permute-start.70 = (bf16[192,2048]{1,0:T(8,128)(2,1)S(1)}, bf16[192,2048]{1,0:T(8,128)(2,1)S(1)}, u32[]{:S(2)}, u32[]{:S(2)}) collective-permute-start(bf16[192,2048]{1,0:T(8,128)(2,1)S(1)} %get-tuple-element.332), channel_id=1, source_target_pairs={{0,0},{1,9},{2,18},{3,27},{4,4},{5,13},{6,22},{7,31},{8,1},{9,10},... | collective-permute-start | bytes 2359304 | tf_op jit(solution)/shard_map/gate_gradient_move/ppermute | solution.py:194
  518.4 41.6 %collective-permute-start.68 = (bf16[128,2048]{1,0:T(8,128)(2,1)S(1)}, bf16[128,2048]{1,0:T(8,128)(2,1)S(1)}, u32[]{:S(2)}, u32[]{:S(2)}) collective-permute-start(bf16[128,2048]{1,0:T(8,128)(2,1)S(1)} %add_convert_fusion.1), channel_id=1, source_target_pairs={{0,1},{1,2},{2,3},{3,0},{4,5},{5,6},{6,7},{7,4},{8,9},{9,10},{10,1... | collective-permute-start | bytes 1572872 | tf_op jit(solution)/shard_map/qkv_gradient_sum/ppermute | solution.py:194
  (99 other events, 1260.0 us)
Sparse Core Ops, SparseCore 0:
  9.9 59.3 all-gather.5
  82.2 34.4 all-gather.3
  362.9 71.1 reduce-scatter.1

commit v6 on v5

--- a/solution.py
+++ b/solution.py
@@ -704,11 +704,14 @@
         chip = plane_chip_sum(normed_grad_partial.astype(LOW))
         chip, qkv_pieces = fence((chip, qkv_pieces))
         normed_grad = plane_columns_sum(chip)
-    qkv_total = named("qkv_gradient_sum", ring_sum, qkv_pieces)
+    running = qkv_pieces[1]
+    for i in range(1, plane_count - 1):
+        running = named("qkv_gradient_sum", ring_step, running, qkv_pieces[i + 1])
     early_sum = named("early_ring", ring_step, early_running, early_term(0), True)
 
     vectors = [attention_gain_terms, query_gain_grad, key_gain_grad / sharing, feedforward_gain_terms]
-    normed_grad, vectors = fence((normed_grad, vectors))
+    normed_grad, vectors, running = fence((normed_grad, vectors, running))
+    qkv_total = named("qkv_gradient_sum", ring_step, running, qkv_pieces[0], True)
     vectors = [vector.reshape(seq_count, plane_count, -1) for vector in vectors]
     small = named("gain_columns", small_columns, jnp.concatenate(vectors, axis=2))
     small, feed_mine = fence((small, feed_mine))

time: 577 us -> 573 us (level)
  waiting for transfers between devices: 253 us -> 244 us
    ppermute x72, waiting for transfers between devices: 251 us -> 243 us  [send(): return lax.ppermute(value, AXES, pairs)]
    unnamed x167 -> x177, local copies, waits for them, and re-layouts: 13.9 us -> 14.1 us
  transfers between devices with their start and end apart: 76 -> 76, of which waited for: 36 -> 37; matrix products, arithmetic and copies ran while one was open for 33% -> 34% of each run, Pallas kernels for 2% -> 2%
where the time goes in v6:
time: 573 us; the launch traced here: 563 us
  waiting for transfers between devices  244 us (43%)
  starting transfers between devices  86.6 us (15%)
  local copies, waits for them, and re-layouts  81 us (14%)
  matrix products  66.9 us (12%)
  other arithmetic  59.6 us (10%)
  between operations  16.2 us (3%)
  Pallas kernels  8.77 us (2%)
    ppermute x72, waiting for transfers between devices, send(): return lax.ppermute(value, AXES, pairs)  243 us
    ppermute x72, starting transfers between devices, send(): return lax.ppermute(value, AXES, pairs)  80.8 us
    dot_general x39, matrix products, dot(): lax.dot_general(left, right, (((left_dim,), (right_dim,)), ((), ())), pre...  66.9 us
    unnamed x177, local copies, waits for them, and re-layouts  14.1 us
  transfers between devices with their start and end apart: 76, of which 37 were waited for; matrix products, arithmetic and copies ran while one was open for 34% of the time, Pallas kernels for 2%

profile of v6, /device:TPU:4, one launch (start us, length us, event | category | flops | bytes accessed | tf_op | source)
XLA Modules:
  0.0 563.0 jit_solution(4161699189854839892)
XLA Ops:
  10.8 2.8 concatenate.137
  25.3 5.5 collective-permute-start.5
  30.7 5.4 collective-permute-start.7
  40.2 3.0 multiply_sine_fusion
  43.5 37.9 %collective-permute-done.5 = bf16[512,768]{1,0:T(8,128)(2,1)} collective-permute-done((bf16[512,768]{1,0:T(8,128)(2,1)}, bf16[512,768]{1,0:T(8,128)(2,1)}, u32[]{:S(2)}, u32[]{:S(2)}) %collective-permute-start.5) | collective-permute-done | bytes 786464 | tf_op jit(solution)/shard_map/head_weights/ppermute | solution.py:194
  84.0 2.9 constant_dynamic-update-slice_fusion.45
  88.2 5.1 constant_dynamic-slice_fusion.10
  93.3 22.0 %collective-permute-done.6 = bf16[512,768]{1,0:T(8,128)(2,1)} collective-permute-done((bf16[512,768]{1,0:T(8,128)(2,1)}, bf16[512,768]{1,0:T(8,128)(2,1)}, u32[]{:S(2)}, u32[]{:S(2)}) %collective-permute-start.6) | collective-permute-done | bytes 786464 | tf_op jit(solution)/shard_map/head_weights/ppermute | solution.py:194
  117.4 3.2 fusion.4
  120.8 3.0 fusion.2
  130.1 6.7 %collective-permute-done.10 = bf16[192,512]{1,0:T(8,128)(2,1)S(1)} collective-permute-done((bf16[192,512]{1,0:T(8,128)(2,1)S(1)}, bf16[192,512]{1,0:T(8,128)(2,1)S(1)}, u32[]{:S(2)}, u32[]{:S(2)}) %collective-permute-start.10) | collective-permute-done | bytes 196640 | tf_op jit(solution)/shard_map/down_weight_planes/ppermute | solution.py:194
  142.0 4.3 collective-permute-start.15
  148.1 3.5 convolution_convert_fusion.15.v_ref
  154.2 3.7 fusion.126
  157.9 2.9 collective-permute-done.12
  166.2 9.0 %collective-permute-done.13 = bf16[128,2048]{1,0:T(8,128)(2,1)} collective-permute-done((bf16[128,2048]{1,0:T(8,128)(2,1)}, bf16[128,2048]{1,0:T(8,128)(2,1)}, u32[]{:S(2)}, u32[]{:S(2)}) %collective-permute-start.13) | collective-permute-done | bytes 524320 | tf_op jit(solution)/shard_map/cotangent_ring/ppermute | solution.py:194
  175.2 3.5 multiply_convert_fusion.1
  200.0 5.5 collective-permute-done.18
  205.5 11.6 %collective-permute-done.19 = bf16[128,2048]{1,0:T(8,128)(2,1)S(1)} collective-permute-done((bf16[128,2048]{1,0:T(8,128)(2,1)S(1)}, bf16[128,2048]{1,0:T(8,128)(2,1)S(1)}, u32[]{:S(2)}, u32[]{:S(2)}) %collective-permute-start.19) | collective-permute-done | bytes 524320 | tf_op jit(solution)/shard_map/attention_out_sum/ppermute | solution.py:194
  230.0 5.1 collective-permute-done.22
  242.9 8.3 %collective-permute-done.24 = bf16[128,2048]{1,0:T(8,128)(2,1)S(1)} collective-permute-done((bf16[128,2048]{1,0:T(8,128)(2,1)S(1)}, bf16[128,2048]{1,0:T(8,128)(2,1)S(1)}, u32[]{:S(2)}, u32[]{:S(2)}) %collective-permute-start.24) | collective-permute-done | bytes 524320 | tf_op jit(solution)/shard_map/normed_two_ring/ppermute | solution.py:194
  258.4 9.2 %collective-permute-done.28 = bf16[128,2048]{1,0:T(8,128)(2,1)S(1)} collective-permute-done((bf16[128,2048]{1,0:T(8,128)(2,1)S(1)}, bf16[128,2048]{1,0:T(8,128)(2,1)S(1)}, u32[]{:S(2)}, u32[]{:S(2)}) %collective-permute-start.28) | collective-permute-done | bytes 524320 | tf_op jit(solution)/shard_map/normed_two_ring/ppermute | solution.py:194
  277.9 7.1 %collective-permute-done.27 = bf16[128,2048]{1,0:T(8,128)(2,1)S(1)} collective-permute-done((bf16[128,2048]{1,0:T(8,128)(2,1)S(1)}, bf16[128,2048]{1,0:T(8,128)(2,1)S(1)}, u32[]{:S(2)}, u32[]{:S(2)}) %collective-permute-start.27) | collective-permute-done | bytes 524320 | tf_op jit(solution)/shard_map/normed_two_grad_sum/ppermute | solution.py:194
  285.4 3.8 convolution_convert_fusion.3
  294.6 3.7 convolution_convert_fusion.2
  298.3 6.3 %collective-permute-done.35 = bf16[128,2048]{1,0:T(8,128)(2,1)S(1)} collective-permute-done((bf16[128,2048]{1,0:T(8,128)(2,1)S(1)}, bf16[128,2048]{1,0:T(8,128)(2,1)S(1)}, u32[]{:S(2)}, u32[]{:S(2)}) %collective-permute-start.35) | collective-permute-done | bytes 524320 | tf_op jit(solution)/shard_map/normed_two_grad_sum/ppermute | solution.py:194
  306.9 3.7 convolution_convert_fusion.1
  322.0 3.8 fusion.72
  329.1 10.2 %collective-permute-done.42 = bf16[128,2048]{1,0:T(8,128)(2,1)S(1)} collective-permute-done((bf16[128,2048]{1,0:T(8,128)(2,1)S(1)}, bf16[128,2048]{1,0:T(8,128)(2,1)S(1)}, u32[]{:S(2)}, u32[]{:S(2)}) %collective-permute-start.42) | collective-permute-done | bytes 524320 | tf_op jit(solution)/shard_map/out_ring/ppermute | solution.py:194
  343.2 9.1 %collective-permute-done.46 = bf16[128,2048]{1,0:T(8,128)(2,1)S(1)} collective-permute-done((bf16[128,2048]{1,0:T(8,128)(2,1)S(1)}, bf16[128,2048]{1,0:T(8,128)(2,1)S(1)}, u32[]{:S(2)}, u32[]{:S(2)}) %collective-permute-start.46) | collective-permute-done | bytes 524320 | tf_op jit(solution)/shard_map/out_ring/ppermute | solution.py:194
  354.5 6.5 %collective-permute-done.44 = bf16[128,2048]{1,0:T(8,128)(2,1)S(1)} collective-permute-done((bf16[128,2048]{1,0:T(8,128)(2,1)S(1)}, bf16[128,2048]{1,0:T(8,128)(2,1)S(1)}, u32[]{:S(2)}, u32[]{:S(2)}) %collective-permute-start.44) | collective-permute-done | bytes 524320 | tf_op jit(solution)/shard_map/attention_grad_columns/ppermute | solution.py:194
  371.9 3.6 fusion.132
  382.8 6.0 %collective-permute-done.48 = bf16[128,2048]{1,0:T(8,128)(2,1)S(1)} collective-permute-done((bf16[128,2048]{1,0:T(8,128)(2,1)}, bf16[128,2048]{1,0:T(8,128)(2,1)S(1)}, u32[]{:S(2)}, u32[]{:S(2)}) %collective-permute-start.48) | collective-permute-done | bytes 524320 | tf_op jit(solution)/shard_map/out_ring/ppermute | solution.py:194
  389.9 2.9 select_bitcast_fusion.1
  393.2 7.3 %collective-permute-done.51 = bf16[64,1536]{1,0:T(8,128)(2,1)S(1)} collective-permute-done((bf16[64,1536]{1,0:T(8,128)(2,1)S(1)}, bf16[64,1536]{1,0:T(8,128)(2,1)S(1)}, u32[]{:S(2)}, u32[]{:S(2)}) %collective-permute-start.51) | collective-permute-done | bytes 196640 | tf_op jit(solution)/shard_map/down_gradient_planes/ppermute | solution.py:194
  405.4 4.3 fusion.46
  411.1 4.9 collective-permute-start.53
  416.1 6.1 %shard_map.264 = (f32[1024,256]{1,0:T(8,128)S(1)}, f32[1024,128]{1,0:T(8,128)S(1)}, f32[1024,128]{1,0:T(8,128)S(1)}) custom-call(bf16[1024,256]{1,0:T(8,128)(2,1)S(1)} %pad_maximum_fusion.4.q_ref, bf16[1024,128]{1,0:T(8,128)(2,1)S(1)} %pad_maximum_fusion.9.k_ref, bf16[1024,128]{1,0:T(8,128)(2,1)S(1)} %convolution_convert_fusion.15.v_ref, ...), custom_call_target="tpu_custom_call" | custom-call | flops 1879048192 | bytes 6291456 | tf_op jit(solution)/shard_map/pallas_call | solution.py:141
  422.3 5.1 collective-permute-done.53
  444.4 6.5 %fusion.3 = (f32[2048]{0:T(1024)S(1)}, bf16[1024,2048]{1,0:T(8,128)(2,1)S(1)}) fusion(bf16[1,1024,2048]{2,1,0:T(8,128)(2,1)} %all-gather.6.cloned.1.call-done, f32[1024]{0:T(1024)S(1)} %copy-done.71, bf16[1024,768]{1,0:T(8,128)(2,1)} %copy-done.62, bf16[2048,256]{1,0:T(8,128)(2,1)} %get-tuple-element.314, bf16[2048,256]{1,0:T(8,128)(2,1)S(1)} %copy-done.46, ...), kind=kOutput, calls=%fused_computation.5 | convolution fusion | flops 3241146368 | bytes 13119488 | tf_op jit(solution)/shard_map/dot_general | solution.py:18
  458.7 5.7 %all-to-all-start = ((bf16[8,64,256]{2,1,0:T(8,128)(2,1)}), bf16[8,64,256]{2,1,0:T(8,128)(2,1)S(1)}, u32[]{:S(2)}, u32[]{:S(2)}) async-start(bf16[8,64,256]{2,1,0:T(8,128)(2,1)} %reshape.241), calls=%async_computation.1 | async-start | bytes 524288 | tf_op jit(solution)/shard_map/all_to_all | solution.py:743
  464.4 3.2 fusion.5
  473.2 10.2 %collective-permute-done.59 = bf16[128,2048]{1,0:T(8,128)(2,1)S(1)} collective-permute-done((bf16[128,2048]{1,0:T(8,128)(2,1)S(1)}, bf16[128,2048]{1,0:T(8,128)(2,1)S(1)}, u32[]{:S(2)}, u32[]{:S(2)}) %collective-permute-start.59) | collective-permute-done | bytes 524320 | tf_op jit(solution)/shard_map/qkv_gradient_sum/ppermute | solution.py:194
  485.3 11.1 %collective-permute-done.57 = bf16[128,2048]{1,0:T(8,128)(2,1)} collective-permute-done((bf16[128,2048]{1,0:T(8,128)(2,1)}, bf16[128,2048]{1,0:T(8,128)(2,1)}, u32[]{:S(2)}, u32[]{:S(2)}) %collective-permute-start.57) | collective-permute-done | bytes 524320 | tf_op jit(solution)/shard_map/normed_grad_sum/ppermute | solution.py:194
  510.1 3.6 collective-permute-start.66
  514.7 3.4 collective-permute-start.71
  518.1 4.2 collective-permute-start.70
  525.3 27.2 %collective-permute-done.71 = bf16[192,2048]{1,0:T(8,128)(2,1)S(1)} collective-permute-done((bf16[192,2048]{1,0:T(8,128)(2,1)S(1)}, bf16[192,2048]{1,0:T(8,128)(2,1)S(1)}, u32[]{:S(2)}, u32[]{:S(2)}) %collective-permute-start.71) | collective-permute-done | bytes 786464 | tf_op jit(solution)/shard_map/up_gradient_move/ppermute | solution.py:194
  (495 shorter events, 213.3 us)
Async XLA Ops:
  7.2 110.2 %all-gather.6.cloned.1.call-start = ((), (), s32[]{:S(2)}) async-start(), calls=%async_computation.4 | async-start | bytes 4718592 | tf_op jit(solution)/shard_map/input_gather/all_gather | solution.py:349
  7.9 122.2 %all-gather.4.cloned.1.call-start = ((), (), s32[]{:S(2)}) async-start(), calls=%async_computation.2 | async-start | bytes 1310720 | tf_op jit(solution)/shard_map/output_weight_gather/all_gather | solution.py:383
  25.3 56.0 %collective-permute-start.5 = (bf16[512,768]{1,0:T(8,128)(2,1)}, bf16[512,768]{1,0:T(8,128)(2,1)}, u32[]{:S(2)}, u32[]{:S(2)}) collective-permute-start(bf16[512,768]{1,0:T(8,128)(2,1)} %pad_maximum_fusion.3), channel_id=1, source_target_pairs={{0,0},{1,9},{2,18},{3,27},{4,4},{5,13},{6,22},{7,31},{8,1},{9,10},... | collective-permute-start | bytes 2359304 | tf_op jit(solution)/shard_map/head_weights/ppermute | solution.py:194
  30.7 93.1 %collective-permute-start.7 = (bf16[512,768]{1,0:T(8,128)(2,1)}, bf16[512,768]{1,0:T(8,128)(2,1)}, u32[]{:S(2)}, u32[]{:S(2)}) collective-permute-start(bf16[512,768]{1,0:T(8,128)(2,1)} %pad_maximum_fusion.3), channel_id=1, source_target_pairs={{0,2},{1,11},{2,16},{3,25},{4,6},{5,15},{6,20},{7,29},{8,3},{9,8},... | collective-permute-start | bytes 2359304 | tf_op jit(solution)/shard_map/head_weights/ppermute | solution.py:194
  36.2 87.6 %collective-permute-start.8 = (bf16[512,768]{1,0:T(8,128)(2,1)}, bf16[512,768]{1,0:T(8,128)(2,1)}, u32[]{:S(2)}, u32[]{:S(2)}) collective-permute-start(bf16[512,768]{1,0:T(8,128)(2,1)} %pad_maximum_fusion.3), channel_id=1, source_target_pairs={{0,3},{1,8},{2,17},{3,26},{4,7},{5,12},{6,21},{7,30},{8,0},{9,9},{... | collective-permute-start | bytes 2359304 | tf_op jit(solution)/shard_map/head_weights/ppermute | solution.py:194
  38.1 77.2 %collective-permute-start.6 = (bf16[512,768]{1,0:T(8,128)(2,1)}, bf16[512,768]{1,0:T(8,128)(2,1)}, u32[]{:S(2)}, u32[]{:S(2)}) collective-permute-start(bf16[512,768]{1,0:T(8,128)(2,1)} %pad_maximum_fusion.3), channel_id=1, source_target_pairs={{0,1},{1,10},{2,19},{3,24},{4,5},{5,14},{6,23},{7,28},{8,2},{9,11}... | collective-permute-start | bytes 2359304 | tf_op jit(solution)/shard_map/head_weights/ppermute | solution.py:194
  82.1 361.3 %reduce-scatter.2.cloned.1.call-start = ((), (), s32[]{:S(2)}) async-start(), calls=%async_computation.3 | async-start | bytes 7864320 | tf_op jit(solution)/shard_map/feed_gradient_columns/reduce_scatter | solution.py:611
  142.0 37.9 %collective-permute-start.14 = (bf16[192,2048]{1,0:T(8,128)(2,1)}, bf16[192,2048]{1,0:T(8,128)(2,1)}, u32[]{:S(2)}, u32[]{:S(2)}) collective-permute-start(bf16[192,2048]{1,0:T(8,128)(2,1)} %constant_dynamic-update-slice_fusion.38), channel_id=1, source_target_pairs={{0,8},{1,9},{2,10},{3,11},{4,12},{5,13},{6,14},{7,15},{8,0},{9,1},... | collective-permute-start | bytes 2359304 | tf_op jit(solution)/shard_map/down_weight_columns/ppermute | solution.py:194
  142.0 38.0 %collective-permute-start.15 = (bf16[192,2048]{1,0:T(8,128)(2,1)}, bf16[192,2048]{1,0:T(8,128)(2,1)}, u32[]{:S(2)}, u32[]{:S(2)}) collective-permute-start(bf16[192,2048]{1,0:T(8,128)(2,1)} %constant_dynamic-update-slice_fusion.38), channel_id=1, source_target_pairs={{0,16},{1,17},{2,18},{3,19},{4,20},{5,21},{6,22},{7,23},{8,24},{9,... | collective-permute-start | bytes 2359304 | tf_op jit(solution)/shard_map/down_weight_columns/ppermute | solution.py:194
  146.4 33.7 %collective-permute-start.16 = (bf16[192,2048]{1,0:T(8,128)(2,1)}, bf16[192,2048]{1,0:T(8,128)(2,1)}, u32[]{:S(2)}, u32[]{:S(2)}) collective-permute-start(bf16[192,2048]{1,0:T(8,128)(2,1)} %constant_dynamic-update-slice_fusion.38), channel_id=1, source_target_pairs={{0,24},{1,25},{2,26},{3,27},{4,28},{5,29},{6,30},{7,31},{8,16},{9,... | collective-permute-start | bytes 2359304 | tf_op jit(solution)/shard_map/down_weight_columns/ppermute | solution.py:194
  183.6 16.4 %collective-permute-start.31 = (bf16[128,2048]{1,0:T(8,128)(2,1)}, bf16[128,2048]{1,0:T(8,128)(2,1)S(1)}, u32[]{:S(2)}, u32[]{:S(2)}) collective-permute-start(bf16[128,2048]{1,0:T(8,128)(2,1)} %collective-permute-done.13), channel_id=1, source_target_pairs={{0,1},{1,2},{2,3},{3,0},{4,5},{5,6},{6,7},{7,4},{8,9},{9,10},{10,1... | collective-permute-start | bytes 1572872 | tf_op jit(solution)/shard_map/cotangent_ring/ppermute | solution.py:194
  185.2 32.6 %collective-permute-start.21 = (bf16[3,128,2048]{2,1,0:T(8,128)(2,1)S(1)}, bf16[3,128,2048]{2,1,0:T(8,128)(2,1)S(1)}, u32[]{:S(2)}, u32[]{:S(2)}) collective-permute-start(bf16[3,128,2048]{2,1,0:T(8,128)(2,1)S(1)} %pad_maximum_fusion.2), channel_id=1, source_target_pairs={{0,4},{1,5},{2,6},{3,7},{4,0},{5,1},{6,2},{7,3},{8,12},{9,13},{10,... | collective-permute-start | bytes 4718600 | tf_op jit(solution)/shard_map/cotangent_core/ppermute | solution.py:194
  190.6 14.8 %collective-permute-start.18 = (bf16[128,2048]{1,0:T(8,128)(2,1)S(1)}, bf16[128,2048]{1,0:T(8,128)(2,1)S(1)}, u32[]{:S(2)}, u32[]{:S(2)}) collective-permute-start(bf16[128,2048]{1,0:T(8,128)(2,1)S(1)} %get-tuple-element.330), channel_id=1, source_target_pairs={{0,8},{1,9},{2,10},{3,11},{4,12},{5,13},{6,14},{7,15},{8,0},{9,1},... | collective-permute-start | bytes 1572872 | tf_op jit(solution)/shard_map/attention_out_sum/ppermute | solution.py:194
  192.1 24.9 %collective-permute-start.19 = (bf16[128,2048]{1,0:T(8,128)(2,1)S(1)}, bf16[128,2048]{1,0:T(8,128)(2,1)S(1)}, u32[]{:S(2)}, u32[]{:S(2)}) collective-permute-start(bf16[128,2048]{1,0:T(8,128)(2,1)S(1)} %get-tuple-element.332), channel_id=1, source_target_pairs={{0,16},{1,17},{2,18},{3,19},{4,20},{5,21},{6,22},{7,23},{8,24},{9,... | collective-permute-start | bytes 1572872 | tf_op jit(solution)/shard_map/attention_out_sum/ppermute | solution.py:194
  193.6 23.5 %collective-permute-start.20 = (bf16[128,2048]{1,0:T(8,128)(2,1)S(1)}, bf16[128,2048]{1,0:T(8,128)(2,1)S(1)}, u32[]{:S(2)}, u32[]{:S(2)}) collective-permute-start(bf16[128,2048]{1,0:T(8,128)(2,1)S(1)} %get-tuple-element.331), channel_id=1, source_target_pairs={{0,24},{1,25},{2,26},{3,27},{4,28},{5,29},{6,30},{7,31},{8,16},{9,... | collective-permute-start | bytes 1572872 | tf_op jit(solution)/shard_map/attention_out_sum/ppermute | solution.py:194
  200.0 23.4 %collective-permute-start.32 = (bf16[128,2048]{1,0:T(8,128)(2,1)S(1)}, bf16[128,2048]{1,0:T(8,128)(2,1)S(1)}, u32[]{:S(2)}, u32[]{:S(2)}) collective-permute-start(bf16[128,2048]{1,0:T(8,128)(2,1)S(1)} %collective-permute-done.31), channel_id=1, source_target_pairs={{0,4},{1,5},{2,6},{3,7},{4,0},{5,1},{6,2},{7,3},{8,12},{9,13},{10,... | collective-permute-start | bytes 1572872 | tf_op jit(solution)/shard_map/cotangent_core/ppermute | solution.py:194
  218.6 16.5 %collective-permute-start.22 = (bf16[128,2048]{1,0:T(8,128)(2,1)S(1)}, bf16[128,2048]{1,0:T(8,128)(2,1)S(1)}, u32[]{:S(2)}, u32[]{:S(2)}) collective-permute-start(bf16[128,2048]{1,0:T(8,128)(2,1)S(1)} %multiply_convert_fusion), channel_id=1, source_target_pairs={{0,1},{1,2},{2,3},{3,0},{4,5},{5,6},{6,7},{7,4},{8,9},{9,10},{10,1... | collective-permute-start | bytes 1572872 | tf_op jit(solution)/shard_map/normed_two_ring/ppermute | solution.py:194
  235.1 16.1 %collective-permute-start.24 = (bf16[128,2048]{1,0:T(8,128)(2,1)S(1)}, bf16[128,2048]{1,0:T(8,128)(2,1)S(1)}, u32[]{:S(2)}, u32[]{:S(2)}) collective-permute-start(bf16[128,2048]{1,0:T(8,128)(2,1)S(1)} %collective-permute-done.22), channel_id=1, source_target_pairs={{0,1},{1,2},{2,3},{3,0},{4,5},{5,6},{6,7},{7,4},{8,9},{9,10},{10,1... | collective-permute-start | bytes 1572872 | tf_op jit(solution)/shard_map/normed_two_ring/ppermute | solution.py:194
  237.1 80.2 %collective-permute-start.37 = (bf16[128,2048]{1,0:T(8,128)(2,1)}, bf16[128,2048]{1,0:T(8,128)(2,1)}, u32[]{:S(2)}, u32[]{:S(2)}) collective-permute-start(bf16[128,2048]{1,0:T(8,128)(2,1)} %slice.216), channel_id=1, source_target_pairs={{0,4},{1,5},{2,6},{3,7},{4,0},{5,1},{6,2},{7,3},{8,12},{9,13},{10,... | collective-permute-start | bytes 1572872 | tf_op jit(solution)/shard_map/normed_two_grad_core/ppermute | solution.py:194
  251.3 16.3 %collective-permute-start.28 = (bf16[128,2048]{1,0:T(8,128)(2,1)S(1)}, bf16[128,2048]{1,0:T(8,128)(2,1)S(1)}, u32[]{:S(2)}, u32[]{:S(2)}) collective-permute-start(bf16[128,2048]{1,0:T(8,128)(2,1)S(1)} %collective-permute-done.24), channel_id=1, source_target_pairs={{0,1},{1,2},{2,3},{3,0},{4,5},{5,6},{6,7},{7,4},{8,9},{9,10},{10,1... | collective-permute-start | bytes 1572872 | tf_op jit(solution)/shard_map/normed_two_ring/ppermute | solution.py:194
  252.5 16.0 %collective-permute-start.26 = (bf16[128,2048]{1,0:T(8,128)(2,1)S(1)}, bf16[128,2048]{1,0:T(8,128)(2,1)S(1)}, u32[]{:S(2)}, u32[]{:S(2)}) collective-permute-start(bf16[128,2048]{1,0:T(8,128)(2,1)S(1)} %slice.200), channel_id=1, source_target_pairs={{0,4},{1,5},{2,6},{3,7},{4,0},{5,1},{6,2},{7,3},{8,12},{9,13},{10,... | collective-permute-start | bytes 1572872 | tf_op jit(solution)/shard_map/normed_two_grad_core/ppermute | solution.py:194
  268.8 16.2 %collective-permute-start.27 = (bf16[128,2048]{1,0:T(8,128)(2,1)S(1)}, bf16[128,2048]{1,0:T(8,128)(2,1)S(1)}, u32[]{:S(2)}, u32[]{:S(2)}) collective-permute-start(bf16[128,2048]{1,0:T(8,128)(2,1)S(1)} %add_convert_fusion.10), channel_id=1, source_target_pairs={{0,1},{1,2},{2,3},{3,0},{4,5},{5,6},{6,7},{7,4},{8,9},{9,10},{10,1... | collective-permute-start | bytes 1572872 | tf_op jit(solution)/shard_map/normed_two_grad_sum/ppermute | solution.py:194
  268.9 16.1 %collective-permute-start.30 = (bf16[128,2048]{1,0:T(8,128)(2,1)S(1)}, bf16[128,2048]{1,0:T(8,128)(2,1)S(1)}, u32[]{:S(2)}, u32[]{:S(2)}) collective-permute-start(bf16[128,2048]{1,0:T(8,128)(2,1)S(1)} %slice.204), channel_id=1, source_target_pairs={{0,4},{1,5},{2,6},{3,7},{4,0},{5,1},{6,2},{7,3},{8,12},{9,13},{10,... | collective-permute-start | bytes 1572872 | tf_op jit(solution)/shard_map/normed_two_grad_core/ppermute | solution.py:194
  289.2 15.4 %collective-permute-start.35 = (bf16[128,2048]{1,0:T(8,128)(2,1)S(1)}, bf16[128,2048]{1,0:T(8,128)(2,1)S(1)}, u32[]{:S(2)}, u32[]{:S(2)}) collective-permute-start(bf16[128,2048]{1,0:T(8,128)(2,1)S(1)} %add_convert_fusion.8), channel_id=1, source_target_pairs={{0,1},{1,2},{2,3},{3,0},{4,5},{5,6},{6,7},{7,4},{8,9},{9,10},{10,1... | collective-permute-start | bytes 1572872 | tf_op jit(solution)/shard_map/normed_two_grad_sum/ppermute | solution.py:194
  290.8 31.2 %collective-permute-start.38 = (bf16[4,128,2048]{2,1,0:T(8,128)(2,1)}, bf16[4,128,2048]{2,1,0:T(8,128)(2,1)}, u32[]{:S(2)}, u32[]{:S(2)}) collective-permute-start(bf16[4,128,2048]{2,1,0:T(8,128)(2,1)} %pad_maximum_fusion.1), channel_id=1, source_target_pairs={{0,4},{1,5},{2,6},{3,7},{4,0},{5,1},{6,2},{7,3},{8,12},{9,13},{10,... | collective-permute-start | bytes 6291464 | tf_op jit(solution)/shard_map/out_core/ppermute | solution.py:194
  292.5 47.0 %collective-permute-start.39 = (bf16[512,768]{1,0:T(8,128)(2,1)}, bf16[512,768]{1,0:T(8,128)(2,1)}, u32[]{:S(2)}, u32[]{:S(2)}) collective-permute-start(bf16[512,768]{1,0:T(8,128)(2,1)} %get-tuple-element.317), channel_id=1, source_target_pairs={{0,8},{1,9},{2,10},{3,11},{4,12},{5,13},{6,14},{7,15},{8,0},{9,1},... | collective-permute-start | bytes 2359304 | tf_op jit(solution)/shard_map/down_gradient_columns/ppermute | solution.py:194
  293.7 45.8 %collective-permute-start.40 = (bf16[512,768]{1,0:T(8,128)(2,1)}, bf16[512,768]{1,0:T(8,128)(2,1)}, u32[]{:S(2)}, u32[]{:S(2)}) collective-permute-start(bf16[512,768]{1,0:T(8,128)(2,1)} %get-tuple-element.316), channel_id=1, source_target_pairs={{0,16},{1,17},{2,18},{3,19},{4,20},{5,21},{6,22},{7,23},{8,24},{9,... | collective-permute-start | bytes 2359304 | tf_op jit(solution)/shard_map/down_gradient_columns/ppermute | solution.py:194
  305.5 15.1 %collective-permute-start.36 = (bf16[128,2048]{1,0:T(8,128)(2,1)}, bf16[128,2048]{1,0:T(8,128)(2,1)S(1)}, u32[]{:S(2)}, u32[]{:S(2)}) collective-permute-start(bf16[128,2048]{1,0:T(8,128)(2,1)} %add_convert_fusion.6), channel_id=1, source_target_pairs={{0,1},{1,2},{2,3},{3,0},{4,5},{5,6},{6,7},{7,4},{8,9},{9,10},{10,1... | collective-permute-start | bytes 1572872 | tf_op jit(solution)/shard_map/normed_two_grad_sum/ppermute | solution.py:194
  317.3 22.2 %collective-permute-start.41 = (bf16[512,768]{1,0:T(8,128)(2,1)}, bf16[512,768]{1,0:T(8,128)(2,1)S(1)}, u32[]{:S(2)}, u32[]{:S(2)}) collective-permute-start(bf16[512,768]{1,0:T(8,128)(2,1)} %get-tuple-element.315), channel_id=1, source_target_pairs={{0,24},{1,25},{2,26},{3,27},{4,28},{5,29},{6,30},{7,31},{8,16},{9,... | collective-permute-start | bytes 2359304 | tf_op jit(solution)/shard_map/down_gradient_columns/ppermute | solution.py:194
  339.6 14.9 %collective-permute-start.43 = (bf16[128,2048]{1,0:T(8,128)(2,1)S(1)}, bf16[128,2048]{1,0:T(8,128)(2,1)S(1)}, u32[]{:S(2)}, u32[]{:S(2)}) collective-permute-start(bf16[128,2048]{1,0:T(8,128)(2,1)S(1)} %get-tuple-element.236), channel_id=1, source_target_pairs={{0,8},{1,9},{2,10},{3,11},{4,12},{5,13},{6,14},{7,15},{8,0},{9,1},... | collective-permute-start | bytes 1572872 | tf_op jit(solution)/shard_map/attention_grad_columns/ppermute | solution.py:194
  340.9 20.2 %collective-permute-start.44 = (bf16[128,2048]{1,0:T(8,128)(2,1)S(1)}, bf16[128,2048]{1,0:T(8,128)(2,1)S(1)}, u32[]{:S(2)}, u32[]{:S(2)}) collective-permute-start(bf16[128,2048]{1,0:T(8,128)(2,1)S(1)} %get-tuple-element.236), channel_id=1, source_target_pairs={{0,16},{1,17},{2,18},{3,19},{4,20},{5,21},{6,22},{7,23},{8,24},{9,... | collective-permute-start | bytes 1572872 | tf_op jit(solution)/shard_map/attention_grad_columns/ppermute | solution.py:194
  341.7 21.1 %collective-permute-start.45 = (bf16[128,2048]{1,0:T(8,128)(2,1)S(1)}, bf16[128,2048]{1,0:T(8,128)(2,1)}, u32[]{:S(2)}, u32[]{:S(2)}) collective-permute-start(bf16[128,2048]{1,0:T(8,128)(2,1)S(1)} %get-tuple-element.236), channel_id=1, source_target_pairs={{0,24},{1,25},{2,26},{3,27},{4,28},{5,29},{6,30},{7,31},{8,16},{9,... | collective-permute-start | bytes 1572872 | tf_op jit(solution)/shard_map/attention_grad_columns/ppermute | solution.py:194
  368.8 21.0 %collective-permute-start.47 = (bf16[4,128,2048]{2,1,0:T(8,128)(2,1)}, bf16[4,128,2048]{2,1,0:T(8,128)(2,1)}, u32[]{:S(2)}, u32[]{:S(2)}) collective-permute-start(bf16[4,128,2048]{2,1,0:T(8,128)(2,1)} %bitcast_dynamic-update-slice_fusion.8), channel_id=1, source_target_pairs={{0,4},{1,5},{2,6},{3,7},{4,0},{5,1},{6,2},{7,3},{8,12},{9,13},{10,... | collective-permute-start | bytes 6291464 | tf_op jit(solution)/shard_map/attention_grad_core/ppermute | solution.py:194
  371.8 17.0 %collective-permute-start.48 = (bf16[128,2048]{1,0:T(8,128)(2,1)}, bf16[128,2048]{1,0:T(8,128)(2,1)S(1)}, u32[]{:S(2)}, u32[]{:S(2)}) collective-permute-start(bf16[128,2048]{1,0:T(8,128)(2,1)} %add_convert_fusion.4), channel_id=1, source_target_pairs={{0,1},{1,2},{2,3},{3,0},{4,5},{5,6},{6,7},{7,4},{8,9},{9,10},{10,1... | collective-permute-start | bytes 1572872 | tf_op jit(solution)/shard_map/out_ring/ppermute | solution.py:194
  375.8 17.3 %collective-permute-start.50 = (bf16[64,1536]{1,0:T(8,128)(2,1)S(1)}, bf16[64,1536]{1,0:T(8,128)(2,1)S(1)}, u32[]{:S(2)}, u32[]{:S(2)}) collective-permute-start(bf16[64,1536]{1,0:T(8,128)(2,1)S(1)} %get-tuple-element.389), channel_id=1, source_target_pairs={{0,1},{1,2},{2,3},{3,0},{4,5},{5,6},{6,7},{7,4},{8,9},{9,10},{10,1... | collective-permute-start | bytes 589832 | tf_op jit(solution)/shard_map/down_gradient_planes/ppermute | solution.py:194
  377.6 22.9 %collective-permute-start.51 = (bf16[64,1536]{1,0:T(8,128)(2,1)S(1)}, bf16[64,1536]{1,0:T(8,128)(2,1)S(1)}, u32[]{:S(2)}, u32[]{:S(2)}) collective-permute-start(bf16[64,1536]{1,0:T(8,128)(2,1)S(1)} %get-tuple-element.388), channel_id=1, source_target_pairs={{0,2},{1,3},{2,0},{3,1},{4,6},{5,7},{6,4},{7,5},{8,10},{9,11},{10,... | collective-permute-start | bytes 589832 | tf_op jit(solution)/shard_map/down_gradient_planes/ppermute | solution.py:194
  380.1 20.4 %collective-permute-start.52 = (bf16[64,1536]{1,0:T(8,128)(2,1)S(1)}, bf16[64,1536]{1,0:T(8,128)(2,1)S(1)}, u32[]{:S(2)}, u32[]{:S(2)}) collective-permute-start(bf16[64,1536]{1,0:T(8,128)(2,1)S(1)} %get-tuple-element.387), channel_id=1, source_target_pairs={{0,3},{1,0},{2,1},{3,2},{4,7},{5,4},{6,5},{7,6},{8,11},{9,8},{10,9... | collective-permute-start | bytes 589832 | tf_op jit(solution)/shard_map/down_gradient_planes/ppermute | solution.py:194
  411.1 16.3 %collective-permute-start.53 = (bf16[128,2048]{1,0:T(8,128)(2,1)S(1)}, bf16[128,2048]{1,0:T(8,128)(2,1)S(1)}, u32[]{:S(2)}, u32[]{:S(2)}) collective-permute-start(bf16[128,2048]{1,0:T(8,128)(2,1)S(1)} %fusion.89), channel_id=1, source_target_pairs={{0,1},{1,2},{2,3},{3,0},{4,5},{5,6},{6,7},{7,4},{8,9},{9,10},{10,1... | collective-permute-start | bytes 1572872 | tf_op jit(solution)/shard_map/early_ring/ppermute | solution.py:194
  427.5 14.9 %collective-permute-start.54 = (bf16[128,2048]{1,0:T(8,128)(2,1)S(1)}, bf16[128,2048]{1,0:T(8,128)(2,1)S(1)}, u32[]{:S(2)}, u32[]{:S(2)}) collective-permute-start(bf16[128,2048]{1,0:T(8,128)(2,1)S(1)} %fusion.71), channel_id=1, source_target_pairs={{0,1},{1,2},{2,3},{3,0},{4,5},{5,6},{6,7},{7,4},{8,9},{9,10},{10,1... | collective-permute-start | bytes 1572872 | tf_op jit(solution)/shard_map/early_ring/ppermute | solution.py:194
  458.7 25.7 %all-to-all-start = ((bf16[8,64,256]{2,1,0:T(8,128)(2,1)}), bf16[8,64,256]{2,1,0:T(8,128)(2,1)S(1)}, u32[]{:S(2)}, u32[]{:S(2)}) async-start(bf16[8,64,256]{2,1,0:T(8,128)(2,1)} %reshape.241), calls=%async_computation.1 | async-start | bytes 524288 | tf_op jit(solution)/shard_map/all_to_all | solution.py:743
  467.6 15.8 %collective-permute-start.59 = (bf16[128,2048]{1,0:T(8,128)(2,1)S(1)}, bf16[128,2048]{1,0:T(8,128)(2,1)S(1)}, u32[]{:S(2)}, u32[]{:S(2)}) collective-permute-start(bf16[128,2048]{1,0:T(8,128)(2,1)S(1)} %copy-done.49), channel_id=1, source_target_pairs={{0,1},{1,2},{2,3},{3,0},{4,5},{5,6},{6,7},{7,4},{8,9},{9,10},{10,1... | collective-permute-start | bytes 1572872 | tf_op jit(solution)/shard_map/qkv_gradient_sum/ppermute | solution.py:194
  469.7 15.6 %collective-permute-start.56 = (bf16[128,2048]{1,0:T(8,128)(2,1)}, bf16[128,2048]{1,0:T(8,128)(2,1)}, u32[]{:S(2)}, u32[]{:S(2)}) collective-permute-start(bf16[128,2048]{1,0:T(8,128)(2,1)} %get-tuple-element.319), channel_id=1, source_target_pairs={{0,8},{1,9},{2,10},{3,11},{4,12},{5,13},{6,14},{7,15},{8,0},{9,1},... | collective-permute-start | bytes 1572872 | tf_op jit(solution)/shard_map/normed_grad_sum/ppermute | solution.py:194
  471.2 25.2 %collective-permute-start.57 = (bf16[128,2048]{1,0:T(8,128)(2,1)}, bf16[128,2048]{1,0:T(8,128)(2,1)}, u32[]{:S(2)}, u32[]{:S(2)}) collective-permute-start(bf16[128,2048]{1,0:T(8,128)(2,1)} %get-tuple-element.321), channel_id=1, source_target_pairs={{0,16},{1,17},{2,18},{3,19},{4,20},{5,21},{6,22},{7,23},{8,24},{9,... | collective-permute-start | bytes 1572872 | tf_op jit(solution)/shard_map/normed_grad_sum/ppermute | solution.py:194
  471.7 24.7 %collective-permute-start.58 = (bf16[128,2048]{1,0:T(8,128)(2,1)}, bf16[128,2048]{1,0:T(8,128)(2,1)}, u32[]{:S(2)}, u32[]{:S(2)}) collective-permute-start(bf16[128,2048]{1,0:T(8,128)(2,1)} %get-tuple-element.320), channel_id=1, source_target_pairs={{0,24},{1,25},{2,26},{3,27},{4,28},{5,29},{6,30},{7,31},{8,16},{9,... | collective-permute-start | bytes 1572872 | tf_op jit(solution)/shard_map/normed_grad_sum/ppermute | solution.py:194
  484.4 15.3 %collective-permute-start.60 = (bf16[128,2048]{1,0:T(8,128)(2,1)}, bf16[128,2048]{1,0:T(8,128)(2,1)}, u32[]{:S(2)}, u32[]{:S(2)}) collective-permute-start(bf16[128,2048]{1,0:T(8,128)(2,1)} %add_convert_fusion.2), channel_id=1, source_target_pairs={{0,1},{1,2},{2,3},{3,0},{4,5},{5,6},{6,7},{7,4},{8,9},{9,10},{10,1... | collective-permute-start | bytes 1572872 | tf_op jit(solution)/shard_map/qkv_gradient_sum/ppermute | solution.py:194
  502.2 21.3 %collective-permute-start.68 = (bf16[128,2048]{1,0:T(8,128)(2,1)}, bf16[128,2048]{1,0:T(8,128)(2,1)S(1)}, u32[]{:S(2)}, u32[]{:S(2)}) collective-permute-start(bf16[128,2048]{1,0:T(8,128)(2,1)} %add_convert_fusion.1), channel_id=1, source_target_pairs={{0,1},{1,2},{2,3},{3,0},{4,5},{5,6},{6,7},{7,4},{8,9},{9,10},{10,1... | collective-permute-start | bytes 1572872 | tf_op jit(solution)/shard_map/qkv_gradient_sum/ppermute | solution.py:194
  514.7 37.9 %collective-permute-start.71 = (bf16[192,2048]{1,0:T(8,128)(2,1)S(1)}, bf16[192,2048]{1,0:T(8,128)(2,1)S(1)}, u32[]{:S(2)}, u32[]{:S(2)}) collective-permute-start(bf16[192,2048]{1,0:T(8,128)(2,1)S(1)} %get-tuple-element.333), channel_id=1, source_target_pairs={{0,2},{1,11},{2,16},{3,25},{4,6},{5,15},{6,20},{7,29},{8,3},{9,8},... | collective-permute-start | bytes 2359304 | tf_op jit(solution)/shard_map/up_gradient_move/ppermute | solution.py:194
  518.1 36.9 %collective-permute-start.70 = (bf16[192,2048]{1,0:T(8,128)(2,1)S(1)}, bf16[192,2048]{1,0:T(8,128)(2,1)S(1)}, u32[]{:S(2)}, u32[]{:S(2)}) collective-permute-start(bf16[192,2048]{1,0:T(8,128)(2,1)S(1)} %get-tuple-element.334), channel_id=1, source_target_pairs={{0,0},{1,9},{2,18},{3,27},{4,4},{5,13},{6,22},{7,31},{8,1},{9,10},... | collective-permute-start | bytes 2359304 | tf_op jit(solution)/shard_map/gate_gradient_move/ppermute | solution.py:194
  (104 other events, 1301.6 us)
Sparse Core Ops, SparseCore 0:
  9.9 59.3 all-gather.5
  82.2 34.4 all-gather.3
  362.9 71.1 reduce-scatter.1
